TPU v7x, 32 devices: a whole 2x2x4 slice. The times are simulated.
32 devices in a mesh: dp: 8 (over y, x, core), mp: 4 (over z).
Axes of the slice: x: 2, y: 2, z: 4, core: 2. Of those that a mesh axis runs over, the one named last changes fastest.
Arguments:
- inputs: bfloat16 [16384, 2048], P('dp', 'mp'), may hold values from -8 to 8, as said below
- cotangent: bfloat16 [16384, 2048], P('dp', 'mp'), may hold values from -6 to 6
- reset_mask: int32 [16384], P('dp'), may hold values 0 or 1
- norm1_gain: bfloat16 [2048], P(('mp', 'dp')), may hold values from 0.25 to 1.75
- w_input: bfloat16 [2048, 2560], P('dp', 'mp'), may hold values from -0.125 to 0.125
- w_branch: bfloat16 [2048, 2560], P('dp', 'mp'), may hold values from -0.125 to 0.125
- w_output: bfloat16 [2560, 2048], P('mp', 'dp'), may hold values from -0.3125 to 0.3125
- conv_weight: bfloat16 [4, 2560], P(None, ('mp', 'dp')), may hold values from -3 to 3
- conv_bias: bfloat16 [2560], P(('mp', 'dp')), may hold values from -3 to 3
- gate_a_weight: bfloat16 [16, 160, 160], P('mp', 'dp'), may hold values from -0.5 to 0.5
- gate_a_bias: bfloat16 [2560], P(('mp', 'dp')), may hold values from -3 to 3
- gate_x_weight: bfloat16 [16, 160, 160], P('mp', 'dp'), may hold values from -0.5 to 0.5
- gate_x_bias: bfloat16 [2560], P(('mp', 'dp')), may hold values from -3 to 3
- decay_param: bfloat16 [2560], P(('mp', 'dp')), may hold values from -8 to -2
- norm2_gain: bfloat16 [2048], P(('mp', 'dp')), may hold values from 0.25 to 1.75
- w_gate: bfloat16 [2048, 6144], P('dp', 'mp'), may hold values from -0.125 to 0.125
- w_up: bfloat16 [2048, 6144], P('dp', 'mp'), may hold values from -0.125 to 0.125
- w_down: bfloat16 [6144, 2048], P('mp', 'dp'), may hold values from -0.125 to 0.125
Outputs:
- output: bfloat16 [16384, 2048], P('dp', 'mp')
- input_grad: float32 [16384, 2048], P('dp', 'mp')
- norm1_gain_grad: float32 [2048], P(('mp', 'dp'))
- w_input_grad: float32 [2048, 2560], P('dp', 'mp')
- w_branch_grad: float32 [2048, 2560], P('dp', 'mp')
- w_output_grad: float32 [2560, 2048], P('mp', 'dp')
- conv_weight_grad: float32 [4, 2560], P(None, ('mp', 'dp'))
- conv_bias_grad: float32 [2560], P(('mp', 'dp'))
- gate_a_weight_grad: float32 [16, 160, 160], P('mp', 'dp')
- gate_a_bias_grad: float32 [2560], P(('mp', 'dp'))
- gate_x_weight_grad: float32 [16, 160, 160], P('mp', 'dp')
- gate_x_bias_grad: float32 [2560], P(('mp', 'dp'))
- decay_param_grad: float32 [2560], P(('mp', 'dp'))
- norm2_gain_grad: float32 [2048], P(('mp', 'dp'))
- w_gate_grad: float32 [2048, 6144], P('dp', 'mp')
- w_up_grad: float32 [2048, 6144], P('dp', 'mp')
- w_down_grad: float32 [6144, 2048], P('mp', 'dp')
Inputs may be any that keep to these rules, and one draw needn't show every extreme that they name: `inputs`: activations of order one. `reset_mask`: 1 marks a token where a new document begins; a token whose index is a multiple of 2048 begins a sequence whatever it holds.
All inputs are finite; a program needn't handle non-finite values. No bound on the sum of `reset_mask` on one device may be relied on, other than what follows from the above.
Results may differ from a plain program's by a relative error of at most 0.0089.
Values may be sent and summed in bfloat16 or wider, within the bound.
A program may use at most 448 MiB of HBM per device.

v0:
```python
import jax
import jax.numpy as jnp
from jax import lax
from jax.sharding import PartitionSpec as P

D = 2048
SEQ = 2048


epsilon = 1e-06


def block_gate(mixed, weight, bias):
    length = mixed.shape[0]
    blocks = mixed.reshape(length, weight.shape[0], weight.shape[2])
    inner = jnp.einsum("thi,hij->thj", blocks, weight, precision=lax.Precision.HIGHEST)
    return jax.nn.sigmoid(inner.reshape(length, -1) + bias)


def linear_scan(carried, driven):

    def combine(earlier, later):
        return (earlier[0] * later[0], later[0] * earlier[1] + later[1])

    return lax.associative_scan(combine, (carried, driven), axis=0)[1]


def recurrence(
    rnn_in,
    gate_in,
    conv_weight,
    conv_bias,
    gate_a_weight,
    gate_a_bias,
    gate_x_weight,
    gate_x_bias,
    decay_param,
    starts,
):
    length = rnn_in.shape[0]
    segment = jnp.cumsum(starts)
    mixed = conv_bias + conv_weight[0] * rnn_in
    for offset in range(1, conv_weight.shape[0]):
        moved = jnp.pad(rnn_in, ((offset, 0), (0, 0)))[:length]
        earlier_seg = jnp.pad(segment, (offset, 0), constant_values=-1)[:length]
        same_doc = (earlier_seg == segment).astype(jnp.float32)[:, None]
        mixed = mixed + conv_weight[offset] * moved * same_doc
    gate_a = block_gate(mixed, gate_a_weight, gate_a_bias)
    gate_x = block_gate(mixed, gate_x_weight, gate_x_bias)
    log_decay = -8.0 * gate_a * jax.nn.softplus(decay_param)
    begins = starts.astype(jnp.float32)[:, None]
    carried = jnp.exp(log_decay) * (1.0 - begins)
    input_scale = jnp.sqrt(-jnp.expm1(2.0 * log_decay)) * (1.0 - begins) + begins
    state = linear_scan(carried, mixed * gate_x * input_scale)
    return jax.nn.gelu(gate_in) * state


def row_norm(values):
    total = lax.psum(jnp.sum(values * values, axis=1), "mp")
    scale = lax.rsqrt(total / D + epsilon)[:, None]
    return (values * scale, scale)


def norm_back(grad_normed, unit, scale, gain):
    weighted = grad_normed * gain
    dots = lax.psum(jnp.sum(weighted * unit, axis=1), "mp")
    grad_values = scale * (weighted - unit * (dots / D)[:, None])
    return (grad_values, jnp.sum(grad_normed * unit, axis=0))


def widen(rows):
    return lax.all_gather(rows, "mp", axis=1, tiled=True)


def widen_grad(rows):
    return lax.all_gather(rows, "mp", axis=1, tiled=True)


def reduce_branch(partial_value):
    return lax.psum_scatter(
        partial_value.astype(jnp.bfloat16), "mp", scatter_dimension=1, tiled=True
    ).astype(jnp.float32)


def reduce_input(partial_value):
    return lax.psum_scatter(partial_value, "mp", scatter_dimension=1, tiled=True)


def matmul(left, right):
    return jnp.dot(left, right, preferred_element_type=jnp.float32)


def matmul_right_t(left, right):
    return lax.dot_general(
        left, right, (((1,), (1,)), ((), ())), preferred_element_type=jnp.float32
    )


def matmul_left_t(left, right):
    return lax.dot_general(
        left, right, (((0,), (0,)), ((), ())), preferred_element_type=jnp.float32
    )


def body(
    inputs,
    cotangent,
    reset_mask,
    norm1_gain,
    w_input,
    w_branch,
    w_output,
    conv_weight,
    conv_bias,
    gate_a_weight,
    gate_a_bias,
    gate_x_weight,
    gate_x_bias,
    decay_param,
    norm2_gain,
    w_gate,
    w_up,
    w_down,
):
    gathered = (
        lax.all_gather(norm1_gain, "dp", axis=0, tiled=True),
        lax.all_gather(w_input, "dp", axis=0, tiled=True),
        lax.all_gather(w_branch, "dp", axis=0, tiled=True),
        lax.all_gather(w_output, "dp", axis=1, tiled=True),
        lax.all_gather(conv_weight, "dp", axis=1, tiled=True),
        lax.all_gather(conv_bias, "dp", axis=0, tiled=True),
        lax.all_gather(gate_a_weight, "dp", axis=1, tiled=True),
        lax.all_gather(gate_a_bias, "dp", axis=0, tiled=True),
        lax.all_gather(gate_x_weight, "dp", axis=1, tiled=True),
        lax.all_gather(gate_x_bias, "dp", axis=0, tiled=True),
        lax.all_gather(decay_param, "dp", axis=0, tiled=True),
        lax.all_gather(norm2_gain, "dp", axis=0, tiled=True),
        lax.all_gather(w_gate, "dp", axis=0, tiled=True),
        lax.all_gather(w_up, "dp", axis=0, tiled=True),
        lax.all_gather(w_down, "dp", axis=1, tiled=True),
    )
    (
        gain_one,
        full_input,
        full_branch,
        full_output,
        full_conv,
        full_conv_bias,
        full_gate_a,
        full_gate_a_bias,
        full_gate_x,
        full_gate_x_bias,
        full_decay,
        gain_two,
        full_gate,
        full_up,
        full_down,
    ) = gathered
    tokens = inputs.shape[0]
    first_pos = (jnp.arange(tokens) % SEQ == 0).astype(jnp.int32)
    starts = jnp.maximum(reset_mask, first_pos)
    gain_one = gain_one.astype(jnp.float32)
    gain_two = gain_two.astype(jnp.float32)
    small_params = tuple(
        (
            weight.astype(jnp.float32)
            for weight in (
                full_conv,
                full_conv_bias,
                full_gate_a,
                full_gate_a_bias,
                full_gate_x,
                full_gate_x_bias,
                full_decay,
            )
        )
    )

    def mixer(rnn_in, gate_in, *weights):
        return recurrence(rnn_in, gate_in, *weights, starts)

    resid_in = inputs.astype(jnp.float32)
    unit_one, scale_one = row_norm(resid_in)
    normed_one = widen((unit_one * gain_one).astype(jnp.bfloat16))
    rnn_in = matmul(normed_one, full_input)
    gate_in = matmul(normed_one, full_branch)
    mixer_val, mixer_pull = jax.vjp(mixer, rnn_in, gate_in, *small_params)
    mixer_out = mixer_val.astype(jnp.bfloat16)
    rec_branch = lax.psum_scatter(
        matmul(mixer_out, full_output), "mp", scatter_dimension=1, tiled=True
    )
    resid_mid = resid_in + rec_branch
    unit_two, scale_two = row_norm(resid_mid)
    normed_two = widen((unit_two * gain_two).astype(jnp.bfloat16))
    gate_val = matmul(normed_two, full_gate)
    up_val = matmul(normed_two, full_up)
    hidden_val, hidden_pull = jax.vjp(
        lambda gate_part, up_part: jax.nn.gelu(gate_part) * up_part, gate_val, up_val
    )
    hidden = hidden_val.astype(jnp.bfloat16)
    output = (resid_mid + reduce_branch(matmul(hidden, full_down))).astype(jnp.bfloat16)
    regathered = (
        lax.all_gather(norm1_gain, "dp", axis=0, tiled=True),
        lax.all_gather(w_input, "dp", axis=0, tiled=True),
        lax.all_gather(w_branch, "dp", axis=0, tiled=True),
        lax.all_gather(w_output, "dp", axis=1, tiled=True),
        lax.all_gather(conv_weight, "dp", axis=1, tiled=True),
        lax.all_gather(conv_bias, "dp", axis=0, tiled=True),
        lax.all_gather(gate_a_weight, "dp", axis=1, tiled=True),
        lax.all_gather(gate_a_bias, "dp", axis=0, tiled=True),
        lax.all_gather(gate_x_weight, "dp", axis=1, tiled=True),
        lax.all_gather(gate_x_bias, "dp", axis=0, tiled=True),
        lax.all_gather(decay_param, "dp", axis=0, tiled=True),
        lax.all_gather(norm2_gain, "dp", axis=0, tiled=True),
        lax.all_gather(w_gate, "dp", axis=0, tiled=True),
        lax.all_gather(w_up, "dp", axis=0, tiled=True),
        lax.all_gather(w_down, "dp", axis=1, tiled=True),
    )
    back_input, back_branch, back_output = (regathered[1], regathered[2], regathered[3])
    back_gate, back_up, back_down = (regathered[12], regathered[13], regathered[14])
    down_grad = widen_grad(cotangent)
    d_hidden = matmul_right_t(down_grad, back_down)
    grad_down = matmul_left_t(hidden, down_grad)
    d_gate, d_up = hidden_pull(d_hidden)
    d_gate = d_gate.astype(jnp.bfloat16)
    d_up = d_up.astype(jnp.bfloat16)
    grad_gate = matmul_left_t(normed_two, d_gate)
    grad_up = matmul_left_t(normed_two, d_up)
    d_normed_two = reduce_input(matmul_right_t(d_gate, back_gate) + matmul_right_t(d_up, back_up))
    d_mid_norm, grad_gain_two = norm_back(d_normed_two, unit_two, scale_two, gain_two)
    d_mid = cotangent.astype(jnp.float32) + d_mid_norm
    branch_grad = widen_grad(d_mid.astype(jnp.bfloat16))
    d_mixer = matmul_right_t(branch_grad, back_output)
    grad_output = matmul_left_t(mixer_out, branch_grad)
    mixer_grads = mixer_pull(d_mixer)
    d_rnn_in = mixer_grads[0].astype(jnp.bfloat16)
    d_gate_in = mixer_grads[1].astype(jnp.bfloat16)
    grad_input_w = matmul_left_t(normed_one, d_rnn_in)
    grad_branch_w = matmul_left_t(normed_one, d_gate_in)
    d_normed_one = reduce_input(
        matmul_right_t(d_rnn_in, back_input) + matmul_right_t(d_gate_in, back_branch)
    )
    d_in_norm, grad_gain_one = norm_back(d_normed_one, unit_one, scale_one, gain_one)
    input_grad = d_mid + d_in_norm
    summed = (
        lax.psum_scatter(grad_gain_one, "dp", scatter_dimension=0, tiled=True),
        lax.psum_scatter(grad_input_w, "dp", scatter_dimension=0, tiled=True),
        lax.psum_scatter(grad_branch_w, "dp", scatter_dimension=0, tiled=True),
        lax.psum_scatter(grad_output, "dp", scatter_dimension=1, tiled=True),
        lax.psum_scatter(mixer_grads[2], "dp", scatter_dimension=1, tiled=True),
        lax.psum_scatter(mixer_grads[3], "dp", scatter_dimension=0, tiled=True),
        lax.psum_scatter(mixer_grads[4], "dp", scatter_dimension=1, tiled=True),
        lax.psum_scatter(mixer_grads[5], "dp", scatter_dimension=0, tiled=True),
        lax.psum_scatter(mixer_grads[6], "dp", scatter_dimension=1, tiled=True),
        lax.psum_scatter(mixer_grads[7], "dp", scatter_dimension=0, tiled=True),
        lax.psum_scatter(mixer_grads[8], "dp", scatter_dimension=0, tiled=True),
        lax.psum_scatter(grad_gain_two, "dp", scatter_dimension=0, tiled=True),
        lax.psum_scatter(grad_gate, "dp", scatter_dimension=0, tiled=True),
        lax.psum_scatter(grad_up, "dp", scatter_dimension=0, tiled=True),
        lax.psum_scatter(grad_down, "dp", scatter_dimension=1, tiled=True),
    )
    return (
        output,
        input_grad,
        summed[0],
        summed[1],
        summed[2],
        summed[3],
        summed[4],
        summed[5],
        summed[6],
        summed[7],
        summed[8],
        summed[9],
        summed[10],
        summed[11],
        summed[12],
        summed[13],
        summed[14],
    )


def solution(mesh):
    in_specs = (
        P("dp", "mp"),
        P("dp", "mp"),
        P("dp"),
        P(("mp", "dp")),
        P("dp", "mp"),
        P("dp", "mp"),
        P("mp", "dp"),
        P(None, ("mp", "dp")),
        P(("mp", "dp")),
        P("mp", "dp", None),
        P(("mp", "dp")),
        P("mp", "dp", None),
        P(("mp", "dp")),
        P(("mp", "dp")),
        P(("mp", "dp")),
        P("dp", "mp"),
        P("dp", "mp"),
        P("mp", "dp"),
    )
    out_specs = (
        P("dp", "mp"),
        P("dp", "mp"),
        P(("mp", "dp")),
        P("dp", "mp"),
        P("dp", "mp"),
        P("mp", "dp"),
        P(None, ("mp", "dp")),
        P(("mp", "dp")),
        P("mp", "dp", None),
        P(("mp", "dp")),
        P("mp", "dp", None),
        P(("mp", "dp")),
        P(("mp", "dp")),
        P(("mp", "dp")),
        P("dp", "mp"),
        P("dp", "mp"),
        P("mp", "dp"),
    )
    return jax.shard_map(body, mesh=mesh, in_specs=in_specs, out_specs=out_specs, check_vma=False)
```

profile of v0, /device:TPU:8, one launch (start us, length us, event | category | flops | bytes accessed | tf_op | source)
XLA Modules:
  0.0 3311.3 jit_solution(16514168364747738892)
XLA Ops:
  15.7 24.5 all-reduce.134
  83.9 117.6 %all-gather.12.cloned.1.call-done = bf16[2048,2048]{1,0:T(8,128)(2,1)} async-done(((bf16[2048,512]{1,0:T(8,128)(2,1)}), bf16[2048,2048]{1,0:T(8,128)(2,1)}) %all-gather.12.cloned.1.call-update) | async-done | bytes 8388624 | tf_op jit(solution)/shard_map/all_gather | solution.py:72
  251.7 21.3 exponential_multiply_fusion
  572.9 277.9 %reduce-scatter.14.cloned.1.call-done = f32[2048,512]{1,0:T(8,128)} async-done(((f32[2048,2048]{1,0:T(8,128)}), f32[2048,512]{1,0:T(8,128)}) %reduce-scatter.14.cloned.1.call-update) | async-done | bytes 4194320 | tf_op jit(solution)/shard_map/reduce_scatter | solution.py:189
  875.1 27.0 all-gather.22.cloned.1.call-done
  902.1 148.9 %all-gather.20.cloned.1.call-done = bf16[2048,2048]{1,0:T(8,128)(2,1)} async-done(((bf16[2048,512]{1,0:T(8,128)(2,1)}), bf16[2048,2048]{1,0:T(8,128)(2,1)}) %all-gather.20.cloned.1.call-update) | async-done | bytes 8388624 | tf_op jit(solution)/shard_map/all_gather | solution.py:72
  1051.0 19.2 fusion.137
  1070.2 29.6 all-gather.24.cloned.1.call-done
  1099.8 19.3 fusion.138
  1119.1 29.5 all-gather.26.cloned.1.call-done
  1148.6 148.2 %all-gather.28.cloned.1.call-done = bf16[2048,2048]{1,0:T(8,128)(2,1)} async-done(((bf16[2048,512]{1,0:T(8,128)(2,1)}), bf16[2048,2048]{1,0:T(8,128)(2,1)}) %all-gather.28.cloned.1.call-update) | async-done | bytes 8388624 | tf_op jit(solution)/shard_map/all_gather | solution.py:76
  1296.7 33.9 %multiply_convert_fusion = (bf16[2048,1536]{1,0:T(8,128)(2,1)}, bf16[2048,1536]{1,0:T(8,128)(2,1)}, bf16[2048,1536]{1,0:T(8,128)(2,1)}) fusion(f32[2048,1536]{1,0:T(8,128)} %fusion.137, f32[2048,1536]{1,0:T(8,128)} %fusion.138, bf16[2048,2048]{1,0:T(8,128)(2,1)} %all-gather.28.cloned.1.call-done, bf16[1536,2048]{1,0:T(8,128)(2,1)} %all-gather.26.cloned.1.call-done), kind=kOutput, calls=%fused_computation.9 | convolution fusion | flops 12966690816 | bytes 58720256 | tf_op jit(solution)/shard_map/dot_general | solution.py:94
  1330.6 19.5 fusion.139
  1350.1 23.3 convolution_add_fusion
  1373.4 278.4 %reduce-scatter.18.cloned.1.call-done = f32[2048,512]{1,0:T(8,128)} async-done(((f32[2048,2048]{1,0:T(8,128)}), f32[2048,512]{1,0:T(8,128)}) %reduce-scatter.18.cloned.1.call-update) | async-done | bytes 4194320 | tf_op jit(solution)/shard_map/reduce_scatter | solution.py:86
  1675.1 146.7 %all-gather.30.cloned.1.call-done = bf16[2048,2048]{1,0:T(8,128)(2,1)} async-done(((bf16[2048,512]{1,0:T(8,128)(2,1)}), bf16[2048,2048]{1,0:T(8,128)(2,1)}) %all-gather.30.cloned.1.call-update) | async-done | bytes 8388624 | tf_op jit(solution)/shard_map/all_gather | solution.py:76
  2176.8 32.4 multiply_reduce_fusion
  2209.9 22.3 fusion.87
  2276.6 21.3 multiply_reduce_fusion.4
  2351.5 19.3 convolution_convert_fusion
  2370.9 19.2 fusion.146
  2390.2 19.2 fusion.147
  2409.4 19.8 fusion.148
  2471.0 210.2 %reduce-scatter.20.cloned.1.call-done = f32[2048,512]{1,0:T(8,128)} async-done(((f32[2048,2048]{1,0:T(8,128)}), f32[2048,512]{1,0:T(8,128)}) %reduce-scatter.20.cloned.1.call-update) | async-done | bytes 4194320 | tf_op jit(solution)/shard_map/reduce_scatter | solution.py:86
  2684.2 24.3 all-reduce.132
  2726.1 105.9 %reduce-scatter.16.cloned.1.call-done = bf16[2048,512]{1,0:T(8,128)(2,1)} async-done(((bf16[2048,2048]{1,0:T(8,128)(2,1)}), bf16[2048,512]{1,0:T(8,128)(2,1)}) %reduce-scatter.16.cloned.1.call-update) | async-done | bytes 2097168 | tf_op jit(solution)/shard_map/reduce_scatter | solution.py:80
  2841.2 88.1 %reduce-scatter.28.cloned.1.call-done = f32[256,1536]{1,0:T(8,128)} async-done(((f32[2048,1536]{1,0:T(8,128)}), f32[256,1536]{1,0:T(8,128)}) %reduce-scatter.28.cloned.1.call-update) | async-done | bytes 1572880 | tf_op jit(solution)/shard_map/reduce_scatter | solution.py:258
  2929.3 96.4 %reduce-scatter.30.cloned.1.call-done = f32[256,1536]{1,0:T(8,128)} async-done(((f32[2048,1536]{1,0:T(8,128)}), f32[256,1536]{1,0:T(8,128)}) %reduce-scatter.30.cloned.1.call-update) | async-done | bytes 1572880 | tf_op jit(solution)/shard_map/reduce_scatter | solution.py:259
  3025.7 96.5 %reduce-scatter.32.cloned.1.call-done = f32[1536,256]{1,0:T(8,128)} async-done(((f32[1536,2048]{1,0:T(8,128)}), f32[1536,256]{1,0:T(8,128)}) %reduce-scatter.32.cloned.1.call-update) | async-done | bytes 1572880 | tf_op jit(solution)/shard_map/reduce_scatter | solution.py:260
  3122.2 60.4 %reduce-scatter.22.cloned.1.call-done = f32[256,640]{1,0:T(8,128)} async-done(((f32[2048,640]{1,0:T(8,128)}), f32[256,640]{1,0:T(8,128)}) %reduce-scatter.22.cloned.1.call-update) | async-done | bytes 655376 | tf_op jit(solution)/shard_map/reduce_scatter | solution.py:247
  3182.6 60.9 %reduce-scatter.24.cloned.1.call-done = f32[256,640]{1,0:T(8,128)} async-done(((f32[2048,640]{1,0:T(8,128)}), f32[256,640]{1,0:T(8,128)}) %reduce-scatter.24.cloned.1.call-update) | async-done | bytes 655376 | tf_op jit(solution)/shard_map/reduce_scatter | solution.py:248
  3243.5 60.5 %reduce-scatter.26.cloned.1.call-done = f32[640,256]{1,0:T(8,128)} async-done(((f32[640,2048]{1,0:T(8,128)}), f32[640,256]{1,0:T(8,128)}) %reduce-scatter.26.cloned.1.call-update) | async-done | bytes 655376 | tf_op jit(solution)/shard_map/reduce_scatter | solution.py:249
  (783 shorter events, 969.0 us)
Async XLA Ops:
  7.2 76.6 %all-gather.16.cloned.1.call-start = ((), (), s32[]{:S(2)}) async-start(), calls=%async_computation.13 | async-start | bytes 2949120 | tf_op jit(solution)/shard_map/all_gather | solution.py:127
  8.0 193.5 %all-gather.12.cloned.1.call-start = ((), (), s32[]{:S(2)}) async-start(), calls=%async_computation.11 | async-start | bytes 10485760 | tf_op jit(solution)/shard_map/all_gather | solution.py:72
  55.5 489.2 %all-gather.14.cloned.1.call-start = ((), (), s32[]{:S(2)}) async-start(), calls=%async_computation.12 | async-start | bytes 2949120 | tf_op jit(solution)/shard_map/all_gather | solution.py:128
  56.2 503.7 %all-gather.18.cloned.1.call-start = ((), (), s32[]{:S(2)}) async-start(), calls=%async_computation.14 | async-start | bytes 2949120 | tf_op jit(solution)/shard_map/all_gather | solution.py:129
  56.8 793.9 %reduce-scatter.14.cloned.1.call-start = ((), (), s32[]{:S(2)}) async-start(), calls=%async_computation.15 | async-start | bytes 20971520 | tf_op jit(solution)/shard_map/reduce_scatter | solution.py:189
  572.2 278.6 %copy-start.1 = (bf16[2048,512]{1,0:T(8,128)(2,1)S(1)}, bf16[2048,512]{1,0:T(8,128)(2,1)}, u32[]{:S(2)}) copy-start(bf16[2048,512]{1,0:T(8,128)(2,1)} %param.18) | copy-start | bytes 6291460
  572.2 329.9 %all-gather.22.cloned.1.call-start = ((), (), s32[]{:S(2)}) async-start(), calls=%async_computation.17 | async-start | bytes 7077888 | tf_op jit(solution)/shard_map/all_gather | solution.py:138
  572.8 478.3 %all-gather.20.cloned.1.call-start = ((), (), s32[]{:S(2)}) async-start(), calls=%async_computation.16 | async-start | bytes 10485760 | tf_op jit(solution)/shard_map/all_gather | solution.py:72
  572.9 295.6 %copy-start.144 = (f32[512]{0:T(512)}, f32[512]{0:T(512)S(1)}, u32[]{:S(2)}) copy-start(f32[512]{0:T(512)S(1)} %convert_element_type.100) | copy-start | bytes 6148
  873.0 226.8 %all-gather.24.cloned.1.call-start = ((), (), s32[]{:S(2)}) async-start(), calls=%async_computation.18 | async-start | bytes 7077888 | tf_op jit(solution)/shard_map/all_gather | solution.py:139
  873.8 274.8 %all-gather.26.cloned.1.call-start = ((), (), s32[]{:S(2)}) async-start(), calls=%async_computation.19 | async-start | bytes 7077888 | tf_op jit(solution)/shard_map/all_gather | solution.py:140
  874.5 422.2 %all-gather.28.cloned.1.call-start = ((), (), s32[]{:S(2)}) async-start(), calls=%async_computation.21 | async-start | bytes 10485760 | tf_op jit(solution)/shard_map/all_gather | solution.py:76
  875.1 776.7 %reduce-scatter.18.cloned.1.call-start = ((), (), s32[]{:S(2)}) async-start(), calls=%async_computation.22 | async-start | bytes 20971520 | tf_op jit(solution)/shard_map/reduce_scatter | solution.py:86
  1373.3 278.5 %copy-start.104 = (f32[2048]{0:T(1024)S(1)}, f32[2048]{0:T(1024)}, u32[]{:S(2)}) copy-start(f32[2048]{0:T(1024)} %copy-done.103) | copy-start | bytes 24580
  1373.3 278.5 %copy-start.145 = (f32[512]{0:T(512)S(1)}, f32[512]{0:T(512)}, u32[]{:S(2)}) copy-start(f32[512]{0:T(512)} %copy-done.144) | copy-start | bytes 6148
  1373.4 296.6 %copy-start.18 = (bf16[2048,512]{1,0:T(8,128)(2,1)S(1)}, bf16[2048,512]{1,0:T(8,128)(2,1)}, u32[]{:S(2)}) copy-start(bf16[2048,512]{1,0:T(8,128)(2,1)} %param.19) | copy-start | bytes 6291460
  1373.4 448.5 %all-gather.30.cloned.1.call-start = ((), (), s32[]{:S(2)}) async-start(), calls=%async_computation.23 | async-start | bytes 10485760 | tf_op jit(solution)/shard_map/all_gather | solution.py:76
  1675.1 792.8 %reduce-scatter.34.cloned.1.call-start = ((), (), s32[]{:S(2)}) async-start(), calls=%async_computation.31 | async-start | bytes 368640
  2305.9 163.5 %all-reduce.137.cloned.1.call-start = ((), (), s32[]{:S(2)}) async-start(), calls=%async_computation.32 | async-start | bytes 2621440
  2325.1 356.0 %reduce-scatter.20.cloned.1.call-start = ((), (), s32[]{:S(2)}) async-start(), calls=%async_computation.24 | async-start | bytes 20971520 | tf_op jit(solution)/shard_map/reduce_scatter | solution.py:86
  2351.5 480.5 %reduce-scatter.16.cloned.1.call-start = ((), (), s32[]{:S(2)}) async-start(), calls=%async_computation.20 | async-start | bytes 10485760 | tf_op jit(solution)/shard_map/reduce_scatter | solution.py:80
  2370.8 558.5 %reduce-scatter.28.cloned.1.call-start = ((), (), s32[]{:S(2)}) async-start(), calls=%async_computation.28 | async-start | bytes 14155776 | tf_op jit(solution)/shard_map/reduce_scatter | solution.py:258
  2390.1 635.6 %reduce-scatter.30.cloned.1.call-start = ((), (), s32[]{:S(2)}) async-start(), calls=%async_computation.29 | async-start | bytes 14155776 | tf_op jit(solution)/shard_map/reduce_scatter | solution.py:259
  2409.4 712.8 %reduce-scatter.32.cloned.1.call-start = ((), (), s32[]{:S(2)}) async-start(), calls=%async_computation.30 | async-start | bytes 14155776 | tf_op jit(solution)/shard_map/reduce_scatter | solution.py:260
  2429.3 753.3 %reduce-scatter.22.cloned.1.call-start = ((), (), s32[]{:S(2)}) async-start(), calls=%async_computation.25 | async-start | bytes 5898240 | tf_op jit(solution)/shard_map/reduce_scatter | solution.py:247
  2441.7 801.8 %reduce-scatter.24.cloned.1.call-start = ((), (), s32[]{:S(2)}) async-start(), calls=%async_computation.26 | async-start | bytes 5898240 | tf_op jit(solution)/shard_map/reduce_scatter | solution.py:248
  2454.5 849.6 %reduce-scatter.26.cloned.1.call-start = ((), (), s32[]{:S(2)}) async-start(), calls=%async_computation.27 | async-start | bytes 5898240 | tf_op jit(solution)/shard_map/reduce_scatter | solution.py:249
  2465.7 218.4 %copy-start.161 = (f32[640]{0:T(1024)S(1)}, f32[640]{0:T(1024)}, u32[]{:S(2)}) copy-start(f32[640]{0:T(1024)} %get-tuple-element.119) | copy-start | bytes 7684
  2465.7 218.4 %copy-start.162 = (f32[640]{0:T(1024)S(1)}, f32[640]{0:T(1024)}, u32[]{:S(2)}) copy-start(f32[640]{0:T(1024)} %get-tuple-element.59) | copy-start | bytes 7684
  2465.8 366.3 %copy-start.105 = (f32[2048]{0:T(1024)S(1)}, f32[2048]{0:T(1024)}, u32[]{:S(2)}) copy-start(f32[2048]{0:T(1024)} %copy-done.103) | copy-start | bytes 24580
  2465.8 366.2 %copy-start.143 = (f32[2048]{0:T(1024)S(1)}, f32[2048]{0:T(1024)}, u32[]{:S(2)}) copy-start(f32[2048]{0:T(1024)} %copy-done.142) | copy-start | bytes 24580
  2465.8 366.2 %copy-start.146 = (f32[512]{0:T(512)S(1)}, f32[512]{0:T(512)}, u32[]{:S(2)}) copy-start(f32[512]{0:T(512)} %copy-done.144) | copy-start | bytes 6148
  (179 other events, 6176.3 us)
Sparse Core Ops, SparseCore 0:
  9.9 31.4 all-gather.15
  55.6 145.7 all-gather.11
  203.3 31.3 all-gather.13
  236.4 30.4 all-gather.17
  572.3 278.3 reduce-scatter.13
  852.6 49.4 all-gather.21
  904.4 146.6 all-gather.19
  1053.1 46.6 all-gather.23
  1101.9 46.6 all-gather.25
  1150.0 146.6 all-gather.27
  1373.5 278.2 reduce-scatter.17
  1675.2 146.6 all-gather.29
  2306.0 34.9 reduce-scatter.33
  2344.6 57.8 all-reduce.136
  2404.8 276.3 reduce-scatter.19
  2683.4 148.5 reduce-scatter.15
  2835.9 93.3 reduce-scatter.27
  2933.2 92.3 reduce-scatter.29
  3029.7 92.3 reduce-scatter.31
  3126.0 56.5 reduce-scatter.21
  3186.9 56.5 reduce-scatter.23
  3247.5 56.5 reduce-scatter.25
where the time goes:
time: 3330 us; the launch traced here: 3310 us
  waiting for transfers between devices  1990 us (60%)
  local copies, waits for them, and re-layouts  574 us (17%)
  matrix products  346 us (10%)
  other arithmetic  259 us (8%)
  blocking collectives  124 us (4%)
    reduce_scatter x2, waiting for transfers between devices, reduce_input(): lax.psum_scatter(partial_value, 'mp', scatter_dimension=1, tiled=True)  489 us
    all_gather x2, waiting for transfers between devices, widen_grad(): return lax.all_gather(rows, 'mp', axis=1, tiled=True)  295 us
    reduce_scatter x1, waiting for transfers between devices, body(): lax.psum_scatter(matmul(mixer_out, full_output), 'mp', scatter_dimension=...  278 us
    pad x88, local copies, waits for them, and re-layouts, linear_scan(): return lax.associative_scan(combine, (carried, driven), axis=0)[1]  272 us
    all_gather x2, waiting for transfers between devices, widen(): return lax.all_gather(rows, 'mp', axis=1, tiled=True)  266 us
    slice x87, local copies, waits for them, and re-layouts, linear_scan(): return lax.associative_scan(combine, (carried, driven), axis=0)[1]  229 us
    dot_general x6, matrix products, matmul_right_t(): lax.dot_general(left, right, (((1,), (1,)), ((), ())), preferred_element_...  119 us
    reduce_scatter x1, waiting for transfers between devices, reduce_branch(): lax.psum_scatter(partial_value.astype(jnp.bfloat16), 'mp', scatter_dimens...  106 us
  transfers between devices with their start and end apart: 22, of which 17 were waited for; matrix products, arithmetic and copies ran while one was open for 18% of the time, Pallas kernels for 0%

commit v1 on v0

v1 whole, which is shorter than its diff:
```python
import functools

import jax
import jax.numpy as jnp
from jax import lax
from jax.experimental import pallas as pl
from jax.experimental.pallas import tpu as pltpu
from jax.sharding import PartitionSpec as P

SEQ = 2048
epsilon = 1e-06
BF = jnp.bfloat16
F32 = jnp.float32
ROWS = 64
HALO = 8


def dot_nt(left, right):
    return lax.dot_general(
        left, right, (((1,), (1,)), ((), ())), preferred_element_type=F32
    )


def dot_nn(left, right):
    return jnp.dot(left, right, preferred_element_type=F32)


def dot_tn(left, right):
    return lax.dot_general(
        left, right, (((0,), (0,)), ((), ())), preferred_element_type=F32
    )


def gelu_parts(value):
    inner = 0.7978845608028654 * (value + 0.044715 * value * value * value)
    tanh = jnp.tanh(inner)
    slope = 0.7978845608028654 * (1.0 + 3.0 * 0.044715 * value * value)
    gelu = 0.5 * value * (1.0 + tanh)
    grad = 0.5 * (1.0 + tanh) + 0.5 * value * (1.0 - tanh * tanh) * slope
    return gelu, grad


def sigmoid(value):
    return 1.0 / (1.0 + jnp.exp(-value))


def one_minus_exp(log_value):
    y = -2.0 * log_value
    series = y * (
        1.0
        - y
        * (1 / 2)
        * (
            1.0
            - y
            * (1 / 3)
            * (1.0 - y * (1 / 4) * (1.0 - y * (1 / 5) * (1.0 - y * (1 / 6))))
        )
    )
    return jnp.where(y < 0.25, series, 1.0 - jnp.exp(-y))


def conv_terms(ext, masks, rows):
    terms = [ext[HALO : HALO + rows]]
    for k in range(1, 4):
        moved = pltpu.roll(ext, k, axis=0)[HALO : HALO + rows]
        terms.append(moved * masks[:, k - 1 : k])
    return terms


def forward_kernel(
    rnn_ref,
    halo_ref,
    mask_ref,
    conv_ref,
    vec_ref,
    wa_ref,
    wx_ref,
    mixed_ref,
    ga_ref,
    gx_ref,
    h_ref,
    p_ref,
    end_ref,
    ext_ref,
):
    length, width = rnn_ref.shape[1:]
    ext_ref[0:HALO, :] = halo_ref[0]
    ext_ref[HALO:, :] = rnn_ref[0]
    row8 = lax.broadcasted_iota(jnp.int32, (ROWS, 1), 0) % 8

    def block(i, carry):
        h_in, p_in = carry
        r0 = pl.multiple_of(i * ROWS, ROWS)
        masks = mask_ref[0, pl.ds(r0, ROWS), :]
        terms = conv_terms(ext_ref[pl.ds(r0, ROWS + HALO), :], masks, ROWS)
        mixed = vec_ref[0:1, :] + conv_ref[0:1, :] * terms[0]
        for k in range(1, 4):
            mixed = mixed + conv_ref[k : k + 1, :] * terms[k]
        high = mixed.astype(BF)
        low = (mixed - high.astype(F32)).astype(BF)
        gate_a = sigmoid(
            dot_nn(high, wa_ref[...]) + dot_nn(low, wa_ref[...]) + vec_ref[1:2, :]
        )
        gate_x = sigmoid(
            dot_nn(high, wx_ref[...]) + dot_nn(low, wx_ref[...]) + vec_ref[2:3, :]
        )
        begins = masks[:, 3:4]
        log_a = gate_a * vec_ref[3:4, :]
        a = jnp.exp(log_a) * (1.0 - begins)
        scale = jnp.sqrt(one_minus_exp(log_a)) * (1.0 - begins) + begins
        b = mixed * gate_x * scale
        mixed_ref[0, pl.ds(r0, ROWS), :] = mixed
        ga_ref[0, pl.ds(r0, ROWS), :] = gate_a
        gx_ref[0, pl.ds(r0, ROWS), :] = gate_x
        for d in (1, 2, 4):
            valid = row8 >= d
            b = jnp.where(valid, a * pltpu.roll(b, d, axis=0) + b, b)
            a = jnp.where(valid, a * pltpu.roll(a, d, axis=0), a)
        for g in range(ROWS // 8):
            rows = slice(8 * g, 8 * g + 8)
            h = b[rows] + a[rows] * h_in
            p = a[rows] * p_in
            h_ref[0, pl.ds(r0 + 8 * g, 8), :] = h
            p_ref[0, pl.ds(r0 + 8 * g, 8), :] = p
            h_in = h[7:8]
            p_in = p[7:8]
        return h_in, p_in

    h_end, p_end = lax.fori_loop(
        0,
        length // ROWS,
        block,
        (jnp.zeros((1, width), F32), jnp.ones((1, width), F32)),
    )
    end_ref[0, 0:4, :] = jnp.broadcast_to(p_end, (4, width))
    end_ref[0, 4:8, :] = jnp.broadcast_to(h_end, (4, width))


def adjoint_kernel(
    dmix_ref,
    gate_ref,
    state_ref,
    ga_ref,
    mask_ref,
    vec_ref,
    lam_ref,
    q_ref,
    dgi_ref,
    end_ref,
):
    length, width = dmix_ref.shape[1:]
    row = lax.broadcasted_iota(jnp.int32, (ROWS, 1), 0)
    row8 = row % 8
    blocks = length // ROWS

    def block(i, carry):
        lam_in, q_in, a_next = carry
        r0 = pl.multiple_of((blocks - 1 - i) * ROWS, ROWS)
        here = pl.ds(r0, ROWS)
        begins = mask_ref[0, here, :][:, 3:4]
        d_mixer = dmix_ref[0, here, :]
        gelu, slope = gelu_parts(gate_ref[0, here, :])
        dgi_ref[0, here, :] = (d_mixer * state_ref[0, here, :] * slope).astype(BF)
        b = d_mixer * gelu
        a = jnp.exp(ga_ref[0, here, :] * vec_ref[3:4, :]) * (1.0 - begins)
        c = jnp.where(row == ROWS - 1, a_next, pltpu.roll(a, ROWS - 1, axis=0))
        for d in (1, 2, 4):
            valid = row8 < 8 - d
            b = jnp.where(valid, c * pltpu.roll(b, ROWS - d, axis=0) + b, b)
            c = jnp.where(valid, c * pltpu.roll(c, ROWS - d, axis=0), c)
        for g in reversed(range(ROWS // 8)):
            rows = slice(8 * g, 8 * g + 8)
            lam = b[rows] + c[rows] * lam_in
            q = c[rows] * q_in
            lam_ref[0, pl.ds(r0 + 8 * g, 8), :] = lam
            q_ref[0, pl.ds(r0 + 8 * g, 8), :] = q
            lam_in = lam[0:1]
            q_in = q[0:1]
        return lam_in, q_in, a[0:1]

    one = jnp.ones((1, width), F32)
    lam0, q0, a0 = lax.fori_loop(
        0, blocks, block, (jnp.zeros((1, width), F32), one, one)
    )
    end_ref[0, 0:4, :] = jnp.broadcast_to(a0 * q0, (4, width))
    end_ref[0, 4:8, :] = jnp.broadcast_to(a0 * lam0, (4, width))


def fold8(value):
    total = value[0:8]
    for g in range(1, value.shape[0] // 8):
        total = total + value[8 * g : 8 * g + 8]
    return total


def backward_kernel(
    lam_ref,
    q_ref,
    state_ref,
    ga_ref,
    gx_ref,
    mixed_ref,
    rnn_ref,
    halo_ref,
    mask_ref,
    edge_ref,
    conv_ref,
    vec_ref,
    wa_ref,
    wx_ref,
    drnn_ref,
    head_ref,
    tail_ref,
    wag_ref,
    wxg_ref,
    vg_ref,
    ext_ref,
    prev_ref,
    dm_ref,
):
    length, width = lam_ref.shape[1:]
    first = pl.program_id(0) == 0

    @pl.when(first)
    def _():
        wag_ref[...] = jnp.zeros_like(wag_ref)
        wxg_ref[...] = jnp.zeros_like(wxg_ref)
        vg_ref[...] = jnp.zeros_like(vg_ref)

    ext_ref[0:HALO, :] = halo_ref[0]
    ext_ref[HALO:, :] = rnn_ref[0]
    prev_ref[0:HALO, :] = jnp.broadcast_to(edge_ref[0, 0:1, :], (HALO, width))
    prev_ref[HALO:, :] = state_ref[0]
    dm_ref[length:, :] = jnp.zeros((HALO, width), F32)

    def block(i, carry):
        r0 = pl.multiple_of(i * ROWS, ROWS)
        here = pl.ds(r0, ROWS)
        masks = mask_ref[0, here, :]
        begins = masks[:, 3:4]
        lam = lam_ref[0, here, :] + q_ref[0, here, :] * edge_ref[0, 4:5, :]
        before = pltpu.roll(prev_ref[pl.ds(r0, ROWS + HALO), :], 1, axis=0)[
            HALO : HALO + ROWS
        ]
        gate_a = ga_ref[0, here, :]
        gate_x = gx_ref[0, here, :]
        mixed = mixed_ref[0, here, :]
        log_a = gate_a * vec_ref[3:4, :]
        decay = jnp.exp(log_a)
        inv_scale = lax.rsqrt(one_minus_exp(log_a))
        scale_raw = jnp.sqrt(one_minus_exp(log_a))
        keep = 1.0 - begins
        scale = scale_raw * keep + begins
        through = lam * mixed
        d_log = lam * before * decay * keep + jnp.where(
            begins > 0.5, 0.0, through * gate_x * (-(decay * decay) * inv_scale)
        )
        log_gate = d_log * gate_a
        d_pre_a = log_gate * (1.0 - gate_a) * vec_ref[3:4, :]
        d_pre_x = through * scale * gate_x * (1.0 - gate_x)
        pa = d_pre_a.astype(BF)
        px = d_pre_x.astype(BF)
        mb = mixed.astype(BF)
        d_mixed = (
            lam * gate_x * scale + dot_nt(pa, wa_ref[...]) + dot_nt(px, wx_ref[...])
        )
        dm_ref[here, :] = d_mixed
        wag_ref[...] += dot_tn(mb, pa)
        wxg_ref[...] += dot_tn(mb, px)
        terms = conv_terms(ext_ref[pl.ds(r0, ROWS + HALO), :], masks, ROWS)
        sums = [d_mixed * term for term in terms]
        sums += [d_mixed, d_pre_a, d_pre_x, log_gate]
        for n, value in enumerate(sums):
            vg_ref[n] += fold8(value)
        return carry

    lax.fori_loop(0, length // ROWS, block, 0)

    def shift(i, carry):
        r0 = pl.multiple_of(i * ROWS, ROWS)
        ext = dm_ref[pl.ds(r0, ROWS + HALO), :]
        masks = mask_ref[0, pl.ds(r0, ROWS + HALO), :]
        total = conv_ref[0:1, :] * ext[0:ROWS]
        for k in range(1, 4):
            moved = pltpu.roll(ext * masks[:, k - 1 : k], ROWS + HALO - k, axis=0)
            total = total + conv_ref[k : k + 1, :] * moved[0:ROWS]
        drnn_ref[0, pl.ds(r0, ROWS), :] = total.astype(BF)

        @pl.when(i == length // ROWS - 1)
        def _():
            tail_ref[0] = total[ROWS - HALO :]

        return carry

    lax.fori_loop(0, length // ROWS, shift, 0)
    head_ref[0] = dm_ref[0:HALO, :]


def block_specs(shapes):
    specs = []
    for shape, moving in shapes:
        if moving:
            specs.append(
                pl.BlockSpec((1,) + shape[1:], lambda i, n=len(shape): (i,) + (0,) * (n - 1))
            )
        else:
            specs.append(pl.BlockSpec(shape, lambda i, n=len(shape): (0,) * n))
    return specs


def seq_call(kernel, moving, fixed, outs, scratch, name, flops=0, trans=0):
    count = moving[0].shape[0]
    out_shape = [jax.ShapeDtypeStruct(shape, dtype) for shape, dtype, _ in outs]
    bytes_accessed = sum(a.size * a.dtype.itemsize for a in moving + fixed) + sum(
        o.size * o.dtype.itemsize for o in out_shape
    )
    return pl.pallas_call(
        kernel,
        grid=(count,),
        in_specs=block_specs(
            [(a.shape, True) for a in moving] + [(a.shape, False) for a in fixed]
        ),
        out_specs=block_specs([(shape, move) for shape, _, move in outs]),
        out_shape=out_shape,
        scratch_shapes=scratch,
        compiler_params=pltpu.CompilerParams(
            dimension_semantics=("arbitrary",), vmem_limit_bytes=60 * 1024 * 1024
        ),
        cost_estimate=pl.CostEstimate(
            flops=flops, bytes_accessed=bytes_accessed, transcendentals=trans
        ),
        name=name,
    )(*moving, *fixed)


def body(
    DP,
    M,
    inputs,
    cotangent,
    reset_mask,
    norm1_gain,
    w_input,
    w_branch,
    w_output,
    conv_weight,
    conv_bias,
    gate_a_weight,
    gate_a_bias,
    gate_x_weight,
    gate_x_bias,
    decay_param,
    norm2_gain,
    w_gate,
    w_up,
    w_down,
):
    heads_here, bw_here, bw = gate_a_weight.shape
    t = 4 if heads_here % 4 == 0 and DP % 4 == 0 else 2
    O = DP // t
    hpg = heads_here // t
    nh = M * hpg
    L, FH = inputs.shape
    D = FH * M
    Dl = w_input.shape[0]
    Lc = L // M
    half_cols = t * Dl
    cz = w_input.shape[1] // t
    fz = w_gate.shape[1] // t
    C = M * cz
    FC = M * fz
    conv = conv_weight.shape[0]
    parts = t // 2

    i_dp = lax.axis_index("dp")
    z = lax.axis_index("mp")
    q = i_dp % t
    o = i_dp // t

    def tp(value, j):
        return lax.ppermute(value, "dp", [(i, i ^ j) for i in range(DP)])

    def oshift(value, r):
        return lax.ppermute(
            value, "dp", [(i, ((i // t + r) % O) * t + i % t) for i in range(DP)]
        )

    def zshift(value, k):
        return lax.ppermute(value, "mp", [(i, (i + k) % M) for i in range(M)])

    def zline(value, k):
        got = lax.ppermute(
            value, "mp", [(i, i + k) for i in range(M) if 0 <= i + k < M]
        )
        return jnp.roll(got, k * cz, axis=-1)

    def after(value, *deps):
        return lax.optimization_barrier((value,) + deps)[0]

    def pick(array, index, axis=0):
        return lax.dynamic_index_in_dim(array, index, axis, keepdims=False)

    def to_chunk(value):
        rows = value.reshape(M, Lc, FH)
        own = jnp.zeros((Lc, D), value.dtype)
        far = jnp.zeros((Lc, D), value.dtype)
        for k in range(M):
            piece = pick(rows, (z + k) % M)
            if k:
                piece = zshift(piece, k)
            column = ((z - k) % M) * FH
            own = lax.dynamic_update_slice(own, piece, (0, column))
            if parts > 1:
                far = lax.dynamic_update_slice(far, tp(piece, 2), (0, column))
        groups = [jnp.concatenate([own, tp(own, 1)])]
        if parts > 1:
            groups.append(jnp.concatenate([far, tp(far, 1)]))
        return own, groups

    def from_chunk(value):
        cols = value.reshape(Lc, M, FH)
        out = jnp.zeros((M, Lc, FH), value.dtype)
        for k in range(M):
            piece = pick(cols, (z + k) % M, 1)
            if k:
                piece = zshift(piece, k)
            out = lax.dynamic_update_slice(out, piece[None], ((z - k) % M, 0, 0))
        return out.reshape(L, FH)

    def spread(own):
        groups = [jnp.concatenate([own, tp(own, 1)])]
        if parts > 1:
            far = tp(own, 2)
            groups.append(jnp.concatenate([far, tp(far, 1)]))
        return groups

    def gather_sum(partials):
        total = None
        for p in reversed(range(parts)):
            part = partials[p]
            mine = part[:Lc].astype(F32) + tp(part[Lc:], 1).astype(F32)
            if p:
                mine = tp(mine.astype(BF), 2).astype(F32)
            total = mine if total is None else total + mine
        return total

    def gather_weight(mine, dep=None):
        rows = mine.shape[1]
        block = jnp.zeros((rows, half_cols), BF)
        for j in range(t):
            piece = pick(mine, q ^ j)
            if j:
                if dep is not None:
                    piece = after(piece, dep)
                piece = tp(piece, j)
            block = lax.dynamic_update_slice(block, piece, (0, (q ^ j) * Dl))
        full = jnp.zeros((M, rows, D), BF)
        for s in range(M):
            if s:
                block = zshift(block, 1)
            for r in range(O):
                piece = oshift(block, r) if r else block
                full = lax.dynamic_update_slice(
                    full, piece[None], (s, 0, ((o - r) % O) * half_cols)
                )
        return full, block

    def scatter_grad(grad):
        rows = grad.shape[1]
        total = None
        for r in range(O):
            piece = lax.dynamic_slice(
                grad, (0, 0, ((o + r) % O) * half_cols), (M, rows, half_cols)
            )
            piece = (oshift(piece, r) if r else piece).astype(F32)
            total = piece if total is None else total + piece
        if M > 1:
            moving = total[1].astype(BF)
            for s in range(1, M):
                moving = zshift(moving, 1)
                moving = moving.astype(F32) + total[(s + 1) % M]
                if s < M - 1:
                    moving = moving.astype(BF)
        else:
            moving = total[0]
        slots = []
        send = moving.astype(BF).reshape(rows, t, Dl)
        for j in range(t):
            piece = pick(send, q ^ j, 1)
            slots.append(tp(piece, j) if j else piece)
        slots = jnp.stack(slots)
        return jnp.stack([pick(slots, q ^ k) for k in range(t)]).astype(F32)

    def rel(array, axis):
        return jnp.stack([pick(array, (z - s) % M, axis) for s in range(M)], axis)

    gate_size = 2 * hpg * bw_here * bw
    gate_rows = -(-gate_size // (16 * Dl)) * 16
    gates_flat = jnp.stack([gate_a_weight, gate_x_weight]).reshape(
        2, t, hpg, bw_here, bw
    )
    gates_flat = gates_flat.transpose(1, 0, 2, 3, 4).reshape(t, gate_size)
    gates_flat = jnp.pad(gates_flat, ((0, 0), (0, gate_rows * Dl - gate_size)))
    mixer_mine = jnp.concatenate(
        [
            w_input.T.reshape(t, cz, Dl),
            w_branch.T.reshape(t, cz, Dl),
            gates_flat.reshape(t, gate_rows, Dl),
        ],
        axis=1,
    )

    own_in, groups_in = to_chunk(inputs)
    full_a, dep_a = gather_weight(mixer_mine)
    full_b, dep_b = gather_weight(w_output.reshape(t, cz, Dl), dep_a)
    full_g, dep_g = gather_weight(w_gate.T.reshape(t, fz, Dl), dep_b)
    full_u, dep_u = gather_weight(w_up.T.reshape(t, fz, Dl), dep_g)
    full_d, _ = gather_weight(w_down.reshape(t, fz, Dl), dep_u)
    _, groups_cot = to_chunk(after(cotangent, dep_a))

    w_in_t = full_a[:, :cz].reshape(C, D)
    w_br_t = full_a[:, cz : 2 * cz].reshape(C, D)
    gates = full_a[:, 2 * cz :].reshape(M, gate_rows, DP, Dl).transpose(0, 2, 1, 3)
    gates = gates.reshape(M, DP, gate_rows * Dl)[:, :, :gate_size]
    gates = gates.reshape(M, DP, 2, hpg, bw_here, bw).transpose(2, 0, 3, 1, 4, 5)
    gates = gates.reshape(2, nh, bw, bw)
    eye = jnp.eye(nh, dtype=BF)
    dense = (gates[:, :, :, None, :] * eye[None, :, None, :, None]).reshape(2, C, C)
    wa, wx = dense[0], dense[1]
    w_out = full_b.reshape(C, D)
    w_gate_t = full_g.reshape(FC, D)
    w_up_t = full_u.reshape(FC, D)
    w_dn = full_d.reshape(FC, D)

    ng, nc = norm1_gain.shape[0], conv_bias.shape[0]
    packed = jnp.concatenate(
        [
            norm1_gain,
            norm2_gain,
            conv_weight.reshape(-1),
            conv_bias,
            gate_a_bias,
            gate_x_bias,
            decay_param,
        ]
    )
    every = lax.all_gather(packed, ("mp", "dp"), axis=0, tiled=False).astype(F32)
    gain_one = every[:, :ng].reshape(1, D)
    gain_two = every[:, ng : 2 * ng].reshape(1, D)
    vectors = every[:, 2 * ng :].reshape(M, DP, conv + 4, nc).transpose(2, 0, 1, 3)
    vectors = pick(vectors.reshape(conv + 4, M, t, cz), q, 2)
    vectors = rel(vectors, 1).reshape(conv + 4, C)
    conv_w = vectors[:conv]
    decay = vectors[conv + 3]
    log_slope = -8.0 * jax.nn.softplus(decay)
    vec = jnp.stack(
        [vectors[conv], vectors[conv + 1], vectors[conv + 2], log_slope]
        + [jnp.zeros_like(decay)] * 4
    )

    starts = jnp.maximum(
        reset_mask, (jnp.arange(L) % SEQ == 0).astype(jnp.int32)
    )
    starts = jnp.stack([starts] + [tp(starts, j) for j in range(1, t)])
    open_ = 1.0 - starts.astype(F32)
    back1 = jnp.pad(open_, ((0, 0), (1, 0)))[:, :L]
    back2 = jnp.pad(open_, ((0, 0), (2, 0)))[:, :L]
    masks = jnp.stack(
        [open_, open_ * back1, open_ * back1 * back2, 1.0 - open_], axis=-1
    )
    masks = jnp.pad(masks, ((0, 0), (0, HALO), (0, 0)))
    masks = lax.dynamic_slice(masks, (0, z * Lc, 0), (t, Lc + HALO, 4))

    def normed(value, gain):
        wide = value.astype(F32)
        scale = lax.rsqrt(jnp.mean(wide * wide, axis=1, keepdims=True) + epsilon)
        return wide * scale, scale

    n1, rnn, gin, fwd, halos = [], [], [], [], []
    for p in range(parts):
        unit, _ = normed(groups_in[p], gain_one)
        n1.append((unit * gain_one).astype(BF))
        rnn.append(dot_nt(n1[p], w_in_t).reshape(2, Lc, C))
        gin.append(dot_nt(n1[p], w_br_t).reshape(2, Lc, C))
        halos.append(zline(rnn[p][:, Lc - HALO :], 1))
        shape = (2, Lc, C)
        fwd.append(
            seq_call(
                forward_kernel,
                [rnn[p], halos[p], masks[2 * p : 2 * p + 2]],
                [conv_w, vec, wa, wx],
                [(shape, F32, True)] * 5 + [((2, 8, C), F32, True)],
                [pltpu.VMEM((Lc + HALO, C), F32)],
                "recurrence",
                flops=2 * Lc * 2 * C * C * 4,
                trans=6 * 2 * Lc * C,
            )
        )

    def chain(ends, sign):
        total = jnp.zeros_like(ends[:, 4:5])
        for k in reversed(range(1, M)):
            got = zline(ends, sign * k)
            total = got[:, 4:5] + got[:, 0:1] * total
        return total

    state, mixer, cin = [], [], []
    rec_partial = []
    for p in range(parts):
        _, _, _, h, prod, ends = fwd[p]
        cin.append(chain(ends, 1))
        state.append(h + prod * cin[p])
        gelu, _ = gelu_parts(gin[p])
        mixer.append((gelu * state[p]).astype(BF).reshape(2 * Lc, C))
        rec_partial.append(dot_nn(mixer[p], w_out).astype(BF))
    resid_mid = own_in.astype(F32) + gather_sum(rec_partial)

    unit_two, scale_two = normed(resid_mid, gain_two)
    n2 = spread((unit_two * gain_two).astype(BF))
    gate_val = [dot_nt(v, w_gate_t) for v in n2]
    up_val = [dot_nt(v, w_up_t) for v in n2]
    hidden = [(gelu_parts(g)[0] * u).astype(BF) for g, u in zip(gate_val, up_val)]
    out_sum = gather_sum([dot_nn(h, w_dn).astype(BF) for h in hidden])
    output = from_chunk((resid_mid + out_sum).astype(BF))

    def summed(lefts, rights):
        total = None
        for left, right in zip(lefts, rights):
            term = dot_tn(left, right)
            total = term if total is None else total + term
        return total.astype(BF).reshape(M, -1, D)

    grad_down = scatter_grad(summed(hidden, groups_cot))
    d_gate, d_up, dn2_partial = [], [], []
    for p in range(parts):
        d_hidden = dot_nt(groups_cot[p], w_dn)
        gelu, slope = gelu_parts(gate_val[p])
        d_gate.append((d_hidden * up_val[p] * slope).astype(BF))
        d_up.append((d_hidden * gelu).astype(BF))
        dn2_partial.append(
            (dot_nn(d_gate[p], w_gate_t) + dot_nn(d_up[p], w_up_t)).astype(BF)
        )
    d_n2 = gather_sum(dn2_partial)
    grad_gate = scatter_grad(summed(d_gate, n2))
    grad_up = scatter_grad(summed(d_up, n2))

    def norm_back(grad, unit, scale, gain):
        weighted = grad * gain
        dots = jnp.mean(weighted * unit, axis=1, keepdims=True)
        return scale * (weighted - unit * dots), jnp.sum(grad * unit, axis=0)

    back_two, gain_two_grad = norm_back(d_n2, unit_two, scale_two, gain_two)
    d_mid = groups_cot[0][:Lc].astype(F32) + back_two
    d_branch = spread(d_mid.astype(BF))

    adj, grad_vec, grad_wa, grad_wx = [], 0.0, 0.0, 0.0
    d_rnn, d_gin, dn1_partial = [], [], []
    grad_output = scatter_grad(summed(mixer, d_branch))
    for p in range(parts):
        d_mixer = dot_nt(d_branch[p], w_out).reshape(2, Lc, C)
        mixed, gate_a, gate_x = fwd[p][:3]
        here = masks[2 * p : 2 * p + 2]
        shape = (2, Lc, C)
        lam, prod, dgi, ends = seq_call(
            adjoint_kernel,
            [d_mixer, gin[p], state[p], gate_a, here],
            [vec],
            [(shape, F32, True)] * 2
            + [(shape, BF, True), ((2, 8, C), F32, True)],
            [],
            "adjoint",
            trans=2 * 2 * Lc * C,
        )
        mu = chain(ends, -1)
        edge = jnp.concatenate(
            [jnp.broadcast_to(cin[p], (2, 4, C)), jnp.broadcast_to(mu, (2, 4, C))], 1
        )
        drnn, head, tail, wag, wxg, vg = seq_call(
            backward_kernel,
            [
                lam,
                prod,
                state[p],
                gate_a,
                gate_x,
                mixed,
                rnn[p],
                halos[p],
                here,
                edge,
            ],
            [conv_w, vec, wa, wx],
            [
                (shape, BF, True),
                ((2, HALO, C), F32, True),
                ((2, HALO, C), F32, True),
                ((C, C), F32, False),
                ((C, C), F32, False),
                ((8, 8, C), F32, False),
            ],
            [pltpu.VMEM((Lc + HALO, C), F32)] * 3,
            "recurrence_back",
            flops=2 * Lc * 2 * C * C * 4,
            trans=4 * 2 * Lc * C,
        )
        following = zline(head, -1)
        fix = [jnp.zeros((2, 1, C), F32)] * HALO
        for k in range(1, 4):
            for n in range(k):
                row = HALO - k + n
                fix[row] = fix[row] + conv_w[k] * (
                    here[:, Lc + n : Lc + n + 1, k - 1 : k] * following[:, n : n + 1]
                )
        tail = (tail + jnp.concatenate(fix, axis=1)).astype(BF)
        drnn = lax.dynamic_update_slice(drnn, tail, (0, Lc - HALO, 0))
        grad_vec = grad_vec + vg
        grad_wa = grad_wa + wag
        grad_wx = grad_wx + wxg
        d_rnn.append(drnn.reshape(2 * Lc, C))
        d_gin.append(dgi.reshape(2 * Lc, C))
        dn1_partial.append(
            (dot_nn(d_rnn[p], w_in_t) + dot_nn(d_gin[p], w_br_t)).astype(BF)
        )
    d_n1 = gather_sum(dn1_partial)
    unit_one, scale_one = normed(own_in, gain_one)
    back_one, gain_one_grad = norm_back(d_n1, unit_one, scale_one, gain_one)
    input_grad = from_chunk((d_mid + back_one).astype(BF)).astype(F32)

    blocks = [
        jnp.stack([g[n * bw : (n + 1) * bw, n * bw : (n + 1) * bw] for n in range(nh)])
        for g in (grad_wa, grad_wx)
    ]
    gates_grad = jnp.stack(blocks).reshape(2, M, hpg, DP, bw_here, bw)
    gates_grad = gates_grad.transpose(1, 3, 0, 2, 4, 5).reshape(M, DP, gate_size)
    gates_grad = jnp.pad(
        gates_grad, ((0, 0), (0, 0), (0, gate_rows * Dl - gate_size))
    )
    gates_grad = gates_grad.reshape(M, DP, gate_rows, Dl).transpose(0, 2, 1, 3)
    gates_grad = gates_grad.reshape(M, gate_rows, D).astype(BF)
    grad_a = scatter_grad(
        jnp.concatenate([summed(d_rnn, n1), summed(d_gin, n1), gates_grad], axis=1)
    )

    small = jnp.sum(grad_vec, axis=1).reshape(2 * conv, M, cz)
    small = jnp.stack(
        [pick(small, (z - b) % M, 1) for b in range(M)], axis=1
    )
    slots = jnp.zeros((2 * conv, M, t, cz), F32)
    slots = lax.dynamic_update_slice(slots, small[:, :, None], (0, 0, q, 0))
    flat = jnp.concatenate([slots.reshape(-1), gain_one_grad, gain_two_grad])
    flat = lax.psum(flat, ("dp", "mp"))
    count = 2 * conv * M * t * cz
    vectors = flat[:count].reshape(2 * conv, M, DP, nc)
    mine = pick(pick(vectors, z, 1), i_dp, 1)
    place = z * DP + i_dp
    gain_one_grad = pick(flat[count : count + D].reshape(-1, ng), place)
    gain_two_grad = pick(flat[count + D :].reshape(-1, ng), place)
    decay_grad = mine[conv + 3] * (-8.0 * jax.nn.sigmoid(decay_param.astype(F32)))

    gates_back = grad_a[:, 2 * cz :].reshape(t, gate_rows * Dl)[:, :gate_size]
    gates_back = gates_back.reshape(t, 2, hpg, bw_here, bw).transpose(1, 0, 2, 3, 4)
    gates_back = gates_back.reshape(2, heads_here, bw_here, bw)

    return (
        output,
        input_grad,
        gain_one_grad,
        grad_a[:, :cz].reshape(t * cz, Dl).T,
        grad_a[:, cz : 2 * cz].reshape(t * cz, Dl).T,
        grad_output.reshape(t * cz, Dl),
        mine[:conv],
        mine[conv],
        gates_back[0],
        mine[conv + 1],
        gates_back[1],
        mine[conv + 2],
        decay_grad,
        gain_two_grad,
        grad_gate.reshape(t * fz, Dl).T,
        grad_up.reshape(t * fz, Dl).T,
        grad_down.reshape(t * fz, Dl),
    )


def solution(mesh):
    both = P(("mp", "dp"))
    wide = P("dp", "mp")
    tall = P("mp", "dp")
    taps = P(None, ("mp", "dp"))
    gate = P("mp", "dp", None)
    params = (both, wide, wide, tall, taps, both, gate, both, gate, both, both, both, wide, wide, tall)
    return jax.shard_map(
        functools.partial(body, mesh.shape["dp"], mesh.shape["mp"]),
        mesh=mesh,
        in_specs=(wide, wide, P("dp")) + params,
        out_specs=(wide, wide) + params,
        check_vma=False,
    )
```

time: 3330 us -> 1820 us (0.55)
  waiting for transfers between devices: 1990 us -> 814 us
  local copies, waits for them, and re-layouts: 574 us -> 231 us
  starting transfers between devices: 0.89 us -> 167 us
  other arithmetic: 259 us -> 125 us
  Pallas kernels: 0 us -> 131 us
  blocking collectives: 124 us -> 39.7 us
  matrix products: 346 us -> 282 us
    reduce_scatter x10 -> x0, waiting for transfers between devices: 1340 us -> none  [the longest x2 489 us: reduce_input(): lax.psum_scatter(partial_value, 'mp', scatter_dimension=1, tiled=True)]
    ppermute x0 -> x146, waiting for transfers between devices: none -> 669 us  [the longest x42 314 us: zshift(): return lax.ppermute(value, 'mp', [(i, (i + k) % M) for i in range(M)])]
    all_gather x10 -> x0, waiting for transfers between devices: 648 us -> none  [the longest x2 295 us: widen_grad(): return lax.all_gather(rows, 'mp', axis=1, tiled=True)]
    pad x88 -> x2, local copies, waits for them, and re-layouts: 272 us -> 0.06 us  [the longest x1 0.04 us: body(): jnp.pad(gates_grad, ((0, 0), (0, 0), (0, gate_rows * Dl - gate_size)))]
    slice x89 -> x62, local copies, waits for them, and re-layouts: 229 us -> 29.6 us  [the longest x8 11.1 us: gather_sum(): mine = part[:Lc].astype(F32) + tp(part[Lc:], 1).astype(F32)]
    ppermute x0 -> x146, starting transfers between devices: none -> 167 us  [the longest x42 67.8 us: zshift(): return lax.ppermute(value, 'mp', [(i, (i + k) % M) for i in range(M)])]
    psum x0 -> x1, waiting for transfers between devices: none -> 145 us  [body(): flat = lax.psum(flat, ('dp', 'mp'))]
    pallas_call x0 -> x6, Pallas kernels: none -> 131 us  [seq_call(): pl.pallas_call(kernel, grid=(count,), in_specs=block_specs([(a.shape, Tru...]
  transfers between devices with their start and end apart: 22 -> 147, of which waited for: 17 -> 55; matrix products, arithmetic and copies ran while one was open for 18% -> 33% of each run, Pallas kernels for 0% -> 7%
where the time goes in v1:
time: 1820 us; the launch traced here: 1810 us
  waiting for transfers between devices  814 us (45%)
  matrix products  282 us (15%)
  local copies, waits for them, and re-layouts  231 us (13%)
  starting transfers between devices  167 us (9%)
  Pallas kernels  131 us (7%)
  other arithmetic  125 us (7%)
  blocking collectives  39.7 us (2%)
    ppermute x42, waiting for transfers between devices, zshift(): return lax.ppermute(value, 'mp', [(i, (i + k) % M) for i in range(M)])  314 us
    ppermute x25, waiting for transfers between devices, oshift(): lax.ppermute(value, 'dp', [(i, (i // t + r) % O * t + i % t) for i in ran...  214 us
    psum x1, waiting for transfers between devices, body(): flat = lax.psum(flat, ('dp', 'mp'))  145 us
    ppermute x63, waiting for transfers between devices, tp(): return lax.ppermute(value, 'dp', [(i, i ^ j) for i in range(DP)])  135 us
    pallas_call x6, Pallas kernels, seq_call(): pl.pallas_call(kernel, grid=(count,), in_specs=block_specs([(a.shape, Tru...  131 us
    dot_general x12, matrix products, dot_nt(): lax.dot_general(left, right, (((1,), (1,)), ((), ())), preferred_element_...  98.1 us
    dot_general x12, matrix products, dot_tn(): lax.dot_general(left, right, (((0,), (0,)), ((), ())), preferred_element_...  96.5 us
    dot_general x12, matrix products, dot_nn(): return jnp.dot(left, right, preferred_element_type=F32)  87.8 us
  transfers between devices with their start and end apart: 147, of which 55 were waited for; matrix products, arithmetic and copies ran while one was open for 33% of the time, Pallas kernels for 7%

profile of v1, /device:TPU:8, one launch (start us, length us, event | category | flops | bytes accessed | tf_op | source)
XLA Modules:
  0.0 1807.4 jit_solution(7938334996202949993)
XLA Ops:
  18.0 39.7 %all-gather.1 = bf16[32,1,768]{2,1,0:T(2,128)(2,1)S(1)} all-gather(bf16[1,1,768]{2,1,0:T(2,128)(2,1)S(1)} %reshape.759), channel_id=2, replica_groups=mesh['dp'=8,'mp'=4] {'mp','dp'}, dimensions={0}, use_global_device_ids=true | all-gather | bytes 50688 | tf_op jit(solution)/shard_map/all_gather | solution.py:548
  199.2 32.5 %collective-permute-done.29 = bf16[160,1024]{1,0:T(8,128)(2,1)} collective-permute-done((bf16[160,1024]{1,0:T(8,128)(2,1)S(1)}, bf16[160,1024]{1,0:T(8,128)(2,1)}, u32[]{:S(2)}, u32[]{:S(2)}) %collective-permute-start.29) | collective-permute-done | bytes 327712 | tf_op jit(solution)/shard_map/ppermute | solution.py:390
  314.4 20.9 %recurrence.3 = (f32[2,512,640]{2,1,0:T(8,128)}, f32[2,512,640]{2,1,0:T(8,128)}, f32[2,512,640]{2,1,0:T(8,128)}, f32[2,512,640]{2,1,0:T(8,128)}, f32[2,512,640]{2,1,0:T(8,128)}, /*index=5*/f32[2,8,640]{2,1,0:T(8,128)}) custom-call(f32[2,512,640]{2,1,0:T(8,128)} %copy-done.56, f32[2,8,640]{2,1,0:T(8,128)} %pad_maximum_fusion.23.halo_ref, ...), custom_call_target="tpu_custom_call" | custom-call | flops 3355443200 | bytes 17496320 | tf_op jit(solution)/shard_map/recurrence/pallas_call | solution.py:318
  339.9 20.8 %recurrence.2 = (f32[2,512,640]{2,1,0:T(8,128)}, f32[2,512,640]{2,1,0:T(8,128)}, f32[2,512,640]{2,1,0:T(8,128)}, f32[2,512,640]{2,1,0:T(8,128)}, f32[2,512,640]{2,1,0:T(8,128)}, /*index=5*/f32[2,8,640]{2,1,0:T(8,128)}) custom-call(f32[2,512,640]{2,1,0:T(8,128)} %copy-done.55, f32[2,8,640]{2,1,0:T(8,128)} %pad_maximum_fusion.22.halo_ref, ...), custom_call_target="tpu_custom_call" | custom-call | flops 3355443200 | bytes 17496320 | tf_op jit(solution)/shard_map/recurrence/pallas_call | solution.py:318
  442.7 12.6 collective-permute-done.53
  463.4 48.2 %collective-permute-done.57 = bf16[384,256]{1,0:T(8,128)(2,1)S(1)} collective-permute-done((bf16[384,256]{1,0:T(8,128)(2,1)S(1)}, bf16[384,256]{1,0:T(8,128)(2,1)S(1)}, u32[]{:S(2)}, u32[]{:S(2)}) %collective-permute-start.57) | collective-permute-done | bytes 196640 | tf_op jit(solution)/shard_map/ppermute | solution.py:382
  513.0 20.0 %collective-permute-done.59 = bf16[384,1024]{1,0:T(8,128)(2,1)S(1)} collective-permute-done((bf16[384,1024]{1,0:T(8,128)(2,1)S(1)}, bf16[384,1024]{1,0:T(8,128)(2,1)S(1)}, u32[]{:S(2)}, u32[]{:S(2)}) %collective-permute-start.59) | collective-permute-done | bytes 786464 | tf_op jit(solution)/shard_map/ppermute | solution.py:390
  533.5 20.0 %collective-permute-done.61 = bf16[384,1024]{1,0:T(8,128)(2,1)S(1)} collective-permute-done((bf16[384,1024]{1,0:T(8,128)(2,1)S(1)}, bf16[384,1024]{1,0:T(8,128)(2,1)S(1)}, u32[]{:S(2)}, u32[]{:S(2)}) %collective-permute-start.61) | collective-permute-done | bytes 786464 | tf_op jit(solution)/shard_map/ppermute | solution.py:390
  558.5 14.7 collective-permute-done.63
  586.0 15.5 collective-permute-done.64
  636.4 26.9 %collective-permute-done.43 = bf16[512,2048]{1,0:T(8,128)(2,1)} collective-permute-done((bf16[512,2048]{1,0:T(8,128)(2,1)S(1)}, bf16[512,2048]{1,0:T(8,128)(2,1)}, u32[]{:S(2)}, u32[]{:S(2)}) %collective-permute-start.43) | collective-permute-done | bytes 2097184 | tf_op jit(solution)/shard_map/ppermute | solution.py:382
  668.8 15.0 collective-permute-done.72
  684.0 13.4 collective-permute-done.74
  706.4 17.2 fusion.21
  756.2 13.1 fusion.147
  802.4 16.2 fusion.15
  936.5 55.8 %collective-permute-done.132 = bf16[4,384,1024]{1,2,0:T(8,128)(2,1)} collective-permute-done((bf16[4,384,1024]{1,2,0:T(8,128)(2,1)}, bf16[4,384,1024]{1,2,0:T(8,128)(2,1)}, u32[]{:S(2)}, u32[]{:S(2)}) %collective-permute-start.132) | collective-permute-done | bytes 3145760 | tf_op jit(solution)/shard_map/ppermute | solution.py:385
  996.3 63.0 %collective-permute-done.139 = bf16[4,384,1024]{1,2,0:T(8,128)(2,1)} collective-permute-done((bf16[4,384,1024]{1,2,0:T(8,128)(2,1)}, bf16[4,384,1024]{1,2,0:T(8,128)(2,1)}, u32[]{:S(2)}, u32[]{:S(2)}) %collective-permute-start.139) | collective-permute-done | bytes 3145760 | tf_op jit(solution)/shard_map/ppermute | solution.py:385
  1068.8 12.8 collective-permute-done.133
  1083.7 13.7 collective-permute-done.140
  1120.5 15.9 collective-permute-done.134
  1138.6 14.5 collective-permute-done.141
  1173.0 13.9 collective-permute-done.135
  1248.1 12.5 adjoint.3
  1277.0 32.2 %recurrence_back.3 = (bf16[2,512,640]{2,1,0:T(8,128)(2,1)}, f32[2,8,640]{2,1,0:T(8,128)}, f32[2,8,640]{2,1,0:T(8,128)}, f32[640,640]{1,0:T(8,128)}, f32[640,640]{1,0:T(8,128)}, /*index=5*/f32[8,8,640]{2,1,0:T(8,128)}) custom-call(f32[2,512,640]{2,1,0:T(8,128)} %get-tuple-element.92.lam_ref, f32[2,512,640]{2,1,0:T(8,128)} %get-tuple-element.93.q_ref, ...), custom_call_target="tpu_custom_call" | custom-call | flops 3355443200 | bytes 24951040 | tf_op jit(solution)/shard_map/recurrence_back/pallas_call | solution.py:318
  1360.9 32.4 %recurrence_back.2 = (bf16[2,512,640]{2,1,0:T(8,128)(2,1)}, f32[2,8,640]{2,1,0:T(8,128)}, f32[2,8,640]{2,1,0:T(8,128)}, f32[640,640]{1,0:T(8,128)}, f32[640,640]{1,0:T(8,128)}, /*index=5*/f32[8,8,640]{2,1,0:T(8,128)}) custom-call(f32[2,512,640]{2,1,0:T(8,128)} %get-tuple-element.82.lam_ref, f32[2,512,640]{2,1,0:T(8,128)} %get-tuple-element.83.q_ref, ...), custom_call_target="tpu_custom_call" | custom-call | flops 3355443200 | bytes 24951040 | tf_op jit(solution)/shard_map/recurrence_back/pallas_call | solution.py:318
  1473.1 20.9 %collective-permute-done.111 = bf16[4,352,1024]{2,1,0:T(8,128)(2,1)} collective-permute-done((bf16[4,352,1024]{2,1,0:T(8,128)(2,1)}, bf16[4,352,1024]{2,1,0:T(8,128)(2,1)}, u32[]{:S(2)}, u32[]{:S(2)}) %collective-permute-start.111) | collective-permute-done | bytes 2883616 | tf_op jit(solution)/shard_map/ppermute | solution.py:385
  1500.6 12.6 collective-permute-done.124
  1550.0 13.4 constant_dynamic-slice_fusion.56
  1578.1 145.1 %all-reduce.7.cloned.1.call-done = f32[24576]{0:T(1024)} async-done(((f32[24576]{0:T(1024)}), f32[24576]{0:T(1024)}) %all-reduce.7.cloned.1.call-update) | async-done | bytes 98320 | tf_op jit(solution)/shard_map/psum | solution.py:752
  1735.7 25.4 %collective-permute-done.109 = bf16[512,512]{1,0:T(8,128)(2,1)S(1)} collective-permute-done((bf16[512,512]{1,0:T(8,128)(2,1)}, bf16[512,512]{1,0:T(8,128)(2,1)S(1)}, u32[]{:S(2)}, u32[]{:S(2)}) %collective-permute-start.109) | collective-permute-done | bytes 524320 | tf_op jit(solution)/shard_map/ppermute | solution.py:390
  1761.1 15.9 collective-permute-done.110
  (1003 shorter events, 942.5 us)
Async XLA Ops:
  7.3 1715.9 %all-reduce.7.cloned.1.call-start = ((), (), s32[]{:S(2)}) async-start(), calls=%async_computation | async-start | bytes 196608 | tf_op jit(solution)/shard_map/psum | solution.py:752
  8.0 76.2 %collective-permute-start.21 = (s32[2048]{0:T(1024)S(1)}, s32[2048]{0:T(1024)S(1)}, u32[]{:S(2)}, u32[]{:S(2)}) collective-permute-start(s32[2048]{0:T(1024)S(1)} %convert_maximum_fusion), channel_id=1, source_target_pairs={{0,12},{4,8},{8,4},{12,0},{16,28},{20,24},{24,20},{28,16},{1,13},{... | collective-permute-start | bytes 24584 | tf_op jit(solution)/shard_map/ppermute | solution.py:382
  9.0 75.9 %collective-permute-start.20 = (s32[2048]{0:T(1024)S(1)}, s32[2048]{0:T(1024)}, u32[]{:S(2)}, u32[]{:S(2)}) collective-permute-start(s32[2048]{0:T(1024)S(1)} %convert_maximum_fusion), channel_id=1, source_target_pairs={{0,8},{4,12},{8,0},{12,4},{16,24},{20,28},{24,16},{28,20},{1,9},{5... | collective-permute-start | bytes 24584 | tf_op jit(solution)/shard_map/ppermute | solution.py:382
  9.6 75.3 %collective-permute-start.19 = (s32[2048]{0:T(1024)S(1)}, s32[2048]{0:T(1024)}, u32[]{:S(2)}, u32[]{:S(2)}) collective-permute-start(s32[2048]{0:T(1024)S(1)} %convert_maximum_fusion), channel_id=1, source_target_pairs={{0,4},{4,0},{8,12},{12,8},{16,20},{20,16},{24,28},{28,24},{1,5},{5... | collective-permute-start | bytes 24584 | tf_op jit(solution)/shard_map/ppermute | solution.py:382
  12.1 104.4 %collective-permute-start.3 = (bf16[512,512]{1,0:T(8,128)(2,1)}, bf16[512,512]{1,0:T(8,128)(2,1)}, u32[]{:S(2)}, u32[]{:S(2)}) collective-permute-start(bf16[512,512]{1,0:T(8,128)(2,1)} %get-tuple-element.240), channel_id=1, source_target_pairs={{0,8},{4,12},{8,0},{12,4},{16,24},{20,28},{24,16},{28,20},{1,9},{5... | collective-permute-start | bytes 1572872 | tf_op jit(solution)/shard_map/ppermute | solution.py:382
  16.2 101.1 %collective-permute-start = (bf16[512,512]{1,0:T(8,128)(2,1)}, bf16[512,512]{1,0:T(8,128)(2,1)}, u32[]{:S(2)}, u32[]{:S(2)}) collective-permute-start(bf16[512,512]{1,0:T(8,128)(2,1)} %get-tuple-element.272), channel_id=1, source_target_pairs={{0,1},{1,2},{2,3},{3,0},{4,5},{5,6},{6,7},{7,4},{8,9},{9,10},{10,1... | collective-permute-start | bytes 1572872 | tf_op jit(solution)/shard_map/ppermute | solution.py:390
  243.8 136.1 %collective-permute-start.86 = (bf16[512,512]{1,0:T(8,128)(2,1)}, bf16[512,512]{1,0:T(8,128)(2,1)}, u32[]{:S(2)}, u32[]{:S(2)}) collective-permute-start(bf16[512,512]{1,0:T(8,128)(2,1)} %collective-permute-done.82), channel_id=1, source_target_pairs={{0,8},{4,12},{8,0},{12,4},{16,24},{20,28},{24,16},{28,20},{1,9},{5... | collective-permute-start | bytes 1572872 | tf_op jit(solution)/shard_map/ppermute | solution.py:382
  254.2 148.3 %collective-permute-start.87 = (bf16[512,512]{1,0:T(8,128)(2,1)}, bf16[512,512]{1,0:T(8,128)(2,1)}, u32[]{:S(2)}, u32[]{:S(2)}) collective-permute-start(bf16[512,512]{1,0:T(8,128)(2,1)} %collective-permute-done.83), channel_id=1, source_target_pairs={{0,8},{4,12},{8,0},{12,4},{16,24},{20,28},{24,16},{28,20},{1,9},{5... | collective-permute-start | bytes 1572872 | tf_op jit(solution)/shard_map/ppermute | solution.py:382
  423.4 130.7 %collective-permute-start.42 = (bf16[512,2048]{1,0:T(8,128)(2,1)}, bf16[512,2048]{1,0:T(8,128)(2,1)}, u32[]{:S(2)}, u32[]{:S(2)}) collective-permute-start(bf16[512,2048]{1,0:T(8,128)(2,1)} %slice.767), channel_id=1, source_target_pairs={{0,4},{4,0},{8,12},{12,8},{16,20},{20,16},{24,28},{28,24},{1,5},{5... | collective-permute-start | bytes 6291464 | tf_op jit(solution)/shard_map/ppermute | solution.py:382
  437.5 74.4 %collective-permute-start.52 = (bf16[384,1024]{1,0:T(8,128)(2,1)S(1)}, bf16[384,1024]{1,0:T(8,128)(2,1)S(1)}, u32[]{:S(2)}, u32[]{:S(2)}) collective-permute-start(bf16[384,1024]{1,0:T(8,128)(2,1)S(1)} %collective-permute-done.51), channel_id=1, source_target_pairs={{0,16},{4,20},{8,24},{12,28},{16,0},{20,4},{24,8},{28,12},{1,17},{... | collective-permute-start | bytes 2359304 | tf_op jit(solution)/shard_map/ppermute | solution.py:385
  458.0 96.1 %collective-permute-start.36 = (bf16[512,2048]{1,0:T(8,128)(2,1)S(1)}, bf16[512,2048]{1,0:T(8,128)(2,1)}, u32[]{:S(2)}, u32[]{:S(2)}) collective-permute-start(bf16[512,2048]{1,0:T(8,128)(2,1)S(1)} %add_convert_fusion.14), channel_id=1, source_target_pairs={{0,8},{4,12},{8,0},{12,4},{16,24},{20,28},{24,16},{28,20},{1,9},{5... | collective-permute-start | bytes 6291464 | tf_op jit(solution)/shard_map/ppermute | solution.py:382
  533.3 164.2 %collective-permute-start.92 = (bf16[512,2048]{1,0:T(8,128)(2,1)S(1)}, bf16[512,2048]{1,0:T(8,128)(2,1)}, u32[]{:S(2)}, u32[]{:S(2)}) collective-permute-start(bf16[512,2048]{1,0:T(8,128)(2,1)S(1)} %copy-done.32), channel_id=1, source_target_pairs={{0,4},{4,0},{8,12},{12,8},{16,20},{20,16},{24,28},{28,24},{1,5},{5... | collective-permute-start | bytes 6291464 | tf_op jit(solution)/shard_map/ppermute | solution.py:382
  601.6 178.6 %collective-permute-start.89 = (bf16[512,2048]{1,0:T(8,128)(2,1)}, bf16[512,2048]{1,0:T(8,128)(2,1)}, u32[]{:S(2)}, u32[]{:S(2)}) collective-permute-start(bf16[512,2048]{1,0:T(8,128)(2,1)} %constant_dynamic-update-slice_fusion.2), channel_id=1, source_target_pairs={{0,4},{4,0},{8,12},{12,8},{16,20},{20,16},{24,28},{28,24},{1,5},{5... | collective-permute-start | bytes 6291464 | tf_op jit(solution)/shard_map/ppermute | solution.py:382
  666.7 125.2 %collective-permute-start.44 = (bf16[512,2048]{1,0:T(8,128)(2,1)}, bf16[512,2048]{1,0:T(8,128)(2,1)}, u32[]{:S(2)}, u32[]{:S(2)}) collective-permute-start(bf16[512,2048]{1,0:T(8,128)(2,1)} %collective-permute-done.43), channel_id=1, source_target_pairs={{0,4},{4,0},{8,12},{12,8},{16,20},{20,16},{24,28},{28,24},{1,5},{5... | collective-permute-start | bytes 6291464 | tf_op jit(solution)/shard_map/ppermute | solution.py:382
  746.6 351.0 %collective-permute-start.93 = (bf16[512,2048]{1,0:T(8,128)(2,1)}, bf16[512,2048]{1,0:T(8,128)(2,1)}, u32[]{:S(2)}, u32[]{:S(2)}) collective-permute-start(bf16[512,2048]{1,0:T(8,128)(2,1)} %slice.776), channel_id=1, source_target_pairs={{0,4},{4,0},{8,12},{12,8},{16,20},{20,16},{24,28},{28,24},{1,5},{5... | collective-permute-start | bytes 6291464 | tf_op jit(solution)/shard_map/ppermute | solution.py:382
  838.6 89.9 %collective-permute-start.90 = (bf16[512,2048]{1,0:T(8,128)(2,1)}, bf16[512,2048]{1,0:T(8,128)(2,1)}, u32[]{:S(2)}, u32[]{:S(2)}) collective-permute-start(bf16[512,2048]{1,0:T(8,128)(2,1)} %slice.774), channel_id=1, source_target_pairs={{0,4},{4,0},{8,12},{12,8},{16,20},{20,16},{24,28},{28,24},{1,5},{5... | collective-permute-start | bytes 6291464 | tf_op jit(solution)/shard_map/ppermute | solution.py:382
  853.7 77.9 %collective-permute-start.125 = (bf16[4,384,1024]{1,2,0:T(8,128)(2,1)}, bf16[4,384,1024]{1,2,0:T(8,128)(2,1)}, u32[]{:S(2)}, u32[]{:S(2)}) collective-permute-start(bf16[4,384,1024]{1,2,0:T(8,128)(2,1)} %copy.345), channel_id=1, source_target_pairs={{0,16},{4,20},{8,24},{12,28},{16,0},{20,4},{24,8},{28,12},{1,17},{... | collective-permute-start | bytes 9437192 | tf_op jit(solution)/shard_map/ppermute | solution.py:385
  896.3 96.0 %collective-permute-start.132 = (bf16[4,384,1024]{1,2,0:T(8,128)(2,1)}, bf16[4,384,1024]{1,2,0:T(8,128)(2,1)}, u32[]{:S(2)}, u32[]{:S(2)}) collective-permute-start(bf16[4,384,1024]{1,2,0:T(8,128)(2,1)} %copy.347), channel_id=1, source_target_pairs={{0,16},{4,20},{8,24},{12,28},{16,0},{20,4},{24,8},{28,12},{1,17},{... | collective-permute-start | bytes 9437192 | tf_op jit(solution)/shard_map/ppermute | solution.py:385
  902.6 156.7 %collective-permute-start.139 = (bf16[4,384,1024]{1,2,0:T(8,128)(2,1)}, bf16[4,384,1024]{1,2,0:T(8,128)(2,1)}, u32[]{:S(2)}, u32[]{:S(2)}) collective-permute-start(bf16[4,384,1024]{1,2,0:T(8,128)(2,1)} %copy.349), channel_id=1, source_target_pairs={{0,16},{4,20},{8,24},{12,28},{16,0},{20,4},{24,8},{28,12},{1,17},{... | collective-permute-start | bytes 9437192 | tf_op jit(solution)/shard_map/ppermute | solution.py:385
  928.5 133.5 %collective-permute-start.75 = (bf16[512,2048]{1,0:T(8,128)(2,1)}, bf16[512,2048]{1,0:T(8,128)(2,1)}, u32[]{:S(2)}, u32[]{:S(2)}) collective-permute-start(bf16[512,2048]{1,0:T(8,128)(2,1)} %slice.770), channel_id=1, source_target_pairs={{0,4},{4,0},{8,12},{12,8},{16,20},{20,16},{24,28},{28,24},{1,5},{5... | collective-permute-start | bytes 6291464 | tf_op jit(solution)/shard_map/ppermute | solution.py:382
  931.6 168.2 %collective-permute-start.91 = (bf16[512,2048]{1,0:T(8,128)(2,1)S(1)}, bf16[512,2048]{1,0:T(8,128)(2,1)S(1)}, u32[]{:S(2)}, u32[]{:S(2)}) collective-permute-start(bf16[512,2048]{1,0:T(8,128)(2,1)S(1)} %add_convert_fusion.11), channel_id=1, source_target_pairs={{0,8},{4,12},{8,0},{12,4},{16,24},{20,28},{24,16},{28,20},{1,9},{5... | collective-permute-start | bytes 6291464 | tf_op jit(solution)/shard_map/ppermute | solution.py:382
  992.3 74.9 %collective-permute-start.126 = (bf16[384,1024]{0,1:T(8,128)(2,1)}, bf16[384,1024]{0,1:T(8,128)(2,1)}, u32[]{:S(2)}, u32[]{:S(2)}) collective-permute-start(bf16[384,1024]{0,1:T(8,128)(2,1)} %fusion.78), channel_id=1, source_target_pairs={{0,1},{1,2},{2,3},{3,0},{4,5},{5,6},{6,7},{7,4},{8,9},{9,10},{10,1... | collective-permute-start | bytes 2359304 | tf_op jit(solution)/shard_map/ppermute | solution.py:390
  1067.2 87.0 %collective-permute-start.78 = (bf16[512,2048]{1,0:T(8,128)(2,1)S(1)}, bf16[512,2048]{1,0:T(8,128)(2,1)S(1)}, u32[]{:S(2)}, u32[]{:S(2)}) collective-permute-start(bf16[512,2048]{1,0:T(8,128)(2,1)S(1)} %copy-done.72), channel_id=1, source_target_pairs={{0,4},{4,0},{8,12},{12,8},{16,20},{20,16},{24,28},{28,24},{1,5},{5... | collective-permute-start | bytes 6291464 | tf_op jit(solution)/shard_map/ppermute | solution.py:382
  1163.9 76.3 %collective-permute-start.102 = (bf16[512,2048]{1,0:T(8,128)(2,1)}, bf16[512,2048]{1,0:T(8,128)(2,1)}, u32[]{:S(2)}, u32[]{:S(2)}) collective-permute-start(bf16[512,2048]{1,0:T(8,128)(2,1)} %get-tuple-element.229), channel_id=1, source_target_pairs={{0,4},{4,0},{8,12},{12,8},{16,20},{20,16},{24,28},{28,24},{1,5},{5... | collective-permute-start | bytes 6291464 | tf_op jit(solution)/shard_map/ppermute | solution.py:382
  1163.9 79.2 %collective-permute-start.94 = (bf16[512,2048]{1,0:T(8,128)(2,1)}, bf16[512,2048]{1,0:T(8,128)(2,1)}, u32[]{:S(2)}, u32[]{:S(2)}) collective-permute-start(bf16[512,2048]{1,0:T(8,128)(2,1)} %get-tuple-element.229), channel_id=1, source_target_pairs={{0,8},{4,12},{8,0},{12,4},{16,24},{20,28},{24,16},{28,20},{1,9},{5... | collective-permute-start | bytes 6291464 | tf_op jit(solution)/shard_map/ppermute | solution.py:382
  1355.2 77.0 %collective-permute-start.118 = (bf16[4,160,1024]{2,1,0:T(8,128)(2,1)}, bf16[4,160,1024]{2,1,0:T(8,128)(2,1)}, u32[]{:S(2)}, u32[]{:S(2)}) collective-permute-start(bf16[4,160,1024]{2,1,0:T(8,128)(2,1)} %constant_dynamic-slice_fusion.41), channel_id=1, source_target_pairs={{0,16},{4,20},{8,24},{12,28},{16,0},{20,4},{24,8},{28,12},{1,17},{... | collective-permute-start | bytes 3932168 | tf_op jit(solution)/shard_map/ppermute | solution.py:385
  1458.3 78.6 %collective-permute-start.107 = (bf16[512,2048]{1,0:T(8,128)(2,1)}, bf16[512,2048]{1,0:T(8,128)(2,1)}, u32[]{:S(2)}, u32[]{:S(2)}) collective-permute-start(bf16[512,2048]{1,0:T(8,128)(2,1)} %slice.811), channel_id=1, source_target_pairs={{0,4},{4,0},{8,12},{12,8},{16,20},{20,16},{24,28},{28,24},{1,5},{5... | collective-permute-start | bytes 6291464 | tf_op jit(solution)/shard_map/ppermute | solution.py:382
  1534.6 192.6 %collective-permute-start.113 = (bf16[352,1024]{1,0:T(8,128)(2,1)}, bf16[352,1024]{1,0:T(8,128)(2,1)}, u32[]{:S(2)}, u32[]{:S(2)}) collective-permute-start(bf16[352,1024]{1,0:T(8,128)(2,1)} %fusion.70), channel_id=1, source_target_pairs={{0,1},{1,2},{2,3},{3,0},{4,5},{5,6},{6,7},{7,4},{8,9},{9,10},{10,1... | collective-permute-start | bytes 2162696 | tf_op jit(solution)/shard_map/ppermute | solution.py:390
  1564.4 166.1 %collective-permute-start.79 = (bf16[512,512]{1,0:T(8,128)(2,1)}, bf16[512,512]{1,0:T(8,128)(2,1)}, u32[]{:S(2)}, u32[]{:S(2)}) collective-permute-start(bf16[512,512]{1,0:T(8,128)(2,1)} %bitcast.544), channel_id=1, source_target_pairs={{0,1},{1,2},{2,3},{3,0},{4,5},{5,6},{6,7},{7,4},{8,9},{9,10},{10,1... | collective-permute-start | bytes 1572872 | tf_op jit(solution)/shard_map/ppermute | solution.py:390
  1565.8 214.0 %collective-permute-start.80 = (bf16[512,512]{1,0:T(8,128)(2,1)}, bf16[512,512]{1,0:T(8,128)(2,1)}, u32[]{:S(2)}, u32[]{:S(2)}) collective-permute-start(bf16[512,512]{1,0:T(8,128)(2,1)} %bitcast.543), channel_id=1, source_target_pairs={{0,2},{1,3},{2,0},{3,1},{4,6},{5,7},{6,4},{7,5},{8,10},{9,11},{10,... | collective-permute-start | bytes 1572872 | tf_op jit(solution)/shard_map/ppermute | solution.py:390
  1568.9 218.6 %collective-permute-start.81 = (bf16[512,512]{1,0:T(8,128)(2,1)}, bf16[512,512]{1,0:T(8,128)(2,1)}, u32[]{:S(2)}, u32[]{:S(2)}) collective-permute-start(bf16[512,512]{1,0:T(8,128)(2,1)} %bitcast.542), channel_id=1, source_target_pairs={{0,3},{1,0},{2,1},{3,2},{4,7},{5,4},{6,5},{7,6},{8,11},{9,8},{10,9... | collective-permute-start | bytes 1572872 | tf_op jit(solution)/shard_map/ppermute | solution.py:390
  1571.7 161.3 %collective-permute-start.108 = (bf16[512,512]{1,0:T(8,128)(2,1)}, bf16[512,512]{1,0:T(8,128)(2,1)}, u32[]{:S(2)}, u32[]{:S(2)}) collective-permute-start(bf16[512,512]{1,0:T(8,128)(2,1)} %bitcast.541), channel_id=1, source_target_pairs={{0,1},{1,2},{2,3},{3,0},{4,5},{5,6},{6,7},{7,4},{8,9},{9,10},{10,1... | collective-permute-start | bytes 1572872 | tf_op jit(solution)/shard_map/ppermute | solution.py:390
  (267 other events, 7010.3 us)
Sparse Core Ops, SparseCore 0:
  1572.7 150.4 all-reduce.6

commit v2 on v1

v2 whole, which is shorter than its diff:
```python
import functools

import jax
import jax.numpy as jnp
from jax import lax
from jax.experimental import pallas as pl
from jax.experimental.pallas import tpu as pltpu
from jax.sharding import PartitionSpec as P

SEQ = 2048
epsilon = 1e-06
BF = jnp.bfloat16
F32 = jnp.float32
ROWS = 64
HALO = 8


def dot_nt(left, right):
    return lax.dot_general(
        left, right, (((1,), (1,)), ((), ())), preferred_element_type=F32
    )


def dot_nn(left, right):
    return jnp.dot(left, right, preferred_element_type=F32)


def dot_tn(left, right):
    return lax.dot_general(
        left, right, (((0,), (0,)), ((), ())), preferred_element_type=F32
    )


def gelu_parts(value):
    inner = 0.7978845608028654 * (value + 0.044715 * value * value * value)
    tanh = jnp.tanh(inner)
    slope = 0.7978845608028654 * (1.0 + 3.0 * 0.044715 * value * value)
    gelu = 0.5 * value * (1.0 + tanh)
    grad = 0.5 * (1.0 + tanh) + 0.5 * value * (1.0 - tanh * tanh) * slope
    return gelu, grad


def sigmoid(value):
    return 1.0 / (1.0 + jnp.exp(-value))


def one_minus_exp(log_value):
    y = -2.0 * log_value
    series = y * (
        1.0
        - y
        * (1 / 2)
        * (
            1.0
            - y
            * (1 / 3)
            * (1.0 - y * (1 / 4) * (1.0 - y * (1 / 5) * (1.0 - y * (1 / 6))))
        )
    )
    return jnp.where(y < 0.25, series, 1.0 - jnp.exp(-y))


def conv_terms(ext, masks, rows):
    terms = [ext[HALO : HALO + rows]]
    for k in range(1, 4):
        moved = pltpu.roll(ext, k, axis=0)[HALO : HALO + rows]
        terms.append(moved * masks[:, k - 1 : k])
    return terms


def forward_kernel(
    rnn_ref,
    halo_ref,
    mask_ref,
    conv_ref,
    vec_ref,
    wa_ref,
    wx_ref,
    mixed_ref,
    ga_ref,
    gx_ref,
    h_ref,
    p_ref,
    end_ref,
    ext_ref,
):
    length, width = rnn_ref.shape[1:]
    ext_ref[0:HALO, :] = halo_ref[0]
    ext_ref[HALO:, :] = rnn_ref[0]
    row8 = lax.broadcasted_iota(jnp.int32, (ROWS, 1), 0) % 8

    def block(i, carry):
        h_in, p_in = carry
        r0 = pl.multiple_of(i * ROWS, ROWS)
        masks = mask_ref[0, pl.ds(r0, ROWS), :]
        terms = conv_terms(ext_ref[pl.ds(r0, ROWS + HALO), :], masks, ROWS)
        mixed = vec_ref[0:1, :] + conv_ref[0:1, :] * terms[0]
        for k in range(1, 4):
            mixed = mixed + conv_ref[k : k + 1, :] * terms[k]
        high = mixed.astype(BF)
        low = (mixed - high.astype(F32)).astype(BF)
        gate_a = sigmoid(
            dot_nn(high, wa_ref[...]) + dot_nn(low, wa_ref[...]) + vec_ref[1:2, :]
        )
        gate_x = sigmoid(
            dot_nn(high, wx_ref[...]) + dot_nn(low, wx_ref[...]) + vec_ref[2:3, :]
        )
        begins = masks[:, 3:4]
        log_a = gate_a * vec_ref[3:4, :]
        a = jnp.exp(log_a) * (1.0 - begins)
        scale = jnp.sqrt(one_minus_exp(log_a)) * (1.0 - begins) + begins
        b = mixed * gate_x * scale
        mixed_ref[0, pl.ds(r0, ROWS), :] = mixed
        ga_ref[0, pl.ds(r0, ROWS), :] = gate_a
        gx_ref[0, pl.ds(r0, ROWS), :] = gate_x
        for d in (1, 2, 4):
            valid = row8 >= d
            b = jnp.where(valid, a * pltpu.roll(b, d, axis=0) + b, b)
            a = jnp.where(valid, a * pltpu.roll(a, d, axis=0), a)
        for g in range(ROWS // 8):
            rows = slice(8 * g, 8 * g + 8)
            h = b[rows] + a[rows] * h_in
            p = a[rows] * p_in
            h_ref[0, pl.ds(r0 + 8 * g, 8), :] = h
            p_ref[0, pl.ds(r0 + 8 * g, 8), :] = p
            h_in = h[7:8]
            p_in = p[7:8]
        return h_in, p_in

    h_end, p_end = lax.fori_loop(
        0,
        length // ROWS,
        block,
        (jnp.zeros((1, width), F32), jnp.ones((1, width), F32)),
    )
    end_ref[0, 0:4, :] = jnp.broadcast_to(p_end, (4, width))
    end_ref[0, 4:8, :] = jnp.broadcast_to(h_end, (4, width))


def adjoint_kernel(
    dmix_ref,
    gate_ref,
    state_ref,
    ga_ref,
    mask_ref,
    vec_ref,
    lam_ref,
    q_ref,
    dgi_ref,
    end_ref,
):
    length, width = dmix_ref.shape[1:]
    row = lax.broadcasted_iota(jnp.int32, (ROWS, 1), 0)
    row8 = row % 8
    blocks = length // ROWS

    def block(i, carry):
        lam_in, q_in, a_next = carry
        r0 = pl.multiple_of((blocks - 1 - i) * ROWS, ROWS)
        here = pl.ds(r0, ROWS)
        begins = mask_ref[0, here, :][:, 3:4]
        d_mixer = dmix_ref[0, here, :]
        gelu, slope = gelu_parts(gate_ref[0, here, :])
        dgi_ref[0, here, :] = (d_mixer * state_ref[0, here, :] * slope).astype(BF)
        b = d_mixer * gelu
        a = jnp.exp(ga_ref[0, here, :] * vec_ref[3:4, :]) * (1.0 - begins)
        c = jnp.where(row == ROWS - 1, a_next, pltpu.roll(a, ROWS - 1, axis=0))
        for d in (1, 2, 4):
            valid = row8 < 8 - d
            b = jnp.where(valid, c * pltpu.roll(b, ROWS - d, axis=0) + b, b)
            c = jnp.where(valid, c * pltpu.roll(c, ROWS - d, axis=0), c)
        for g in reversed(range(ROWS // 8)):
            rows = slice(8 * g, 8 * g + 8)
            lam = b[rows] + c[rows] * lam_in
            q = c[rows] * q_in
            lam_ref[0, pl.ds(r0 + 8 * g, 8), :] = lam
            q_ref[0, pl.ds(r0 + 8 * g, 8), :] = q
            lam_in = lam[0:1]
            q_in = q[0:1]
        return lam_in, q_in, a[0:1]

    one = jnp.ones((1, width), F32)
    lam0, q0, a0 = lax.fori_loop(
        0, blocks, block, (jnp.zeros((1, width), F32), one, one)
    )
    end_ref[0, 0:4, :] = jnp.broadcast_to(a0 * q0, (4, width))
    end_ref[0, 4:8, :] = jnp.broadcast_to(a0 * lam0, (4, width))


def fold8(value):
    total = value[0:8]
    for g in range(1, value.shape[0] // 8):
        total = total + value[8 * g : 8 * g + 8]
    return total


def backward_kernel(
    lam_ref,
    q_ref,
    state_ref,
    ga_ref,
    gx_ref,
    mixed_ref,
    rnn_ref,
    halo_ref,
    mask_ref,
    edge_ref,
    conv_ref,
    vec_ref,
    wa_ref,
    wx_ref,
    drnn_ref,
    head_ref,
    tail_ref,
    wag_ref,
    wxg_ref,
    vg_ref,
    ext_ref,
    prev_ref,
    dm_ref,
):
    length, width = lam_ref.shape[1:]
    first = pl.program_id(0) == 0

    @pl.when(first)
    def _():
        wag_ref[...] = jnp.zeros_like(wag_ref)
        wxg_ref[...] = jnp.zeros_like(wxg_ref)
        vg_ref[...] = jnp.zeros_like(vg_ref)

    ext_ref[0:HALO, :] = halo_ref[0]
    ext_ref[HALO:, :] = rnn_ref[0]
    prev_ref[0:HALO, :] = jnp.broadcast_to(edge_ref[0, 0:1, :], (HALO, width))
    prev_ref[HALO:, :] = state_ref[0]
    dm_ref[length:, :] = jnp.zeros((HALO, width), F32)

    def block(i, carry):
        r0 = pl.multiple_of(i * ROWS, ROWS)
        here = pl.ds(r0, ROWS)
        masks = mask_ref[0, here, :]
        begins = masks[:, 3:4]
        lam = lam_ref[0, here, :] + q_ref[0, here, :] * edge_ref[0, 4:5, :]
        before = pltpu.roll(prev_ref[pl.ds(r0, ROWS + HALO), :], 1, axis=0)[
            HALO : HALO + ROWS
        ]
        gate_a = ga_ref[0, here, :]
        gate_x = gx_ref[0, here, :]
        mixed = mixed_ref[0, here, :]
        log_a = gate_a * vec_ref[3:4, :]
        decay = jnp.exp(log_a)
        inv_scale = lax.rsqrt(one_minus_exp(log_a))
        scale_raw = jnp.sqrt(one_minus_exp(log_a))
        keep = 1.0 - begins
        scale = scale_raw * keep + begins
        through = lam * mixed
        d_log = lam * before * decay * keep + jnp.where(
            begins > 0.5, 0.0, through * gate_x * (-(decay * decay) * inv_scale)
        )
        log_gate = d_log * gate_a
        d_pre_a = log_gate * (1.0 - gate_a) * vec_ref[3:4, :]
        d_pre_x = through * scale * gate_x * (1.0 - gate_x)
        pa = d_pre_a.astype(BF)
        px = d_pre_x.astype(BF)
        mb = mixed.astype(BF)
        d_mixed = (
            lam * gate_x * scale + dot_nt(pa, wa_ref[...]) + dot_nt(px, wx_ref[...])
        )
        dm_ref[here, :] = d_mixed
        wag_ref[...] += dot_tn(mb, pa)
        wxg_ref[...] += dot_tn(mb, px)
        terms = conv_terms(ext_ref[pl.ds(r0, ROWS + HALO), :], masks, ROWS)
        sums = [d_mixed * term for term in terms]
        sums += [d_mixed, d_pre_a, d_pre_x, log_gate]
        for n, value in enumerate(sums):
            vg_ref[n] += fold8(value)
        return carry

    lax.fori_loop(0, length // ROWS, block, 0)

    def shift(i, carry):
        r0 = pl.multiple_of(i * ROWS, ROWS)
        ext = dm_ref[pl.ds(r0, ROWS + HALO), :]
        masks = mask_ref[0, pl.ds(r0, ROWS + HALO), :]
        total = conv_ref[0:1, :] * ext[0:ROWS]
        for k in range(1, 4):
            moved = pltpu.roll(ext * masks[:, k - 1 : k], ROWS + HALO - k, axis=0)
            total = total + conv_ref[k : k + 1, :] * moved[0:ROWS]
        drnn_ref[0, pl.ds(r0, ROWS), :] = total.astype(BF)

        @pl.when(i == length // ROWS - 1)
        def _():
            tail_ref[0] = total[ROWS - HALO :]

        return carry

    lax.fori_loop(0, length // ROWS, shift, 0)
    head_ref[0] = dm_ref[0:HALO, :]


def block_specs(shapes):
    specs = []
    for shape, moving in shapes:
        if moving:
            specs.append(
                pl.BlockSpec((1,) + shape[1:], lambda i, n=len(shape): (i,) + (0,) * (n - 1))
            )
        else:
            specs.append(pl.BlockSpec(shape, lambda i, n=len(shape): (0,) * n))
    return specs


def seq_call(kernel, moving, fixed, outs, scratch, name, flops=0, trans=0):
    count = moving[0].shape[0]
    out_shape = [jax.ShapeDtypeStruct(shape, dtype) for shape, dtype, _ in outs]
    bytes_accessed = sum(a.size * a.dtype.itemsize for a in moving + fixed) + sum(
        o.size * o.dtype.itemsize for o in out_shape
    )
    return pl.pallas_call(
        kernel,
        grid=(count,),
        in_specs=block_specs(
            [(a.shape, True) for a in moving] + [(a.shape, False) for a in fixed]
        ),
        out_specs=block_specs([(shape, move) for shape, _, move in outs]),
        out_shape=out_shape,
        scratch_shapes=scratch,
        compiler_params=pltpu.CompilerParams(
            dimension_semantics=("arbitrary",), vmem_limit_bytes=60 * 1024 * 1024
        ),
        cost_estimate=pl.CostEstimate(
            flops=flops, bytes_accessed=bytes_accessed, transcendentals=trans
        ),
        name=name,
    )(*moving, *fixed)


def body(
    DP,
    M,
    inputs,
    cotangent,
    reset_mask,
    norm1_gain,
    w_input,
    w_branch,
    w_output,
    conv_weight,
    conv_bias,
    gate_a_weight,
    gate_a_bias,
    gate_x_weight,
    gate_x_bias,
    decay_param,
    norm2_gain,
    w_gate,
    w_up,
    w_down,
):
    heads_here, bw_here, bw = gate_a_weight.shape
    t = 4 if heads_here % 4 == 0 and DP % 4 == 0 else 2
    O = DP // t
    hpg = heads_here // t
    nh = M * hpg
    L, FH = inputs.shape
    D = FH * M
    Dl = w_input.shape[0]
    Lc = L // M
    half = t * Dl
    cz = w_input.shape[1] // t
    fz = w_gate.shape[1] // t
    C = M * cz
    FC = M * fz
    conv = conv_weight.shape[0]
    parts = t // 2
    last = parts - 1

    i_dp = lax.axis_index("dp")
    z = lax.axis_index("mp")
    q = i_dp % t
    o = i_dp // t

    def tp(value, j):
        return lax.ppermute(value, "dp", [(i, i ^ j) for i in range(DP)])

    def oshift(value, r):
        return lax.ppermute(
            value, "dp", [(i, ((i // t + r) % O) * t + i % t) for i in range(DP)]
        )

    def zshift(value, k):
        return lax.ppermute(value, "mp", [(i, (i + k) % M) for i in range(M)])

    def zline(value, k):
        got = lax.ppermute(
            value, "mp", [(i, i + k) for i in range(M) if 0 <= i + k < M]
        )
        return jnp.roll(got, k * cz, axis=-1)

    class Live(dict):
        __getattr__ = dict.__getitem__
        __setattr__ = dict.__setitem__

        def barrier(self):
            held = lax.optimization_barrier(dict(self))
            self.clear()
            self.update(held)

        def take(self, name):
            return self.pop(name)

    v = Live()

    def cut(array, index, size, axis):
        return lax.dynamic_slice_in_dim(array, index * size, size, axis)

    def put(array, piece, *starts):
        return lax.dynamic_update_slice(array, piece, starts)

    def pick(array, index, axis=0):
        return lax.dynamic_index_in_dim(array, index, axis, keepdims=False)

    def chunk_pieces(value):
        pieces = [cut(value, (z + k) % M, Lc, 0) for k in range(M)]
        return [zshift(piece, k) if k else piece for k, piece in enumerate(pieces)]

    def joined(pieces):
        own = jnp.zeros((Lc, D), pieces[0].dtype)
        for k, piece in enumerate(pieces):
            own = put(own, piece, 0, ((z - k) % M) * FH)
        return own

    def far(value):
        return tp(value, 2) if parts > 1 else None

    def back_pieces(value):
        return [cut(value, (z + k) % M, FH, 1) for k in range(M)]

    def back_joined(pieces):
        out = jnp.zeros((L, FH), pieces[0].dtype)
        for k, piece in enumerate(pieces):
            out = put(out, piece, ((z - k) % M) * Lc, 0)
        return out

    def send_sum(part, p):
        mine = part[:Lc].astype(F32) + tp(part[Lc:], 1).astype(F32)
        if p:
            mine = tp(mine.astype(BF), 2).astype(F32)
        return mine

    def stacked(blocks):
        return jnp.concatenate(blocks) if len(blocks) > 1 else blocks[0]

    def parted(joint, blocks):
        at, out = 0, []
        for block in blocks:
            out.append(joint[at : at + block.shape[0]])
            at += block.shape[0]
        return out

    def exchange(mine):
        if parts == 1:
            return [mine(q), tp(mine(q ^ 1), 1)]
        got = tp(jnp.stack([mine(q ^ 1), mine(q ^ 3)]), 1)
        after = tp(jnp.stack([mine(q ^ 2), got[1]]), 2)
        return [mine(q), got[0], after[0], after[1]]

    def from_group(pieces):
        block = jnp.zeros((pieces[0].shape[0], half), BF)
        for j, piece in enumerate(pieces):
            block = put(block, piece, 0, (q ^ j) * Dl)
        return block

    def to_groups(*blocks):
        joint = stacked(blocks)
        got = [parted(oshift(joint, r), blocks) for r in range(1, O)]
        return [[g[n] for g in got] for n in range(len(blocks))]

    def ring_next(*blocks):
        return parted(zshift(stacked(blocks), 1), blocks)

    def fill(full, block, others, s):
        rows = block.shape[0]
        for r, piece in enumerate([block] + others):
            full = put(full, piece, s * rows, ((o - r) % O) * half)
        return full

    def grad_y(*grads):
        own = [cut(g, o, half, 1) for g in grads]
        got = [
            parted(oshift(stacked([cut(g, (o + r) % O, half, 1) for g in grads]), r), own)
            for r in range(1, O)
        ]
        return [[own[n]] + [g[n] for g in got] for n in range(len(grads))]

    def slot(pieces, k):
        size = pieces[0].shape[0] // M
        return sum(piece[k * size : (k + 1) * size].astype(F32) for piece in pieces)

    def ring_step(*rings):
        sends = []
        for pieces, k, moving in rings:
            total = slot(pieces, k)
            if moving is not None:
                total = total + moving.astype(F32)
            sends.append(total.astype(BF))
        return ring_next(*sends)

    def ring_end(pieces, moving):
        for k in range(4, M):
            (moving,) = ring_step((pieces, k, moving))
        return (moving.astype(F32) + slot(pieces, 0)).astype(BF)

    def direct_sends(*grads):
        return [[slot(pieces, k).astype(BF) for pieces in grads] for k in range(M)]

    def grad_end(pieces):
        size = pieces[0].shape[0]
        out = jnp.zeros((t * size, Dl), BF)
        for j, piece in enumerate(pieces):
            out = put(out, piece, (q ^ j) * size, 0)
        return out

    def exchange_grads(*totals):
        joint = stacked(totals)
        got = [
            parted(piece, totals) for piece in exchange(lambda k: cut(joint, k, Dl, 1))
        ]
        return [[g[n] for g in got] for n in range(len(totals))]

    ng, nc = norm1_gain.shape[0], conv_bias.shape[0]
    packed = jnp.concatenate(
        [
            norm1_gain,
            norm2_gain,
            conv_weight.reshape(-1),
            conv_bias,
            gate_a_bias,
            gate_x_bias,
            decay_param,
        ]
    )
    every = put(jnp.zeros((DP, packed.shape[0]), BF), packed[None], i_dp, 0)
    step = 1
    while step < DP:
        every = every + tp(every, step)
        step *= 2
    gate_size = 2 * hpg * bw_here * bw
    gate_rows = -(-(gate_size + 2 * conv * nc + ng) // (16 * Dl)) * 16
    gates_flat = jnp.stack([gate_a_weight, gate_x_weight]).reshape(
        2, t, hpg, bw_here, bw
    )
    gates_flat = gates_flat.transpose(1, 0, 2, 3, 4).reshape(t, gate_size)
    gates_flat = jnp.pad(gates_flat, ((0, 0), (0, gate_rows * Dl - gate_size)))
    mine_all = jnp.concatenate(
        [
            w_input.T.reshape(t, cz, Dl),
            w_branch.T.reshape(t, cz, Dl),
            gates_flat.reshape(t, gate_rows, Dl),
            w_output.reshape(t, cz, Dl),
            w_gate.T.reshape(t, fz, Dl),
            w_up.T.reshape(t, fz, Dl),
            w_down.reshape(t, fz, Dl),
        ],
        axis=1,
    )
    starts = jnp.maximum(reset_mask, (jnp.arange(L) % SEQ == 0).astype(jnp.int32))
    starts = jnp.stack([starts] + [tp(starts, j) for j in range(1, t)])
    open_ = 1.0 - starts.astype(F32)
    back1 = jnp.pad(open_, ((0, 0), (1, 0)))[:, :L]
    back2 = jnp.pad(open_, ((0, 0), (2, 0)))[:, :L]
    masks = jnp.stack([open_, open_ * back1, open_ * back1 * back2, 1.0 - open_], axis=1)
    masks = jnp.pad(masks, ((0, 0), (0, 0), (0, HALO)))
    masks = lax.dynamic_slice(masks, (0, 0, z * Lc), (t, 4, Lc + HALO))
    masks = masks.transpose(0, 2, 1)

    def normed(value, gain):
        wide = value.astype(F32)
        scale = lax.rsqrt(jnp.mean(wide * wide, axis=1, keepdims=True) + epsilon)
        return wide * scale, scale

    rows_a = 2 * cz + gate_rows
    v.z_in = chunk_pieces(inputs)
    v.blocks = exchange(lambda k: pick(mine_all, k))
    v.every, v.masks, v.cotangent = every, masks, cotangent
    v.barrier()

    block = from_group(v.take("blocks"))
    block_a = block[:rows_a]
    block_b = block[rows_a : rows_a + cz]
    block_g = block[rows_a + cz : rows_a + cz + 2 * fz]
    v.d = [block[rows_a + cz + 2 * fz :]]
    v.ring_a = [block_a] + [zshift(block_a, k) for k in range(1, M)]
    v.b, v.g = [block_b], [block_g]
    v.y_a, v.y_b, v.y_g = [[y] for y in to_groups(block_a, block_b, block_g)]
    v.every = [v.every] + [zshift(v.every, k) for k in range(1, M)]
    v.own_in = joined(v.take("z_in"))
    v.far_in = far(v.own_in)
    v.near_in = tp(v.own_in, 1)
    v.barrier()

    v.y_a = v.y_a + to_groups(*v.ring_a[1:])
    v.b = v.b + [zshift(v.b[0], k) for k in range(1, M)]
    v.g = v.g + ring_next(v.g[0])
    every = jnp.stack(v.take("every")).astype(F32)
    gains = jnp.stack([pick(every[:, :, : 2 * ng], (z - b) % M) for b in range(M)])
    gain_one = gains[:, :, :ng].reshape(1, D)
    gain_two = gains[:, :, ng:].reshape(1, D)
    vectors = every[:, :, 2 * ng :].reshape(M, DP, conv + 4, nc).transpose(2, 0, 1, 3)
    vectors = pick(vectors.reshape(conv + 4, M, t, cz), q, 2).reshape(conv + 4, C)
    conv_w = vectors[:conv]
    decay = vectors[conv + 3]
    log_slope = -8.0 * jax.nn.softplus(decay)
    vec = jnp.stack(
        [vectors[conv], vectors[conv + 1], vectors[conv + 2], log_slope]
        + [jnp.zeros_like(decay)] * 4
    )

    v.vec, v.conv_w, v.gain_one, v.gain_two = vec, conv_w, gain_one, gain_two
    groups_in = [jnp.concatenate([v.own_in, v.take("near_in")])]
    if parts > 1:
        groups_in.append(jnp.concatenate([v.far_in, tp(v.far_in, 1)]))
    v.take("far_in")
    v.n1 = [(normed(g, v.gain_one)[0] * v.gain_one).astype(BF) for g in groups_in]
    v.barrier()

    got = to_groups(*(v.b[1:] + v.g[1:]))
    v.y_b = v.y_b + got[: M - 1]
    v.y_g = v.y_g + got[M - 1 :]
    g_next, d_next = ring_next(v.g[-1], v.d[-1])
    v.g, v.d = v.g + [g_next], v.d + [d_next]
    w_in_t, w_br_t = jnp.zeros((C, D), BF), jnp.zeros((C, D), BF)
    rest = jnp.zeros((M * gate_rows, D), BF)
    for k, (mine, others) in enumerate(zip(v.take("ring_a"), v.take("y_a"))):
        w_in_t = fill(w_in_t, mine[:cz], [y[:cz] for y in others], k)
        w_br_t = fill(w_br_t, mine[cz : 2 * cz], [y[cz : 2 * cz] for y in others], k)
        rest = fill(rest, mine[2 * cz :], [y[2 * cz :] for y in others], k)
    rest = rest.reshape(M, gate_rows, DP, Dl).transpose(0, 2, 1, 3)
    rest = rest.reshape(M, DP, gate_rows * Dl)
    gates = rest[:, :, :gate_size].reshape(M, DP, 2, hpg, bw_here, bw)
    gates = gates.transpose(2, 0, 3, 1, 4, 5).reshape(2, nh, bw, bw)
    dense = []
    for kind in range(2):
        rows = [
            jnp.pad(gates[kind, n], ((0, 0), (n * bw, (nh - 1 - n) * bw)))
            for n in range(nh)
        ]
        dense.append(jnp.concatenate(rows))
    wa, wx = dense
    v.w_in_t, v.w_br_t, v.wa, v.wx = w_in_t, w_br_t, wa, wx

    def chain(ends, sign):
        total = jnp.zeros_like(ends[..., 4:5, :])
        for k in reversed(range(1, M)):
            got = zline(ends, sign * k)
            total = got[..., 4:5, :] + got[..., 0:1, :] * total
        return total

    shape = (2, Lc, C)

    def run_forward(p):
        return seq_call(
            forward_kernel,
            [v.rnn[p], v.halos[p], v.masks[2 * p : 2 * p + 2]],
            [v.conv_w, v.vec, v.wa, v.wx],
            [(shape, F32, True)] * 5 + [((2, 8, C), F32, True)],
            [pltpu.VMEM((Lc + HALO, C), F32)],
            "recurrence",
            flops=2 * Lc * 2 * C * C * 4,
            trans=6 * 2 * Lc * C,
        )

    v.rnn = [dot_nt(n, v.w_in_t).reshape(shape) for n in v.n1]
    v.gin = [dot_nt(n, v.w_br_t).reshape(shape) for n in v.n1]
    tails = jnp.stack([r[:, Lc - HALO :] for r in v.rnn])
    v.halos = list(zline(tails, 1))
    v.fwd = [None] * parts
    v.fwd[last] = run_forward(last)
    v.barrier()

    got = to_groups(v.g[2], v.d[0])
    v.y_g, v.y_d = v.y_g + [got[0]], [got[1]]
    g_next, d_next = ring_next(v.g[-1], v.d[-1])
    v.g, v.d = v.g + [g_next], v.d + [d_next]
    while len(v.g) < M:
        v.g = v.g + ring_next(v.g[-1])
    w_out = jnp.zeros((C, D), BF)
    for k, (mine, others) in enumerate(zip(v.take("b"), v.take("y_b"))):
        w_out = fill(w_out, mine, others, k)
    v.w_out = w_out
    for p in range(last):
        v.fwd[p] = run_forward(p)
    enters = chain(jnp.stack([f[5] for f in v.fwd]), 1)
    v.cin, v.state, v.mixer = [], [], []
    for p in range(parts):
        _, _, _, h, prod, _ = v.fwd[p]
        v.cin.append(enters[p])
        v.state.append(h + prod * v.cin[p])
        v.mixer.append((gelu_parts(v.gin[p])[0] * v.state[p]).astype(BF).reshape(2 * Lc, C))
    v.fwd = [f[:3] for f in v.fwd]
    v.barrier()

    got = to_groups(*(v.g[3:] + v.d[1:2]))
    v.y_g, v.y_d = v.y_g + got[:-1], v.y_d + got[-1:]
    while len(v.d) < M:
        v.d = v.d + ring_next(v.d[-1])
    rec_sum = None
    for p in reversed(range(parts)):
        part = send_sum(dot_nn(v.mixer[p], v.w_out).astype(BF), p)
        rec_sum = part if rec_sum is None else rec_sum + part
    v.resid_mid = v.own_in.astype(F32) + rec_sum
    v.unit_two, v.scale_two = normed(v.resid_mid, v.gain_two)
    v.n2_own = (v.unit_two * v.gain_two).astype(BF)
    v.barrier()

    v.y_d = v.y_d + to_groups(*v.d[2:])
    w_gate_t, w_up_t = jnp.zeros((FC, D), BF), jnp.zeros((FC, D), BF)
    for k, (mine, others) in enumerate(zip(v.take("g"), v.take("y_g"))):
        w_gate_t = fill(w_gate_t, mine[:fz], [y[:fz] for y in others], k)
        w_up_t = fill(w_up_t, mine[fz:], [y[fz:] for y in others], k)
    v.w_gate_t, v.w_up_t = w_gate_t, w_up_t
    v.z_cot = chunk_pieces(v.take("cotangent"))
    v.n2_far = far(v.n2_own)
    v.n2 = [jnp.concatenate([v.n2_own, tp(v.n2_own, 1)])]
    v.take("n2_own")

    def mlp_forward(p):
        gate, up = dot_nt(v.n2[p], v.w_gate_t), dot_nt(v.n2[p], v.w_up_t)
        return gate, up, (gelu_parts(gate)[0] * up).astype(BF)

    v.mlp = [mlp_forward(0)]
    v.barrier()

    w_dn = jnp.zeros((FC, D), BF)
    for k, (mine, others) in enumerate(zip(v.take("d"), v.take("y_d"))):
        w_dn = fill(w_dn, mine, others, k)
    v.w_dn = w_dn
    cot_own = joined(v.take("z_cot"))
    v.cot = [jnp.concatenate([cot_own, tp(cot_own, 1)])]
    v.far_cot = far(cot_own)
    if parts > 1:
        v.n2.append(jnp.concatenate([v.n2_far, tp(v.n2_far, 1)]))
        v.mlp.append(mlp_forward(1))
    v.take("n2_far")
    v.barrier()

    def summed(lefts, rights):
        total = None
        for left, right in zip(lefts, rights):
            term = dot_tn(left, right)
            total = term if total is None else total + term
        return total.astype(BF)

    if parts > 1:
        v.cot.append(jnp.concatenate([v.far_cot, tp(v.far_cot, 1)]))
    v.take("far_cot")

    def mlp_back(p):
        d_hidden = dot_nt(v.cot[p], v.w_dn)
        gate, up, _ = v.mlp[p]
        gelu, slope = gelu_parts(gate)
        return (d_hidden * up * slope).astype(BF), (d_hidden * gelu).astype(BF)

    def mlp_back_in(p):
        gate, up = v.d_mlp[p]
        return (dot_nn(gate, v.w_gate_t) + dot_nn(up, v.w_up_t)).astype(BF)

    v.grad_down = summed([m[2] for m in v.mlp], v.cot)
    v.d_mlp = [None] * parts
    v.d_mlp[last] = mlp_back(last)
    v.barrier()

    (v.y_down,) = grad_y(v.take("grad_down"))
    v.dn2 = [None] * parts
    v.dn2[last] = mlp_back_in(last)
    v.dn2_sum = send_sum(v.dn2[last], last) if last else None
    for p in range(last):
        v.d_mlp[p] = mlp_back(p)
        v.dn2[p] = mlp_back_in(p)
    v.grad_gate = summed([d[0] for d in v.d_mlp], v.n2)
    v.hidden = [m[2] for m in v.take("mlp")]
    v.cot_own = v.take("cot")[0][:Lc]
    v.barrier()

    (v.r_down,) = ring_step((v.y_down, 1, None))
    (v.y_gate,) = grad_y(v.take("grad_gate"))
    dn2_sum = v.take("dn2_sum")
    for p in reversed(range(last if last else 1)):
        part = send_sum(v.dn2[p], p)
        dn2_sum = part if dn2_sum is None else dn2_sum + part
    v.take("dn2")

    def norm_back(grad, unit, scale, gain):
        weighted = grad * gain
        dots = jnp.mean(weighted * unit, axis=1, keepdims=True)
        return scale * (weighted - unit * dots), jnp.sum(grad * unit, axis=0)

    back_two, v.gain_two_grad = norm_back(dn2_sum, v.unit_two, v.scale_two, v.gain_two)
    v.d_mid = v.take("cot_own").astype(F32) + back_two
    v.d_own = v.d_mid.astype(BF)
    v.far_branch = far(v.d_own)
    v.grad_up = summed([d[1] for d in v.d_mlp], v.n2)
    v.take("n2")
    v.take("d_mlp")
    v.out = [dot_nn(h, v.w_dn).astype(BF) for h in v.take("hidden")]
    v.barrier()

    v.r_down, v.r_gate = ring_step((v.y_down, 2, v.r_down), (v.y_gate, 1, None))
    (v.y_up,) = grad_y(v.take("grad_up"))
    v.d_branch = [jnp.concatenate([v.d_own, tp(v.d_own, 1)])]
    v.take("d_own")
    if parts > 1:
        v.d_branch.append(jnp.concatenate([v.far_branch, tp(v.far_branch, 1)]))
    v.take("far_branch")
    out_sum = None
    for p in reversed(range(parts)):
        part = send_sum(v.out[p], p)
        out_sum = part if out_sum is None else out_sum + part
    v.take("out")
    v.output = (v.take("resid_mid") + out_sum).astype(BF)

    def run_adjoint(p):
        return seq_call(
            adjoint_kernel,
            [
                dot_nt(v.d_branch[p], v.w_out).reshape(shape),
                v.gin[p],
                v.state[p],
                v.fwd[p][1],
                v.masks[2 * p : 2 * p + 2],
            ],
            [v.vec],
            [(shape, F32, True)] * 2 + [(shape, BF, True), ((2, 8, C), F32, True)],
            [],
            "adjoint",
            trans=2 * 2 * Lc * C,
        )

    v.adjoint = [run_adjoint(p) for p in range(parts)]
    enters = chain(jnp.stack([a[3] for a in v.adjoint]), -1)
    v.edges = [
        jnp.concatenate(
            [
                jnp.broadcast_to(v.cin[p], (2, 4, C)),
                jnp.broadcast_to(enters[p], (2, 4, C)),
            ],
            1,
        )
        for p in range(parts)
    ]
    v.take("cin")
    v.grad_output = summed(v.take("mixer"), v.take("d_branch"))
    v.d_gin = [v.adjoint[p][2].reshape(2 * Lc, C) for p in range(parts)]
    v.grad_branch = summed(v.d_gin, v.n1)
    v.barrier()

    v.r_down, v.r_gate, v.r_up = ring_step(
        (v.y_down, 3, v.r_down), (v.y_gate, 2, v.r_gate), (v.y_up, 1, None)
    )
    v.y_output, v.y_branch = grad_y(v.take("grad_output"), v.take("grad_branch"))
    pieces = back_pieces(v.take("output"))
    v.z_out = [zshift(piece, k) if k else piece for k, piece in enumerate(pieces)]
    grad_vec, grad_wa, grad_wx = 0.0, 0.0, 0.0
    v.d_rnn = [None] * parts
    for p in reversed(range(parts)):
        mixed, gate_a, gate_x = v.fwd[p]
        here = v.masks[2 * p : 2 * p + 2]
        lam, prod, _, _ = v.adjoint[p]
        drnn, head, tail, wag, wxg, vg = seq_call(
            backward_kernel,
            [
                lam,
                prod,
                v.state[p],
                gate_a,
                gate_x,
                mixed,
                v.rnn[p],
                v.halos[p],
                here,
                v.edges[p],
            ],
            [v.conv_w, v.vec, v.wa, v.wx],
            [
                (shape, BF, True),
                ((2, HALO, C), F32, True),
                ((2, HALO, C), F32, True),
                ((C, C), F32, False),
                ((C, C), F32, False),
                ((8, 8, C), F32, False),
            ],
            [pltpu.VMEM((Lc + HALO, C), F32)] * 3,
            "recurrence_back",
            flops=2 * Lc * 2 * C * C * 4,
            trans=4 * 2 * Lc * C,
        )
        following = zline(head, -1)
        fix = [jnp.zeros((2, 1, C), F32)] * HALO
        for k in range(1, 4):
            for n in range(k):
                row = HALO - k + n
                fix[row] = fix[row] + v.conv_w[k] * (
                    here[:, Lc + n : Lc + n + 1, k - 1 : k] * following[:, n : n + 1]
                )
        tail = (tail + jnp.concatenate(fix, axis=1)).astype(BF)
        drnn = put(drnn, tail, 0, Lc - HALO, 0)
        grad_vec = grad_vec + vg
        grad_wa = grad_wa + wag
        grad_wx = grad_wx + wxg
        v.d_rnn[p] = drnn.reshape(2 * Lc, C)
    for name in ("adjoint", "fwd", "state", "rnn", "halos", "edges", "gin"):
        v.take(name)
    v.grad_vec, v.grad_wa, v.grad_wx = grad_vec, grad_wa, grad_wx
    v.barrier()

    z_down = ring_end(v.take("y_down"), v.take("r_down"))
    v.r_gate, v.r_up = ring_step((v.y_gate, 3, v.r_gate), (v.y_up, 2, v.r_up))
    v.z_mixer = [
        zshift(stacked(send), M - k) if k else stacked(send)
        for k, send in enumerate(direct_sends(v.take("y_output"), v.take("y_branch")))
    ]
    v.output = back_joined(v.take("z_out"))
    gates_grad = jnp.stack(
        [
            jnp.stack(
                [g[n * bw : (n + 1) * bw, n * bw : (n + 1) * bw] for n in range(nh)]
            )
            for g in (v.take("grad_wa"), v.take("grad_wx"))
        ]
    )
    gates_grad = gates_grad.reshape(2, M, hpg, DP, bw_here, bw)
    gates_grad = gates_grad.transpose(1, 3, 0, 2, 4, 5).reshape(M, DP, gate_size)
    small = jnp.sum(v.take("grad_vec"), axis=1).reshape(2 * conv, M, O, nc)
    small = small.transpose(1, 2, 0, 3).reshape(M, O, 2 * conv * nc)
    small = put(jnp.zeros((M, DP, 2 * conv * nc), F32), small, 0, q * O, 0)
    gain_two_grad = v.take("gain_two_grad").reshape(M, DP, ng)
    gain_two_grad = jnp.stack([pick(gain_two_grad, (z - k) % M) for k in range(M)])
    gates_grad = jnp.concatenate([gates_grad, small, gain_two_grad], axis=2)
    gates_grad = jnp.pad(
        gates_grad, ((0, 0), (0, 0), (0, gate_rows * Dl - gates_grad.shape[2]))
    )
    gates_grad = gates_grad.reshape(M, DP, gate_rows, Dl).transpose(0, 2, 1, 3)
    gates_grad = gates_grad.reshape(M, gate_rows, D).astype(BF)
    grad_in = jnp.concatenate(
        [summed(v.d_rnn, v.n1).reshape(M, cz, D), gates_grad], axis=1
    ).reshape(M * (cz + gate_rows), D)
    (v.y_in,) = grad_y(grad_in)
    v.take("n1")
    dn1_sum = None
    for p in reversed(range(parts)):
        part = (dot_nn(v.d_rnn[p], v.w_in_t) + dot_nn(v.d_gin[p], v.w_br_t)).astype(BF)
        part = send_sum(part, p)
        dn1_sum = part if dn1_sum is None else dn1_sum + part
    v.dn1, v.z_down = dn1_sum, z_down
    for name in ("d_rnn", "d_gin", "w_in_t", "w_br_t", "wa", "wx", "masks", "vec"):
        v.take(name)
    v.barrier()

    z_gate = ring_end(v.take("y_gate"), v.take("r_gate"))
    (v.r_up,) = ring_step((v.y_up, 3, v.r_up))
    z_mixer = sum(piece.astype(F32) for piece in v.take("z_mixer")).astype(BF)
    v.tp_down, v.tp_gate, v.tp_mixer = exchange_grads(v.take("z_down"), z_gate, z_mixer)
    unit_one, scale_one = normed(v.own_in, v.gain_one)
    back_one, gain_one_grad = norm_back(v.take("dn1"), unit_one, scale_one, v.gain_one)
    pieces = back_pieces((v.d_mid + back_one).astype(BF))
    rows_in = cz + gate_rows
    sums = jnp.broadcast_to(gain_one_grad.astype(BF), (16, D))
    joints = []
    for k, (send,) in enumerate(direct_sends(v.take("y_in"))):
        there = (M - k) % M
        mine = [pieces[there], cut(sums, (z + there) % M, FH, 1)]
        mine += [send[:, n * FH : (n + 1) * FH] for n in range(half // FH)]
        joint = jnp.concatenate(mine)
        joints.append(zshift(joint, there) if there else joint)
    v.joints = joints
    v.barrier()

    parts_in = [joint[Lc + 16 :] for joint in v.joints]
    grad_in = sum(piece.astype(F32) for piece in parts_in).astype(BF)
    grad_in = jnp.concatenate(
        [grad_in[n * rows_in : (n + 1) * rows_in] for n in range(half // FH)], axis=1
    )
    z_up = ring_end(v.y_up, v.r_up)
    tp_up, tp_in = exchange_grads(z_up, grad_in)
    grad_up = grad_end(tp_up)
    rest_in = [piece[cz:].reshape(-1).astype(F32) for piece in tp_in]
    small = sum(piece[gate_size:] for piece in rest_in)
    grad_a = grad_end(tp_in).reshape(t, rows_in, Dl)
    input_grad = back_joined([v.joints[(M - j) % M][:Lc] for j in range(M)]).astype(F32)
    gain_one_grad = sum(joint[Lc].astype(F32) for joint in v.joints)
    step = 1
    while step < DP:
        gain_one_grad = gain_one_grad + tp(gain_one_grad, step)
        step *= 2
    gain_one_grad = cut(gain_one_grad, i_dp, ng, 0)
    grad_output = grad_end([piece[:cz] for piece in v.tp_mixer])
    grad_branch = grad_end([piece[cz:] for piece in v.tp_mixer])
    grad_down, grad_gate = grad_end(v.tp_down), grad_end(v.tp_gate)
    output = v.output

    mine = small[: 2 * conv * nc].reshape(2 * conv, nc)
    gain_two_grad = small[2 * conv * nc : 2 * conv * nc + ng]
    decay_grad = mine[conv + 3] * (-8.0 * jax.nn.sigmoid(decay_param.astype(F32)))

    gates_back = grad_a[:, cz:].reshape(t, gate_rows * Dl)[:, :gate_size]
    gates_back = gates_back.reshape(t, 2, hpg, bw_here, bw).transpose(1, 0, 2, 3, 4)
    gates_back = gates_back.reshape(2, heads_here, bw_here, bw).astype(F32)

    def flipped(value):
        rows = value.shape[-2] * (value.shape[0] if value.ndim > 2 else 1)
        return lax.optimization_barrier(value.reshape(rows, Dl)).T.astype(F32)

    return (
        output,
        input_grad,
        gain_one_grad,
        flipped(grad_a[:, :cz]),
        flipped(grad_branch),
        grad_output.astype(F32),
        mine[:conv],
        mine[conv],
        gates_back[0],
        mine[conv + 1],
        gates_back[1],
        mine[conv + 2],
        decay_grad,
        gain_two_grad,
        flipped(grad_gate),
        flipped(grad_up),
        grad_down.astype(F32),
    )


def solution(mesh):
    both = P(("mp", "dp"))
    wide = P("dp", "mp")
    tall = P("mp", "dp")
    taps = P(None, ("mp", "dp"))
    gate = P("mp", "dp", None)
    params = (both, wide, wide, tall, taps, both, gate, both, gate, both, both, both, wide, wide, tall)
    return jax.shard_map(
        functools.partial(body, mesh.shape["dp"], mesh.shape["mp"]),
        mesh=mesh,
        in_specs=(wide, wide, P("dp")) + params,
        out_specs=(wide, wide) + params,
        check_vma=False,
    )
```

time: 1820 us -> 1420 us (0.78)
  waiting for transfers between devices: 814 us -> 566 us
  starting transfers between devices: 167 us -> 104 us
  blocking collectives: 39.7 us -> 0 us
  local copies, waits for them, and re-layouts: 231 us -> 205 us
    psum x1 -> x0, waiting for transfers between devices: 145 us -> none  [body(): flat = lax.psum(flat, ('dp', 'mp'))]
    ppermute x42 -> x33, waiting for transfers between devices: 314 us -> 204 us  [zshift(): return lax.ppermute(value, 'mp', [(i, (i + k) % M) for i in range(M)])]
    ppermute x25 -> x11, waiting for transfers between devices: 214 us -> 149 us  [oshift(): lax.ppermute(value, 'dp', [(i, (i // t + r) % O * t + i % t) for i in ran...]
    ppermute x63 -> x39, waiting for transfers between devices: 135 us -> 197 us  [tp(): return lax.ppermute(value, 'dp', [(i, i ^ j) for i in range(DP)])]
    all_gather x1 -> x0, blocking collectives: 39.7 us -> none  [body(): lax.all_gather(packed, ('mp', 'dp'), axis=0, tiled=False).astype(F32)]
    slice x24 -> x70, local copies, waits for them, and re-layouts: 23 us -> 50.4 us  [the longest x29 28.2 us: parted(): out.append(joint[at:at + block.shape[0]])]
    ppermute x25 -> x11, starting transfers between devices: 33.5 us -> 9.82 us  [oshift(): lax.ppermute(value, 'dp', [(i, (i // t + r) % O * t + i % t) for i in ran...]
    dynamic_slice x25 -> x2, local copies, waits for them, and re-layouts: 22.6 us -> 1.14 us  [pick(): return lax.dynamic_index_in_dim(array, index, axis, keepdims=False)]
  transfers between devices with their start and end apart: 147 -> 92, of which waited for: 55 -> 34; matrix products, arithmetic and copies ran while one was open for 33% -> 31% of each run, Pallas kernels for 7% -> 8%
where the time goes in v2:
time: 1420 us; the launch traced here: 1410 us
  waiting for transfers between devices  566 us (40%)
  matrix products  279 us (20%)
  local copies, waits for them, and re-layouts  205 us (14%)
  Pallas kernels  131 us (9%)
  other arithmetic  123 us (9%)
  starting transfers between devices  104 us (7%)
    ppermute x33, waiting for transfers between devices, zshift(): return lax.ppermute(value, 'mp', [(i, (i + k) % M) for i in range(M)])  204 us
    ppermute x39, waiting for transfers between devices, tp(): return lax.ppermute(value, 'dp', [(i, i ^ j) for i in range(DP)])  197 us
    ppermute x11, waiting for transfers between devices, oshift(): lax.ppermute(value, 'dp', [(i, (i // t + r) % O * t + i % t) for i in ran...  149 us
    pallas_call x6, Pallas kernels, seq_call(): pl.pallas_call(kernel, grid=(count,), in_specs=block_specs([(a.shape, Tru...  131 us
    dot_general x12, matrix products, dot_nt(): lax.dot_general(left, right, (((1,), (1,)), ((), ())), preferred_element_...  110 us
    dot_general x12, matrix products, dot_tn(): lax.dot_general(left, right, (((0,), (0,)), ((), ())), preferred_element_...  91.2 us
    dot_general x12, matrix products, dot_nn(): return jnp.dot(left, right, preferred_element_type=F32)  78.4 us
    unnamed x374, local copies, waits for them, and re-layouts  52.7 us
  transfers between devices with their start and end apart: 92, of which 34 were waited for; matrix products, arithmetic and copies ran while one was open for 31% of the time, Pallas kernels for 8%

profile of v2, /device:TPU:8, one launch (start us, length us, event | category | flops | bytes accessed | tf_op | source)
XLA Modules:
  0.0 1412.4 jit_solution(1422763685947666312)
XLA Ops:
  28.9 32.5 %collective-permute-done.6 = s32[2048]{0:T(1024)S(1)} collective-permute-done((s32[2048]{0:T(1024)S(1)}, s32[2048]{0:T(1024)S(1)}, u32[]{:S(2)}, u32[]{:S(2)}) %collective-permute-start.6) | collective-permute-done | bytes 8224 | tf_op jit(solution)/shard_map/ppermute | solution.py:383
  111.3 38.4 %collective-permute-done.19 = bf16[1280,1024]{1,0:T(8,128)(2,1)} collective-permute-done((bf16[1280,1024]{1,0:T(8,128)(2,1)}, bf16[1280,1024]{1,0:T(8,128)(2,1)}, u32[]{:S(2)}, u32[]{:S(2)}) %collective-permute-start.19) | collective-permute-done | bytes 2621472 | tf_op jit(solution)/shard_map/ppermute | solution.py:386
  159.5 12.0 collective-permute-done.18
  198.3 28.2 %collective-permute-done.25 = bf16[1056,1024]{1,0:T(8,128)(2,1)} collective-permute-done((bf16[1056,1024]{1,0:T(8,128)(2,1)}, bf16[1056,1024]{1,0:T(8,128)(2,1)}, u32[]{:S(2)}, u32[]{:S(2)}) %collective-permute-start.25) | collective-permute-done | bytes 2162720 | tf_op jit(solution)/shard_map/ppermute | solution.py:386
  228.3 12.2 collective-permute-done.21
  291.9 20.8 %recurrence.2 = (f32[2,512,640]{2,1,0:T(8,128)}, f32[2,512,640]{2,1,0:T(8,128)}, f32[2,512,640]{2,1,0:T(8,128)}, f32[2,512,640]{2,1,0:T(8,128)}, f32[2,512,640]{2,1,0:T(8,128)}, /*index=5*/f32[2,8,640]{2,1,0:T(8,128)}) custom-call(f32[2,512,640]{2,1,0:T(8,128)} %bitcast.316, f32[2,8,640]{2,1,0:T(8,128)} %get-tuple-element.1062.halo_ref, ...), custom_call_target="tpu_custom_call" | custom-call | flops 3355443200 | bytes 17496320 | tf_op jit(solution)/shard_map/recurrence/pallas_call | solution.py:318
  312.8 18.5 %collective-permute-done.26 = bf16[1152,1024]{1,0:T(8,128)(2,1)} collective-permute-done((bf16[1152,1024]{1,0:T(8,128)(2,1)}, bf16[1152,1024]{1,0:T(8,128)(2,1)}, u32[]{:S(2)}, u32[]{:S(2)}) %collective-permute-start.26) | collective-permute-done | bytes 2359328 | tf_op jit(solution)/shard_map/ppermute | solution.py:391
  341.6 20.9 %recurrence.3 = (f32[2,512,640]{2,1,0:T(8,128)}, f32[2,512,640]{2,1,0:T(8,128)}, f32[2,512,640]{2,1,0:T(8,128)}, f32[2,512,640]{2,1,0:T(8,128)}, f32[2,512,640]{2,1,0:T(8,128)}, /*index=5*/f32[2,8,640]{2,1,0:T(8,128)}) custom-call(f32[2,512,640]{2,1,0:T(8,128)} %bitcast.319, f32[2,8,640]{2,1,0:T(8,128)} %get-tuple-element.1046.halo_ref, ...), custom_call_target="tpu_custom_call" | custom-call | flops 3355443200 | bytes 17496320 | tf_op jit(solution)/shard_map/recurrence/pallas_call | solution.py:318
  384.8 39.9 %collective-permute-done.32 = bf16[1152,1024]{1,0:T(8,128)(2,1)S(1)} collective-permute-done((bf16[1152,1024]{1,0:T(8,128)(2,1)S(1)}, bf16[1152,1024]{1,0:T(8,128)(2,1)S(1)}, u32[]{:S(2)}, u32[]{:S(2)}) %collective-permute-start.32) | collective-permute-done | bytes 2359328 | tf_op jit(solution)/shard_map/ppermute | solution.py:391
  438.6 46.1 %collective-permute-done.38 = bf16[1152,1024]{1,0:T(8,128)(2,1)S(1)} collective-permute-done((bf16[1152,1024]{1,0:T(8,128)(2,1)S(1)}, bf16[1152,1024]{1,0:T(8,128)(2,1)S(1)}, u32[]{:S(2)}, u32[]{:S(2)}) %collective-permute-start.38) | collective-permute-done | bytes 2359328 | tf_op jit(solution)/shard_map/ppermute | solution.py:386
  507.2 21.2 %collective-permute-done.41 = bf16[768,1024]{1,0:T(8,128)(2,1)S(1)} collective-permute-done((bf16[768,1024]{1,0:T(8,128)(2,1)S(1)}, bf16[768,1024]{1,0:T(8,128)(2,1)S(1)}, u32[]{:S(2)}, u32[]{:S(2)}) %collective-permute-start.41) | collective-permute-done | bytes 1572896 | tf_op jit(solution)/shard_map/ppermute | solution.py:386
  543.8 12.9 fusion.11
  584.7 12.1 fusion.17
  623.1 11.8 add_convert_fusion.2
  634.9 17.6 %multiply_convert_fusion.1 = (bf16[1024,1536]{1,0:T(8,128)(2,1)S(1)}, bf16[1024,1536]{1,0:T(8,128)(2,1)}) fusion(f32[1024,1536]{1,0:T(8,128)} %fusion.168, f32[1024,1536]{1,0:T(8,128)} %get-tuple-element.849, bf16[1024,2048]{1,0:T(8,128)(2,1)} %copy-done.120, bf16[1536,2048]{1,0:T(8,128)(2,1)} %copy-done.28), kind=kOutput, calls=%fused_computation.52 | convolution fusion | flops 6478626816 | bytes 29360128 | tf_op jit(solution)/shard_map/dot_general | solution.py:19
  652.5 13.4 fusion.172
  689.4 17.4 %multiply_convert_fusion = (bf16[1024,1536]{1,0:T(8,128)(2,1)}, bf16[1024,1536]{1,0:T(8,128)(2,1)}) fusion(f32[1024,1536]{1,0:T(8,128)} %fusion.167, f32[1024,1536]{1,0:T(8,128)} %get-tuple-element.895, bf16[1024,2048]{1,0:T(8,128)(2,1)S(1)} %copy-done.23, bf16[1536,2048]{1,0:T(8,128)(2,1)} %copy-done.28), kind=kOutput, calls=%fused_computation.51 | convolution fusion | flops 6478626816 | bytes 29360128 | tf_op jit(solution)/shard_map/dot_general | solution.py:19
  706.8 13.3 add_convert_fusion.1
  744.9 36.5 %collective-permute-done.50 = bf16[512,2048]{1,0:T(8,128)(2,1)S(1)} collective-permute-done((bf16[512,2048]{1,0:T(8,128)(2,1)S(1)}, bf16[512,2048]{1,0:T(8,128)(2,1)S(1)}, u32[]{:S(2)}, u32[]{:S(2)}) %collective-permute-start.50) | collective-permute-done | bytes 2097184 | tf_op jit(solution)/shard_map/ppermute | solution.py:383
  804.2 13.3 add_convert_fusion
  844.2 14.6 %collective-permute-done.55 = bf16[1536,1024]{1,0:T(8,128)(2,1)} collective-permute-done((bf16[1536,1024]{1,0:T(8,128)(2,1)}, bf16[1536,1024]{1,0:T(8,128)(2,1)}, u32[]{:S(2)}, u32[]{:S(2)}) %collective-permute-start.55) | collective-permute-done | bytes 3145760 | tf_op jit(solution)/shard_map/ppermute | solution.py:386
  858.8 13.3 collective-permute-done.53
  886.5 25.7 %collective-permute-done.64 = bf16[768,1024]{1,0:T(8,128)(2,1)S(1)} collective-permute-done((bf16[768,1024]{1,0:T(8,128)(2,1)S(1)}, bf16[768,1024]{1,0:T(8,128)(2,1)S(1)}, u32[]{:S(2)}, u32[]{:S(2)}) %collective-permute-start.64) | collective-permute-done | bytes 1572896 | tf_op jit(solution)/shard_map/ppermute | solution.py:391
  919.9 12.5 adjoint.3
  942.9 12.5 adjoint.2
  983.8 29.9 %collective-permute-done.62 = bf16[512,2048]{1,0:T(8,128)(2,1)S(1)} collective-permute-done((bf16[512,2048]{1,0:T(8,128)(2,1)S(1)}, bf16[512,2048]{1,0:T(8,128)(2,1)S(1)}, u32[]{:S(2)}, u32[]{:S(2)}) %collective-permute-start.62) | collective-permute-done | bytes 2097184 | tf_op jit(solution)/shard_map/ppermute | solution.py:383
  1032.4 32.3 %recurrence_back.2 = (bf16[2,512,640]{2,1,0:T(8,128)(2,1)}, f32[2,8,640]{2,1,0:T(8,128)}, f32[2,8,640]{2,1,0:T(8,128)}, f32[640,640]{1,0:T(8,128)}, f32[640,640]{1,0:T(8,128)}, /*index=5*/f32[8,8,640]{2,1,0:T(8,128)}) custom-call(f32[2,512,640]{2,1,0:T(8,128)} %get-tuple-element.1039.lam_ref, f32[2,512,640]{2,1,0:T(8,128)} %get-tuple-element.1040.q_ref, ...), custom_call_target="tpu_custom_call" | custom-call | flops 3355443200 | bytes 24951040 | tf_op jit(solution)/shard_map/recurrence_back/pallas_call | solution.py:318
  1066.6 32.3 %recurrence_back.3 = (bf16[2,512,640]{2,1,0:T(8,128)(2,1)}, f32[2,8,640]{2,1,0:T(8,128)}, f32[2,8,640]{2,1,0:T(8,128)}, f32[640,640]{1,0:T(8,128)}, f32[640,640]{1,0:T(8,128)}, /*index=5*/f32[8,8,640]{2,1,0:T(8,128)}) custom-call(f32[2,512,640]{2,1,0:T(8,128)} %get-tuple-element.1055.lam_ref, f32[2,512,640]{2,1,0:T(8,128)} %get-tuple-element.1056.q_ref, ...), custom_call_target="tpu_custom_call" | custom-call | flops 3355443200 | bytes 24951040 | tf_op jit(solution)/shard_map/recurrence_back/pallas_call | solution.py:318
  1107.8 16.5 %collective-permute-done.67 = f32[2,8,640]{2,1,0:T(8,128)S(1)} collective-permute-done((f32[2,8,640]{2,1,0:T(8,128)}, f32[2,8,640]{2,1,0:T(8,128)S(1)}, u32[]{:S(2)}, u32[]{:S(2)}) %collective-permute-start.67) | collective-permute-done | bytes 40992 | tf_op jit(solution)/shard_map/ppermute | solution.py:394
  1216.3 31.5 %collective-permute-done.74 = bf16[512,2048]{1,0:T(8,128)(2,1)S(1)} collective-permute-done((bf16[512,2048]{1,0:T(8,128)(2,1)S(1)}, bf16[512,2048]{1,0:T(8,128)(2,1)S(1)}, u32[]{:S(2)}, u32[]{:S(2)}) %collective-permute-start.74) | collective-permute-done | bytes 2097184 | tf_op jit(solution)/shard_map/ppermute | solution.py:383
  1275.9 24.3 %collective-permute-done.86 = bf16[2,1088,256]{2,1,0:T(8,128)(2,1)S(1)} collective-permute-done((bf16[2,1088,256]{2,1,0:T(8,128)(2,1)S(1)}, bf16[2,1088,256]{2,1,0:T(8,128)(2,1)S(1)}, u32[]{:S(2)}, u32[]{:S(2)}) %collective-permute-start.86) | collective-permute-done | bytes 1114144 | tf_op jit(solution)/shard_map/ppermute | solution.py:383
  1303.9 57.3 %collective-permute-done.82 = bf16[912,512]{1,0:T(8,128)(2,1)S(1)} collective-permute-done((bf16[912,512]{1,0:T(8,128)(2,1)S(1)}, bf16[912,512]{1,0:T(8,128)(2,1)S(1)}, u32[]{:S(2)}, u32[]{:S(2)}) %collective-permute-start.82) | collective-permute-done | bytes 933920 | tf_op jit(solution)/shard_map/ppermute | solution.py:391
  (973 shorter events, 665.9 us)
Async XLA Ops:
  21.7 60.6 %collective-permute-start.1 = (bf16[2,1664,256]{2,1,0:T(8,128)(2,1)}, bf16[2,1664,256]{2,1,0:T(8,128)(2,1)}, u32[]{:S(2)}, u32[]{:S(2)}) collective-permute-start(bf16[2,1664,256]{2,1,0:T(8,128)(2,1)} %pad_maximum_fusion.14), channel_id=1, source_target_pairs={{0,8},{4,12},{8,0},{12,4},{16,24},{20,28},{24,16},{28,20},{1,9},{5... | collective-permute-start | bytes 5111816 | tf_op jit(solution)/shard_map/ppermute | solution.py:383
  26.5 57.7 %collective-permute-start.10 = (bf16[512,512]{1,0:T(8,128)(2,1)}, bf16[512,512]{1,0:T(8,128)(2,1)}, u32[]{:S(2)}, u32[]{:S(2)}) collective-permute-start(bf16[512,512]{1,0:T(8,128)(2,1)} %get-tuple-element.1360), channel_id=1, source_target_pairs={{0,3},{1,0},{2,1},{3,2},{4,7},{5,4},{6,5},{7,6},{8,11},{9,8},{10,9... | collective-permute-start | bytes 1572872 | tf_op jit(solution)/shard_map/ppermute | solution.py:391
  27.3 56.9 %collective-permute-start.8 = (bf16[512,512]{1,0:T(8,128)(2,1)}, bf16[512,512]{1,0:T(8,128)(2,1)}, u32[]{:S(2)}, u32[]{:S(2)}) collective-permute-start(bf16[512,512]{1,0:T(8,128)(2,1)} %get-tuple-element.1361), channel_id=1, source_target_pairs={{0,1},{1,2},{2,3},{3,0},{4,5},{5,6},{6,7},{7,4},{8,9},{9,10},{10,1... | collective-permute-start | bytes 1572872 | tf_op jit(solution)/shard_map/ppermute | solution.py:391
  90.6 59.1 %collective-permute-start.19 = (bf16[1280,1024]{1,0:T(8,128)(2,1)}, bf16[1280,1024]{1,0:T(8,128)(2,1)}, u32[]{:S(2)}, u32[]{:S(2)}) collective-permute-start(bf16[1280,1024]{1,0:T(8,128)(2,1)} %slice.1431), channel_id=1, source_target_pairs={{0,16},{4,20},{8,24},{12,28},{16,0},{20,4},{24,8},{28,12},{1,17},{... | collective-permute-start | bytes 7864328 | tf_op jit(solution)/shard_map/ppermute | solution.py:386
  97.0 74.5 %collective-permute-start.14 = (bf16[512,2048]{1,0:T(8,128)(2,1)S(1)}, bf16[512,2048]{1,0:T(8,128)(2,1)}, u32[]{:S(2)}, u32[]{:S(2)}) collective-permute-start(bf16[512,2048]{1,0:T(8,128)(2,1)S(1)} %constant_dynamic-update-slice_fusion.39), channel_id=1, source_target_pairs={{0,8},{4,12},{8,0},{12,4},{16,24},{20,28},{24,16},{28,20},{1,9},{5... | collective-permute-start | bytes 6291464 | tf_op jit(solution)/shard_map/ppermute | solution.py:383
  98.5 72.9 %collective-permute-start.15 = (bf16[512,2048]{1,0:T(8,128)(2,1)S(1)}, bf16[512,2048]{1,0:T(8,128)(2,1)S(1)}, u32[]{:S(2)}, u32[]{:S(2)}) collective-permute-start(bf16[512,2048]{1,0:T(8,128)(2,1)S(1)} %constant_dynamic-update-slice_fusion.39), channel_id=1, source_target_pairs={{0,4},{4,0},{8,12},{12,8},{16,20},{20,16},{24,28},{28,24},{1,5},{5... | collective-permute-start | bytes 6291464 | tf_op jit(solution)/shard_map/ppermute | solution.py:383
  105.5 54.0 %collective-permute-start.16 = (bf16[352,1024]{1,0:T(8,128)(2,1)S(1)}, bf16[352,1024]{1,0:T(8,128)(2,1)S(1)}, u32[]{:S(2)}, u32[]{:S(2)}) collective-permute-start(bf16[352,1024]{1,0:T(8,128)(2,1)S(1)} %slice.1430), channel_id=1, source_target_pairs={{0,1},{1,2},{2,3},{3,0},{4,5},{5,6},{6,7},{7,4},{8,9},{9,10},{10,1... | collective-permute-start | bytes 2162696 | tf_op jit(solution)/shard_map/ppermute | solution.py:391
  107.1 52.4 %collective-permute-start.17 = (bf16[352,1024]{1,0:T(8,128)(2,1)S(1)}, bf16[352,1024]{1,0:T(8,128)(2,1)S(1)}, u32[]{:S(2)}, u32[]{:S(2)}) collective-permute-start(bf16[352,1024]{1,0:T(8,128)(2,1)S(1)} %slice.1430), channel_id=1, source_target_pairs={{0,2},{1,3},{2,0},{3,1},{4,6},{5,7},{6,4},{7,5},{8,10},{9,11},{10,... | collective-permute-start | bytes 2162696 | tf_op jit(solution)/shard_map/ppermute | solution.py:391
  177.8 66.6 %collective-permute-start.23 = (bf16[768,1024]{1,0:T(8,128)(2,1)}, bf16[768,1024]{1,0:T(8,128)(2,1)}, u32[]{:S(2)}, u32[]{:S(2)}) collective-permute-start(bf16[768,1024]{1,0:T(8,128)(2,1)} %slice.1429), channel_id=1, source_target_pairs={{0,1},{1,2},{2,3},{3,0},{4,5},{5,6},{6,7},{7,4},{8,9},{9,10},{10,1... | collective-permute-start | bytes 4718600 | tf_op jit(solution)/shard_map/ppermute | solution.py:391
  183.0 57.5 %collective-permute-start.21 = (bf16[160,1024]{1,0:T(8,128)(2,1)}, bf16[160,1024]{1,0:T(8,128)(2,1)S(1)}, u32[]{:S(2)}, u32[]{:S(2)}) collective-permute-start(bf16[160,1024]{1,0:T(8,128)(2,1)} %slice.1427), channel_id=1, source_target_pairs={{0,2},{1,3},{2,0},{3,1},{4,6},{5,7},{6,4},{7,5},{8,10},{9,11},{10,... | collective-permute-start | bytes 983048 | tf_op jit(solution)/shard_map/ppermute | solution.py:391
  187.8 56.6 %collective-permute-start.22 = (bf16[160,1024]{1,0:T(8,128)(2,1)}, bf16[160,1024]{1,0:T(8,128)(2,1)S(1)}, u32[]{:S(2)}, u32[]{:S(2)}) collective-permute-start(bf16[160,1024]{1,0:T(8,128)(2,1)} %slice.1427), channel_id=1, source_target_pairs={{0,3},{1,0},{2,1},{3,2},{4,7},{5,4},{6,5},{7,6},{8,11},{9,8},{10,9... | collective-permute-start | bytes 983048 | tf_op jit(solution)/shard_map/ppermute | solution.py:391
  247.3 88.7 %collective-permute-start.28 = (bf16[1248,1024]{1,0:T(8,128)(2,1)}, bf16[1248,1024]{1,0:T(8,128)(2,1)}, u32[]{:S(2)}, u32[]{:S(2)}) collective-permute-start(bf16[1248,1024]{1,0:T(8,128)(2,1)} %pad_maximum_fusion.5), channel_id=1, source_target_pairs={{0,16},{4,20},{8,24},{12,28},{16,0},{20,4},{24,8},{28,12},{1,17},{... | collective-permute-start | bytes 7667720 | tf_op jit(solution)/shard_map/ppermute | solution.py:386
  277.9 53.4 %collective-permute-start.26 = (bf16[1152,1024]{1,0:T(8,128)(2,1)}, bf16[1152,1024]{1,0:T(8,128)(2,1)}, u32[]{:S(2)}, u32[]{:S(2)}) collective-permute-start(bf16[1152,1024]{1,0:T(8,128)(2,1)} %pad_maximum_fusion.8), channel_id=1, source_target_pairs={{0,1},{1,2},{2,3},{3,0},{4,5},{5,6},{6,7},{7,4},{8,9},{9,10},{10,1... | collective-permute-start | bytes 7077896 | tf_op jit(solution)/shard_map/ppermute | solution.py:391
  371.6 53.2 %collective-permute-start.32 = (bf16[1152,1024]{1,0:T(8,128)(2,1)S(1)}, bf16[1152,1024]{1,0:T(8,128)(2,1)S(1)}, u32[]{:S(2)}, u32[]{:S(2)}) collective-permute-start(bf16[1152,1024]{1,0:T(8,128)(2,1)S(1)} %get-tuple-element.1389), channel_id=1, source_target_pairs={{0,1},{1,2},{2,3},{3,0},{4,5},{5,6},{6,7},{7,4},{8,9},{9,10},{10,1... | collective-permute-start | bytes 7077896 | tf_op jit(solution)/shard_map/ppermute | solution.py:391
  371.9 53.1 %collective-permute-start.33 = (bf16[1152,1024]{1,0:T(8,128)(2,1)S(1)}, bf16[1152,1024]{1,0:T(8,128)(2,1)S(1)}, u32[]{:S(2)}, u32[]{:S(2)}) collective-permute-start(bf16[1152,1024]{1,0:T(8,128)(2,1)S(1)} %get-tuple-element.1388), channel_id=1, source_target_pairs={{0,16},{4,20},{8,24},{12,28},{16,0},{20,4},{24,8},{28,12},{1,17},{... | collective-permute-start | bytes 7077896 | tf_op jit(solution)/shard_map/ppermute | solution.py:386
  431.9 52.8 %collective-permute-start.38 = (bf16[1152,1024]{1,0:T(8,128)(2,1)S(1)}, bf16[1152,1024]{1,0:T(8,128)(2,1)S(1)}, u32[]{:S(2)}, u32[]{:S(2)}) collective-permute-start(bf16[1152,1024]{1,0:T(8,128)(2,1)S(1)} %pad_maximum_fusion.9), channel_id=1, source_target_pairs={{0,16},{4,20},{8,24},{12,28},{16,0},{20,4},{24,8},{28,12},{1,17},{... | collective-permute-start | bytes 7077896 | tf_op jit(solution)/shard_map/ppermute | solution.py:386
  437.7 53.4 %collective-permute-start.34 = (bf16[384,1024]{1,0:T(8,128)(2,1)S(1)}, bf16[384,1024]{1,0:T(8,128)(2,1)S(1)}, u32[]{:S(2)}, u32[]{:S(2)}) collective-permute-start(bf16[384,1024]{1,0:T(8,128)(2,1)S(1)} %slice.1468), channel_id=1, source_target_pairs={{0,1},{1,2},{2,3},{3,0},{4,5},{5,6},{6,7},{7,4},{8,9},{9,10},{10,1... | collective-permute-start | bytes 2359304 | tf_op jit(solution)/shard_map/ppermute | solution.py:391
  491.2 65.6 %collective-permute-start.40 = (bf16[512,2048]{1,0:T(8,128)(2,1)S(1)}, bf16[512,2048]{1,0:T(8,128)(2,1)}, u32[]{:S(2)}, u32[]{:S(2)}) collective-permute-start(bf16[512,2048]{1,0:T(8,128)(2,1)S(1)} %get-tuple-element.762), channel_id=1, source_target_pairs={{0,8},{4,12},{8,0},{12,4},{16,24},{20,28},{24,16},{28,20},{1,9},{5... | collective-permute-start | bytes 6291464 | tf_op jit(solution)/shard_map/ppermute | solution.py:383
  496.4 60.3 %collective-permute-start.42 = (bf16[512,512]{1,0:T(8,128)(2,1)}, bf16[512,512]{1,0:T(8,128)(2,1)S(1)}, u32[]{:S(2)}, u32[]{:S(2)}) collective-permute-start(bf16[512,512]{1,0:T(8,128)(2,1)} %get-tuple-element.1358), channel_id=1, source_target_pairs={{0,1},{1,2},{2,3},{3,0},{4,5},{5,6},{6,7},{7,4},{8,9},{9,10},{10,1... | collective-permute-start | bytes 1572872 | tf_op jit(solution)/shard_map/ppermute | solution.py:391
  497.7 59.0 %collective-permute-start.43 = (bf16[512,512]{1,0:T(8,128)(2,1)}, bf16[512,512]{1,0:T(8,128)(2,1)S(1)}, u32[]{:S(2)}, u32[]{:S(2)}) collective-permute-start(bf16[512,512]{1,0:T(8,128)(2,1)} %get-tuple-element.1357), channel_id=1, source_target_pairs={{0,2},{1,3},{2,0},{3,1},{4,6},{5,7},{6,4},{7,5},{8,10},{9,11},{10,... | collective-permute-start | bytes 1572872 | tf_op jit(solution)/shard_map/ppermute | solution.py:391
  688.8 93.1 %collective-permute-start.51 = (bf16[1536,1024]{1,0:T(8,128)(2,1)S(1)}, bf16[1536,1024]{1,0:T(8,128)(2,1)S(1)}, u32[]{:S(2)}, u32[]{:S(2)}) collective-permute-start(bf16[1536,1024]{1,0:T(8,128)(2,1)S(1)} %get-tuple-element.1308), channel_id=1, source_target_pairs={{0,16},{4,20},{8,24},{12,28},{16,0},{20,4},{24,8},{28,12},{1,17},{... | collective-permute-start | bytes 9437192 | tf_op jit(solution)/shard_map/ppermute | solution.py:386
  783.8 60.4 %collective-permute-start.54 = (bf16[384,1024]{1,0:T(8,128)(2,1)}, bf16[384,1024]{1,0:T(8,128)(2,1)}, u32[]{:S(2)}, u32[]{:S(2)}) collective-permute-start(bf16[384,1024]{1,0:T(8,128)(2,1)} %add_convert_fusion.26), channel_id=1, source_target_pairs={{0,1},{1,2},{2,3},{3,0},{4,5},{5,6},{6,7},{7,4},{8,9},{9,10},{10,1... | collective-permute-start | bytes 2359304 | tf_op jit(solution)/shard_map/ppermute | solution.py:391
  789.0 69.7 %collective-permute-start.55 = (bf16[1536,1024]{1,0:T(8,128)(2,1)}, bf16[1536,1024]{1,0:T(8,128)(2,1)}, u32[]{:S(2)}, u32[]{:S(2)}) collective-permute-start(bf16[1536,1024]{1,0:T(8,128)(2,1)} %get-tuple-element.1306), channel_id=1, source_target_pairs={{0,16},{4,20},{8,24},{12,28},{16,0},{20,4},{24,8},{28,12},{1,17},{... | collective-permute-start | bytes 9437192 | tf_op jit(solution)/shard_map/ppermute | solution.py:386
  877.0 86.9 %collective-permute-start.61 = (bf16[512,2048]{1,0:T(8,128)(2,1)}, bf16[512,2048]{1,0:T(8,128)(2,1)}, u32[]{:S(2)}, u32[]{:S(2)}) collective-permute-start(bf16[512,2048]{1,0:T(8,128)(2,1)} %slice.1231), channel_id=1, source_target_pairs={{0,4},{4,0},{8,12},{12,8},{16,20},{20,16},{24,28},{28,24},{1,5},{5... | collective-permute-start | bytes 6291464 | tf_op jit(solution)/shard_map/ppermute | solution.py:383
  878.9 104.9 %collective-permute-start.63 = (bf16[512,2048]{1,0:T(8,128)(2,1)}, bf16[512,2048]{1,0:T(8,128)(2,1)}, u32[]{:S(2)}, u32[]{:S(2)}) collective-permute-start(bf16[512,2048]{1,0:T(8,128)(2,1)} %slice.1233), channel_id=1, source_target_pairs={{0,4},{4,0},{8,12},{12,8},{16,20},{20,16},{24,28},{28,24},{1,5},{5... | collective-permute-start | bytes 6291464 | tf_op jit(solution)/shard_map/ppermute | solution.py:383
  879.0 53.4 %collective-permute-start.56 = (bf16[512,2048]{1,0:T(8,128)(2,1)S(1)}, bf16[512,2048]{1,0:T(8,128)(2,1)}, u32[]{:S(2)}, u32[]{:S(2)}) collective-permute-start(bf16[512,2048]{1,0:T(8,128)(2,1)S(1)} %get-tuple-element.984), channel_id=1, source_target_pairs={{0,4},{4,0},{8,12},{12,8},{16,20},{20,16},{24,28},{28,24},{1,5},{5... | collective-permute-start | bytes 6291464 | tf_op jit(solution)/shard_map/ppermute | solution.py:383
  912.3 104.7 %collective-permute-start.65 = (bf16[1536,1024]{1,0:T(8,128)(2,1)}, bf16[1536,1024]{1,0:T(8,128)(2,1)}, u32[]{:S(2)}, u32[]{:S(2)}) collective-permute-start(bf16[1536,1024]{1,0:T(8,128)(2,1)} %get-tuple-element.1304), channel_id=1, source_target_pairs={{0,16},{4,20},{8,24},{12,28},{16,0},{20,4},{24,8},{28,12},{1,17},{... | collective-permute-start | bytes 9437192 | tf_op jit(solution)/shard_map/ppermute | solution.py:386
  1026.7 98.9 %collective-permute-start.68 = (bf16[1152,1024]{1,0:T(8,128)(2,1)}, bf16[1152,1024]{1,0:T(8,128)(2,1)}, u32[]{:S(2)}, u32[]{:S(2)}) collective-permute-start(bf16[1152,1024]{1,0:T(8,128)(2,1)} %pad_maximum_fusion.10), channel_id=1, source_target_pairs={{0,1},{1,2},{2,3},{3,0},{4,5},{5,6},{6,7},{7,4},{8,9},{9,10},{10,1... | collective-permute-start | bytes 7077896 | tf_op jit(solution)/shard_map/ppermute | solution.py:391
  1030.4 98.3 %collective-permute-start.69 = (bf16[1280,1024]{1,0:T(8,128)(2,1)}, bf16[1280,1024]{1,0:T(8,128)(2,1)}, u32[]{:S(2)}, u32[]{:S(2)}) collective-permute-start(bf16[1280,1024]{1,0:T(8,128)(2,1)} %pad_maximum_fusion.4), channel_id=1, source_target_pairs={{0,16},{4,20},{8,24},{12,28},{16,0},{20,4},{24,8},{28,12},{1,17},{... | collective-permute-start | bytes 7864328 | tf_op jit(solution)/shard_map/ppermute | solution.py:386
  1152.8 96.1 %collective-permute-start.80 = (bf16[320,1024]{1,0:T(8,128)(2,1)}, bf16[320,1024]{1,0:T(8,128)(2,1)}, u32[]{:S(2)}, u32[]{:S(2)}) collective-permute-start(bf16[320,1024]{1,0:T(8,128)(2,1)} %pad_maximum_fusion.27), channel_id=1, source_target_pairs={{0,1},{1,2},{2,3},{3,0},{4,5},{5,6},{6,7},{7,4},{8,9},{9,10},{10,1... | collective-permute-start | bytes 1966088 | tf_op jit(solution)/shard_map/ppermute | solution.py:391
  1272.5 88.7 %collective-permute-start.82 = (bf16[912,512]{1,0:T(8,128)(2,1)S(1)}, bf16[912,512]{1,0:T(8,128)(2,1)S(1)}, u32[]{:S(2)}, u32[]{:S(2)}) collective-permute-start(bf16[912,512]{1,0:T(8,128)(2,1)S(1)} %pad_maximum_fusion.22), channel_id=1, source_target_pairs={{0,2},{1,3},{2,0},{3,1},{4,6},{5,7},{6,4},{7,5},{8,10},{9,11},{10,... | collective-permute-start | bytes 2801672 | tf_op jit(solution)/shard_map/ppermute | solution.py:391
  1275.3 88.7 %collective-permute-start.81 = (bf16[912,512]{1,0:T(8,128)(2,1)S(1)}, bf16[912,512]{1,0:T(8,128)(2,1)S(1)}, u32[]{:S(2)}, u32[]{:S(2)}) collective-permute-start(bf16[912,512]{1,0:T(8,128)(2,1)S(1)} %pad_maximum_fusion.21), channel_id=1, source_target_pairs={{0,3},{1,0},{2,1},{3,2},{4,7},{5,4},{6,5},{7,6},{8,11},{9,8},{10,9... | collective-permute-start | bytes 2801672 | tf_op jit(solution)/shard_map/ppermute | solution.py:391
  (238 other events, 4218.8 us)

commit v3 on v2

v3 whole, which is shorter than its diff:
```python
import functools

import jax
import jax.numpy as jnp
from jax import lax
from jax.experimental import pallas as pl
from jax.experimental.pallas import tpu as pltpu
from jax.sharding import PartitionSpec as P

SEQ = 2048
epsilon = 1e-06
BF = jnp.bfloat16
F32 = jnp.float32
ROWS = 64
HALO = 8


def dot_nt(left, right):
    return lax.dot_general(
        left, right, (((1,), (1,)), ((), ())), preferred_element_type=F32
    )


def dot_nn(left, right):
    return jnp.dot(left, right, preferred_element_type=F32)


def dot_tn(left, right):
    return lax.dot_general(
        left, right, (((0,), (0,)), ((), ())), preferred_element_type=F32
    )


def gelu_parts(value):
    inner = 0.7978845608028654 * (value + 0.044715 * value * value * value)
    tanh = jnp.tanh(inner)
    slope = 0.7978845608028654 * (1.0 + 3.0 * 0.044715 * value * value)
    gelu = 0.5 * value * (1.0 + tanh)
    grad = 0.5 * (1.0 + tanh) + 0.5 * value * (1.0 - tanh * tanh) * slope
    return gelu, grad


def sigmoid(value):
    return 1.0 / (1.0 + jnp.exp(-value))


def one_minus_exp(log_value):
    y = -2.0 * log_value
    series = y * (
        1.0
        - y
        * (1 / 2)
        * (
            1.0
            - y
            * (1 / 3)
            * (1.0 - y * (1 / 4) * (1.0 - y * (1 / 5) * (1.0 - y * (1 / 6))))
        )
    )
    return jnp.where(y < 0.25, series, 1.0 - jnp.exp(-y))


def conv_terms(ext, masks, rows):
    terms = [ext[HALO : HALO + rows]]
    for k in range(1, 4):
        moved = pltpu.roll(ext, k, axis=0)[HALO : HALO + rows]
        terms.append(moved * masks[:, k - 1 : k])
    return terms


def forward_kernel(
    rnn_ref,
    halo_ref,
    mask_ref,
    conv_ref,
    vec_ref,
    wa_ref,
    wx_ref,
    mixed_ref,
    ga_ref,
    gx_ref,
    h_ref,
    p_ref,
    end_ref,
    ext_ref,
):
    length, width = rnn_ref.shape[1:]
    ext_ref[0:HALO, :] = halo_ref[0]
    ext_ref[HALO:, :] = rnn_ref[0]
    row8 = lax.broadcasted_iota(jnp.int32, (ROWS, 1), 0) % 8

    def block(i, carry):
        h_in, p_in = carry
        r0 = pl.multiple_of(i * ROWS, ROWS)
        masks = mask_ref[0, pl.ds(r0, ROWS), :]
        terms = conv_terms(ext_ref[pl.ds(r0, ROWS + HALO), :], masks, ROWS)
        mixed = vec_ref[0:1, :] + conv_ref[0:1, :] * terms[0]
        for k in range(1, 4):
            mixed = mixed + conv_ref[k : k + 1, :] * terms[k]
        high = mixed.astype(BF)
        low = (mixed - high.astype(F32)).astype(BF)
        gate_a = sigmoid(
            dot_nn(high, wa_ref[...]) + dot_nn(low, wa_ref[...]) + vec_ref[1:2, :]
        )
        gate_x = sigmoid(
            dot_nn(high, wx_ref[...]) + dot_nn(low, wx_ref[...]) + vec_ref[2:3, :]
        )
        begins = masks[:, 3:4]
        log_a = gate_a * vec_ref[3:4, :]
        a = jnp.exp(log_a) * (1.0 - begins)
        scale = jnp.sqrt(one_minus_exp(log_a)) * (1.0 - begins) + begins
        b = mixed * gate_x * scale
        mixed_ref[0, pl.ds(r0, ROWS), :] = mixed
        ga_ref[0, pl.ds(r0, ROWS), :] = gate_a
        gx_ref[0, pl.ds(r0, ROWS), :] = gate_x
        for d in (1, 2, 4):
            valid = row8 >= d
            b = jnp.where(valid, a * pltpu.roll(b, d, axis=0) + b, b)
            a = jnp.where(valid, a * pltpu.roll(a, d, axis=0), a)
        for g in range(ROWS // 8):
            rows = slice(8 * g, 8 * g + 8)
            h = b[rows] + a[rows] * h_in
            p = a[rows] * p_in
            h_ref[0, pl.ds(r0 + 8 * g, 8), :] = h
            p_ref[0, pl.ds(r0 + 8 * g, 8), :] = p
            h_in = h[7:8]
            p_in = p[7:8]
        return h_in, p_in

    h_end, p_end = lax.fori_loop(
        0,
        length // ROWS,
        block,
        (jnp.zeros((1, width), F32), jnp.ones((1, width), F32)),
    )
    end_ref[0, 0:4, :] = jnp.broadcast_to(p_end, (4, width))
    end_ref[0, 4:8, :] = jnp.broadcast_to(h_end, (4, width))


def adjoint_kernel(
    dmix_ref,
    gate_ref,
    state_ref,
    ga_ref,
    mask_ref,
    vec_ref,
    lam_ref,
    q_ref,
    dgi_ref,
    end_ref,
):
    length, width = dmix_ref.shape[1:]
    row = lax.broadcasted_iota(jnp.int32, (ROWS, 1), 0)
    row8 = row % 8
    blocks = length // ROWS

    def block(i, carry):
        lam_in, q_in, a_next = carry
        r0 = pl.multiple_of((blocks - 1 - i) * ROWS, ROWS)
        here = pl.ds(r0, ROWS)
        begins = mask_ref[0, here, :][:, 3:4]
        d_mixer = dmix_ref[0, here, :]
        gelu, slope = gelu_parts(gate_ref[0, here, :])
        dgi_ref[0, here, :] = (d_mixer * state_ref[0, here, :] * slope).astype(BF)
        b = d_mixer * gelu
        a = jnp.exp(ga_ref[0, here, :] * vec_ref[3:4, :]) * (1.0 - begins)
        c = jnp.where(row == ROWS - 1, a_next, pltpu.roll(a, ROWS - 1, axis=0))
        for d in (1, 2, 4):
            valid = row8 < 8 - d
            b = jnp.where(valid, c * pltpu.roll(b, ROWS - d, axis=0) + b, b)
            c = jnp.where(valid, c * pltpu.roll(c, ROWS - d, axis=0), c)
        for g in reversed(range(ROWS // 8)):
            rows = slice(8 * g, 8 * g + 8)
            lam = b[rows] + c[rows] * lam_in
            q = c[rows] * q_in
            lam_ref[0, pl.ds(r0 + 8 * g, 8), :] = lam
            q_ref[0, pl.ds(r0 + 8 * g, 8), :] = q
            lam_in = lam[0:1]
            q_in = q[0:1]
        return lam_in, q_in, a[0:1]

    one = jnp.ones((1, width), F32)
    lam0, q0, a0 = lax.fori_loop(
        0, blocks, block, (jnp.zeros((1, width), F32), one, one)
    )
    end_ref[0, 0:4, :] = jnp.broadcast_to(a0 * q0, (4, width))
    end_ref[0, 4:8, :] = jnp.broadcast_to(a0 * lam0, (4, width))


def fold8(value):
    total = value[0:8]
    for g in range(1, value.shape[0] // 8):
        total = total + value[8 * g : 8 * g + 8]
    return total


def backward_kernel(
    lam_ref,
    q_ref,
    state_ref,
    ga_ref,
    gx_ref,
    mixed_ref,
    rnn_ref,
    halo_ref,
    mask_ref,
    edge_ref,
    conv_ref,
    vec_ref,
    wa_ref,
    wx_ref,
    drnn_ref,
    head_ref,
    tail_ref,
    wag_ref,
    wxg_ref,
    vg_ref,
    ext_ref,
    prev_ref,
    dm_ref,
):
    length, width = lam_ref.shape[1:]
    first = pl.program_id(0) == 0

    @pl.when(first)
    def _():
        wag_ref[...] = jnp.zeros_like(wag_ref)
        wxg_ref[...] = jnp.zeros_like(wxg_ref)
        vg_ref[...] = jnp.zeros_like(vg_ref)

    ext_ref[0:HALO, :] = halo_ref[0]
    ext_ref[HALO:, :] = rnn_ref[0]
    prev_ref[0:HALO, :] = jnp.broadcast_to(edge_ref[0, 0:1, :], (HALO, width))
    prev_ref[HALO:, :] = state_ref[0]
    dm_ref[length:, :] = jnp.zeros((HALO, width), F32)

    def block(i, carry):
        r0 = pl.multiple_of(i * ROWS, ROWS)
        here = pl.ds(r0, ROWS)
        masks = mask_ref[0, here, :]
        begins = masks[:, 3:4]
        lam = lam_ref[0, here, :] + q_ref[0, here, :] * edge_ref[0, 4:5, :]
        before = pltpu.roll(prev_ref[pl.ds(r0, ROWS + HALO), :], 1, axis=0)[
            HALO : HALO + ROWS
        ]
        gate_a = ga_ref[0, here, :]
        gate_x = gx_ref[0, here, :]
        mixed = mixed_ref[0, here, :]
        log_a = gate_a * vec_ref[3:4, :]
        decay = jnp.exp(log_a)
        inv_scale = lax.rsqrt(one_minus_exp(log_a))
        scale_raw = jnp.sqrt(one_minus_exp(log_a))
        keep = 1.0 - begins
        scale = scale_raw * keep + begins
        through = lam * mixed
        d_log = lam * before * decay * keep + jnp.where(
            begins > 0.5, 0.0, through * gate_x * (-(decay * decay) * inv_scale)
        )
        log_gate = d_log * gate_a
        d_pre_a = log_gate * (1.0 - gate_a) * vec_ref[3:4, :]
        d_pre_x = through * scale * gate_x * (1.0 - gate_x)
        pa = d_pre_a.astype(BF)
        px = d_pre_x.astype(BF)
        mb = mixed.astype(BF)
        d_mixed = (
            lam * gate_x * scale + dot_nt(pa, wa_ref[...]) + dot_nt(px, wx_ref[...])
        )
        dm_ref[here, :] = d_mixed
        wag_ref[...] += dot_tn(mb, pa)
        wxg_ref[...] += dot_tn(mb, px)
        terms = conv_terms(ext_ref[pl.ds(r0, ROWS + HALO), :], masks, ROWS)
        sums = [d_mixed * term for term in terms]
        sums += [d_mixed, d_pre_a, d_pre_x, log_gate]
        for n, value in enumerate(sums):
            vg_ref[n] += fold8(value)
        return carry

    lax.fori_loop(0, length // ROWS, block, 0)

    def shift(i, carry):
        r0 = pl.multiple_of(i * ROWS, ROWS)
        ext = dm_ref[pl.ds(r0, ROWS + HALO), :]
        masks = mask_ref[0, pl.ds(r0, ROWS + HALO), :]
        total = conv_ref[0:1, :] * ext[0:ROWS]
        for k in range(1, 4):
            moved = pltpu.roll(ext * masks[:, k - 1 : k], ROWS + HALO - k, axis=0)
            total = total + conv_ref[k : k + 1, :] * moved[0:ROWS]
        drnn_ref[0, pl.ds(r0, ROWS), :] = total.astype(BF)

        @pl.when(i == length // ROWS - 1)
        def _():
            tail_ref[0] = total[ROWS - HALO :]

        return carry

    lax.fori_loop(0, length // ROWS, shift, 0)
    head_ref[0] = dm_ref[0:HALO, :]


def block_specs(shapes):
    specs = []
    for shape, moving in shapes:
        if moving:
            specs.append(
                pl.BlockSpec((1,) + shape[1:], lambda i, n=len(shape): (i,) + (0,) * (n - 1))
            )
        else:
            specs.append(pl.BlockSpec(shape, lambda i, n=len(shape): (0,) * n))
    return specs


def cost(time):
    return pl.CostEstimate(flops=int(time * 2.5e8), bytes_accessed=0, transcendentals=0)


NT = (((1,), (1,)), ((), ()))
NN = (((1,), (0,)), ((), ()))
TN = (((0,), (0,)), ((), ()))


def seq_call(kernel, moving, fixed, outs, scratch, name, time):
    count = moving[0].shape[0]
    return pl.pallas_call(
        kernel,
        grid=(count,),
        in_specs=block_specs(
            [(a.shape, True) for a in moving] + [(a.shape, False) for a in fixed]
        ),
        out_specs=block_specs([(shape, move) for shape, _, move in outs]),
        out_shape=[jax.ShapeDtypeStruct(shape, dtype) for shape, dtype, _ in outs],
        scratch_shapes=scratch,
        compiler_params=pltpu.CompilerParams(
            dimension_semantics=("arbitrary",), vmem_limit_bytes=60 * 1024 * 1024
        ),
        cost_estimate=cost(time),
        name=name,
    )(*moving, *fixed)


def products(dims, sums, extras, outs, finish, name, base=None, width=None, halves=False):
    full = sums[0][0][1].shape[0 if dims == NT else 1]
    width = width or full
    columns = min(256, width)
    lefts, rights, where = [], [], []
    for pairs in sums:
        places = []
        for left, right in pairs:
            left = left if isinstance(left, tuple) else (left, 0, 1)
            known = [n for n, other in enumerate(lefts) if other[0] is left[0]]
            places.append(known[0] if known else len(lefts))
            if not known:
                lefts.append(left)
            rights.append(right)
        where.append(places)
    array, _, count = lefts[0]
    rows = array.shape[1] if dims == TN else array.shape[0] // count
    cuts = 2 if halves else 1
    near = len(lefts) + len(rights)

    def kernel(_, *refs):
        at, totals = len(lefts), []
        for places in where:
            total = None
            for place in places:
                term = lax.dot_general(
                    refs[place][...], refs[at][...], dims, preferred_element_type=F32
                )
                total = term if total is None else total + term
                at += 1
            totals.append(total)
        values = finish(*totals, *(ref[...] for ref in refs[near : near + len(extras)]))
        size = rows // cuts
        at = near + len(extras)
        for value in values:
            for n in range(cuts):
                refs[at][...] = value[n * size : (n + 1) * size].astype(refs[at].dtype)
                at += 1

    def whole(left):
        array, part, count = left
        shape = (array.shape[0] // count, array.shape[1])
        return pl.BlockSpec(shape, lambda j, b: (part, 0))

    def moving(array):
        if dims == NT:
            return pl.BlockSpec((columns, array.shape[1]), lambda j, b: (b[0] + j, 0))
        return pl.BlockSpec((array.shape[0], columns), lambda j, b: (0, b[0] + j))

    base = jnp.zeros((1,), jnp.int32) if base is None else (base // columns).reshape(1)
    tile = pl.BlockSpec((rows, columns), lambda j, b: (0, j))
    part = pl.BlockSpec((rows // cuts, columns), lambda j, b: (0, j))
    return pl.pallas_call(
        kernel,
        grid_spec=pltpu.PrefetchScalarGridSpec(
            num_scalar_prefetch=1,
            grid=(width // columns,),
            in_specs=[whole(a) for a in lefts]
            + [moving(a) for a in rights]
            + [tile] * len(extras),
            out_specs=[part] * (len(outs) * cuts),
        ),
        out_shape=[
            jax.ShapeDtypeStruct((rows // cuts, width), dtype)
            for dtype in outs
            for _ in range(cuts)
        ],
        compiler_params=pltpu.CompilerParams(
            dimension_semantics=("arbitrary",), vmem_limit_bytes=60 * 1024 * 1024
        ),
        cost_estimate=cost(sum(a.size for a in rights) // (width and full) * width * rows / 3.4e8),
        name=name,
    )(base, *(left[0] for left in lefts), *rights, *extras)


@jax.tree_util.register_pytree_node_class
class Joint:
    def __init__(self, rows, sizes):
        self.rows, self.sizes = rows, sizes

    def tree_flatten(self):
        return (self.rows,), self.sizes

    @classmethod
    def tree_unflatten(cls, sizes, children):
        return cls(children[0], sizes)

    def parts(self):
        at, out = 0, []
        for size in self.sizes:
            out.append(self.rows[at : at + size])
            at += size
        return out


def body(
    DP,
    M,
    inputs,
    cotangent,
    reset_mask,
    norm1_gain,
    w_input,
    w_branch,
    w_output,
    conv_weight,
    conv_bias,
    gate_a_weight,
    gate_a_bias,
    gate_x_weight,
    gate_x_bias,
    decay_param,
    norm2_gain,
    w_gate,
    w_up,
    w_down,
):
    heads_here, bw_here, bw = gate_a_weight.shape
    t = 4 if heads_here % 4 == 0 and DP % 4 == 0 else 2
    O = DP // t
    hpg = heads_here // t
    nh = M * hpg
    L, FH = inputs.shape
    D = FH * M
    Dl = w_input.shape[0]
    Lc = L // M
    half = t * Dl
    cz = w_input.shape[1] // t
    fz = w_gate.shape[1] // t
    C = M * cz
    FC = M * fz
    conv = conv_weight.shape[0]
    parts = t // 2
    last = parts - 1

    i_dp = lax.axis_index("dp")
    z = lax.axis_index("mp")
    q = i_dp % t
    o = i_dp // t

    def tp(value, j):
        return lax.ppermute(value, "dp", [(i, i ^ j) for i in range(DP)])

    def oshift(value, r):
        return lax.ppermute(
            value, "dp", [(i, ((i // t + r) % O) * t + i % t) for i in range(DP)]
        )

    def zshift(value, k):
        return lax.ppermute(value, "mp", [(i, (i + k) % M) for i in range(M)])

    def zline(value, k):
        got = lax.ppermute(
            value, "mp", [(i, i + k) for i in range(M) if 0 <= i + k < M]
        )
        return jnp.roll(got, k * cz, axis=-1)

    class Live(dict):
        __getattr__ = dict.__getitem__
        __setattr__ = dict.__setitem__

        def barrier(self):
            held = lax.optimization_barrier(dict(self))
            self.clear()
            self.update(held)

        def take(self, name):
            return self.pop(name)

    v = Live()

    def cut(array, index, size, axis):
        return lax.dynamic_slice_in_dim(array, index * size, size, axis)

    def put(array, piece, *starts):
        return lax.dynamic_update_slice(array, piece, starts)

    def pick(array, index, axis=0):
        return lax.dynamic_index_in_dim(array, index, axis, keepdims=False)

    def chunk_pieces(value, ahead=0, rider=None):
        if ahead:
            value = jnp.concatenate([jnp.zeros((ahead, FH), value.dtype), value])
        pieces = [
            lax.dynamic_slice_in_dim(value, (z + k) % M * Lc, Lc + ahead, 0)
            for k in range(M)
        ]
        if rider is not None:
            pieces[1] = jnp.concatenate([pieces[1], rider])
        return [zshift(piece, k) if k else piece for k, piece in enumerate(pieces)]

    def joined(pieces):
        own = jnp.zeros((pieces[0].shape[0], D), pieces[0].dtype)
        for k, piece in enumerate(pieces):
            own = put(own, piece, 0, ((z - k) % M) * FH)
        return own

    def far(value):
        return tp(value, 2) if parts > 1 else None

    def back_pieces(value):
        return [cut(value, (z + k) % M, FH, 1) for k in range(M)]

    def back_joined(pieces):
        out = jnp.zeros((L, FH), pieces[0].dtype)
        for k, piece in enumerate(pieces):
            out = put(out, piece, ((z - k) % M) * Lc, 0)
        return out

    def send_sum(part, p):
        mine = part[0].astype(F32) + tp(part[1], 1).astype(F32)
        if p:
            mine = tp(mine.astype(BF), 2).astype(F32)
        return mine

    def stacked(blocks):
        return jnp.concatenate(blocks) if len(blocks) > 1 else blocks[0]

    def joint(transfer, blocks):
        return Joint(transfer(stacked(blocks)), tuple(b.shape[0] for b in blocks))

    def exchange(mine):
        if parts == 1:
            return [mine(q), tp(mine(q ^ 1), 1)]
        got = tp(jnp.stack([mine(q ^ 1), mine(q ^ 3)]), 1)
        after = tp(jnp.stack([mine(q ^ 2), got[1]]), 2)
        return [mine(q), got[0], after[0], after[1]]

    def from_group(pieces):
        block = jnp.zeros((pieces[0].shape[0], half), BF)
        for j, piece in enumerate(pieces):
            block = put(block, piece, 0, (q ^ j) * Dl)
        return block

    def to_groups(*blocks):
        return [joint(lambda b: oshift(b, r), blocks) for r in range(1, O)]

    def by_block(got):
        return [list(same) for same in zip(*(g.parts() for g in got))]

    def ring_next(*blocks):
        return joint(lambda b: zshift(b, 1), blocks)

    def fill_own(full, block, s):
        return put(full, block, s * block.shape[0], o * half)

    def fill_far(full, others, s):
        for r, piece in enumerate(others, 1):
            full = put(full, piece, s * piece.shape[0], ((o - r) % O) * half)
        return full

    def mixer_parts(block):
        return block[:cz], block[cz : 2 * cz], block[2 * cz :]

    def fill_mixer_far(full, others, s):
        split = [mixer_parts(piece) for piece in others]
        return [fill_far(f, [g[n] for g in split], s) for n, f in enumerate(full)]

    def folded(block):
        return jnp.concatenate(
            [block[:, n * FH : (n + 1) * FH] for n in range(half // FH)]
        )

    def unfolded(rows):
        size = rows.shape[0] // (half // FH)
        return jnp.concatenate(
            [rows[n * size : (n + 1) * size] for n in range(half // FH)], axis=1
        )

    def grad_y(*grads):
        return [g[0] for g in grads], to_groups_of(grads)

    def to_groups_of(grads):
        return [joint(lambda b: oshift(b, r), [g[r] for g in grads]) for r in range(1, O)]

    def y_parts(held):
        own, got = held
        return [list(same) for same in zip(own, *(g.parts() for g in got))]

    def slot(pieces, k):
        size = pieces[0].shape[0] // M
        return sum(piece[k * size : (k + 1) * size].astype(F32) for piece in pieces)

    def ring_sends(*rings):
        sends = []
        for pieces, k, moving in rings:
            total = slot(pieces, k)
            if moving is not None:
                total = total + moving.astype(F32)
            sends.append(total.astype(BF))
        return sends

    def ring_step(*rings):
        return ring_next(*ring_sends(*rings))

    def ring_end(pieces, moving):
        for k in range(4, M):
            (moving,) = ring_step((pieces, k, moving)).parts()
        return (moving.astype(F32) + slot(pieces, 0)).astype(BF)

    def direct_sends(*grads):
        return [[slot(pieces, k).astype(BF) for pieces in grads] for k in range(M)]

    def grad_end(pieces):
        size = pieces[0].shape[0]
        out = jnp.zeros((t * size, Dl), BF)
        for j, piece in enumerate(pieces):
            out = put(out, piece, (q ^ j) * size, 0)
        return out

    def exchange_grads(*totals):
        sizes = tuple(total.shape[0] for total in totals)
        rows = stacked(totals)
        return [Joint(p, sizes) for p in exchange(lambda k: cut(rows, k, Dl, 1))]

    def by_grad(got):
        return [list(same) for same in zip(*(g.parts() for g in got))]

    ng, nc = norm1_gain.shape[0], conv_bias.shape[0]
    packed = jnp.concatenate(
        [
            norm1_gain,
            norm2_gain,
            conv_weight.reshape(-1),
            conv_bias,
            gate_a_bias,
            gate_x_bias,
            decay_param,
        ]
    )
    gate_size = 2 * hpg * bw_here * bw
    gate_rows = -(-(gate_size + packed.shape[0]) // (16 * Dl)) * 16
    gates_flat = jnp.stack([gate_a_weight, gate_x_weight]).reshape(
        2, t, hpg, bw_here, bw
    )
    gates_flat = gates_flat.transpose(1, 0, 2, 3, 4).reshape(t, gate_size)
    extra = gate_size + packed.shape[0]
    gates_flat = jnp.concatenate(
        [
            gates_flat,
            jnp.broadcast_to(packed, (t,) + packed.shape),
            jnp.zeros((t, gate_rows * Dl - extra), BF),
        ],
        axis=1,
    )
    mine_all = jnp.concatenate(
        [
            w_input.T.reshape(t, cz, Dl),
            w_branch.T.reshape(t, cz, Dl),
            gates_flat.reshape(t, gate_rows, Dl),
            w_output.reshape(t, cz, Dl),
            w_gate.T.reshape(t, fz, Dl),
            w_up.T.reshape(t, fz, Dl),
            w_down.reshape(t, fz, Dl),
        ],
        axis=1,
    )
    def normed(value, gain):
        wide = value.astype(F32)
        scale = lax.rsqrt(jnp.mean(wide * wide, axis=1, keepdims=True) + epsilon)
        return wide * scale, scale

    rows_a = 2 * cz + gate_rows
    v.z_in = chunk_pieces(inputs, 16)
    v.blocks = exchange(lambda k: pick(mine_all, k))
    v.cotangent = cotangent
    v.barrier()

    block = from_group(v.take("blocks"))
    block_a = block[:rows_a]
    block_b = block[rows_a : rows_a + cz]
    block_g = block[rows_a + cz : rows_a + cz + 2 * fz]
    v.d = [block[rows_a + cz + 2 * fz :]]
    v.ring_a = [block_a] + [zshift(block_a, k) for k in range(1, M)]
    v.b, v.g = [block_b], [block_g]
    v.y_first = to_groups(block_a, block_b, block_g)
    resets = jnp.pad(reset_mask.astype(BF), (0, 16 * D - L)).reshape(16, D)
    v.own_in = jnp.concatenate([joined(v.take("z_in")), resets])
    v.far_in = far(v.own_in)
    v.barrier()

    y_next = to_groups(*v.ring_a[1:])
    ring_bg = ring_next(v.b[-1], v.g[-1])
    y_a, y_b, y_g = by_block(v.take("y_first"))
    full_a = [
        jnp.zeros((M * size, D), BF) for size in (cz, cz, gate_rows)
    ]
    for k, mine in enumerate(v.take("ring_a")):
        full_a = [fill_own(f, p, k) for f, p in zip(full_a, mixer_parts(mine))]
    v.full_a = fill_mixer_far(full_a, y_a, 0)
    v.full_b = fill_far(fill_own(jnp.zeros((C, D), BF), v.b[0], 0), y_b, 0)
    full_g = [jnp.zeros((FC, D), BF)] * 2
    full_g = [fill_own(f, p, 0) for f, p in zip(full_g, (v.g[0][:fz], v.g[0][fz:]))]
    v.full_g = [
        fill_far(f, [y[n * fz : (n + 1) * fz] for y in y_g], 0)
        for n, f in enumerate(full_g)
    ]
    v.full_d = fill_own(jnp.zeros((FC, D), BF), v.d[0], 0)
    v.take("b")
    v.take("g")
    v.ring_bg = ring_bg
    slots_in = [v.own_in, tp(v.own_in, 1)]
    if parts > 1:
        slots_in += [v.far_in, tp(v.far_in, 1)]
    v.take("far_in")
    resets = jnp.stack([e[16 + Lc :].reshape(-1)[:L].astype(F32) for e in slots_in])
    open_ = 1.0 - jnp.maximum(resets, (jnp.arange(L) % SEQ == 0).astype(F32))
    back1 = jnp.pad(open_, ((0, 0), (1, 0)))[:, :L]
    back2 = jnp.pad(open_, ((0, 0), (2, 0)))[:, :L]
    masks = jnp.stack([open_, open_ * back1, open_ * back1 * back2, 1.0 - open_], axis=1)
    masks = jnp.pad(masks, ((0, 0), (0, 0), (0, HALO)))
    masks = lax.dynamic_slice(masks, (0, 0, z * Lc), (t, 4, Lc + HALO))
    masks = masks.transpose(0, 2, 1)

    v.masks = masks
    v.own_in = v.own_in[16 : 16 + Lc]
    v.groups_in = jnp.concatenate([e[16 : 16 + Lc] for e in slots_in])
    v.ahead_in = jnp.concatenate([e[:16] for e in slots_in])
    v.scale_in = normed(v.groups_in, None)[1]
    v.y_a = y_next
    v.barrier()

    def fill_gate(k, own=None, others=None):
        for n in range(2):
            rows = slice(n * fz, (n + 1) * fz)
            if own is not None:
                v.full_g[n] = fill_own(v.full_g[n], own[rows], k)
            if others is not None:
                v.full_g[n] = fill_far(v.full_g[n], [y[rows] for y in others], k)

    b_1, g_1 = v.take("ring_bg").parts()
    v.y_1 = to_groups(b_1, g_1, v.d[0])
    ring = ring_next(b_1, g_1, v.take("d")[0])
    v.full_b = fill_own(v.full_b, b_1, 1)
    fill_gate(1, own=g_1)
    b_next, g_next, v.d = ring.parts()
    v.b, v.g = [b_next], [g_next]
    v.y_2 = to_groups(b_next, g_next)
    while len(v.b) < M - 2:
        b_next, g_next = ring_next(b_next, g_next).parts()
        v.b, v.g = v.b + [b_next], v.g + [g_next]
    for k, others in enumerate(by_block(v.take("y_a")), 1):
        v.full_a = fill_mixer_far(v.full_a, others, k)
    w_in_t, w_br_t, rest = v.take("full_a")
    rest = rest.reshape(M, gate_rows, DP, Dl).transpose(0, 2, 1, 3)
    rest = rest.reshape(M, DP, gate_rows * Dl)
    gates = rest[:, :, :gate_size].reshape(M, DP, 2, hpg, bw_here, bw)
    gates = gates.transpose(2, 0, 3, 1, 4, 5).reshape(2, nh, bw, bw)
    dense = []
    for kind in range(2):
        rows = [
            jnp.pad(gates[kind, n], ((0, 0), (n * bw, (nh - 1 - n) * bw)))
            for n in range(nh)
        ]
        dense.append(jnp.concatenate(rows))
    wa, wx = dense
    v.w_in_t, v.w_br_t, v.wa, v.wx = w_in_t, w_br_t, wa, wx
    every = rest[:, :, gate_size : gate_size + packed.shape[0]].astype(F32)
    gains = jnp.stack([pick(every[:, :, : 2 * ng], (z - b) % M) for b in range(M)])
    gain_one = gains[:, :, :ng].reshape(1, D)
    gain_two = gains[:, :, ng:].reshape(1, D)
    vectors = every[:, :, 2 * ng :].reshape(M, DP, conv + 4, nc).transpose(2, 0, 1, 3)
    vectors = pick(vectors.reshape(conv + 4, M, t, cz), q, 2).reshape(conv + 4, C)
    conv_w = vectors[:conv]
    decay = vectors[conv + 3]
    log_slope = -8.0 * jax.nn.softplus(decay)
    vec = jnp.stack(
        [vectors[conv], vectors[conv + 1], vectors[conv + 2], log_slope]
        + [jnp.zeros_like(decay)] * 4
    )

    v.vec, v.conv_w, v.gain_one, v.gain_two = vec, conv_w, gain_one, gain_two
    v.n1 = (v.take("groups_in").astype(F32) * v.take("scale_in") * v.gain_one).astype(BF)
    ahead = (normed(v.take("ahead_in"), None)[0] * v.gain_one).astype(BF)

    def mixed_sum(*pairs):
        return products(
            NN, [list(pairs)], [], [BF], lambda total: (total,), "product", halves=True
        )

    def chain(ends, sign):
        total = jnp.zeros_like(ends[..., 4:5, :])
        for k in reversed(range(1, M)):
            got = zline(ends, sign * k)
            total = got[..., 4:5, :] + got[..., 0:1, :] * total
        return total

    shape = (t, Lc, C)
    v.rnn = dot_nt(v.n1, v.w_in_t).reshape(shape)
    v.gin = dot_nt(v.n1, v.w_br_t).reshape(shape)
    v.halos = dot_nt(ahead, v.w_in_t).reshape(t, 16, C)[:, 16 - HALO :]
    v.fwd = seq_call(
        forward_kernel,
        [v.rnn, v.halos, v.masks],
        [v.conv_w, v.vec, v.wa, v.wx],
        [(shape, F32, True)] * 5 + [((t, 8, C), F32, True)],
        [pltpu.VMEM((Lc + HALO, C), F32)],
        "recurrence",
        40,
    )
    v.barrier()

    y_next = to_groups(*v.b[1:])
    y_b, y_g, y_d = by_block(v.take("y_1"))
    v.full_b = fill_far(v.full_b, y_b, 1)
    fill_gate(1, others=y_g)
    v.full_d = fill_far(v.full_d, y_d, 0)
    y_b, y_g = by_block(v.take("y_2"))
    v.full_b = fill_far(v.full_b, y_b, 2)
    fill_gate(2, others=y_g)
    for k, mine in enumerate(v.take("b"), 2):
        v.full_b = fill_own(v.full_b, mine, k)
    for k, mine in enumerate(v.g, 2):
        fill_gate(k, own=mine)
    v.full_d = fill_own(v.full_d, v.d, 1)
    v.cin = chain(v.fwd[5], 1)
    v.state = v.fwd[3] + v.fwd[4] * v.cin
    v.mixer = (gelu_parts(v.gin)[0] * v.state).astype(BF).reshape(t * Lc, C)
    v.fwd = v.fwd[:3]
    v.y_b = y_next
    v.barrier()

    for k, others in enumerate(by_block(v.take("y_b")), 3):
        v.full_b = fill_far(v.full_b, others, k)
    v.w_out = v.take("full_b")
    v.y_g = to_groups(*v.take("g")[1:], v.d)
    v.d = [v.d]
    while len(v.d) < M - 2:
        v.d = v.d + ring_next(v.d[-1]).parts()
    rec_sum = None
    for p in reversed(range(parts)):
        part = send_sum(mixed_sum(((v.mixer, p, parts), v.w_out)), p)
        rec_sum = part if rec_sum is None else rec_sum + part
    v.resid_mid = v.own_in.astype(F32) + rec_sum
    v.unit_two, v.scale_two = normed(v.resid_mid, v.gain_two)
    v.n2_own = (v.unit_two * v.gain_two).astype(BF)
    v.barrier()

    got = by_block(v.take("y_g"))
    for k, others in enumerate(got[:-1], 3):
        fill_gate(k, others=others)
    v.full_d = fill_far(v.full_d, got[-1], 1)
    v.w_gate_t, v.w_up_t = v.take("full_g")
    for k, mine in enumerate(v.d[1:], 2):
        v.full_d = fill_own(v.full_d, mine, k)
    v.z_cot = chunk_pieces(v.take("cotangent"), rider=folded(v.d[-1]))
    v.n2_far = far(v.n2_own)
    v.n2 = [jnp.concatenate([v.n2_own, tp(v.n2_own, 1)])]
    v.take("n2_own")

    def mlp_forward(p):
        return products(
            NT,
            [[(v.n2[p], v.w_gate_t)], [(v.n2[p], v.w_up_t)]],
            [],
            [F32, F32, BF],
            lambda gate, up: (gate, up, gelu_parts(gate)[0] * up),
            "mlp",
        )

    v.mlp = [mlp_forward(0)]
    v.barrier()

    v.d = v.d[1:] + [unfolded(v.z_cot[1][Lc:])]
    v.z_cot[1] = v.z_cot[1][:Lc]
    v.y_d = to_groups(*v.d)
    cot_own = joined(v.take("z_cot"))
    v.cot = [jnp.concatenate([cot_own, tp(cot_own, 1)])]
    v.far_cot = far(cot_own)
    if parts > 1:
        v.n2.append(jnp.concatenate([v.n2_far, tp(v.n2_far, 1)]))
        v.mlp.append(mlp_forward(1))
    v.take("n2_far")
    v.barrier()

    def summed(lefts, rights):
        out = [
            products(
                TN,
                [list(zip(lefts, rights))],
                [],
                [BF],
                lambda total: (total,),
                "gradient",
                base=((o + r) % O) * half,
                width=half,
            )[0]
            for r in reversed(range(O))
        ]
        return out[::-1]

    v.full_d = fill_own(v.full_d, v.take("d")[-1], M - 1)
    for k, others in enumerate(by_block(v.take("y_d")), 2):
        v.full_d = fill_far(v.full_d, others, k)
    v.w_dn = v.take("full_d")
    if parts > 1:
        v.cot.append(jnp.concatenate([v.far_cot, tp(v.far_cot, 1)]))
    v.take("far_cot")

    def mlp_back(p):
        def finish(d_hidden, gate, up):
            gelu, slope = gelu_parts(gate)
            return d_hidden * up * slope, d_hidden * gelu

        return products(
            NT, [[(v.cot[p], v.w_dn)]], list(v.mlp[p][:2]), [BF, BF], finish, "mlp_back"
        )

    def mlp_back_in(p):
        gate, up = v.d_mlp[p]
        return mixed_sum((gate, v.w_gate_t), (up, v.w_up_t))

    v.grad_down = summed([m[2] for m in v.mlp], v.cot)
    v.d_mlp = [None] * parts
    v.d_mlp[last] = mlp_back(last)
    v.barrier()

    v.y_down = grad_y(v.take("grad_down"))
    v.dn2 = [None] * parts
    v.dn2[last] = mlp_back_in(last)
    v.dn2_sum = send_sum(v.dn2[last], last) if last else None
    for p in range(last):
        v.d_mlp[p] = mlp_back(p)
        v.dn2[p] = mlp_back_in(p)
    v.grad_gate = summed([d[0] for d in v.d_mlp], v.n2)
    v.hidden = [m[2] for m in v.take("mlp")]
    v.cot_own = v.take("cot")[0][:Lc]
    v.barrier()

    (v.y_down,) = y_parts(v.y_down)
    v.ring = ring_step((v.y_down, 1, None))
    v.y_gate = grad_y(v.take("grad_gate"))
    dn2_sum = v.take("dn2_sum")
    for p in reversed(range(last if last else 1)):
        part = send_sum(v.dn2[p], p)
        dn2_sum = part if dn2_sum is None else dn2_sum + part
    v.take("dn2")

    def norm_back(grad, unit, scale, gain):
        weighted = grad * gain
        dots = jnp.mean(weighted * unit, axis=1, keepdims=True)
        return scale * (weighted - unit * dots), jnp.sum(grad * unit, axis=0)

    back_two, v.gain_two_grad = norm_back(dn2_sum, v.unit_two, v.scale_two, v.gain_two)
    v.d_mid = v.take("cot_own").astype(F32) + back_two
    v.d_own = v.d_mid.astype(BF)
    v.far_branch = far(v.d_own)
    v.near_branch = tp(v.d_own, 1)
    v.grad_up = summed([d[1] for d in v.d_mlp], v.n2)
    v.take("n2")
    v.take("d_mlp")
    v.out = [mixed_sum((h, v.w_dn)) for h in v.take("hidden")]
    v.barrier()

    (v.y_gate,) = y_parts(v.y_gate)
    (r_down,) = v.ring.parts()
    v.ring = ring_step((v.y_down, 2, r_down), (v.y_gate, 1, None))
    v.y_up = grad_y(v.take("grad_up"))
    slots_of = [v.take("d_own"), v.take("near_branch")]
    if parts > 1:
        slots_of += [v.far_branch, tp(v.far_branch, 1)]
    v.take("far_branch")
    v.d_branch = jnp.concatenate(slots_of)
    out = v.take("out")
    got = joint(lambda b: tp(b, 1), [part[1] for part in out]).parts()
    out_sum = out[0][0].astype(F32) + got[0].astype(F32)
    if parts > 1:
        there = out[1][0].astype(F32) + got[1].astype(F32)
        out_sum = out_sum + tp(there.astype(BF), 2).astype(F32)
    v.output = (v.take("resid_mid") + out_sum).astype(BF)

    v.adjoint = seq_call(
        adjoint_kernel,
        [
            dot_nt(v.d_branch, v.w_out).reshape(shape),
            v.take("gin"),
            v.state,
            v.fwd[1],
            v.masks,
        ],
        [v.vec],
        [(shape, F32, True)] * 2 + [(shape, BF, True), ((t, 8, C), F32, True)],
        [],
        "adjoint",
        24,
    )
    v.barrier()

    r_down, r_gate = v.ring.parts()
    v.ring = ring_step((v.y_down, 3, r_down), (v.y_gate, 2, r_gate))
    (v.y_up,) = y_parts(v.y_up)
    v.edges = jnp.concatenate(
        [
            jnp.broadcast_to(v.take("cin"), (t, 4, C)),
            jnp.broadcast_to(chain(v.adjoint[3], -1), (t, 4, C)),
        ],
        1,
    )
    v.grad_output = summed([v.take("mixer")], [v.take("d_branch")])
    v.d_gin = v.adjoint[2].reshape(t * Lc, C)
    v.grad_branch = summed([v.d_gin], [v.n1])
    v.barrier()

    v.r_down, r_gate = v.ring.parts()
    v.ring = ring_step((v.y_gate, 3, r_gate), (v.y_up, 1, None))
    v.y_mixer = grad_y(v.take("grad_output"), v.take("grad_branch"))
    pieces = back_pieces(v.take("output"))
    v.z_out = [zshift(piece, k) if k else piece for k, piece in enumerate(pieces)]
    mixed, gate_a, gate_x = v.fwd
    lam, prod, _, _ = v.adjoint
    v.d_rnn, v.heads, v.tails, v.grad_wa, v.grad_wx, v.grad_vec = seq_call(
        backward_kernel,
        [
            lam,
            prod,
            v.state,
            gate_a,
            gate_x,
            mixed,
            v.rnn,
            v.halos,
            v.masks,
            v.edges,
        ],
        [v.conv_w, v.vec, v.wa, v.wx],
        [
            (shape, BF, True),
            ((t, HALO, C), F32, True),
            ((t, HALO, C), F32, True),
            ((C, C), F32, False),
            ((C, C), F32, False),
            ((8, 8, C), F32, False),
        ],
        [pltpu.VMEM((Lc + HALO, C), F32)] * 3,
        "recurrence_back",
        64,
    )
    for name in ("adjoint", "fwd", "state", "rnn", "halos", "edges"):
        v.take(name)
    v.barrier()

    following = zline(v.take("heads"), -1)
    fix = [jnp.zeros((t, 1, C), F32)] * HALO
    for k in range(1, 4):
        for n in range(k):
            row = HALO - k + n
            fix[row] = fix[row] + v.conv_w[k] * (
                v.masks[:, Lc + n : Lc + n + 1, k - 1 : k] * following[:, n : n + 1]
            )
    tail = (v.take("tails") + jnp.concatenate(fix, axis=1)).astype(BF)
    v.d_rnn = put(v.d_rnn, tail, 0, Lc - HALO, 0).reshape(t * Lc, C)
    z_down = ring_end(v.take("y_down"), v.take("r_down"))
    r_gate, r_up = v.take("ring").parts()
    z_gate = ring_end(v.take("y_gate"), r_gate)
    y_output, y_branch = y_parts(v.take("y_mixer"))
    rings = ring_sends((v.y_up, 2, r_up))

    def direct(rings, *grads):
        got = []
        for k, send in enumerate(direct_sends(*grads)):
            send = send + rings if k == M - 1 else send
            got.append(joint(lambda b: zshift(b, M - k) if k else b, send))
        return got

    v.z_mixer = direct(rings, y_output, y_branch)
    v.output = back_joined(v.take("z_out"))
    gates_grad = jnp.stack(
        [
            jnp.stack(
                [g[n * bw : (n + 1) * bw, n * bw : (n + 1) * bw] for n in range(nh)]
            )
            for g in (v.take("grad_wa"), v.take("grad_wx"))
        ]
    )
    gates_grad = gates_grad.reshape(2, M, hpg, DP, bw_here, bw)
    gates_grad = gates_grad.transpose(1, 3, 0, 2, 4, 5).reshape(M, DP, gate_size)
    small = jnp.sum(v.take("grad_vec"), axis=1).reshape(2 * conv, M, O, nc)
    small = small.transpose(1, 2, 0, 3).reshape(M, O, 2 * conv * nc)
    small = put(jnp.zeros((M, DP, 2 * conv * nc), F32), small, 0, q * O, 0)
    gain_two_grad = v.take("gain_two_grad").reshape(M, DP, ng)
    gain_two_grad = jnp.stack([pick(gain_two_grad, (z - k) % M) for k in range(M)])
    gates_grad = jnp.concatenate([gates_grad, small, gain_two_grad], axis=2)
    gates_grad = jnp.pad(
        gates_grad, ((0, 0), (0, 0), (0, gate_rows * Dl - gates_grad.shape[2]))
    )
    gates_grad = gates_grad.reshape(M, DP, gate_rows, Dl).transpose(0, 2, 1, 3)
    gates_grad = gates_grad.reshape(M * gate_rows, D).astype(BF)
    gates_grad = [cut(gates_grad, (o + r) % O, half, 1) for r in range(O)]
    v.y_in = grad_y(summed([v.d_rnn], [v.n1]), gates_grad)
    v.take("n1")
    v.dn1 = [
        mixed_sum(((v.d_rnn, p, parts), v.w_in_t), ((v.d_gin, p, parts), v.w_br_t))
        for p in range(parts)
    ]
    v.z_down, v.z_gate = z_down, z_gate
    for name in ("d_rnn", "d_gin", "w_in_t", "w_br_t", "wa", "wx", "masks", "vec"):
        v.take(name)
    v.barrier()

    r_up = v.z_mixer[M - 1].parts()[2]
    v.z_in = direct(ring_sends((v.y_up, 3, r_up)), *y_parts(v.take("y_in")))
    dn1_sum = None
    for p in reversed(range(parts)):
        part = send_sum(v.dn1[p], p)
        dn1_sum = part if dn1_sum is None else dn1_sum + part
    v.dn1 = dn1_sum
    v.barrier()

    def added(pieces):
        return [
            sum(p.astype(F32) for p in same).astype(BF)
            for same in zip(*(piece.parts()[:2] for piece in pieces))
        ]

    r_up = v.z_in[M - 1].parts()[2]

    z_output, z_branch = added(v.take("z_mixer"))
    z_in, z_gates = added(v.take("z_in"))
    z_up = ring_end(v.take("y_up"), r_up)
    totals = exchange_grads(
        v.take("z_down"), v.take("z_gate"), z_up, z_output, z_branch, z_in, z_gates
    )
    unit_one, scale_one = normed(v.own_in, v.gain_one)
    back_one, gain_one_grad = norm_back(v.take("dn1"), unit_one, scale_one, v.gain_one)
    pieces = back_pieces((v.d_mid + back_one).astype(BF))
    sums = jnp.broadcast_to(gain_one_grad.astype(BF), (16, D))
    joints = []
    for k, piece in enumerate(pieces):
        joint = jnp.concatenate([piece, cut(sums, (z + k) % M, FH, 1)])
        joints.append(zshift(joint, k) if k else joint)
    *whole, last_rows = by_grad(totals)
    v.joints = joints
    v.grads = [grad_end(total) for total in whole]
    v.last_rows = last_rows
    v.barrier()

    grad_down, grad_gate, grad_up, grad_output, grad_branch, grad_in = v.grads
    input_grad = back_joined([joint[:Lc] for joint in v.joints]).astype(F32)
    gain_one_grad = sum(joint[Lc].astype(F32) for joint in v.joints)
    step = 1
    while step < DP:
        gain_one_grad = gain_one_grad + tp(gain_one_grad, step)
        step *= 2
    gain_one_grad = cut(gain_one_grad, i_dp, ng, 0)
    output = v.output

    rest_in = jnp.stack([piece.reshape(-1) for piece in v.last_rows])
    small = jnp.sum(rest_in[:, gate_size:].astype(F32), axis=0)
    rest_in = jnp.stack([pick(rest_in, q ^ k) for k in range(t)])
    mine = small[: 2 * conv * nc].reshape(2 * conv, nc)
    gain_two_grad = small[2 * conv * nc : 2 * conv * nc + ng]
    decay_grad = mine[conv + 3] * (-8.0 * jax.nn.sigmoid(decay_param.astype(F32)))

    gates_back = rest_in[:, :gate_size].reshape(t, 2, hpg, bw_here, bw)
    gates_back = gates_back.transpose(1, 0, 2, 3, 4)
    gates_back = gates_back.reshape(2, heads_here, bw_here, bw).astype(F32)

    def flipped(value):
        return lax.optimization_barrier(value).T.astype(F32)

    return (
        output,
        input_grad,
        gain_one_grad,
        flipped(grad_in),
        flipped(grad_branch),
        grad_output.astype(F32),
        mine[:conv],
        mine[conv],
        gates_back[0],
        mine[conv + 1],
        gates_back[1],
        mine[conv + 2],
        decay_grad,
        gain_two_grad,
        flipped(grad_gate),
        flipped(grad_up),
        grad_down.astype(F32),
    )


def solution(mesh):
    both = P(("mp", "dp"))
    wide = P("dp", "mp")
    tall = P("mp", "dp")
    taps = P(None, ("mp", "dp"))
    gate = P("mp", "dp", None)
    params = (both, wide, wide, tall, taps, both, gate, both, gate, both, both, both, wide, wide, tall)
    return jax.shard_map(
        functools.partial(body, mesh.shape["dp"], mesh.shape["mp"]),
        mesh=mesh,
        in_specs=(wide, wide, P("dp")) + params,
        out_specs=(wide, wide) + params,
        check_vma=False,
    )
```

time: 1420 us -> 1320 us (0.930)
  Pallas kernels: 131 us -> 399 us
  matrix products: 279 us -> 34.3 us
  waiting for transfers between devices: 566 us -> 428 us
  other arithmetic: 123 us -> 153 us
  starting transfers between devices: 104 us -> 88.4 us
    pallas_call x0 -> x24, Pallas kernels: none -> 285 us  [products(): pl.pallas_call(kernel, grid_spec=pltpu.PrefetchScalarGridSpec(num_scalar_...]
    dot_general x24 -> x0, matrix products: 170 us -> none  [the longest x12 91.2 us: dot_tn(): lax.dot_general(left, right, (((0,), (0,)), ((), ())), preferred_element_...]
    ppermute x11 -> x12, waiting for transfers between devices: 149 us -> 49.3 us  [oshift(): lax.ppermute(value, 'dp', [(i, (i // t + r) % O * t + i % t) for i in ran...]
    dot_general x12 -> x4, matrix products: 110 us -> 34.3 us  [dot_nt(): lax.dot_general(left, right, (((1,), (1,)), ((), ())), preferred_element_...]
    dynamic_update_slice x85 -> x72, local copies, waits for them, and re-layouts: 26.9 us -> 58 us  [put(): return lax.dynamic_update_slice(array, piece, starts)]
    slice x55 -> x23, local copies, waits for them, and re-layouts: 42.2 us -> 19.8 us  [the longest x9 6.9 us: parts(): out.append(self.rows[at:at + size])]
    pallas_call x6 -> x3, Pallas kernels: 131 us -> 114 us  [seq_call(): pl.pallas_call(kernel, grid=(count,), in_specs=block_specs([(a.shape, Tru...]
    unnamed x374 -> x228, local copies, waits for them, and re-layouts: 52.7 us -> 36.7 us
  transfers between devices with their start and end apart: 92 -> 78, of which waited for: 34 -> 35; matrix products, arithmetic and copies ran while one was open for 31% -> 24% of each run, Pallas kernels for 8% -> 25%
where the time goes in v3:
time: 1320 us; the launch traced here: 1300 us
  waiting for transfers between devices  428 us (32%)
  Pallas kernels  399 us (30%)
  local copies, waits for them, and re-layouts  199 us (15%)
  other arithmetic  153 us (12%)
  starting transfers between devices  88.4 us (7%)
  matrix products  34.3 us (3%)
    pallas_call x24, Pallas kernels, products(): pl.pallas_call(kernel, grid_spec=pltpu.PrefetchScalarGridSpec(num_scalar_...  285 us
    ppermute x29, waiting for transfers between devices, zshift(): return lax.ppermute(value, 'mp', [(i, (i + k) % M) for i in range(M)])  188 us
    ppermute x30, waiting for transfers between devices, tp(): return lax.ppermute(value, 'dp', [(i, i ^ j) for i in range(DP)])  181 us
    pallas_call x3, Pallas kernels, seq_call(): pl.pallas_call(kernel, grid=(count,), in_specs=block_specs([(a.shape, Tru...  114 us
    dynamic_update_slice x72, local copies, waits for them, and re-layouts, put(): return lax.dynamic_update_slice(array, piece, starts)  58 us
    ppermute x12, waiting for transfers between devices, oshift(): lax.ppermute(value, 'dp', [(i, (i // t + r) % O * t + i % t) for i in ran...  49.3 us
    ppermute x29, starting transfers between devices, zshift(): return lax.ppermute(value, 'mp', [(i, (i + k) % M) for i in range(M)])  46.5 us
    unnamed x228, local copies, waits for them, and re-layouts  36.7 us
  transfers between devices with their start and end apart: 78, of which 35 were waited for; matrix products, arithmetic and copies ran while one was open for 24% of the time, Pallas kernels for 25%

profile of v3, /device:TPU:8, one launch (start us, length us, event | category | flops | bytes accessed | tf_op | source)
XLA Modules:
  0.0 1304.0 jit_solution(687892450308687377)
XLA Ops:
  34.8 32.1 %collective-permute-done.1 = bf16[2,1664,256]{2,1,0:T(8,128)(2,1)} collective-permute-done((bf16[2,1664,256]{2,1,0:T(8,128)(2,1)}, bf16[2,1664,256]{2,1,0:T(8,128)(2,1)}, u32[]{:S(2)}, u32[]{:S(2)}) %collective-permute-start.1) | collective-permute-done | bytes 1703968 | tf_op jit(solution)/shard_map/ppermute | solution.py:481
  93.3 15.4 %collective-permute-done.6 = bf16[352,1024]{1,0:T(8,128)(2,1)} collective-permute-done((bf16[352,1024]{1,0:T(8,128)(2,1)}, bf16[352,1024]{1,0:T(8,128)(2,1)}, u32[]{:S(2)}, u32[]{:S(2)}) %collective-permute-start.6) | collective-permute-done | bytes 720928 | tf_op jit(solution)/shard_map/ppermute | solution.py:489
  108.7 42.6 %collective-permute-done.7 = bf16[352,1024]{1,0:T(8,128)(2,1)} collective-permute-done((bf16[352,1024]{1,0:T(8,128)(2,1)}, bf16[352,1024]{1,0:T(8,128)(2,1)}, u32[]{:S(2)}, u32[]{:S(2)}) %collective-permute-start.7) | collective-permute-done | bytes 720928 | tf_op jit(solution)/shard_map/ppermute | solution.py:489
  206.5 22.7 %collective-permute-done.13 = bf16[1056,1024]{1,0:T(8,128)(2,1)S(1)} collective-permute-done((bf16[1056,1024]{1,0:T(8,128)(2,1)S(1)}, bf16[1056,1024]{1,0:T(8,128)(2,1)S(1)}, u32[]{:S(2)}, u32[]{:S(2)}) %collective-permute-start.13) | collective-permute-done | bytes 2162720 | tf_op jit(solution)/shard_map/ppermute | solution.py:484
  272.5 11.5 fusion.134
  283.9 37.0 %recurrence.1 = (f32[4,512,640]{2,1,0:T(8,128)}, f32[4,512,640]{2,1,0:T(8,128)}, f32[4,512,640]{2,1,0:T(8,128)}, f32[4,512,640]{2,1,0:T(8,128)}, f32[4,512,640]{2,1,0:T(8,128)}, /*index=5*/f32[4,8,640]{2,1,0:T(8,128)}) custom-call(f32[4,512,640]{2,1,0:T(8,128)} %bitcast.304, f32[4,8,640]{2,1,0:T(8,128)} %slice.1371.halo_ref, f32[4,520,4]{2,1,0:T(8,128)} %copy.87.mask_ref, ...), custom_call_target="tpu_custom_call" | custom-call | flops 10000000000 | tf_op jit(solution)/shard_map/recurrence/pallas_call | solution.py:323
  338.7 25.9 %collective-permute-done.15 = bf16[928,1024]{1,0:T(8,128)(2,1)S(1)} collective-permute-done((bf16[928,1024]{1,0:T(8,128)(2,1)S(1)}, bf16[928,1024]{1,0:T(8,128)(2,1)S(1)}, u32[]{:S(2)}, u32[]{:S(2)}) %collective-permute-start.15) | collective-permute-done | bytes 1900576 | tf_op jit(solution)/shard_map/ppermute | solution.py:489
  412.5 45.0 %collective-permute-done.24 = bf16[512,2048]{1,0:T(8,128)(2,1)S(1)} collective-permute-done((bf16[512,2048]{1,0:T(8,128)(2,1)S(1)}, bf16[512,2048]{1,0:T(8,128)(2,1)S(1)}, u32[]{:S(2)}, u32[]{:S(2)}) %collective-permute-start.24) | collective-permute-done | bytes 2097184 | tf_op jit(solution)/shard_map/ppermute | solution.py:481
  483.5 19.4 %mlp.2 = (f32[1024,1536]{1,0:T(8,128)}, f32[1024,1536]{1,0:T(8,128)}, bf16[1024,1536]{1,0:T(8,128)(2,1)}) custom-call(s32[1]{0:T(128)} %constant.418.clone.1._, bf16[1024,2048]{1,0:T(8,128)(2,1)} %constant_dynamic-update-slice_fusion.8.refs_0_.refs_2_, bf16[1536,2048]{1,0:T(8,128)(2,1)} %get-tuple-element.756.refs_1_.refs_2_, ...), custom_call_target="tpu_custom_call" | custom-call | flops 4737096192 | tf_op jit(solution)/shard_map/mlp/pallas_call | solution.py:392
  503.0 30.5 %collective-permute-done.30 = bf16[512,512]{1,0:T(8,128)(2,1)S(1)} collective-permute-done((bf16[512,512]{1,0:T(8,128)(2,1)}, bf16[512,512]{1,0:T(8,128)(2,1)S(1)}, u32[]{:S(2)}, u32[]{:S(2)}) %collective-permute-start.30) | collective-permute-done | bytes 524320 | tf_op jit(solution)/shard_map/ppermute | solution.py:489
  553.0 19.5 %mlp.3 = (f32[1024,1536]{1,0:T(8,128)}, f32[1024,1536]{1,0:T(8,128)}, bf16[1024,1536]{1,0:T(8,128)(2,1)}) custom-call(s32[1]{0:T(128)} %constant.418.clone.1._, bf16[1024,2048]{1,0:T(8,128)(2,1)} %constant_dynamic-update-slice_fusion.10.refs_0_.refs_3_, bf16[1536,2048]{1,0:T(8,128)(2,1)} %get-tuple-element.756.refs_1_.refs_2_, ...), custom_call_target="tpu_custom_call" | custom-call | flops 4737096192 | tf_op jit(solution)/shard_map/mlp/pallas_call | solution.py:392
  600.7 11.6 gradient.12
  612.3 11.7 gradient.13
  623.9 16.5 %mlp_back.2 = (bf16[1024,1536]{1,0:T(8,128)(2,1)}, bf16[1024,1536]{1,0:T(8,128)(2,1)}) custom-call(s32[1]{0:T(128)} %constant.418.clone.1._, bf16[1024,2048]{1,0:T(8,128)(2,1)} %constant_dynamic-update-slice_fusion.12.refs_0_.refs_3_, bf16[1536,2048]{1,0:T(8,128)(2,1)} %slice_dynamic-update-slice_fusion.refs_1_, f32[1024,1536]{1,0:T(8,128)} %get-tuple-element.712.refs_2_, ...), custom_call_target="tpu_custom_call" | custom-call | flops 2368548096 | tf_op jit(solution)/shard_map/mlp_back/pallas_call | solution.py:392
  640.4 19.3 %product.11 = (bf16[512,2048]{1,0:T(8,128)(2,1)}, bf16[512,2048]{1,0:T(8,128)(2,1)}) custom-call(s32[1]{0:T(128)} %constant.418.clone.1._, bf16[1024,1536]{1,0:T(8,128)(2,1)} %get-tuple-element.754.refs_0_.refs_1_, bf16[1024,1536]{1,0:T(8,128)(2,1)} %get-tuple-element.805.refs_1_, bf16[1536,2048]{1,0:T(8,128)(2,1)} %get-tuple-element.756.refs_1_.refs_2_, ...), custom_call_target="tpu_custom_call" | custom-call | flops 4737096192 | tf_op jit(solution)/shard_map/product/pallas_call | solution.py:392
  668.4 16.4 %mlp_back.3 = (bf16[1024,1536]{1,0:T(8,128)(2,1)}, bf16[1024,1536]{1,0:T(8,128)(2,1)}) custom-call(s32[1]{0:T(128)} %constant.418.clone.1._, bf16[1024,2048]{1,0:T(8,128)(2,1)} %pad_maximum_fusion.1.refs_2_.refs_0_, bf16[1536,2048]{1,0:T(8,128)(2,1)} %slice_dynamic-update-slice_fusion.refs_1_, f32[1024,1536]{1,0:T(8,128)} %get-tuple-element.750.refs_2_, ...), custom_call_target="tpu_custom_call" | custom-call | flops 2368548096 | tf_op jit(solution)/shard_map/mlp_back/pallas_call | solution.py:392
  684.8 11.6 gradient.14
  696.5 11.6 gradient.15
  708.1 18.7 %product.10 = (bf16[512,2048]{1,0:T(8,128)(2,1)}, bf16[512,2048]{1,0:T(8,128)(2,1)}) custom-call(s32[1]{0:T(128)} %constant.418.clone.1._, bf16[1024,1536]{1,0:T(8,128)(2,1)} %get-tuple-element.752.refs_0_, bf16[1024,1536]{1,0:T(8,128)(2,1)} %get-tuple-element.804.refs_1_.refs_0_, bf16[1536,2048]{1,0:T(8,128)(2,1)} %get-tuple-element.756.refs_1_.refs_2_, ...), custom_call_target="tpu_custom_call" | custom-call | flops 4737096192 | tf_op jit(solution)/shard_map/product/pallas_call | solution.py:392
  742.6 11.6 gradient.16
  754.2 11.6 gradient.17
  765.8 11.7 product.12
  777.5 11.7 product.13
  789.2 11.9 collective-permute-done.44
  835.9 19.7 %adjoint.1 = (f32[4,512,640]{2,1,0:T(8,128)}, f32[4,512,640]{2,1,0:T(8,128)}, bf16[4,512,640]{2,1,0:T(8,128)(2,1)}, f32[4,8,640]{2,1,0:T(8,128)}) custom-call(f32[4,512,640]{2,1,0:T(8,128)} %bitcast.306, f32[4,512,640]{2,1,0:T(8,128)} %bitcast.250, f32[4,512,640]{2,1,0:T(8,128)} %get-tuple-element.912.state_ref, f32[4,512,640]{2,1,0:T(8,128)} %get-tuple-element.913.ga_ref, ...), custom_call_target="tpu_custom_call" | custom-call | flops 6000000000 | tf_op jit(solution)/shard_map/adjoint/pallas_call | solution.py:323
  855.6 17.0 %collective-permute-done.47 = bf16[512,2048]{1,0:T(8,128)(2,1)} collective-permute-done((bf16[512,2048]{1,0:T(8,128)(2,1)}, bf16[512,2048]{1,0:T(8,128)(2,1)}, u32[]{:S(2)}, u32[]{:S(2)}) %collective-permute-start.47) | collective-permute-done | bytes 2097184 | tf_op jit(solution)/shard_map/ppermute | solution.py:481
  951.5 57.0 %recurrence_back.1 = (bf16[4,512,640]{2,1,0:T(8,128)(2,1)}, f32[4,8,640]{2,1,0:T(8,128)}, f32[4,8,640]{2,1,0:T(8,128)}, f32[640,640]{1,0:T(8,128)}, f32[640,640]{1,0:T(8,128)}, /*index=5*/f32[8,8,640]{2,1,0:T(8,128)}) custom-call(f32[4,512,640]{2,1,0:T(8,128)} %get-tuple-element.910.lam_ref, f32[4,512,640]{2,1,0:T(8,128)} %get-tuple-element.911.q_ref, ...), custom_call_target="tpu_custom_call" | custom-call | flops 16000000000 | tf_op jit(solution)/shard_map/recurrence_back/pallas_call | solution.py:323
  1098.4 11.6 product.14
  1110.0 11.7 product.15
  1121.7 12.8 collective-permute-done.62
  1162.9 30.0 %collective-permute-done.65 = bf16[512,2048]{1,0:T(8,128)(2,1)} collective-permute-done((bf16[512,2048]{1,0:T(8,128)(2,1)}, bf16[512,2048]{1,0:T(8,128)(2,1)}, u32[]{:S(2)}, u32[]{:S(2)}) %collective-permute-start.65) | collective-permute-done | bytes 2097184 | tf_op jit(solution)/shard_map/ppermute | solution.py:481
  1229.4 31.5 %collective-permute-done.71 = bf16[2,1664,256]{2,1,0:T(8,128)(2,1)S(1)} collective-permute-done((bf16[2,1664,256]{2,1,0:T(8,128)(2,1)S(1)}, bf16[2,1664,256]{2,1,0:T(8,128)(2,1)S(1)}, u32[]{:S(2)}, u32[]{:S(2)}) %collective-permute-start.71) | collective-permute-done | bytes 1703968 | tf_op jit(solution)/shard_map/ppermute | solution.py:481
  (720 shorter events, 631.9 us)
Async XLA Ops:
  83.5 69.3 %collective-permute-start.9 = (bf16[1280,1024]{1,0:T(8,128)(2,1)}, bf16[1280,1024]{1,0:T(8,128)(2,1)}, u32[]{:S(2)}, u32[]{:S(2)}) collective-permute-start(bf16[1280,1024]{1,0:T(8,128)(2,1)} %slice.1357), channel_id=1, source_target_pairs={{0,16},{4,20},{8,24},{12,28},{16,0},{20,4},{24,8},{28,12},{1,17},{... | collective-permute-start | bytes 7864328 | tf_op jit(solution)/shard_map/ppermute | solution.py:484
  87.3 65.6 %collective-permute-start.5 = (bf16[544,2048]{1,0:T(8,128)(2,1)}, bf16[544,2048]{1,0:T(8,128)(2,1)}, u32[]{:S(2)}, u32[]{:S(2)}) collective-permute-start(bf16[544,2048]{1,0:T(8,128)(2,1)} %pad_maximum_fusion.5), channel_id=1, source_target_pairs={{0,8},{4,12},{8,0},{12,4},{16,24},{20,28},{24,16},{28,20},{1,9},{5... | collective-permute-start | bytes 6684680 | tf_op jit(solution)/shard_map/ppermute | solution.py:481
  89.3 62.0 %collective-permute-start.7 = (bf16[352,1024]{1,0:T(8,128)(2,1)}, bf16[352,1024]{1,0:T(8,128)(2,1)}, u32[]{:S(2)}, u32[]{:S(2)}) collective-permute-start(bf16[352,1024]{1,0:T(8,128)(2,1)} %slice.1356), channel_id=1, source_target_pairs={{0,2},{1,3},{2,0},{3,1},{4,6},{5,7},{6,4},{7,5},{8,10},{9,11},{10,... | collective-permute-start | bytes 2162696 | tf_op jit(solution)/shard_map/ppermute | solution.py:489
  91.1 61.7 %collective-permute-start.8 = (bf16[352,1024]{1,0:T(8,128)(2,1)}, bf16[352,1024]{1,0:T(8,128)(2,1)}, u32[]{:S(2)}, u32[]{:S(2)}) collective-permute-start(bf16[352,1024]{1,0:T(8,128)(2,1)} %slice.1356), channel_id=1, source_target_pairs={{0,3},{1,0},{2,1},{3,2},{4,7},{5,4},{6,5},{7,6},{8,11},{9,8},{10,9... | collective-permute-start | bytes 2162696 | tf_op jit(solution)/shard_map/ppermute | solution.py:489
  180.1 49.1 %collective-permute-start.13 = (bf16[1056,1024]{1,0:T(8,128)(2,1)S(1)}, bf16[1056,1024]{1,0:T(8,128)(2,1)S(1)}, u32[]{:S(2)}, u32[]{:S(2)}) collective-permute-start(bf16[1056,1024]{1,0:T(8,128)(2,1)S(1)} %pad_maximum_fusion.6), channel_id=1, source_target_pairs={{0,16},{4,20},{8,24},{12,28},{16,0},{20,4},{24,8},{28,12},{1,17},{... | collective-permute-start | bytes 6488072 | tf_op jit(solution)/shard_map/ppermute | solution.py:484
  238.7 82.2 %collective-permute-start.14 = (bf16[1312,1024]{1,0:T(8,128)(2,1)}, bf16[1312,1024]{1,0:T(8,128)(2,1)}, u32[]{:S(2)}, u32[]{:S(2)}) collective-permute-start(bf16[1312,1024]{1,0:T(8,128)(2,1)} %constant_dynamic-update-slice_fusion.6), channel_id=1, source_target_pairs={{0,1},{1,2},{2,3},{3,0},{4,5},{5,6},{6,7},{7,4},{8,9},{9,10},{10,1... | collective-permute-start | bytes 8060936 | tf_op jit(solution)/shard_map/ppermute | solution.py:489
  241.4 123.4 %collective-permute-start.16 = (bf16[1312,1024]{1,0:T(8,128)(2,1)}, bf16[1312,1024]{1,0:T(8,128)(2,1)}, u32[]{:S(2)}, u32[]{:S(2)}) collective-permute-start(bf16[1312,1024]{1,0:T(8,128)(2,1)} %constant_dynamic-update-slice_fusion.6), channel_id=1, source_target_pairs={{0,16},{4,20},{8,24},{12,28},{16,0},{20,4},{24,8},{28,12},{1,17},{... | collective-permute-start | bytes 8060936 | tf_op jit(solution)/shard_map/ppermute | solution.py:484
  410.7 53.0 %collective-permute-start.26 = (bf16[1152,1024]{1,0:T(8,128)(2,1)S(1)}, bf16[1152,1024]{1,0:T(8,128)(2,1)S(1)}, u32[]{:S(2)}, u32[]{:S(2)}) collective-permute-start(bf16[1152,1024]{1,0:T(8,128)(2,1)S(1)} %pad_maximum_fusion.4), channel_id=1, source_target_pairs={{0,16},{4,20},{8,24},{12,28},{16,0},{20,4},{24,8},{28,12},{1,17},{... | collective-permute-start | bytes 7077896 | tf_op jit(solution)/shard_map/ppermute | solution.py:484
  411.9 50.4 %collective-permute-start.22 = (bf16[384,1024]{1,0:T(8,128)(2,1)S(1)}, bf16[384,1024]{1,0:T(8,128)(2,1)S(1)}, u32[]{:S(2)}, u32[]{:S(2)}) collective-permute-start(bf16[384,1024]{1,0:T(8,128)(2,1)S(1)} %slice.1368), channel_id=1, source_target_pairs={{0,1},{1,2},{2,3},{3,0},{4,5},{5,6},{6,7},{7,4},{8,9},{9,10},{10,1... | collective-permute-start | bytes 2359304 | tf_op jit(solution)/shard_map/ppermute | solution.py:489
  465.1 73.0 %collective-permute-start.28 = (bf16[512,2048]{1,0:T(8,128)(2,1)S(1)}, bf16[512,2048]{1,0:T(8,128)(2,1)}, u32[]{:S(2)}, u32[]{:S(2)}) collective-permute-start(bf16[512,2048]{1,0:T(8,128)(2,1)S(1)} %get-tuple-element.645), channel_id=1, source_target_pairs={{0,8},{4,12},{8,0},{12,4},{16,24},{20,28},{24,16},{28,20},{1,9},{5... | collective-permute-start | bytes 6291464 | tf_op jit(solution)/shard_map/ppermute | solution.py:481
  470.5 67.7 %collective-permute-start.29 = (bf16[1280,512]{1,0:T(8,128)(2,1)}, bf16[1280,512]{1,0:T(8,128)(2,1)}, u32[]{:S(2)}, u32[]{:S(2)}) collective-permute-start(bf16[1280,512]{1,0:T(8,128)(2,1)} %pad_maximum_fusion.17), channel_id=1, source_target_pairs={{0,1},{1,2},{2,3},{3,0},{4,5},{5,6},{6,7},{7,4},{8,9},{9,10},{10,1... | collective-permute-start | bytes 3932168 | tf_op jit(solution)/shard_map/ppermute | solution.py:489
  471.0 62.4 %collective-permute-start.30 = (bf16[512,512]{1,0:T(8,128)(2,1)}, bf16[512,512]{1,0:T(8,128)(2,1)S(1)}, u32[]{:S(2)}, u32[]{:S(2)}) collective-permute-start(bf16[512,512]{1,0:T(8,128)(2,1)} %get-tuple-element.1172), channel_id=1, source_target_pairs={{0,2},{1,3},{2,0},{3,1},{4,6},{5,7},{6,4},{7,5},{8,10},{9,11},{10,... | collective-permute-start | bytes 1572872 | tf_op jit(solution)/shard_map/ppermute | solution.py:489
  476.1 62.1 %collective-permute-start.31 = (bf16[512,512]{1,0:T(8,128)(2,1)}, bf16[512,512]{1,0:T(8,128)(2,1)}, u32[]{:S(2)}, u32[]{:S(2)}) collective-permute-start(bf16[512,512]{1,0:T(8,128)(2,1)} %get-tuple-element.1171), channel_id=1, source_target_pairs={{0,3},{1,0},{2,1},{3,2},{4,7},{5,4},{6,5},{7,6},{8,11},{9,8},{10,9... | collective-permute-start | bytes 1572872 | tf_op jit(solution)/shard_map/ppermute | solution.py:489
  541.4 47.7 %collective-permute-start.33 = (bf16[512,2048]{1,0:T(8,128)(2,1)S(1)}, bf16[512,2048]{1,0:T(8,128)(2,1)}, u32[]{:S(2)}, u32[]{:S(2)}) collective-permute-start(bf16[512,2048]{1,0:T(8,128)(2,1)S(1)} %constant_dynamic-update-slice_fusion.25), channel_id=1, source_target_pairs={{0,8},{4,12},{8,0},{12,4},{16,24},{20,28},{24,16},{28,20},{1,9},{5... | collective-permute-start | bytes 6291464 | tf_op jit(solution)/shard_map/ppermute | solution.py:481
  660.2 70.2 %collective-permute-start.39 = (bf16[1536,1024]{1,0:T(8,128)(2,1)S(1)}, bf16[1536,1024]{1,0:T(8,128)(2,1)}, u32[]{:S(2)}, u32[]{:S(2)}) collective-permute-start(bf16[1536,1024]{1,0:T(8,128)(2,1)S(1)} %copy-done.28), channel_id=1, source_target_pairs={{0,16},{4,20},{8,24},{12,28},{16,0},{20,4},{24,8},{28,12},{1,17},{... | collective-permute-start | bytes 9437192 | tf_op jit(solution)/shard_map/ppermute | solution.py:484
  667.8 58.9 %collective-permute-start.38 = (bf16[512,2048]{1,0:T(8,128)(2,1)}, bf16[512,2048]{1,0:T(8,128)(2,1)}, u32[]{:S(2)}, u32[]{:S(2)}) collective-permute-start(bf16[512,2048]{1,0:T(8,128)(2,1)} %add_convert_fusion.3), channel_id=1, source_target_pairs={{0,8},{4,12},{8,0},{12,4},{16,24},{20,28},{24,16},{28,20},{1,9},{5... | collective-permute-start | bytes 6291464 | tf_op jit(solution)/shard_map/ppermute | solution.py:481
  730.3 70.8 %collective-permute-start.44 = (bf16[1536,1024]{1,0:T(8,128)(2,1)}, bf16[1536,1024]{1,0:T(8,128)(2,1)}, u32[]{:S(2)}, u32[]{:S(2)}) collective-permute-start(bf16[1536,1024]{1,0:T(8,128)(2,1)} %gradient.15), channel_id=1, source_target_pairs={{0,16},{4,20},{8,24},{12,28},{16,0},{20,4},{24,8},{28,12},{1,17},{... | collective-permute-start | bytes 9437192 | tf_op jit(solution)/shard_map/ppermute | solution.py:484
  740.1 61.0 %collective-permute-start.41 = (bf16[512,2048]{1,0:T(8,128)(2,1)S(1)}, bf16[512,2048]{1,0:T(8,128)(2,1)}, u32[]{:S(2)}, u32[]{:S(2)}) collective-permute-start(bf16[512,2048]{1,0:T(8,128)(2,1)S(1)} %get-tuple-element.833), channel_id=1, source_target_pairs={{0,8},{4,12},{8,0},{12,4},{16,24},{20,28},{24,16},{28,20},{1,9},{5... | collective-permute-start | bytes 6291464 | tf_op jit(solution)/shard_map/ppermute | solution.py:481
  740.8 60.4 %collective-permute-start.42 = (bf16[512,2048]{1,0:T(8,128)(2,1)S(1)}, bf16[512,2048]{1,0:T(8,128)(2,1)}, u32[]{:S(2)}, u32[]{:S(2)}) collective-permute-start(bf16[512,2048]{1,0:T(8,128)(2,1)S(1)} %get-tuple-element.833), channel_id=1, source_target_pairs={{0,4},{4,0},{8,12},{12,8},{16,20},{20,16},{24,28},{28,24},{1,5},{5... | collective-permute-start | bytes 6291464 | tf_op jit(solution)/shard_map/ppermute | solution.py:481
  812.7 66.8 %collective-permute-start.48 = (bf16[768,1024]{1,0:T(8,128)(2,1)}, bf16[768,1024]{1,0:T(8,128)(2,1)}, u32[]{:S(2)}, u32[]{:S(2)}) collective-permute-start(bf16[768,1024]{1,0:T(8,128)(2,1)} %pad_maximum_fusion.12), channel_id=1, source_target_pairs={{0,1},{1,2},{2,3},{3,0},{4,5},{5,6},{6,7},{7,4},{8,9},{9,10},{10,1... | collective-permute-start | bytes 4718600 | tf_op jit(solution)/shard_map/ppermute | solution.py:489
  812.7 70.3 %collective-permute-start.49 = (bf16[1536,1024]{1,0:T(8,128)(2,1)}, bf16[1536,1024]{1,0:T(8,128)(2,1)}, u32[]{:S(2)}, u32[]{:S(2)}) collective-permute-start(bf16[1536,1024]{1,0:T(8,128)(2,1)} %gradient.17), channel_id=1, source_target_pairs={{0,16},{4,20},{8,24},{12,28},{16,0},{20,4},{24,8},{28,12},{1,17},{... | collective-permute-start | bytes 9437192 | tf_op jit(solution)/shard_map/ppermute | solution.py:484
  934.8 90.9 %collective-permute-start.55 = (bf16[1280,1024]{1,0:T(8,128)(2,1)}, bf16[1280,1024]{1,0:T(8,128)(2,1)}, u32[]{:S(2)}, u32[]{:S(2)}) collective-permute-start(bf16[1280,1024]{1,0:T(8,128)(2,1)} %pad_maximum_fusion.3), channel_id=1, source_target_pairs={{0,16},{4,20},{8,24},{12,28},{16,0},{20,4},{24,8},{28,12},{1,17},{... | collective-permute-start | bytes 7864328 | tf_op jit(solution)/shard_map/ppermute | solution.py:484
  941.3 84.4 %collective-permute-start.54 = (bf16[768,1024]{1,0:T(8,128)(2,1)}, bf16[768,1024]{1,0:T(8,128)(2,1)}, u32[]{:S(2)}, u32[]{:S(2)}) collective-permute-start(bf16[768,1024]{1,0:T(8,128)(2,1)} %pad_maximum_fusion.14), channel_id=1, source_target_pairs={{0,1},{1,2},{2,3},{3,0},{4,5},{5,6},{6,7},{7,4},{8,9},{9,10},{10,1... | collective-permute-start | bytes 4718600 | tf_op jit(solution)/shard_map/ppermute | solution.py:489
  945.0 65.7 %collective-permute-start.56 = (bf16[512,512]{1,0:T(8,128)(2,1)}, bf16[512,512]{1,0:T(8,128)(2,1)}, u32[]{:S(2)}, u32[]{:S(2)}) collective-permute-start(bf16[512,512]{1,0:T(8,128)(2,1)} %get-tuple-element.1169), channel_id=1, source_target_pairs={{0,1},{1,2},{2,3},{3,0},{4,5},{5,6},{6,7},{7,4},{8,9},{9,10},{10,1... | collective-permute-start | bytes 1572872 | tf_op jit(solution)/shard_map/ppermute | solution.py:489
  945.2 75.7 %collective-permute-start.57 = (bf16[512,512]{1,0:T(8,128)(2,1)}, bf16[512,512]{1,0:T(8,128)(2,1)}, u32[]{:S(2)}, u32[]{:S(2)}) collective-permute-start(bf16[512,512]{1,0:T(8,128)(2,1)} %get-tuple-element.1168), channel_id=1, source_target_pairs={{0,2},{1,3},{2,0},{3,1},{4,6},{5,7},{6,4},{7,5},{8,10},{9,11},{10,... | collective-permute-start | bytes 1572872 | tf_op jit(solution)/shard_map/ppermute | solution.py:489
  949.6 76.1 %collective-permute-start.58 = (bf16[512,512]{1,0:T(8,128)(2,1)}, bf16[512,512]{1,0:T(8,128)(2,1)}, u32[]{:S(2)}, u32[]{:S(2)}) collective-permute-start(bf16[512,512]{1,0:T(8,128)(2,1)} %get-tuple-element.1167), channel_id=1, source_target_pairs={{0,3},{1,0},{2,1},{3,2},{4,7},{5,4},{6,5},{7,6},{8,11},{9,8},{10,9... | collective-permute-start | bytes 1572872 | tf_op jit(solution)/shard_map/ppermute | solution.py:489
  1053.5 68.2 %collective-permute-start.61 = (bf16[320,1024]{1,0:T(8,128)(2,1)}, bf16[320,1024]{1,0:T(8,128)(2,1)}, u32[]{:S(2)}, u32[]{:S(2)}) collective-permute-start(bf16[320,1024]{1,0:T(8,128)(2,1)} %pad_maximum_fusion.21), channel_id=1, source_target_pairs={{0,3},{1,0},{2,1},{3,2},{4,7},{5,4},{6,5},{7,6},{8,11},{9,8},{10,9... | collective-permute-start | bytes 1966088 | tf_op jit(solution)/shard_map/ppermute | solution.py:489
  1071.0 63.6 %collective-permute-start.60 = (bf16[768,1024]{1,0:T(8,128)(2,1)S(1)}, bf16[768,1024]{1,0:T(8,128)(2,1)S(1)}, u32[]{:S(2)}, u32[]{:S(2)}) collective-permute-start(bf16[768,1024]{1,0:T(8,128)(2,1)S(1)} %pad_maximum_fusion.15), channel_id=1, source_target_pairs={{0,16},{4,20},{8,24},{12,28},{16,0},{20,4},{24,8},{28,12},{1,17},{... | collective-permute-start | bytes 4718600 | tf_op jit(solution)/shard_map/ppermute | solution.py:484
  1073.2 61.3 %collective-permute-start.63 = (bf16[704,1024]{1,0:T(8,128)(2,1)}, bf16[704,1024]{1,0:T(8,128)(2,1)}, u32[]{:S(2)}, u32[]{:S(2)}) collective-permute-start(bf16[704,1024]{1,0:T(8,128)(2,1)} %pad_maximum_fusion.16), channel_id=1, source_target_pairs={{0,1},{1,2},{2,3},{3,0},{4,5},{5,6},{6,7},{7,4},{8,9},{9,10},{10,1... | collective-permute-start | bytes 4325384 | tf_op jit(solution)/shard_map/ppermute | solution.py:489
  1076.5 58.0 %collective-permute-start.62 = (bf16[320,1024]{1,0:T(8,128)(2,1)}, bf16[320,1024]{1,0:T(8,128)(2,1)}, u32[]{:S(2)}, u32[]{:S(2)}) collective-permute-start(bf16[320,1024]{1,0:T(8,128)(2,1)} %pad_maximum_fusion.22), channel_id=1, source_target_pairs={{0,2},{1,3},{2,0},{3,1},{4,6},{5,7},{6,4},{7,5},{8,10},{9,11},{10,... | collective-permute-start | bytes 1966088 | tf_op jit(solution)/shard_map/ppermute | solution.py:489
  1144.9 48.0 %collective-permute-start.65 = (bf16[512,2048]{1,0:T(8,128)(2,1)}, bf16[512,2048]{1,0:T(8,128)(2,1)}, u32[]{:S(2)}, u32[]{:S(2)}) collective-permute-start(bf16[512,2048]{1,0:T(8,128)(2,1)} %add_convert_fusion), channel_id=1, source_target_pairs={{0,8},{4,12},{8,0},{12,4},{16,24},{20,28},{24,16},{28,20},{1,9},{5... | collective-permute-start | bytes 6291464 | tf_op jit(solution)/shard_map/ppermute | solution.py:481
  1152.9 53.7 %collective-permute-start.69 = (bf16[576,1024]{1,0:T(8,128)(2,1)}, bf16[576,1024]{1,0:T(8,128)(2,1)}, u32[]{:S(2)}, u32[]{:S(2)}) collective-permute-start(bf16[576,1024]{1,0:T(8,128)(2,1)} %pad_maximum_fusion.18), channel_id=1, source_target_pairs={{0,1},{1,2},{2,3},{3,0},{4,5},{5,6},{6,7},{7,4},{8,9},{9,10},{10,1... | collective-permute-start | bytes 3538952 | tf_op jit(solution)/shard_map/ppermute | solution.py:489
  (142 other events, 2560.5 us)

commit v4 on v3

--- a/solution.py
+++ b/solution.py
@@ -11,7 +11,6 @@
 epsilon = 1e-06
 BF = jnp.bfloat16
 F32 = jnp.float32
-ROWS = 64
 HALO = 8
 
 
@@ -85,15 +84,16 @@
     ext_ref,
 ):
     length, width = rnn_ref.shape[1:]
+    block_rows = min(256, length)
     ext_ref[0:HALO, :] = halo_ref[0]
     ext_ref[HALO:, :] = rnn_ref[0]
-    row8 = lax.broadcasted_iota(jnp.int32, (ROWS, 1), 0) % 8
+    row8 = lax.broadcasted_iota(jnp.int32, (block_rows, 1), 0) % 8
 
     def block(i, carry):
         h_in, p_in = carry
-        r0 = pl.multiple_of(i * ROWS, ROWS)
-        masks = mask_ref[0, pl.ds(r0, ROWS), :]
-        terms = conv_terms(ext_ref[pl.ds(r0, ROWS + HALO), :], masks, ROWS)
+        r0 = pl.multiple_of(i * block_rows, block_rows)
+        masks = mask_ref[0, pl.ds(r0, block_rows), :]
+        terms = conv_terms(ext_ref[pl.ds(r0, block_rows + HALO), :], masks, block_rows)
         mixed = vec_ref[0:1, :] + conv_ref[0:1, :] * terms[0]
         for k in range(1, 4):
             mixed = mixed + conv_ref[k : k + 1, :] * terms[k]
@@ -110,14 +110,14 @@
         a = jnp.exp(log_a) * (1.0 - begins)
         scale = jnp.sqrt(one_minus_exp(log_a)) * (1.0 - begins) + begins
         b = mixed * gate_x * scale
-        mixed_ref[0, pl.ds(r0, ROWS), :] = mixed
-        ga_ref[0, pl.ds(r0, ROWS), :] = gate_a
-        gx_ref[0, pl.ds(r0, ROWS), :] = gate_x
+        mixed_ref[0, pl.ds(r0, block_rows), :] = mixed
+        ga_ref[0, pl.ds(r0, block_rows), :] = gate_a
+        gx_ref[0, pl.ds(r0, block_rows), :] = gate_x
         for d in (1, 2, 4):
             valid = row8 >= d
             b = jnp.where(valid, a * pltpu.roll(b, d, axis=0) + b, b)
             a = jnp.where(valid, a * pltpu.roll(a, d, axis=0), a)
-        for g in range(ROWS // 8):
+        for g in range(block_rows // 8):
             rows = slice(8 * g, 8 * g + 8)
             h = b[rows] + a[rows] * h_in
             p = a[rows] * p_in
@@ -129,7 +129,7 @@
 
     h_end, p_end = lax.fori_loop(
         0,
-        length // ROWS,
+        length // block_rows,
         block,
         (jnp.zeros((1, width), F32), jnp.ones((1, width), F32)),
     )
@@ -150,26 +150,27 @@
     end_ref,
 ):
     length, width = dmix_ref.shape[1:]
-    row = lax.broadcasted_iota(jnp.int32, (ROWS, 1), 0)
+    block_rows = min(64, length)
+    row = lax.broadcasted_iota(jnp.int32, (block_rows, 1), 0)
     row8 = row % 8
-    blocks = length // ROWS
+    blocks = length // block_rows
 
     def block(i, carry):
         lam_in, q_in, a_next = carry
-        r0 = pl.multiple_of((blocks - 1 - i) * ROWS, ROWS)
-        here = pl.ds(r0, ROWS)
+        r0 = pl.multiple_of((blocks - 1 - i) * block_rows, block_rows)
+        here = pl.ds(r0, block_rows)
         begins = mask_ref[0, here, :][:, 3:4]
         d_mixer = dmix_ref[0, here, :]
         gelu, slope = gelu_parts(gate_ref[0, here, :])
         dgi_ref[0, here, :] = (d_mixer * state_ref[0, here, :] * slope).astype(BF)
         b = d_mixer * gelu
         a = jnp.exp(ga_ref[0, here, :] * vec_ref[3:4, :]) * (1.0 - begins)
-        c = jnp.where(row == ROWS - 1, a_next, pltpu.roll(a, ROWS - 1, axis=0))
+        c = jnp.where(row == block_rows - 1, a_next, pltpu.roll(a, block_rows - 1, axis=0))
         for d in (1, 2, 4):
             valid = row8 < 8 - d
-            b = jnp.where(valid, c * pltpu.roll(b, ROWS - d, axis=0) + b, b)
-            c = jnp.where(valid, c * pltpu.roll(c, ROWS - d, axis=0), c)
-        for g in reversed(range(ROWS // 8)):
+            b = jnp.where(valid, c * pltpu.roll(b, block_rows - d, axis=0) + b, b)
+            c = jnp.where(valid, c * pltpu.roll(c, block_rows - d, axis=0), c)
+        for g in reversed(range(block_rows // 8)):
             rows = slice(8 * g, 8 * g + 8)
             lam = b[rows] + c[rows] * lam_in
             q = c[rows] * q_in
@@ -220,6 +221,7 @@
     dm_ref,
 ):
     length, width = lam_ref.shape[1:]
+    block_rows = min(256, length)
     first = pl.program_id(0) == 0
 
     @pl.when(first)
@@ -235,13 +237,13 @@
     dm_ref[length:, :] = jnp.zeros((HALO, width), F32)
 
     def block(i, carry):
-        r0 = pl.multiple_of(i * ROWS, ROWS)
-        here = pl.ds(r0, ROWS)
+        r0 = pl.multiple_of(i * block_rows, block_rows)
+        here = pl.ds(r0, block_rows)
         masks = mask_ref[0, here, :]
         begins = masks[:, 3:4]
         lam = lam_ref[0, here, :] + q_ref[0, here, :] * edge_ref[0, 4:5, :]
-        before = pltpu.roll(prev_ref[pl.ds(r0, ROWS + HALO), :], 1, axis=0)[
-            HALO : HALO + ROWS
+        before = pltpu.roll(prev_ref[pl.ds(r0, block_rows + HALO), :], 1, axis=0)[
+            HALO : HALO + block_rows
         ]
         gate_a = ga_ref[0, here, :]
         gate_x = gx_ref[0, here, :]
@@ -268,32 +270,32 @@
         dm_ref[here, :] = d_mixed
         wag_ref[...] += dot_tn(mb, pa)
         wxg_ref[...] += dot_tn(mb, px)
-        terms = conv_terms(ext_ref[pl.ds(r0, ROWS + HALO), :], masks, ROWS)
+        terms = conv_terms(ext_ref[pl.ds(r0, block_rows + HALO), :], masks, block_rows)
         sums = [d_mixed * term for term in terms]
         sums += [d_mixed, d_pre_a, d_pre_x, log_gate]
         for n, value in enumerate(sums):
             vg_ref[n] += fold8(value)
         return carry
 
-    lax.fori_loop(0, length // ROWS, block, 0)
+    lax.fori_loop(0, length // block_rows, block, 0)
 
     def shift(i, carry):
-        r0 = pl.multiple_of(i * ROWS, ROWS)
-        ext = dm_ref[pl.ds(r0, ROWS + HALO), :]
-        masks = mask_ref[0, pl.ds(r0, ROWS + HALO), :]
-        total = conv_ref[0:1, :] * ext[0:ROWS]
+        r0 = pl.multiple_of(i * block_rows, block_rows)
+        ext = dm_ref[pl.ds(r0, block_rows + HALO), :]
+        masks = mask_ref[0, pl.ds(r0, block_rows + HALO), :]
+        total = conv_ref[0:1, :] * ext[0:block_rows]
         for k in range(1, 4):
-            moved = pltpu.roll(ext * masks[:, k - 1 : k], ROWS + HALO - k, axis=0)
-            total = total + conv_ref[k : k + 1, :] * moved[0:ROWS]
-        drnn_ref[0, pl.ds(r0, ROWS), :] = total.astype(BF)
-
-        @pl.when(i == length // ROWS - 1)
+            moved = pltpu.roll(ext * masks[:, k - 1 : k], block_rows + HALO - k, axis=0)
+            total = total + conv_ref[k : k + 1, :] * moved[0:block_rows]
+        drnn_ref[0, pl.ds(r0, block_rows), :] = total.astype(BF)
+
+        @pl.when(i == length // block_rows - 1)
         def _():
-            tail_ref[0] = total[ROWS - HALO :]
+            tail_ref[0] = total[block_rows - HALO :]
 
         return carry
 
-    lax.fori_loop(0, length // ROWS, shift, 0)
+    lax.fori_loop(0, length // block_rows, shift, 0)
     head_ref[0] = dm_ref[0:HALO, :]
 
 
@@ -310,7 +312,7 @@
 
 
 def cost(time):
-    return pl.CostEstimate(flops=int(time * 2.5e8), bytes_accessed=0, transcendentals=0)
+    return pl.CostEstimate(flops=int(time * 1.0e8), bytes_accessed=0, transcendentals=0)
 
 
 NT = (((1,), (1,)), ((), ()))
@@ -690,7 +692,6 @@
             w_output.reshape(t, cz, Dl),
             w_gate.T.reshape(t, fz, Dl),
             w_up.T.reshape(t, fz, Dl),
-            w_down.reshape(t, fz, Dl),
         ],
         axis=1,
     )
@@ -702,17 +703,24 @@
     rows_a = 2 * cz + gate_rows
     v.z_in = chunk_pieces(inputs, 16)
     v.blocks = exchange(lambda k: pick(mine_all, k))
-    v.cotangent = cotangent
+    v.cotangent, v.w_down = cotangent, w_down
+    v.zeros = [jnp.zeros((M * size, D), BF) for size in (cz, cz, gate_rows, cz, fz, fz, fz)]
     v.barrier()
 
     block = from_group(v.take("blocks"))
     block_a = block[:rows_a]
     block_b = block[rows_a : rows_a + cz]
-    block_g = block[rows_a + cz : rows_a + cz + 2 * fz]
-    v.d = [block[rows_a + cz + 2 * fz :]]
+    block_g = block[rows_a + cz :]
     v.ring_a = [block_a] + [zshift(block_a, k) for k in range(1, M)]
     v.b, v.g = [block_b], [block_g]
     v.y_first = to_groups(block_a, block_b, block_g)
+    zeros = v.take("zeros")
+    v.full_a = [fill_own(f, p, 0) for f, p in zip(zeros[:3], mixer_parts(block_a))]
+    v.full_b = fill_own(zeros[3], block_b, 0)
+    v.full_g = [
+        fill_own(f, p, 0) for f, p in zip(zeros[4:6], (block_g[:fz], block_g[fz:]))
+    ]
+    v.full_d = zeros[6]
     resets = jnp.pad(reset_mask.astype(BF), (0, 16 * D - L)).reshape(16, D)
     v.own_in = jnp.concatenate([joined(v.take("z_in")), resets])
     v.far_in = far(v.own_in)
@@ -721,20 +729,16 @@
     y_next = to_groups(*v.ring_a[1:])
     ring_bg = ring_next(v.b[-1], v.g[-1])
     y_a, y_b, y_g = by_block(v.take("y_first"))
-    full_a = [
-        jnp.zeros((M * size, D), BF) for size in (cz, cz, gate_rows)
-    ]
-    for k, mine in enumerate(v.take("ring_a")):
-        full_a = [fill_own(f, p, k) for f, p in zip(full_a, mixer_parts(mine))]
-    v.full_a = fill_mixer_far(full_a, y_a, 0)
-    v.full_b = fill_far(fill_own(jnp.zeros((C, D), BF), v.b[0], 0), y_b, 0)
-    full_g = [jnp.zeros((FC, D), BF)] * 2
-    full_g = [fill_own(f, p, 0) for f, p in zip(full_g, (v.g[0][:fz], v.g[0][fz:]))]
+    v.d = exchange(lambda k: cut(v.w_down, k, fz, 0))
+    v.take("w_down")
+    v.full_a = fill_mixer_far(v.full_a, y_a, 0)
+    for k, mine in enumerate(v.take("ring_a")[1:], 1):
+        v.full_a = [fill_own(f, p, k) for f, p in zip(v.full_a, mixer_parts(mine))]
+    v.full_b = fill_far(v.full_b, y_b, 0)
     v.full_g = [
         fill_far(f, [y[n * fz : (n + 1) * fz] for y in y_g], 0)
-        for n, f in enumerate(full_g)
+        for n, f in enumerate(v.full_g)
     ]
-    v.full_d = fill_own(jnp.zeros((FC, D), BF), v.d[0], 0)
     v.take("b")
     v.take("g")
     v.ring_bg = ring_bg
@@ -768,16 +772,12 @@
                 v.full_g[n] = fill_far(v.full_g[n], [y[rows] for y in others], k)
 
     b_1, g_1 = v.take("ring_bg").parts()
-    v.y_1 = to_groups(b_1, g_1, v.d[0])
-    ring = ring_next(b_1, g_1, v.take("d")[0])
+    d_0 = from_group(v.take("d"))
+    v.full_d = fill_own(v.full_d, d_0, 0)
+    v.y_1 = to_groups(b_1, g_1, d_0)
+    v.ring = ring_next(b_1, g_1, d_0)
     v.full_b = fill_own(v.full_b, b_1, 1)
     fill_gate(1, own=g_1)
-    b_next, g_next, v.d = ring.parts()
-    v.b, v.g = [b_next], [g_next]
-    v.y_2 = to_groups(b_next, g_next)
-    while len(v.b) < M - 2:
-        b_next, g_next = ring_next(b_next, g_next).parts()
-        v.b, v.g = v.b + [b_next], v.g + [g_next]
     for k, others in enumerate(by_block(v.take("y_a")), 1):
         v.full_a = fill_mixer_far(v.full_a, others, k)
     w_in_t, w_br_t, rest = v.take("full_a")
@@ -828,6 +828,14 @@
     v.rnn = dot_nt(v.n1, v.w_in_t).reshape(shape)
     v.gin = dot_nt(v.n1, v.w_br_t).reshape(shape)
     v.halos = dot_nt(ahead, v.w_in_t).reshape(t, 16, C)[:, 16 - HALO :]
+    v.barrier()
+
+    b_next, g_next, v.d = v.take("ring").parts()
+    v.b, v.g = [b_next], [g_next]
+    v.y_2 = to_groups(b_next, g_next)
+    while len(v.b) < M - 2:
+        b_next, g_next = ring_next(b_next, g_next).parts()
+        v.b, v.g = v.b + [b_next], v.g + [g_next]
     v.fwd = seq_call(
         forward_kernel,
         [v.rnn, v.halos, v.masks],
@@ -912,7 +920,8 @@
     v.take("n2_far")
     v.barrier()
 
-    def summed(lefts, rights):
+    def summed(lefts, rights, groups=None):
+        groups = range(O) if groups is None else groups
         out = [
             products(
                 TN,
@@ -924,7 +933,7 @@
                 base=((o + r) % O) * half,
                 width=half,
             )[0]
-            for r in reversed(range(O))
+            for r in reversed(groups)
         ]
         return out[::-1]
 
@@ -949,26 +958,38 @@
         gate, up = v.d_mlp[p]
         return mixed_sum((gate, v.w_gate_t), (up, v.w_up_t))
 
+    out = [mixed_sum((m[2], v.w_dn)) for m in v.mlp]
+    got = joint(lambda b: tp(b, 1), [part[1] for part in out]).parts()
+    out_sum = out[0][0].astype(F32) + got[0].astype(F32)
+    if parts > 1:
+        there = out[1][0].astype(F32) + got[1].astype(F32)
+        out_sum = out_sum + tp(there.astype(BF), 2).astype(F32)
+    v.output = (v.take("resid_mid") + out_sum).astype(BF)
     v.grad_down = summed([m[2] for m in v.mlp], v.cot)
     v.d_mlp = [None] * parts
     v.d_mlp[last] = mlp_back(last)
     v.barrier()
 
     v.y_down = grad_y(v.take("grad_down"))
+    pieces = back_pieces(v.take("output"))
+    v.z_out = [zshift(piece, k) if k else piece for k, piece in enumerate(pieces)]
     v.dn2 = [None] * parts
     v.dn2[last] = mlp_back_in(last)
     v.dn2_sum = send_sum(v.dn2[last], last) if last else None
     for p in range(last):
         v.d_mlp[p] = mlp_back(p)
         v.dn2[p] = mlp_back_in(p)
-    v.grad_gate = summed([d[0] for d in v.d_mlp], v.n2)
-    v.hidden = [m[2] for m in v.take("mlp")]
+    v.grad_gate = summed([d[0] for d in v.d_mlp], v.n2, range(1, O))
+    v.take("mlp")
     v.cot_own = v.take("cot")[0][:Lc]
     v.barrier()
 
     (v.y_down,) = y_parts(v.y_down)
+    v.output = back_joined(v.take("z_out"))
     v.ring = ring_step((v.y_down, 1, None))
-    v.y_gate = grad_y(v.take("grad_gate"))
+    v.y_gate = grad_y(
+        summed([d[0] for d in v.d_mlp], v.n2, range(1)) + v.take("grad_gate")
+    )
     dn2_sum = v.take("dn2_sum")
     for p in reversed(range(last if last else 1)):
         part = send_sum(v.dn2[p], p)
@@ -988,7 +1009,6 @@
     v.grad_up = summed([d[1] for d in v.d_mlp], v.n2)
     v.take("n2")
     v.take("d_mlp")
-    v.out = [mixed_sum((h, v.w_dn)) for h in v.take("hidden")]
     v.barrier()
 
     (v.y_gate,) = y_parts(v.y_gate)
@@ -1000,14 +1020,6 @@
         slots_of += [v.far_branch, tp(v.far_branch, 1)]
     v.take("far_branch")
     v.d_branch = jnp.concatenate(slots_of)
-    out = v.take("out")
-    got = joint(lambda b: tp(b, 1), [part[1] for part in out]).parts()
-    out_sum = out[0][0].astype(F32) + got[0].astype(F32)
-    if parts > 1:
-        there = out[1][0].astype(F32) + got[1].astype(F32)
-        out_sum = out_sum + tp(there.astype(BF), 2).astype(F32)
-    v.output = (v.take("resid_mid") + out_sum).astype(BF)
-
     v.adjoint = seq_call(
         adjoint_kernel,
         [
@@ -1023,10 +1035,10 @@
         "adjoint",
         24,
     )
-    v.barrier()
-
-    r_down, r_gate = v.ring.parts()
-    v.ring = ring_step((v.y_down, 3, r_down), (v.y_gate, 2, r_gate))
+    v.d_gin = v.adjoint[2].reshape(t * Lc, C)
+    v.grad_branch = summed([v.d_gin], [v.n1])
+    v.barrier()
+
     (v.y_up,) = y_parts(v.y_up)
     v.edges = jnp.concatenate(
         [
@@ -1036,49 +1048,42 @@
         1,
     )
     v.grad_output = summed([v.take("mixer")], [v.take("d_branch")])
-    v.d_gin = v.adjoint[2].reshape(t * Lc, C)
-    v.grad_branch = summed([v.d_gin], [v.n1])
-    v.barrier()
-
-    v.r_down, r_gate = v.ring.parts()
-    v.ring = ring_step((v.y_gate, 3, r_gate), (v.y_up, 1, None))
+    v.barrier()
+
+    r_down, r_gate = v.ring.parts()
+    v.ring = ring_step((v.y_down, 3, r_down), (v.y_gate, 2, r_gate), (v.y_up, 1, None))
     v.y_mixer = grad_y(v.take("grad_output"), v.take("grad_branch"))
-    pieces = back_pieces(v.take("output"))
-    v.z_out = [zshift(piece, k) if k else piece for k, piece in enumerate(pieces)]
     mixed, gate_a, gate_x = v.fwd
     lam, prod, _, _ = v.adjoint
-    v.d_rnn, v.heads, v.tails, v.grad_wa, v.grad_wx, v.grad_vec = seq_call(
-        backward_kernel,
-        [
-            lam,
-            prod,
-            v.state,
-            gate_a,
-            gate_x,
-            mixed,
-            v.rnn,
-            v.halos,
-            v.masks,
-            v.edges,
-        ],
-        [v.conv_w, v.vec, v.wa, v.wx],
-        [
-            (shape, BF, True),
-            ((t, HALO, C), F32, True),
-            ((t, HALO, C), F32, True),
-            ((C, C), F32, False),
-            ((C, C), F32, False),
-            ((8, 8, C), F32, False),
-        ],
-        [pltpu.VMEM((Lc + HALO, C), F32)] * 3,
-        "recurrence_back",
-        64,
-    )
+
+    def run_back(rows, time):
+        tokens = [lam, prod, v.state, gate_a, gate_x, mixed, v.rnn]
+        if rows < Lc:
+            tokens = [array[:, :rows] for array in tokens]
+        return seq_call(
+            backward_kernel,
+            tokens + [v.halos, v.masks[:, : rows + HALO], v.edges],
+            [v.conv_w, v.vec, v.wa, v.wx],
+            [
+                ((t, rows, C), BF, True),
+                ((t, HALO, C), F32, True),
+                ((t, HALO, C), F32, True),
+                ((C, C), F32, False),
+                ((C, C), F32, False),
+                ((8, 8, C), F32, False),
+            ],
+            [pltpu.VMEM((rows + HALO, C), F32)] * 3,
+            "recurrence_back",
+            time,
+        )
+
+    v.following = zline(run_back(2 * HALO, 4)[1], -1)
+    v.d_rnn, _, v.tails, v.grad_wa, v.grad_wx, v.grad_vec = run_back(Lc, 40)
     for name in ("adjoint", "fwd", "state", "rnn", "halos", "edges"):
         v.take(name)
     v.barrier()
 
-    following = zline(v.take("heads"), -1)
+    following = v.take("following")
     fix = [jnp.zeros((t, 1, C), F32)] * HALO
     for k in range(1, 4):
         for n in range(k):
@@ -1088,11 +1093,9 @@
             )
     tail = (v.take("tails") + jnp.concatenate(fix, axis=1)).astype(BF)
     v.d_rnn = put(v.d_rnn, tail, 0, Lc - HALO, 0).reshape(t * Lc, C)
-    z_down = ring_end(v.take("y_down"), v.take("r_down"))
-    r_gate, r_up = v.take("ring").parts()
-    z_gate = ring_end(v.take("y_gate"), r_gate)
+    v.r_down, r_gate, r_up = v.take("ring").parts()
     y_output, y_branch = y_parts(v.take("y_mixer"))
-    rings = ring_sends((v.y_up, 2, r_up))
+    rings = ring_sends((v.y_gate, 3, r_gate), (v.y_up, 2, r_up))
 
     def direct(rings, *grads):
         got = []
@@ -1102,7 +1105,6 @@
         return got
 
     v.z_mixer = direct(rings, y_output, y_branch)
-    v.output = back_joined(v.take("z_out"))
     gates_grad = jnp.stack(
         [
             jnp.stack(
@@ -1131,12 +1133,13 @@
         mixed_sum(((v.d_rnn, p, parts), v.w_in_t), ((v.d_gin, p, parts), v.w_br_t))
         for p in range(parts)
     ]
-    v.z_down, v.z_gate = z_down, z_gate
     for name in ("d_rnn", "d_gin", "w_in_t", "w_br_t", "wa", "wx", "masks", "vec"):
         v.take(name)
     v.barrier()
 
-    r_up = v.z_mixer[M - 1].parts()[2]
+    v.z_down = ring_end(v.take("y_down"), v.take("r_down"))
+    r_gate, r_up = v.z_mixer[M - 1].parts()[2:]
+    v.z_gate = ring_end(v.take("y_gate"), r_gate)
     v.z_in = direct(ring_sends((v.y_up, 3, r_up)), *y_parts(v.take("y_in")))
     dn1_sum = None
     for p in reversed(range(parts)):

time: 1320 us -> 1250 us (0.947)
  waiting for transfers between devices: 428 us -> 368 us
  Pallas kernels: 399 us -> 381 us
  local copies, waits for them, and re-layouts: 199 us -> 217 us
    ppermute x29 -> x28, waiting for transfers between devices: 188 us -> 132 us  [zshift(): return lax.ppermute(value, 'mp', [(i, (i + k) % M) for i in range(M)])]
    unnamed x228 -> x234, local copies, waits for them, and re-layouts: 36.7 us -> 56.6 us
    pallas_call x3 -> x4, Pallas kernels: 114 us -> 95.5 us  [seq_call(): pl.pallas_call(kernel, grid=(count,), in_specs=block_specs([(a.shape, Tru...]
    ppermute x29 -> x28, starting transfers between devices: 46.5 us -> 34.5 us  [zshift(): return lax.ppermute(value, 'mp', [(i, (i + k) % M) for i in range(M)])]
    dynamic_update_slice x72 -> x74, local copies, waits for them, and re-layouts: 58 us -> 50 us  [put(): return lax.dynamic_update_slice(array, piece, starts)]
    ppermute x30 -> x32, waiting for transfers between devices: 181 us -> 177 us  [tp(): return lax.ppermute(value, 'dp', [(i, i ^ j) for i in range(DP)])]
  transfers between devices with their start and end apart: 78 -> 79, of which waited for: 35 -> 33; matrix products, arithmetic and copies ran while one was open for 24% -> 26% of each run, Pallas kernels for 25% -> 27%
where the time goes in v4:
time: 1250 us; the launch traced here: 1230 us
  Pallas kernels  381 us (30%)
  waiting for transfers between devices  368 us (29%)
  local copies, waits for them, and re-layouts  217 us (17%)
  other arithmetic  140 us (11%)
  starting transfers between devices  80.7 us (6%)
  matrix products  35.3 us (3%)
    pallas_call x24, Pallas kernels, products(): pl.pallas_call(kernel, grid_spec=pltpu.PrefetchScalarGridSpec(num_scalar_...  286 us
    ppermute x32, waiting for transfers between devices, tp(): return lax.ppermute(value, 'dp', [(i, i ^ j) for i in range(DP)])  177 us
    ppermute x28, waiting for transfers between devices, zshift(): return lax.ppermute(value, 'mp', [(i, (i + k) % M) for i in range(M)])  132 us
    pallas_call x4, Pallas kernels, seq_call(): pl.pallas_call(kernel, grid=(count,), in_specs=block_specs([(a.shape, Tru...  95.5 us
    ppermute x12, waiting for transfers between devices, oshift(): lax.ppermute(value, 'dp', [(i, (i // t + r) % O * t + i % t) for i in ran...  58.7 us
    unnamed x234, local copies, waits for them, and re-layouts  56.6 us
    dynamic_update_slice x74, local copies, waits for them, and re-layouts, put(): return lax.dynamic_update_slice(array, piece, starts)  50 us
    dot_general x4, matrix products, dot_nt(): lax.dot_general(left, right, (((1,), (1,)), ((), ())), preferred_element_...  35.3 us
  transfers between devices with their start and end apart: 79, of which 33 were waited for; matrix products, arithmetic and copies ran while one was open for 26% of the time, Pallas kernels for 27%

profile of v4, /device:TPU:8, one launch (start us, length us, event | category | flops | bytes accessed | tf_op | source)
XLA Modules:
  0.0 1225.3 jit_solution(12633436980336146229)
XLA Ops:
  29.8 23.6 %collective-permute-done.1 = bf16[2,1280,256]{2,1,0:T(8,128)(2,1)} collective-permute-done((bf16[2,1280,256]{2,1,0:T(8,128)(2,1)}, bf16[2,1280,256]{2,1,0:T(8,128)(2,1)}, u32[]{:S(2)}, u32[]{:S(2)}) %collective-permute-start.1) | collective-permute-done | bytes 1310752 | tf_op jit(solution)/shard_map/ppermute | solution.py:483
  62.9 10.5 collective-permute-done.3
  109.0 33.7 %collective-permute-done.7 = bf16[352,1024]{1,0:T(8,128)(2,1)S(1)} collective-permute-done((bf16[352,1024]{1,0:T(8,128)(2,1)S(1)}, bf16[352,1024]{1,0:T(8,128)(2,1)S(1)}, u32[]{:S(2)}, u32[]{:S(2)}) %collective-permute-start.7) | collective-permute-done | bytes 720928 | tf_op jit(solution)/shard_map/ppermute | solution.py:491
  178.8 12.9 %collective-permute-done.14 = bf16[928,1024]{1,0:T(8,128)(2,1)S(1)} collective-permute-done((bf16[928,1024]{1,0:T(8,128)(2,1)S(1)}, bf16[928,1024]{1,0:T(8,128)(2,1)S(1)}, u32[]{:S(2)}, u32[]{:S(2)}) %collective-permute-start.14) | collective-permute-done | bytes 1900576 | tf_op jit(solution)/shard_map/ppermute | solution.py:491
  225.9 11.5 fusion.135
  250.0 10.6 fusion.134
  273.4 31.3 %recurrence.1 = (f32[4,512,640]{2,1,0:T(8,128)}, f32[4,512,640]{2,1,0:T(8,128)}, f32[4,512,640]{2,1,0:T(8,128)}, f32[4,512,640]{2,1,0:T(8,128)}, f32[4,512,640]{2,1,0:T(8,128)}, /*index=5*/f32[4,8,640]{2,1,0:T(8,128)}) custom-call(f32[4,512,640]{2,1,0:T(8,128)} %bitcast.264, f32[4,8,640]{2,1,0:T(8,128)} %slice.1422.halo_ref, f32[4,520,4]{2,1,0:T(8,128)} %copy.89.mask_ref, ...), custom_call_target="tpu_custom_call" | custom-call | flops 4000000000 | tf_op jit(solution)/shard_map/recurrence/pallas_call | solution.py:325
  361.0 44.8 %collective-permute-done.26 = bf16[512,2048]{1,0:T(8,128)(2,1)S(1)} collective-permute-done((bf16[512,2048]{1,0:T(8,128)(2,1)S(1)}, bf16[512,2048]{1,0:T(8,128)(2,1)S(1)}, u32[]{:S(2)}, u32[]{:S(2)}) %collective-permute-start.26) | collective-permute-done | bytes 2097184 | tf_op jit(solution)/shard_map/ppermute | solution.py:483
  431.2 19.5 %mlp.2 = (f32[1024,1536]{1,0:T(8,128)}, f32[1024,1536]{1,0:T(8,128)}, bf16[1024,1536]{1,0:T(8,128)(2,1)}) custom-call(s32[1]{0:T(128)} %constant.420.clone.1._, bf16[1024,2048]{1,0:T(8,128)(2,1)} %constant_dynamic-update-slice_fusion.5.refs_0_.refs_2_, bf16[1536,2048]{1,0:T(8,128)(2,1)} %get-tuple-element.832.refs_1_.refs_2_, ...), custom_call_target="tpu_custom_call" | custom-call | flops 1894838528 | tf_op jit(solution)/shard_map/mlp/pallas_call | solution.py:394
  450.7 29.5 %collective-permute-done.32 = bf16[512,512]{1,0:T(8,128)(2,1)S(1)} collective-permute-done((bf16[512,512]{1,0:T(8,128)(2,1)}, bf16[512,512]{1,0:T(8,128)(2,1)S(1)}, u32[]{:S(2)}, u32[]{:S(2)}) %collective-permute-start.32) | collective-permute-done | bytes 524320 | tf_op jit(solution)/shard_map/ppermute | solution.py:491
  497.5 19.5 %mlp.3 = (f32[1024,1536]{1,0:T(8,128)}, f32[1024,1536]{1,0:T(8,128)}, bf16[1024,1536]{1,0:T(8,128)(2,1)}) custom-call(s32[1]{0:T(128)} %constant.420.clone.1._, bf16[1024,2048]{1,0:T(8,128)(2,1)} %constant_dynamic-update-slice_fusion.7.refs_0_.refs_3_, bf16[1536,2048]{1,0:T(8,128)(2,1)} %get-tuple-element.832.refs_1_.refs_2_, ...), custom_call_target="tpu_custom_call" | custom-call | flops 1894838528 | tf_op jit(solution)/shard_map/mlp/pallas_call | solution.py:394
  540.7 11.7 product.10
  552.5 11.8 product.11
  586.6 11.6 gradient.13
  598.2 11.8 gradient.12
  610.0 16.4 %mlp_back.2 = (bf16[1024,1536]{1,0:T(8,128)(2,1)}, bf16[1024,1536]{1,0:T(8,128)(2,1)}) custom-call(s32[1]{0:T(128)} %constant.420.clone.1._, bf16[1024,2048]{1,0:T(8,128)(2,1)} %constant_dynamic-update-slice_fusion.9.refs_0_.refs_3_, bf16[1536,2048]{1,0:T(8,128)(2,1)} %slice_dynamic-update-slice_fusion.2.refs_1_, f32[1024,1536]{1,0:T(8,128)} %get-tuple-element.784.refs_2_, ...), custom_call_target="tpu_custom_call" | custom-call | flops 947419264 | tf_op jit(solution)/shard_map/mlp_back/pallas_call | solution.py:394
  632.2 18.7 %product.13 = (bf16[512,2048]{1,0:T(8,128)(2,1)}, bf16[512,2048]{1,0:T(8,128)(2,1)}) custom-call(s32[1]{0:T(128)} %constant.420.clone.1._, bf16[1024,1536]{1,0:T(8,128)(2,1)} %get-tuple-element.902.refs_0_.refs_1_, bf16[1024,1536]{1,0:T(8,128)(2,1)} %get-tuple-element.879.refs_1_, bf16[1536,2048]{1,0:T(8,128)(2,1)} %get-tuple-element.832.refs_1_.refs_2_, ...), custom_call_target="tpu_custom_call" | custom-call | flops 1894838528 | tf_op jit(solution)/shard_map/product/pallas_call | solution.py:394
  663.5 16.7 %mlp_back.3 = (bf16[1024,1536]{1,0:T(8,128)(2,1)}, bf16[1024,1536]{1,0:T(8,128)(2,1)}) custom-call(s32[1]{0:T(128)} %constant.420.clone.1._, bf16[1024,2048]{1,0:T(8,128)(2,1)} %pad_maximum_fusion.1.refs_2_.refs_0_, bf16[1536,2048]{1,0:T(8,128)(2,1)} %slice_dynamic-update-slice_fusion.2.refs_1_, f32[1024,1536]{1,0:T(8,128)} %get-tuple-element.826.refs_2_, ...), custom_call_target="tpu_custom_call" | custom-call | flops 947419264 | tf_op jit(solution)/shard_map/mlp_back/pallas_call | solution.py:394
  680.2 11.7 gradient.14
  691.9 18.7 %product.12 = (bf16[512,2048]{1,0:T(8,128)(2,1)}, bf16[512,2048]{1,0:T(8,128)(2,1)}) custom-call(s32[1]{0:T(128)} %constant.420.clone.1._, bf16[1024,1536]{1,0:T(8,128)(2,1)} %get-tuple-element.901.refs_0_, bf16[1024,1536]{1,0:T(8,128)(2,1)} %get-tuple-element.878.refs_1_.refs_0_, bf16[1536,2048]{1,0:T(8,128)(2,1)} %get-tuple-element.832.refs_1_.refs_2_, ...), custom_call_target="tpu_custom_call" | custom-call | flops 1894838528 | tf_op jit(solution)/shard_map/product/pallas_call | solution.py:394
  736.4 12.1 gradient.16
  748.5 11.6 gradient.15
  760.1 11.7 gradient.17
  773.3 19.3 %collective-permute-done.51 = bf16[1536,1024]{1,0:T(8,128)(2,1)} collective-permute-done((bf16[1536,1024]{1,0:T(8,128)(2,1)}, bf16[1536,1024]{1,0:T(8,128)(2,1)}, u32[]{:S(2)}, u32[]{:S(2)}) %collective-permute-start.51) | collective-permute-done | bytes 3145760 | tf_op jit(solution)/shard_map/ppermute | solution.py:486
  806.7 12.3 %fusion.136 = f32[2048,640]{1,0:T(8,128)} fusion(bf16[2048,2048]{1,0:T(8,128)(2,1)S(1)} %constant_dynamic-update-slice_fusion.11.refs_1_, bf16[640,2048]{1,0:T(8,128)(2,1)} %constant_dynamic-update-slice_fusion.41.refs_1_), kind=kOutput, calls=%fused_computation.481 | convolution fusion | flops 5368709120 | bytes 16252928 | tf_op jit(solution)/shard_map/dot_general | solution.py:18
  819.0 19.8 %adjoint.1 = (f32[4,512,640]{2,1,0:T(8,128)}, f32[4,512,640]{2,1,0:T(8,128)}, bf16[4,512,640]{2,1,0:T(8,128)(2,1)}, f32[4,8,640]{2,1,0:T(8,128)}) custom-call(f32[4,512,640]{2,1,0:T(8,128)} %bitcast.267, f32[4,512,640]{2,1,0:T(8,128)} %bitcast.259, f32[4,512,640]{2,1,0:T(8,128)} %get-tuple-element.981.state_ref, f32[4,512,640]{2,1,0:T(8,128)} %get-tuple-element.982.ga_ref, ...), custom_call_target="tpu_custom_call" | custom-call | flops 2400000000 | tf_op jit(solution)/shard_map/adjoint/pallas_call | solution.py:325
  852.8 16.7 %collective-permute-done.54 = bf16[1536,1024]{1,0:T(8,128)(2,1)} collective-permute-done((bf16[1536,1024]{1,0:T(8,128)(2,1)}, bf16[1536,1024]{1,0:T(8,128)(2,1)}, u32[]{:S(2)}, u32[]{:S(2)}) %collective-permute-start.54) | collective-permute-done | bytes 3145760 | tf_op jit(solution)/shard_map/ppermute | solution.py:486
  927.1 36.2 %recurrence_back.2 = (bf16[4,512,640]{2,1,0:T(8,128)(2,1)}, f32[4,8,640]{2,1,0:T(8,128)}, f32[4,8,640]{2,1,0:T(8,128)}, f32[640,640]{1,0:T(8,128)}, f32[640,640]{1,0:T(8,128)}, /*index=5*/f32[8,8,640]{2,1,0:T(8,128)}) custom-call(f32[4,512,640]{2,1,0:T(8,128)} %get-tuple-element.979.lam_ref, f32[4,512,640]{2,1,0:T(8,128)} %get-tuple-element.980.q_ref, ...), custom_call_target="tpu_custom_call" | custom-call | flops 4000000000 | tf_op jit(solution)/shard_map/recurrence_back/pallas_call | solution.py:325
  1030.0 11.7 product.15
  1041.6 11.7 product.14
  1089.9 34.4 %collective-permute-done.66 = bf16[512,2048]{1,0:T(8,128)(2,1)} collective-permute-done((bf16[512,2048]{1,0:T(8,128)(2,1)}, bf16[512,2048]{1,0:T(8,128)(2,1)}, u32[]{:S(2)}, u32[]{:S(2)}) %collective-permute-start.66) | collective-permute-done | bytes 2097184 | tf_op jit(solution)/shard_map/ppermute | solution.py:483
  1156.9 29.6 %collective-permute-done.72 = bf16[2,1664,256]{2,1,0:T(8,128)(2,1)S(1)} collective-permute-done((bf16[2,1664,256]{2,1,0:T(8,128)(2,1)S(1)}, bf16[2,1664,256]{2,1,0:T(8,128)(2,1)S(1)}, u32[]{:S(2)}, u32[]{:S(2)}) %collective-permute-start.72) | collective-permute-done | bytes 1703968 | tf_op jit(solution)/shard_map/ppermute | solution.py:483
  (740 shorter events, 618.3 us)
Async XLA Ops:
  76.6 67.5 %collective-permute-start.9 = (bf16[1280,1024]{1,0:T(8,128)(2,1)S(1)}, bf16[1280,1024]{1,0:T(8,128)(2,1)}, u32[]{:S(2)}, u32[]{:S(2)}) collective-permute-start(bf16[1280,1024]{1,0:T(8,128)(2,1)S(1)} %constant_dynamic-update-slice_fusion.35), channel_id=1, source_target_pairs={{0,16},{4,20},{8,24},{12,28},{16,0},{20,4},{24,8},{28,12},{1,17},{... | collective-permute-start | bytes 7864328 | tf_op jit(solution)/shard_map/ppermute | solution.py:486
  80.4 63.7 %collective-permute-start.5 = (bf16[544,2048]{1,0:T(8,128)(2,1)}, bf16[544,2048]{1,0:T(8,128)(2,1)}, u32[]{:S(2)}, u32[]{:S(2)}) collective-permute-start(bf16[544,2048]{1,0:T(8,128)(2,1)} %pad_maximum_fusion.7), channel_id=1, source_target_pairs={{0,8},{4,12},{8,0},{12,4},{16,24},{20,28},{24,16},{28,20},{1,9},{5... | collective-permute-start | bytes 6684680 | tf_op jit(solution)/shard_map/ppermute | solution.py:483
  81.1 61.6 %collective-permute-start.7 = (bf16[352,1024]{1,0:T(8,128)(2,1)S(1)}, bf16[352,1024]{1,0:T(8,128)(2,1)S(1)}, u32[]{:S(2)}, u32[]{:S(2)}) collective-permute-start(bf16[352,1024]{1,0:T(8,128)(2,1)S(1)} %slice.1406), channel_id=1, source_target_pairs={{0,2},{1,3},{2,0},{3,1},{4,6},{5,7},{6,4},{7,5},{8,10},{9,11},{10,... | collective-permute-start | bytes 2162696 | tf_op jit(solution)/shard_map/ppermute | solution.py:491
  83.0 61.0 %collective-permute-start.8 = (bf16[352,1024]{1,0:T(8,128)(2,1)S(1)}, bf16[352,1024]{1,0:T(8,128)(2,1)S(1)}, u32[]{:S(2)}, u32[]{:S(2)}) collective-permute-start(bf16[352,1024]{1,0:T(8,128)(2,1)S(1)} %slice.1406), channel_id=1, source_target_pairs={{0,3},{1,0},{2,1},{3,2},{4,7},{5,4},{6,5},{7,6},{8,11},{9,8},{10,9... | collective-permute-start | bytes 2162696 | tf_op jit(solution)/shard_map/ppermute | solution.py:491
  146.8 49.5 %collective-permute-start.15 = (bf16[1056,1024]{1,0:T(8,128)(2,1)S(1)}, bf16[1056,1024]{1,0:T(8,128)(2,1)S(1)}, u32[]{:S(2)}, u32[]{:S(2)}) collective-permute-start(bf16[1056,1024]{1,0:T(8,128)(2,1)S(1)} %pad_maximum_fusion.9), channel_id=1, source_target_pairs={{0,16},{4,20},{8,24},{12,28},{16,0},{20,4},{24,8},{28,12},{1,17},{... | collective-permute-start | bytes 6488072 | tf_op jit(solution)/shard_map/ppermute | solution.py:486
  200.0 60.5 %collective-permute-start.16 = (bf16[1312,1024]{1,0:T(8,128)(2,1)}, bf16[1312,1024]{1,0:T(8,128)(2,1)}, u32[]{:S(2)}, u32[]{:S(2)}) collective-permute-start(bf16[1312,1024]{1,0:T(8,128)(2,1)} %pad_maximum_fusion.3), channel_id=1, source_target_pairs={{0,1},{1,2},{2,3},{3,0},{4,5},{5,6},{6,7},{7,4},{8,9},{9,10},{10,1... | collective-permute-start | bytes 8060936 | tf_op jit(solution)/shard_map/ppermute | solution.py:491
  200.2 60.3 %collective-permute-start.17 = (bf16[1312,1024]{1,0:T(8,128)(2,1)}, bf16[1312,1024]{1,0:T(8,128)(2,1)}, u32[]{:S(2)}, u32[]{:S(2)}) collective-permute-start(bf16[1312,1024]{1,0:T(8,128)(2,1)} %pad_maximum_fusion.3), channel_id=1, source_target_pairs={{0,16},{4,20},{8,24},{12,28},{16,0},{20,4},{24,8},{28,12},{1,17},{... | collective-permute-start | bytes 8060936 | tf_op jit(solution)/shard_map/ppermute | solution.py:486
  360.0 53.0 %collective-permute-start.28 = (bf16[1152,1024]{1,0:T(8,128)(2,1)S(1)}, bf16[1152,1024]{1,0:T(8,128)(2,1)S(1)}, u32[]{:S(2)}, u32[]{:S(2)}) collective-permute-start(bf16[1152,1024]{1,0:T(8,128)(2,1)S(1)} %pad_maximum_fusion.5), channel_id=1, source_target_pairs={{0,16},{4,20},{8,24},{12,28},{16,0},{20,4},{24,8},{28,12},{1,17},{... | collective-permute-start | bytes 7077896 | tf_op jit(solution)/shard_map/ppermute | solution.py:486
  361.0 49.7 %collective-permute-start.24 = (bf16[384,1024]{1,0:T(8,128)(2,1)S(1)}, bf16[384,1024]{1,0:T(8,128)(2,1)S(1)}, u32[]{:S(2)}, u32[]{:S(2)}) collective-permute-start(bf16[384,1024]{1,0:T(8,128)(2,1)S(1)} %slice.1165), channel_id=1, source_target_pairs={{0,1},{1,2},{2,3},{3,0},{4,5},{5,6},{6,7},{7,4},{8,9},{9,10},{10,1... | collective-permute-start | bytes 2359304 | tf_op jit(solution)/shard_map/ppermute | solution.py:491
  414.5 70.0 %collective-permute-start.30 = (bf16[512,2048]{1,0:T(8,128)(2,1)S(1)}, bf16[512,2048]{1,0:T(8,128)(2,1)}, u32[]{:S(2)}, u32[]{:S(2)}) collective-permute-start(bf16[512,2048]{1,0:T(8,128)(2,1)S(1)} %get-tuple-element.717), channel_id=1, source_target_pairs={{0,8},{4,12},{8,0},{12,4},{16,24},{20,28},{24,16},{28,20},{1,9},{5... | collective-permute-start | bytes 6291464 | tf_op jit(solution)/shard_map/ppermute | solution.py:483
  418.9 65.5 %collective-permute-start.31 = (bf16[1280,512]{1,0:T(8,128)(2,1)}, bf16[1280,512]{1,0:T(8,128)(2,1)}, u32[]{:S(2)}, u32[]{:S(2)}) collective-permute-start(bf16[1280,512]{1,0:T(8,128)(2,1)} %pad_maximum_fusion.17), channel_id=1, source_target_pairs={{0,1},{1,2},{2,3},{3,0},{4,5},{5,6},{6,7},{7,4},{8,9},{9,10},{10,1... | collective-permute-start | bytes 3932168 | tf_op jit(solution)/shard_map/ppermute | solution.py:491
  418.9 61.2 %collective-permute-start.32 = (bf16[512,512]{1,0:T(8,128)(2,1)}, bf16[512,512]{1,0:T(8,128)(2,1)S(1)}, u32[]{:S(2)}, u32[]{:S(2)}) collective-permute-start(bf16[512,512]{1,0:T(8,128)(2,1)} %get-tuple-element.1248), channel_id=1, source_target_pairs={{0,2},{1,3},{2,0},{3,1},{4,6},{5,7},{6,4},{7,5},{8,10},{9,11},{10,... | collective-permute-start | bytes 1572872 | tf_op jit(solution)/shard_map/ppermute | solution.py:491
  423.9 60.5 %collective-permute-start.33 = (bf16[512,512]{1,0:T(8,128)(2,1)}, bf16[512,512]{1,0:T(8,128)(2,1)}, u32[]{:S(2)}, u32[]{:S(2)}) collective-permute-start(bf16[512,512]{1,0:T(8,128)(2,1)} %get-tuple-element.1247), channel_id=1, source_target_pairs={{0,3},{1,0},{2,1},{3,2},{4,7},{5,4},{6,5},{7,6},{8,11},{9,8},{10,9... | collective-permute-start | bytes 1572872 | tf_op jit(solution)/shard_map/ppermute | solution.py:491
  578.8 47.8 %collective-permute-start.40 = (bf16[512,2048]{1,0:T(8,128)(2,1)S(1)}, bf16[512,2048]{1,0:T(8,128)(2,1)}, u32[]{:S(2)}, u32[]{:S(2)}) collective-permute-start(bf16[512,2048]{1,0:T(8,128)(2,1)S(1)} %add_convert_fusion.3), channel_id=1, source_target_pairs={{0,8},{4,12},{8,0},{12,4},{16,24},{20,28},{24,16},{28,20},{1,9},{5... | collective-permute-start | bytes 6291464 | tf_op jit(solution)/shard_map/ppermute | solution.py:483
  650.9 70.8 %collective-permute-start.43 = (bf16[1536,1024]{1,0:T(8,128)(2,1)}, bf16[1536,1024]{1,0:T(8,128)(2,1)}, u32[]{:S(2)}, u32[]{:S(2)}) collective-permute-start(bf16[1536,1024]{1,0:T(8,128)(2,1)} %gradient.13), channel_id=1, source_target_pairs={{0,16},{4,20},{8,24},{12,28},{16,0},{20,4},{24,8},{28,12},{1,17},{... | collective-permute-start | bytes 9437192 | tf_op jit(solution)/shard_map/ppermute | solution.py:486
  659.0 51.6 %collective-permute-start.42 = (bf16[512,2048]{1,0:T(8,128)(2,1)}, bf16[512,2048]{1,0:T(8,128)(2,1)}, u32[]{:S(2)}, u32[]{:S(2)}) collective-permute-start(bf16[512,2048]{1,0:T(8,128)(2,1)} %add_convert_fusion.1), channel_id=1, source_target_pairs={{0,8},{4,12},{8,0},{12,4},{16,24},{20,28},{24,16},{28,20},{1,9},{5... | collective-permute-start | bytes 6291464 | tf_op jit(solution)/shard_map/ppermute | solution.py:483
  661.5 51.3 %collective-permute-start.44 = (bf16[512,512]{1,0:T(8,128)(2,1)S(1)}, bf16[512,512]{1,0:T(8,128)(2,1)S(1)}, u32[]{:S(2)}, u32[]{:S(2)}) collective-permute-start(bf16[512,512]{1,0:T(8,128)(2,1)S(1)} %get-tuple-element.1245), channel_id=1, source_target_pairs={{0,1},{1,2},{2,3},{3,0},{4,5},{5,6},{6,7},{7,4},{8,9},{9,10},{10,1... | collective-permute-start | bytes 1572872 | tf_op jit(solution)/shard_map/ppermute | solution.py:491
  661.5 51.4 %collective-permute-start.45 = (bf16[512,512]{1,0:T(8,128)(2,1)S(1)}, bf16[512,512]{1,0:T(8,128)(2,1)S(1)}, u32[]{:S(2)}, u32[]{:S(2)}) collective-permute-start(bf16[512,512]{1,0:T(8,128)(2,1)S(1)} %get-tuple-element.1244), channel_id=1, source_target_pairs={{0,2},{1,3},{2,0},{3,1},{4,6},{5,7},{6,4},{7,5},{8,10},{9,11},{10,... | collective-permute-start | bytes 1572872 | tf_op jit(solution)/shard_map/ppermute | solution.py:491
  661.5 51.4 %collective-permute-start.46 = (bf16[512,512]{1,0:T(8,128)(2,1)S(1)}, bf16[512,512]{1,0:T(8,128)(2,1)S(1)}, u32[]{:S(2)}, u32[]{:S(2)}) collective-permute-start(bf16[512,512]{1,0:T(8,128)(2,1)S(1)} %get-tuple-element.1243), channel_id=1, source_target_pairs={{0,3},{1,0},{2,1},{3,2},{4,7},{5,4},{6,5},{7,6},{8,11},{9,8},{10,9... | collective-permute-start | bytes 1572872 | tf_op jit(solution)/shard_map/ppermute | solution.py:491
  721.7 70.8 %collective-permute-start.51 = (bf16[1536,1024]{1,0:T(8,128)(2,1)}, bf16[1536,1024]{1,0:T(8,128)(2,1)}, u32[]{:S(2)}, u32[]{:S(2)}) collective-permute-start(bf16[1536,1024]{1,0:T(8,128)(2,1)} %gradient.14), channel_id=1, source_target_pairs={{0,16},{4,20},{8,24},{12,28},{16,0},{20,4},{24,8},{28,12},{1,17},{... | collective-permute-start | bytes 9437192 | tf_op jit(solution)/shard_map/ppermute | solution.py:486
  732.4 60.2 %collective-permute-start.48 = (bf16[512,2048]{1,0:T(8,128)(2,1)}, bf16[512,2048]{1,0:T(8,128)(2,1)}, u32[]{:S(2)}, u32[]{:S(2)}) collective-permute-start(bf16[512,2048]{1,0:T(8,128)(2,1)} %get-tuple-element.904), channel_id=1, source_target_pairs={{0,8},{4,12},{8,0},{12,4},{16,24},{20,28},{24,16},{28,20},{1,9},{5... | collective-permute-start | bytes 6291464 | tf_op jit(solution)/shard_map/ppermute | solution.py:483
  733.9 58.7 %collective-permute-start.49 = (bf16[512,2048]{1,0:T(8,128)(2,1)}, bf16[512,2048]{1,0:T(8,128)(2,1)}, u32[]{:S(2)}, u32[]{:S(2)}) collective-permute-start(bf16[512,2048]{1,0:T(8,128)(2,1)} %get-tuple-element.904), channel_id=1, source_target_pairs={{0,4},{4,0},{8,12},{12,8},{16,20},{20,16},{24,28},{28,24},{1,5},{5... | collective-permute-start | bytes 6291464 | tf_op jit(solution)/shard_map/ppermute | solution.py:483
  797.4 55.4 %collective-permute-start.53 = (bf16[768,1024]{1,0:T(8,128)(2,1)}, bf16[768,1024]{1,0:T(8,128)(2,1)}, u32[]{:S(2)}, u32[]{:S(2)}) collective-permute-start(bf16[768,1024]{1,0:T(8,128)(2,1)} %pad_maximum_fusion.13), channel_id=1, source_target_pairs={{0,1},{1,2},{2,3},{3,0},{4,5},{5,6},{6,7},{7,4},{8,9},{9,10},{10,1... | collective-permute-start | bytes 4718600 | tf_op jit(solution)/shard_map/ppermute | solution.py:491
  798.8 70.8 %collective-permute-start.54 = (bf16[1536,1024]{1,0:T(8,128)(2,1)}, bf16[1536,1024]{1,0:T(8,128)(2,1)}, u32[]{:S(2)}, u32[]{:S(2)}) collective-permute-start(bf16[1536,1024]{1,0:T(8,128)(2,1)} %gradient.16), channel_id=1, source_target_pairs={{0,16},{4,20},{8,24},{12,28},{16,0},{20,4},{24,8},{28,12},{1,17},{... | collective-permute-start | bytes 9437192 | tf_op jit(solution)/shard_map/ppermute | solution.py:486
  893.7 70.4 %collective-permute-start.60 = (bf16[1280,1024]{1,0:T(8,128)(2,1)}, bf16[1280,1024]{1,0:T(8,128)(2,1)}, u32[]{:S(2)}, u32[]{:S(2)}) collective-permute-start(bf16[1280,1024]{1,0:T(8,128)(2,1)} %pad_maximum_fusion.4), channel_id=1, source_target_pairs={{0,16},{4,20},{8,24},{12,28},{16,0},{20,4},{24,8},{28,12},{1,17},{... | collective-permute-start | bytes 7864328 | tf_op jit(solution)/shard_map/ppermute | solution.py:486
  901.1 63.0 %collective-permute-start.59 = (bf16[1152,1024]{1,0:T(8,128)(2,1)}, bf16[1152,1024]{1,0:T(8,128)(2,1)}, u32[]{:S(2)}, u32[]{:S(2)}) collective-permute-start(bf16[1152,1024]{1,0:T(8,128)(2,1)} %pad_maximum_fusion.6), channel_id=1, source_target_pairs={{0,1},{1,2},{2,3},{3,0},{4,5},{5,6},{6,7},{7,4},{8,9},{9,10},{10,1... | collective-permute-start | bytes 7077896 | tf_op jit(solution)/shard_map/ppermute | solution.py:491
  973.5 92.5 %collective-permute-start.64 = (bf16[1088,1024]{1,0:T(8,128)(2,1)}, bf16[1088,1024]{1,0:T(8,128)(2,1)}, u32[]{:S(2)}, u32[]{:S(2)}) collective-permute-start(bf16[1088,1024]{1,0:T(8,128)(2,1)} %pad_maximum_fusion.8), channel_id=1, source_target_pairs={{0,1},{1,2},{2,3},{3,0},{4,5},{5,6},{6,7},{7,4},{8,9},{9,10},{10,1... | collective-permute-start | bytes 6684680 | tf_op jit(solution)/shard_map/ppermute | solution.py:491
  1014.6 51.3 %collective-permute-start.61 = (bf16[768,1024]{1,0:T(8,128)(2,1)}, bf16[768,1024]{1,0:T(8,128)(2,1)}, u32[]{:S(2)}, u32[]{:S(2)}) collective-permute-start(bf16[768,1024]{1,0:T(8,128)(2,1)} %pad_maximum_fusion.14), channel_id=1, source_target_pairs={{0,16},{4,20},{8,24},{12,28},{16,0},{20,4},{24,8},{28,12},{1,17},{... | collective-permute-start | bytes 4718600 | tf_op jit(solution)/shard_map/ppermute | solution.py:486
  1076.3 48.0 %collective-permute-start.66 = (bf16[512,2048]{1,0:T(8,128)(2,1)}, bf16[512,2048]{1,0:T(8,128)(2,1)}, u32[]{:S(2)}, u32[]{:S(2)}) collective-permute-start(bf16[512,2048]{1,0:T(8,128)(2,1)} %add_convert_fusion), channel_id=1, source_target_pairs={{0,8},{4,12},{8,0},{12,4},{16,24},{20,28},{24,16},{28,20},{1,9},{5... | collective-permute-start | bytes 6291464 | tf_op jit(solution)/shard_map/ppermute | solution.py:483
  1084.1 52.8 %collective-permute-start.70 = (bf16[576,1024]{1,0:T(8,128)(2,1)S(1)}, bf16[576,1024]{1,0:T(8,128)(2,1)S(1)}, u32[]{:S(2)}, u32[]{:S(2)}) collective-permute-start(bf16[576,1024]{1,0:T(8,128)(2,1)S(1)} %pad_maximum_fusion.18), channel_id=1, source_target_pairs={{0,1},{1,2},{2,3},{3,0},{4,5},{5,6},{6,7},{7,4},{8,9},{9,10},{10,1... | collective-permute-start | bytes 3538952 | tf_op jit(solution)/shard_map/ppermute | solution.py:491
  1084.3 50.8 %collective-permute-start.69 = (bf16[192,1024]{1,0:T(8,128)(2,1)S(1)}, bf16[192,1024]{1,0:T(8,128)(2,1)S(1)}, u32[]{:S(2)}, u32[]{:S(2)}) collective-permute-start(bf16[192,1024]{1,0:T(8,128)(2,1)S(1)} %pad_maximum_fusion.31), channel_id=1, source_target_pairs={{0,2},{1,3},{2,0},{3,1},{4,6},{5,7},{6,4},{7,5},{8,10},{9,11},{10,... | collective-permute-start | bytes 1179656 | tf_op jit(solution)/shard_map/ppermute | solution.py:491
  1085.8 51.2 %collective-permute-start.68 = (bf16[192,1024]{1,0:T(8,128)(2,1)S(1)}, bf16[192,1024]{1,0:T(8,128)(2,1)S(1)}, u32[]{:S(2)}, u32[]{:S(2)}) collective-permute-start(bf16[192,1024]{1,0:T(8,128)(2,1)S(1)} %pad_maximum_fusion.30), channel_id=1, source_target_pairs={{0,3},{1,0},{2,1},{3,2},{4,7},{5,4},{6,5},{7,6},{8,11},{9,8},{10,9... | collective-permute-start | bytes 1179656 | tf_op jit(solution)/shard_map/ppermute | solution.py:491
  (148 other events, 2185.4 us)

commit v5 on v4

--- a/solution.py
+++ b/solution.py
@@ -519,7 +519,7 @@
     def pick(array, index, axis=0):
         return lax.dynamic_index_in_dim(array, index, axis, keepdims=False)
 
-    def chunk_pieces(value, ahead=0, rider=None):
+    def chunk_pieces(value, ahead=0, rider=None, which=range(M)):
         if ahead:
             value = jnp.concatenate([jnp.zeros((ahead, FH), value.dtype), value])
         pieces = [
@@ -528,11 +528,11 @@
         ]
         if rider is not None:
             pieces[1] = jnp.concatenate([pieces[1], rider])
-        return [zshift(piece, k) if k else piece for k, piece in enumerate(pieces)]
+        return {k: zshift(pieces[k], k) if k else pieces[k] for k in which}
 
     def joined(pieces):
         own = jnp.zeros((pieces[0].shape[0], D), pieces[0].dtype)
-        for k, piece in enumerate(pieces):
+        for k, piece in pieces.items():
             own = put(own, piece, 0, ((z - k) % M) * FH)
         return own
 
@@ -711,7 +711,9 @@
     block_a = block[:rows_a]
     block_b = block[rows_a : rows_a + cz]
     block_g = block[rows_a + cz :]
-    v.ring_a = [block_a] + [zshift(block_a, k) for k in range(1, M)]
+    v.ring_a = [block_a]
+    for _ in range(1, M):
+        v.ring_a.append(zshift(v.ring_a[-1], 1))
     v.b, v.g = [block_b], [block_g]
     v.y_first = to_groups(block_a, block_b, block_g)
     zeros = v.take("zeros")
@@ -872,8 +874,9 @@
     v.w_out = v.take("full_b")
     v.y_g = to_groups(*v.take("g")[1:], v.d)
     v.d = [v.d]
-    while len(v.d) < M - 2:
+    while len(v.d) < M - 3:
         v.d = v.d + ring_next(v.d[-1]).parts()
+    v.z_cot = chunk_pieces(v.cotangent, rider=folded(v.d[-1]), which=(0, 1, M - 1))
     rec_sum = None
     for p in reversed(range(parts)):
         part = send_sum(mixed_sum(((v.mixer, p, parts), v.w_out)), p)
@@ -888,9 +891,14 @@
         fill_gate(k, others=others)
     v.full_d = fill_far(v.full_d, got[-1], 1)
     v.w_gate_t, v.w_up_t = v.take("full_g")
+    v.d = v.d + [unfolded(v.z_cot[1][Lc:])]
+    v.z_cot[1] = v.z_cot[1][:Lc]
     for k, mine in enumerate(v.d[1:], 2):
         v.full_d = fill_own(v.full_d, mine, k)
-    v.z_cot = chunk_pieces(v.take("cotangent"), rider=folded(v.d[-1]))
+    v.d_last = ring_next(v.d[-1])
+    v.z_cot = {
+        **v.z_cot, **chunk_pieces(v.take("cotangent"), which=range(2, M - 1))
+    }
     v.n2_far = far(v.n2_own)
     v.n2 = [jnp.concatenate([v.n2_own, tp(v.n2_own, 1)])]
     v.take("n2_own")
@@ -908,8 +916,7 @@
     v.mlp = [mlp_forward(0)]
     v.barrier()
 
-    v.d = v.d[1:] + [unfolded(v.z_cot[1][Lc:])]
-    v.z_cot[1] = v.z_cot[1][:Lc]
+    v.d = v.d[1:] + v.take("d_last").parts()
     v.y_d = to_groups(*v.d)
     cot_own = joined(v.take("z_cot"))
     v.cot = [jnp.concatenate([cot_own, tp(cot_own, 1)])]
@@ -958,19 +965,18 @@
         gate, up = v.d_mlp[p]
         return mixed_sum((gate, v.w_gate_t), (up, v.w_up_t))
 
-    out = [mixed_sum((m[2], v.w_dn)) for m in v.mlp]
-    got = joint(lambda b: tp(b, 1), [part[1] for part in out]).parts()
-    out_sum = out[0][0].astype(F32) + got[0].astype(F32)
-    if parts > 1:
-        there = out[1][0].astype(F32) + got[1].astype(F32)
-        out_sum = out_sum + tp(there.astype(BF), 2).astype(F32)
+    out_sum = None
+    for p in reversed(range(parts)):
+        part = send_sum(mixed_sum((v.mlp[p][2], v.w_dn)), p)
+        out_sum = part if out_sum is None else out_sum + part
     v.output = (v.take("resid_mid") + out_sum).astype(BF)
-    v.grad_down = summed([m[2] for m in v.mlp], v.cot)
+    v.grad_down = summed([m[2] for m in v.mlp], v.cot, range(1, O))
     v.d_mlp = [None] * parts
     v.d_mlp[last] = mlp_back(last)
     v.barrier()
 
-    v.y_down = grad_y(v.take("grad_down"))
+    v.y_down = to_groups_of([[None] + v.take("grad_down")])
+    v.hidden = [m[2] for m in v.mlp]
     pieces = back_pieces(v.take("output"))
     v.z_out = [zshift(piece, k) if k else piece for k, piece in enumerate(pieces)]
     v.dn2 = [None] * parts
@@ -981,15 +987,14 @@
         v.dn2[p] = mlp_back_in(p)
     v.grad_gate = summed([d[0] for d in v.d_mlp], v.n2, range(1, O))
     v.take("mlp")
-    v.cot_own = v.take("cot")[0][:Lc]
-    v.barrier()
-
-    (v.y_down,) = y_parts(v.y_down)
+    v.cot_own = v.cot[0][:Lc]
+    v.barrier()
+
+    own = summed(v.take("hidden"), v.take("cot"), range(1))
+    (v.y_down,) = y_parts((own, v.y_down))
     v.output = back_joined(v.take("z_out"))
     v.ring = ring_step((v.y_down, 1, None))
-    v.y_gate = grad_y(
-        summed([d[0] for d in v.d_mlp], v.n2, range(1)) + v.take("grad_gate")
-    )
+    v.y_gate = to_groups_of([[None] + v.take("grad_gate")])
     dn2_sum = v.take("dn2_sum")
     for p in reversed(range(last if last else 1)):
         part = send_sum(v.dn2[p], p)
@@ -1007,11 +1012,10 @@
     v.far_branch = far(v.d_own)
     v.near_branch = tp(v.d_own, 1)
     v.grad_up = summed([d[1] for d in v.d_mlp], v.n2)
-    v.take("n2")
-    v.take("d_mlp")
-    v.barrier()
-
-    (v.y_gate,) = y_parts(v.y_gate)
+    v.gate_own = summed([d[0] for d in v.take("d_mlp")], v.take("n2"), range(1))
+    v.barrier()
+
+    (v.y_gate,) = y_parts((v.take("gate_own"), v.y_gate))
     (r_down,) = v.ring.parts()
     v.ring = ring_step((v.y_down, 2, r_down), (v.y_gate, 1, None))
     v.y_up = grad_y(v.take("grad_up"))
@@ -1105,6 +1109,16 @@
         return got
 
     v.z_mixer = direct(rings, y_output, y_branch)
+    v.y_in = grad_y(summed([v.d_rnn], [v.n1]))
+    v.take("n1")
+    v.dn1 = [
+        mixed_sum(((v.d_rnn, p, parts), v.w_in_t), ((v.d_gin, p, parts), v.w_br_t))
+        for p in range(parts)
+    ]
+    for name in ("d_rnn", "d_gin", "w_in_t", "w_br_t", "wa", "wx", "masks", "vec"):
+        v.take(name)
+    v.barrier()
+
     gates_grad = jnp.stack(
         [
             jnp.stack(
@@ -1127,16 +1141,7 @@
     gates_grad = gates_grad.reshape(M, DP, gate_rows, Dl).transpose(0, 2, 1, 3)
     gates_grad = gates_grad.reshape(M * gate_rows, D).astype(BF)
     gates_grad = [cut(gates_grad, (o + r) % O, half, 1) for r in range(O)]
-    v.y_in = grad_y(summed([v.d_rnn], [v.n1]), gates_grad)
-    v.take("n1")
-    v.dn1 = [
-        mixed_sum(((v.d_rnn, p, parts), v.w_in_t), ((v.d_gin, p, parts), v.w_br_t))
-        for p in range(parts)
-    ]
-    for name in ("d_rnn", "d_gin", "w_in_t", "w_br_t", "wa", "wx", "masks", "vec"):
-        v.take(name)
-    v.barrier()
-
+    v.y_gates = grad_y(gates_grad)
     v.z_down = ring_end(v.take("y_down"), v.take("r_down"))
     r_gate, r_up = v.z_mixer[M - 1].parts()[2:]
     v.z_gate = ring_end(v.take("y_gate"), r_gate)
@@ -1148,36 +1153,39 @@
     v.dn1 = dn1_sum
     v.barrier()
 
-    def added(pieces):
+    def added(pieces, count=1):
         return [
             sum(p.astype(F32) for p in same).astype(BF)
-            for same in zip(*(piece.parts()[:2] for piece in pieces))
+            for same in zip(*(p.parts()[:count] for p in pieces))
         ]
 
-    r_up = v.z_in[M - 1].parts()[2]
-
-    z_output, z_branch = added(v.take("z_mixer"))
-    z_in, z_gates = added(v.take("z_in"))
+    r_up = v.z_in[M - 1].parts()[1]
+
+    z_output, z_branch = added(v.take("z_mixer"), 2)
+    (z_in,) = added(v.take("z_in"))
     z_up = ring_end(v.take("y_up"), r_up)
     totals = exchange_grads(
-        v.take("z_down"), v.take("z_gate"), z_up, z_output, z_branch, z_in, z_gates
+        v.take("z_down"), v.take("z_gate"), z_up, z_output, z_branch, z_in
     )
     unit_one, scale_one = normed(v.own_in, v.gain_one)
     back_one, gain_one_grad = norm_back(v.take("dn1"), unit_one, scale_one, v.gain_one)
     pieces = back_pieces((v.d_mid + back_one).astype(BF))
     sums = jnp.broadcast_to(gain_one_grad.astype(BF), (16, D))
     joints = []
+    sends = direct_sends(*y_parts(v.take("y_gates")))
     for k, piece in enumerate(pieces):
-        joint = jnp.concatenate([piece, cut(sums, (z + k) % M, FH, 1)])
+        gates_send = folded(sends[(M - k) % M][0])
+        joint = jnp.concatenate([piece, cut(sums, (z + k) % M, FH, 1), gates_send])
         joints.append(zshift(joint, k) if k else joint)
-    *whole, last_rows = by_grad(totals)
     v.joints = joints
-    v.grads = [grad_end(total) for total in whole]
-    v.last_rows = last_rows
+    v.grads = [grad_end(total) for total in by_grad(totals)]
     v.barrier()
 
     grad_down, grad_gate, grad_up, grad_output, grad_branch, grad_in = v.grads
     input_grad = back_joined([joint[:Lc] for joint in v.joints]).astype(F32)
+    gates_sum = unfolded(sum(joint[Lc + 16 :].astype(F32) for joint in v.joints))
+    gates_sum = gates_sum.astype(BF)
+    last_rows = exchange(lambda k: cut(gates_sum, k, Dl, 1))
     gain_one_grad = sum(joint[Lc].astype(F32) for joint in v.joints)
     step = 1
     while step < DP:
@@ -1186,7 +1194,7 @@
     gain_one_grad = cut(gain_one_grad, i_dp, ng, 0)
     output = v.output
 
-    rest_in = jnp.stack([piece.reshape(-1) for piece in v.last_rows])
+    rest_in = jnp.stack([piece.reshape(-1) for piece in last_rows])
     small = jnp.sum(rest_in[:, gate_size:].astype(F32), axis=0)
     rest_in = jnp.stack([pick(rest_in, q ^ k) for k in range(t)])
     mine = small[: 2 * conv * nc].reshape(2 * conv, nc)

time: 1250 us -> 1210 us (0.968)
  local copies, waits for them, and re-layouts: 217 us -> 180 us
  starting transfers between devices: 80.7 us -> 106 us
  waiting for transfers between devices: 368 us -> 350 us
    ppermute x28, starting transfers between devices: 34.5 us -> 58.7 us  [zshift(): return lax.ppermute(value, 'mp', [(i, (i + k) % M) for i in range(M)])]
    ppermute x12 -> x13, waiting for transfers between devices: 58.7 us -> 39.4 us  [oshift(): lax.ppermute(value, 'dp', [(i, (i // t + r) % O * t + i % t) for i in ran...]
    unnamed x234 -> x206, local copies, waits for them, and re-layouts: 56.6 us -> 44.3 us
    dynamic_update_slice x74 -> x73, local copies, waits for them, and re-layouts: 50 us -> 42.7 us  [put(): return lax.dynamic_update_slice(array, piece, starts)]
    ppermute x32 -> x35, waiting for transfers between devices: 177 us -> 177 us  [tp(): return lax.ppermute(value, 'dp', [(i, i ^ j) for i in range(DP)])]
  transfers between devices with their start and end apart: 79 -> 83, of which waited for: 33 -> 33; matrix products, arithmetic and copies ran while one was open for 26% -> 24% of each run, Pallas kernels for 27% -> 29%
where the time goes in v5:
time: 1210 us; the launch traced here: 1200 us
  Pallas kernels  380 us (31%)
  waiting for transfers between devices  350 us (29%)
  local copies, waits for them, and re-layouts  180 us (15%)
  other arithmetic  142 us (12%)
  starting transfers between devices  106 us (9%)
  matrix products  35.5 us (3%)
    pallas_call x24, Pallas kernels, products(): pl.pallas_call(kernel, grid_spec=pltpu.PrefetchScalarGridSpec(num_scalar_...  285 us
    ppermute x35, waiting for transfers between devices, tp(): return lax.ppermute(value, 'dp', [(i, i ^ j) for i in range(DP)])  177 us
    ppermute x28, waiting for transfers between devices, zshift(): return lax.ppermute(value, 'mp', [(i, (i + k) % M) for i in range(M)])  134 us
    pallas_call x4, Pallas kernels, seq_call(): pl.pallas_call(kernel, grid=(count,), in_specs=block_specs([(a.shape, Tru...  95.3 us
    ppermute x28, starting transfers between devices, zshift(): return lax.ppermute(value, 'mp', [(i, (i + k) % M) for i in range(M)])  58.7 us
    unnamed x206, local copies, waits for them, and re-layouts  44.3 us
    dynamic_update_slice x73, local copies, waits for them, and re-layouts, put(): return lax.dynamic_update_slice(array, piece, starts)  42.7 us
    ppermute x13, waiting for transfers between devices, oshift(): lax.ppermute(value, 'dp', [(i, (i // t + r) % O * t + i % t) for i in ran...  39.4 us
  transfers between devices with their start and end apart: 83, of which 33 were waited for; matrix products, arithmetic and copies ran while one was open for 24% of the time, Pallas kernels for 29%

profile of v5, /device:TPU:8, one launch (start us, length us, event | category | flops | bytes accessed | tf_op | source)
XLA Modules:
  0.0 1197.5 jit_solution(6904600885830932990)
XLA Ops:
  29.8 23.6 %collective-permute-done.1 = bf16[2,1280,256]{2,1,0:T(8,128)(2,1)} collective-permute-done((bf16[2,1280,256]{2,1,0:T(8,128)(2,1)}, bf16[2,1280,256]{2,1,0:T(8,128)(2,1)}, u32[]{:S(2)}, u32[]{:S(2)}) %collective-permute-start.1) | collective-permute-done | bytes 1310752 | tf_op jit(solution)/shard_map/ppermute | solution.py:483
  81.0 17.5 %collective-permute-done.6 = bf16[352,1024]{1,0:T(8,128)(2,1)S(1)} collective-permute-done((bf16[352,1024]{1,0:T(8,128)(2,1)S(1)}, bf16[352,1024]{1,0:T(8,128)(2,1)S(1)}, u32[]{:S(2)}, u32[]{:S(2)}) %collective-permute-start.6) | collective-permute-done | bytes 720928 | tf_op jit(solution)/shard_map/ppermute | solution.py:491
  117.0 14.3 %collective-permute-done.8 = bf16[352,1024]{1,0:T(8,128)(2,1)S(1)} collective-permute-done((bf16[352,1024]{1,0:T(8,128)(2,1)}, bf16[352,1024]{1,0:T(8,128)(2,1)S(1)}, u32[]{:S(2)}, u32[]{:S(2)}) %collective-permute-start.8) | collective-permute-done | bytes 720928 | tf_op jit(solution)/shard_map/ppermute | solution.py:491
  171.5 13.3 %collective-permute-done.14 = bf16[928,1024]{1,0:T(8,128)(2,1)S(1)} collective-permute-done((bf16[928,1024]{1,0:T(8,128)(2,1)S(1)}, bf16[928,1024]{1,0:T(8,128)(2,1)S(1)}, u32[]{:S(2)}, u32[]{:S(2)}) %collective-permute-start.14) | collective-permute-done | bytes 1900576 | tf_op jit(solution)/shard_map/ppermute | solution.py:491
  192.7 11.5 collective-permute-start.16
  230.4 11.6 fusion.147
  276.1 31.4 %recurrence.1 = (f32[4,512,640]{2,1,0:T(8,128)}, f32[4,512,640]{2,1,0:T(8,128)}, f32[4,512,640]{2,1,0:T(8,128)}, f32[4,512,640]{2,1,0:T(8,128)}, f32[4,512,640]{2,1,0:T(8,128)}, /*index=5*/f32[4,8,640]{2,1,0:T(8,128)}) custom-call(f32[4,512,640]{2,1,0:T(8,128)} %bitcast.265, f32[4,8,640]{2,1,0:T(8,128)} %slice.1419.halo_ref, f32[4,520,4]{2,1,0:T(8,128)} %copy.89.mask_ref, ...), custom_call_target="tpu_custom_call" | custom-call | flops 4000000000 | tf_op jit(solution)/shard_map/recurrence/pallas_call | solution.py:325
  371.6 39.4 %collective-permute-done.25 = bf16[512,2048]{1,0:T(8,128)(2,1)} collective-permute-done((bf16[512,2048]{1,0:T(8,128)(2,1)}, bf16[512,2048]{1,0:T(8,128)(2,1)}, u32[]{:S(2)}, u32[]{:S(2)}) %collective-permute-start.25) | collective-permute-done | bytes 2097184 | tf_op jit(solution)/shard_map/ppermute | solution.py:483
  437.2 19.5 %mlp.2 = (f32[1024,1536]{1,0:T(8,128)}, f32[1024,1536]{1,0:T(8,128)}, bf16[1024,1536]{1,0:T(8,128)(2,1)}) custom-call(s32[1]{0:T(128)} %constant.420.clone.1._, bf16[1024,2048]{1,0:T(8,128)(2,1)} %constant_dynamic-update-slice_fusion.5.refs_0_.refs_2_, bf16[1536,2048]{1,0:T(8,128)(2,1)} %get-tuple-element.845.refs_1_.refs_2_, ...), custom_call_target="tpu_custom_call" | custom-call | flops 1894838528 | tf_op jit(solution)/shard_map/mlp/pallas_call | solution.py:394
  478.6 19.4 %mlp.3 = (f32[1024,1536]{1,0:T(8,128)}, f32[1024,1536]{1,0:T(8,128)}, bf16[1024,1536]{1,0:T(8,128)(2,1)}) custom-call(s32[1]{0:T(128)} %constant.420.clone.1._, bf16[1024,2048]{1,0:T(8,128)(2,1)} %constant_dynamic-update-slice_fusion.7.refs_0_.refs_3_, bf16[1536,2048]{1,0:T(8,128)(2,1)} %get-tuple-element.845.refs_1_.refs_2_, ...), custom_call_target="tpu_custom_call" | custom-call | flops 1894838528 | tf_op jit(solution)/shard_map/mlp/pallas_call | solution.py:394
  520.8 11.7 product.10
  532.4 11.7 product.11
  556.7 11.6 gradient.12
  568.3 16.9 %mlp_back.2 = (bf16[1024,1536]{1,0:T(8,128)(2,1)}, bf16[1024,1536]{1,0:T(8,128)(2,1)}) custom-call(s32[1]{0:T(128)} %constant.420.clone.1._, bf16[1024,2048]{1,0:T(8,128)(2,1)} %constant_dynamic-update-slice_fusion.9.refs_0_.refs_3_, bf16[1536,2048]{1,0:T(8,128)(2,1)} %slice_dynamic-update-slice_fusion.2.refs_1_, f32[1024,1536]{1,0:T(8,128)} %get-tuple-element.796.refs_2_, ...), custom_call_target="tpu_custom_call" | custom-call | flops 947419264 | tf_op jit(solution)/shard_map/mlp_back/pallas_call | solution.py:394
  585.1 12.2 %collective-permute-done.40 = bf16[512,2048]{1,0:T(8,128)(2,1)} collective-permute-done((bf16[512,2048]{1,0:T(8,128)(2,1)S(1)}, bf16[512,2048]{1,0:T(8,128)(2,1)}, u32[]{:S(2)}, u32[]{:S(2)}) %collective-permute-start.40) | collective-permute-done | bytes 2097184 | tf_op jit(solution)/shard_map/ppermute | solution.py:483
  603.0 18.7 %product.13 = (bf16[512,2048]{1,0:T(8,128)(2,1)}, bf16[512,2048]{1,0:T(8,128)(2,1)}) custom-call(s32[1]{0:T(128)} %constant.420.clone.1._, bf16[1024,1536]{1,0:T(8,128)(2,1)} %get-tuple-element.892.refs_0_.refs_1_, bf16[1024,1536]{1,0:T(8,128)(2,1)} %get-tuple-element.897.refs_1_, bf16[1536,2048]{1,0:T(8,128)(2,1)} %get-tuple-element.845.refs_1_.refs_2_, ...), custom_call_target="tpu_custom_call" | custom-call | flops 1894838528 | tf_op jit(solution)/shard_map/product/pallas_call | solution.py:394
  640.0 16.6 %mlp_back.3 = (bf16[1024,1536]{1,0:T(8,128)(2,1)}, bf16[1024,1536]{1,0:T(8,128)(2,1)}) custom-call(s32[1]{0:T(128)} %constant.420.clone.1._, bf16[1024,2048]{1,0:T(8,128)(2,1)} %pad_maximum_fusion.1.refs_2_.refs_0_, bf16[1536,2048]{1,0:T(8,128)(2,1)} %slice_dynamic-update-slice_fusion.2.refs_1_, f32[1024,1536]{1,0:T(8,128)} %get-tuple-element.839.refs_2_, ...), custom_call_target="tpu_custom_call" | custom-call | flops 947419264 | tf_op jit(solution)/shard_map/mlp_back/pallas_call | solution.py:394
  656.5 11.6 gradient.13
  668.2 18.7 %product.12 = (bf16[512,2048]{1,0:T(8,128)(2,1)}, bf16[512,2048]{1,0:T(8,128)(2,1)}) custom-call(s32[1]{0:T(128)} %constant.420.clone.1._, bf16[1024,1536]{1,0:T(8,128)(2,1)} %get-tuple-element.891.refs_0_, bf16[1024,1536]{1,0:T(8,128)(2,1)} %get-tuple-element.896.refs_1_.refs_0_, bf16[1536,2048]{1,0:T(8,128)(2,1)} %get-tuple-element.845.refs_1_.refs_2_, ...), custom_call_target="tpu_custom_call" | custom-call | flops 1894838528 | tf_op jit(solution)/shard_map/product/pallas_call | solution.py:394
  704.0 11.6 gradient.17
  722.2 12.0 %gradient.16 = bf16[1536,1024]{1,0:T(8,128)(2,1)} custom-call(s32[1]{0:T(128)} %bitcast.52._, bf16[1024,1536]{1,0:T(8,128)(2,1)} %get-tuple-element.896.refs_1_.refs_0_, bf16[1024,1536]{1,0:T(8,128)(2,1)} %get-tuple-element.897.refs_1_, bf16[1024,2048]{1,0:T(8,128)(2,1)} %constant_dynamic-update-slice_fusion.5.refs_0_.refs_2_, ...), custom_call_target="tpu_custom_call" | custom-call | flops 947419264 | tf_op jit(solution)/shard_map/gradient/pallas_call | solution.py:394
  734.2 11.6 gradient.15
  745.8 11.7 gradient.14
  782.0 12.3 %fusion.148 = f32[2048,640]{1,0:T(8,128)} fusion(bf16[2048,2048]{1,0:T(8,128)(2,1)S(1)} %constant_dynamic-update-slice_fusion.11.refs_1_, bf16[640,2048]{1,0:T(8,128)(2,1)} %constant_dynamic-update-slice_fusion.42.refs_1_), kind=kOutput, calls=%fused_computation.498 | convolution fusion | flops 5368709120 | bytes 16252928 | tf_op jit(solution)/shard_map/dot_general | solution.py:18
  794.4 19.9 %adjoint.1 = (f32[4,512,640]{2,1,0:T(8,128)}, f32[4,512,640]{2,1,0:T(8,128)}, bf16[4,512,640]{2,1,0:T(8,128)(2,1)}, f32[4,8,640]{2,1,0:T(8,128)}) custom-call(f32[4,512,640]{2,1,0:T(8,128)} %bitcast.268, f32[4,512,640]{2,1,0:T(8,128)} %bitcast.260, f32[4,512,640]{2,1,0:T(8,128)} %get-tuple-element.998.state_ref, f32[4,512,640]{2,1,0:T(8,128)} %get-tuple-element.999.ga_ref, ...), custom_call_target="tpu_custom_call" | custom-call | flops 2400000000 | tf_op jit(solution)/shard_map/adjoint/pallas_call | solution.py:325
  828.3 15.8 %collective-permute-done.55 = bf16[1536,1024]{1,0:T(8,128)(2,1)} collective-permute-done((bf16[1536,1024]{1,0:T(8,128)(2,1)}, bf16[1536,1024]{1,0:T(8,128)(2,1)}, u32[]{:S(2)}, u32[]{:S(2)}) %collective-permute-start.55) | collective-permute-done | bytes 3145760 | tf_op jit(solution)/shard_map/ppermute | solution.py:486
  901.9 36.0 %recurrence_back.2 = (bf16[4,512,640]{2,1,0:T(8,128)(2,1)}, f32[4,8,640]{2,1,0:T(8,128)}, f32[4,8,640]{2,1,0:T(8,128)}, f32[640,640]{1,0:T(8,128)}, f32[640,640]{1,0:T(8,128)}, /*index=5*/f32[8,8,640]{2,1,0:T(8,128)}) custom-call(f32[4,512,640]{2,1,0:T(8,128)} %get-tuple-element.996.lam_ref, f32[4,512,640]{2,1,0:T(8,128)} %get-tuple-element.997.q_ref, ...), custom_call_target="tpu_custom_call" | custom-call | flops 4000000000 | tf_op jit(solution)/shard_map/recurrence_back/pallas_call | solution.py:325
  974.4 11.7 product.15
  986.1 11.7 product.14
  998.7 39.7 %collective-permute-done.64 = bf16[320,1024]{1,0:T(8,128)(2,1)} collective-permute-done((bf16[320,1024]{1,0:T(8,128)(2,1)}, bf16[320,1024]{1,0:T(8,128)(2,1)}, u32[]{:S(2)}, u32[]{:S(2)}) %collective-permute-start.64) | collective-permute-done | bytes 655392 | tf_op jit(solution)/shard_map/ppermute | solution.py:491
  1065.6 38.3 %collective-permute-done.67 = bf16[512,2048]{1,0:T(8,128)(2,1)} collective-permute-done((bf16[512,2048]{1,0:T(8,128)(2,1)}, bf16[512,2048]{1,0:T(8,128)(2,1)}, u32[]{:S(2)}, u32[]{:S(2)}) %collective-permute-start.67) | collective-permute-done | bytes 2097184 | tf_op jit(solution)/shard_map/ppermute | solution.py:483
  1126.0 33.5 %collective-permute-done.74 = bf16[2,1632,256]{2,1,0:T(8,128)(2,1)S(1)} collective-permute-done((bf16[2,1632,256]{2,1,0:T(8,128)(2,1)S(1)}, bf16[2,1632,256]{2,1,0:T(8,128)(2,1)S(1)}, u32[]{:S(2)}, u32[]{:S(2)}) %collective-permute-start.74) | collective-permute-done | bytes 1671200 | tf_op jit(solution)/shard_map/ppermute | solution.py:483
  (720 shorter events, 597.0 us)
Async XLA Ops:
  76.6 59.0 %collective-permute-start.9 = (bf16[1280,1024]{1,0:T(8,128)(2,1)S(1)}, bf16[1280,1024]{1,0:T(8,128)(2,1)}, u32[]{:S(2)}, u32[]{:S(2)}) collective-permute-start(bf16[1280,1024]{1,0:T(8,128)(2,1)S(1)} %constant_dynamic-update-slice_fusion.36), channel_id=1, source_target_pairs={{0,16},{4,20},{8,24},{12,28},{16,0},{20,4},{24,8},{28,12},{1,17},{... | collective-permute-start | bytes 7864328 | tf_op jit(solution)/shard_map/ppermute | solution.py:486
  80.4 51.0 %collective-permute-start.5 = (bf16[544,2048]{1,0:T(8,128)(2,1)}, bf16[544,2048]{1,0:T(8,128)(2,1)}, u32[]{:S(2)}, u32[]{:S(2)}) collective-permute-start(bf16[544,2048]{1,0:T(8,128)(2,1)} %pad_maximum_fusion.6), channel_id=1, source_target_pairs={{0,8},{4,12},{8,0},{12,4},{16,24},{20,28},{24,16},{28,20},{1,9},{5... | collective-permute-start | bytes 6684680 | tf_op jit(solution)/shard_map/ppermute | solution.py:483
  139.5 49.5 %collective-permute-start.15 = (bf16[1056,1024]{1,0:T(8,128)(2,1)S(1)}, bf16[1056,1024]{1,0:T(8,128)(2,1)S(1)}, u32[]{:S(2)}, u32[]{:S(2)}) collective-permute-start(bf16[1056,1024]{1,0:T(8,128)(2,1)S(1)} %pad_maximum_fusion.8), channel_id=1, source_target_pairs={{0,16},{4,20},{8,24},{12,28},{16,0},{20,4},{24,8},{28,12},{1,17},{... | collective-permute-start | bytes 6488072 | tf_op jit(solution)/shard_map/ppermute | solution.py:486
  192.7 72.5 %collective-permute-start.16 = (bf16[1312,1024]{1,0:T(8,128)(2,1)}, bf16[1312,1024]{1,0:T(8,128)(2,1)}, u32[]{:S(2)}, u32[]{:S(2)}) collective-permute-start(bf16[1312,1024]{1,0:T(8,128)(2,1)} %pad_maximum_fusion.2), channel_id=1, source_target_pairs={{0,1},{1,2},{2,3},{3,0},{4,5},{5,6},{6,7},{7,4},{8,9},{9,10},{10,1... | collective-permute-start | bytes 8060936 | tf_op jit(solution)/shard_map/ppermute | solution.py:491
  204.2 61.0 %collective-permute-start.17 = (bf16[1312,1024]{1,0:T(8,128)(2,1)}, bf16[1312,1024]{1,0:T(8,128)(2,1)}, u32[]{:S(2)}, u32[]{:S(2)}) collective-permute-start(bf16[1312,1024]{1,0:T(8,128)(2,1)} %pad_maximum_fusion.2), channel_id=1, source_target_pairs={{0,16},{4,20},{8,24},{12,28},{16,0},{20,4},{24,8},{28,12},{1,17},{... | collective-permute-start | bytes 8060936 | tf_op jit(solution)/shard_map/ppermute | solution.py:486
  363.2 47.9 %collective-permute-start.25 = (bf16[512,2048]{1,0:T(8,128)(2,1)}, bf16[512,2048]{1,0:T(8,128)(2,1)}, u32[]{:S(2)}, u32[]{:S(2)}) collective-permute-start(bf16[512,2048]{1,0:T(8,128)(2,1)} %add_convert_fusion.4), channel_id=1, source_target_pairs={{0,8},{4,12},{8,0},{12,4},{16,24},{20,28},{24,16},{28,20},{1,9},{5... | collective-permute-start | bytes 6291464 | tf_op jit(solution)/shard_map/ppermute | solution.py:483
  365.8 53.2 %collective-permute-start.27 = (bf16[1152,1024]{1,0:T(8,128)(2,1)}, bf16[1152,1024]{1,0:T(8,128)(2,1)}, u32[]{:S(2)}, u32[]{:S(2)}) collective-permute-start(bf16[1152,1024]{1,0:T(8,128)(2,1)} %pad_maximum_fusion.4), channel_id=1, source_target_pairs={{0,16},{4,20},{8,24},{12,28},{16,0},{20,4},{24,8},{28,12},{1,17},{... | collective-permute-start | bytes 7077896 | tf_op jit(solution)/shard_map/ppermute | solution.py:486
  368.8 49.1 %collective-permute-start.28 = (bf16[1280,512]{1,0:T(8,128)(2,1)S(1)}, bf16[1280,512]{1,0:T(8,128)(2,1)S(1)}, u32[]{:S(2)}, u32[]{:S(2)}) collective-permute-start(bf16[1280,512]{1,0:T(8,128)(2,1)S(1)} %pad_maximum_fusion.16), channel_id=1, source_target_pairs={{0,1},{1,2},{2,3},{3,0},{4,5},{5,6},{6,7},{7,4},{8,9},{9,10},{10,1... | collective-permute-start | bytes 3932168 | tf_op jit(solution)/shard_map/ppermute | solution.py:491
  368.9 49.1 %collective-permute-start.29 = (bf16[512,512]{1,0:T(8,128)(2,1)S(1)}, bf16[512,512]{1,0:T(8,128)(2,1)S(1)}, u32[]{:S(2)}, u32[]{:S(2)}) collective-permute-start(bf16[512,512]{1,0:T(8,128)(2,1)S(1)} %get-tuple-element.1265), channel_id=1, source_target_pairs={{0,3},{1,0},{2,1},{3,2},{4,7},{5,4},{6,5},{7,6},{8,11},{9,8},{10,9... | collective-permute-start | bytes 1572872 | tf_op jit(solution)/shard_map/ppermute | solution.py:491
  419.2 48.0 %collective-permute-start.32 = (bf16[512,2048]{1,0:T(8,128)(2,1)S(1)}, bf16[512,2048]{1,0:T(8,128)(2,1)}, u32[]{:S(2)}, u32[]{:S(2)}) collective-permute-start(bf16[512,2048]{1,0:T(8,128)(2,1)S(1)} %get-tuple-element.726), channel_id=1, source_target_pairs={{0,8},{4,12},{8,0},{12,4},{16,24},{20,28},{24,16},{28,20},{1,9},{5... | collective-permute-start | bytes 6291464 | tf_op jit(solution)/shard_map/ppermute | solution.py:483
  549.2 48.2 %collective-permute-start.40 = (bf16[512,2048]{1,0:T(8,128)(2,1)S(1)}, bf16[512,2048]{1,0:T(8,128)(2,1)}, u32[]{:S(2)}, u32[]{:S(2)}) collective-permute-start(bf16[512,2048]{1,0:T(8,128)(2,1)S(1)} %add_convert_fusion.3), channel_id=1, source_target_pairs={{0,8},{4,12},{8,0},{12,4},{16,24},{20,28},{24,16},{28,20},{1,9},{5... | collective-permute-start | bytes 6291464 | tf_op jit(solution)/shard_map/ppermute | solution.py:483
  621.7 70.8 %collective-permute-start.44 = (bf16[1536,1024]{1,0:T(8,128)(2,1)}, bf16[1536,1024]{1,0:T(8,128)(2,1)}, u32[]{:S(2)}, u32[]{:S(2)}) collective-permute-start(bf16[1536,1024]{1,0:T(8,128)(2,1)} %gradient.12), channel_id=1, source_target_pairs={{0,16},{4,20},{8,24},{12,28},{16,0},{20,4},{24,8},{28,12},{1,17},{... | collective-permute-start | bytes 9437192 | tf_op jit(solution)/shard_map/ppermute | solution.py:486
  629.7 57.2 %collective-permute-start.43 = (bf16[512,2048]{1,0:T(8,128)(2,1)}, bf16[512,2048]{1,0:T(8,128)(2,1)}, u32[]{:S(2)}, u32[]{:S(2)}) collective-permute-start(bf16[512,2048]{1,0:T(8,128)(2,1)} %add_convert_fusion.1), channel_id=1, source_target_pairs={{0,8},{4,12},{8,0},{12,4},{16,24},{20,28},{24,16},{28,20},{1,9},{5... | collective-permute-start | bytes 6291464 | tf_op jit(solution)/shard_map/ppermute | solution.py:483
  631.7 57.4 %collective-permute-start.45 = (bf16[512,512]{1,0:T(8,128)(2,1)S(1)}, bf16[512,512]{1,0:T(8,128)(2,1)S(1)}, u32[]{:S(2)}, u32[]{:S(2)}) collective-permute-start(bf16[512,512]{1,0:T(8,128)(2,1)S(1)} %get-tuple-element.1263), channel_id=1, source_target_pairs={{0,1},{1,2},{2,3},{3,0},{4,5},{5,6},{6,7},{7,4},{8,9},{9,10},{10,1... | collective-permute-start | bytes 1572872 | tf_op jit(solution)/shard_map/ppermute | solution.py:491
  635.8 53.4 %collective-permute-start.46 = (bf16[512,512]{1,0:T(8,128)(2,1)S(1)}, bf16[512,512]{1,0:T(8,128)(2,1)S(1)}, u32[]{:S(2)}, u32[]{:S(2)}) collective-permute-start(bf16[512,512]{1,0:T(8,128)(2,1)S(1)} %get-tuple-element.1262), channel_id=1, source_target_pairs={{0,2},{1,3},{2,0},{3,1},{4,6},{5,7},{6,4},{7,5},{8,10},{9,11},{10,... | collective-permute-start | bytes 1572872 | tf_op jit(solution)/shard_map/ppermute | solution.py:491
  640.0 49.3 %collective-permute-start.47 = (bf16[512,512]{1,0:T(8,128)(2,1)S(1)}, bf16[512,512]{1,0:T(8,128)(2,1)S(1)}, u32[]{:S(2)}, u32[]{:S(2)}) collective-permute-start(bf16[512,512]{1,0:T(8,128)(2,1)S(1)} %get-tuple-element.1261), channel_id=1, source_target_pairs={{0,3},{1,0},{2,1},{3,2},{4,7},{5,4},{6,5},{7,6},{8,11},{9,8},{10,9... | collective-permute-start | bytes 1572872 | tf_op jit(solution)/shard_map/ppermute | solution.py:491
  692.5 70.8 %collective-permute-start.52 = (bf16[1536,1024]{1,0:T(8,128)(2,1)}, bf16[1536,1024]{1,0:T(8,128)(2,1)}, u32[]{:S(2)}, u32[]{:S(2)}) collective-permute-start(bf16[1536,1024]{1,0:T(8,128)(2,1)} %gradient.13), channel_id=1, source_target_pairs={{0,16},{4,20},{8,24},{12,28},{16,0},{20,4},{24,8},{28,12},{1,17},{... | collective-permute-start | bytes 9437192 | tf_op jit(solution)/shard_map/ppermute | solution.py:486
  703.0 60.3 %collective-permute-start.49 = (bf16[512,2048]{1,0:T(8,128)(2,1)}, bf16[512,2048]{1,0:T(8,128)(2,1)}, u32[]{:S(2)}, u32[]{:S(2)}) collective-permute-start(bf16[512,2048]{1,0:T(8,128)(2,1)} %get-tuple-element.921), channel_id=1, source_target_pairs={{0,8},{4,12},{8,0},{12,4},{16,24},{20,28},{24,16},{28,20},{1,9},{5... | collective-permute-start | bytes 6291464 | tf_op jit(solution)/shard_map/ppermute | solution.py:483
  704.0 59.4 %collective-permute-start.50 = (bf16[512,2048]{1,0:T(8,128)(2,1)}, bf16[512,2048]{1,0:T(8,128)(2,1)}, u32[]{:S(2)}, u32[]{:S(2)}) collective-permute-start(bf16[512,2048]{1,0:T(8,128)(2,1)} %get-tuple-element.921), channel_id=1, source_target_pairs={{0,4},{4,0},{8,12},{12,8},{16,20},{20,16},{24,28},{28,24},{1,5},{5... | collective-permute-start | bytes 6291464 | tf_op jit(solution)/shard_map/ppermute | solution.py:483
  768.2 60.1 %collective-permute-start.54 = (bf16[768,1024]{1,0:T(8,128)(2,1)}, bf16[768,1024]{1,0:T(8,128)(2,1)}, u32[]{:S(2)}, u32[]{:S(2)}) collective-permute-start(bf16[768,1024]{1,0:T(8,128)(2,1)} %pad_maximum_fusion.13), channel_id=1, source_target_pairs={{0,1},{1,2},{2,3},{3,0},{4,5},{5,6},{6,7},{7,4},{8,9},{9,10},{10,1... | collective-permute-start | bytes 4718600 | tf_op jit(solution)/shard_map/ppermute | solution.py:491
  773.5 70.5 %collective-permute-start.55 = (bf16[1536,1024]{1,0:T(8,128)(2,1)}, bf16[1536,1024]{1,0:T(8,128)(2,1)}, u32[]{:S(2)}, u32[]{:S(2)}) collective-permute-start(bf16[1536,1024]{1,0:T(8,128)(2,1)} %gradient.16), channel_id=1, source_target_pairs={{0,16},{4,20},{8,24},{12,28},{16,0},{20,4},{24,8},{28,12},{1,17},{... | collective-permute-start | bytes 9437192 | tf_op jit(solution)/shard_map/ppermute | solution.py:486
  868.5 69.6 %collective-permute-start.61 = (bf16[1280,1024]{1,0:T(8,128)(2,1)}, bf16[1280,1024]{1,0:T(8,128)(2,1)}, u32[]{:S(2)}, u32[]{:S(2)}) collective-permute-start(bf16[1280,1024]{1,0:T(8,128)(2,1)} %pad_maximum_fusion.3), channel_id=1, source_target_pairs={{0,16},{4,20},{8,24},{12,28},{16,0},{20,4},{24,8},{28,12},{1,17},{... | collective-permute-start | bytes 7864328 | tf_op jit(solution)/shard_map/ppermute | solution.py:486
  876.7 61.4 %collective-permute-start.60 = (bf16[1152,1024]{1,0:T(8,128)(2,1)}, bf16[1152,1024]{1,0:T(8,128)(2,1)}, u32[]{:S(2)}, u32[]{:S(2)}) collective-permute-start(bf16[1152,1024]{1,0:T(8,128)(2,1)} %pad_maximum_fusion.5), channel_id=1, source_target_pairs={{0,1},{1,2},{2,3},{3,0},{4,5},{5,6},{6,7},{7,4},{8,9},{9,10},{10,1... | collective-permute-start | bytes 7077896 | tf_op jit(solution)/shard_map/ppermute | solution.py:491
  947.5 92.9 %collective-permute-start.65 = (bf16[1088,1024]{1,0:T(8,128)(2,1)}, bf16[1088,1024]{1,0:T(8,128)(2,1)}, u32[]{:S(2)}, u32[]{:S(2)}) collective-permute-start(bf16[1088,1024]{1,0:T(8,128)(2,1)} %pad_maximum_fusion.7), channel_id=1, source_target_pairs={{0,1},{1,2},{2,3},{3,0},{4,5},{5,6},{6,7},{7,4},{8,9},{9,10},{10,1... | collective-permute-start | bytes 6684680 | tf_op jit(solution)/shard_map/ppermute | solution.py:491
  957.6 82.8 %collective-permute-start.62 = (bf16[640,1024]{1,0:T(8,128)(2,1)}, bf16[640,1024]{1,0:T(8,128)(2,1)}, u32[]{:S(2)}, u32[]{:S(2)}) collective-permute-start(bf16[640,1024]{1,0:T(8,128)(2,1)} %gradient.23), channel_id=1, source_target_pairs={{0,16},{4,20},{8,24},{12,28},{16,0},{20,4},{24,8},{28,12},{1,17},{... | collective-permute-start | bytes 3932168 | tf_op jit(solution)/shard_map/ppermute | solution.py:486
  960.0 78.4 %collective-permute-start.64 = (bf16[320,1024]{1,0:T(8,128)(2,1)}, bf16[320,1024]{1,0:T(8,128)(2,1)}, u32[]{:S(2)}, u32[]{:S(2)}) collective-permute-start(bf16[320,1024]{1,0:T(8,128)(2,1)} %pad_maximum_fusion.21), channel_id=1, source_target_pairs={{0,2},{1,3},{2,0},{3,1},{4,6},{5,7},{6,4},{7,5},{8,10},{9,11},{10,... | collective-permute-start | bytes 1966088 | tf_op jit(solution)/shard_map/ppermute | solution.py:491
  963.4 77.0 %collective-permute-start.63 = (bf16[320,1024]{1,0:T(8,128)(2,1)}, bf16[320,1024]{1,0:T(8,128)(2,1)}, u32[]{:S(2)}, u32[]{:S(2)}) collective-permute-start(bf16[320,1024]{1,0:T(8,128)(2,1)} %pad_maximum_fusion.20), channel_id=1, source_target_pairs={{0,3},{1,0},{2,1},{3,2},{4,7},{5,4},{6,5},{7,6},{8,11},{9,8},{10,9... | collective-permute-start | bytes 1966088 | tf_op jit(solution)/shard_map/ppermute | solution.py:491
  1047.7 59.6 %collective-permute-start.72 = (bf16[544,1024]{1,0:T(8,128)(2,1)S(1)}, bf16[544,1024]{1,0:T(8,128)(2,1)}, u32[]{:S(2)}, u32[]{:S(2)}) collective-permute-start(bf16[544,1024]{1,0:T(8,128)(2,1)S(1)} %pad_maximum_fusion.17), channel_id=1, source_target_pairs={{0,1},{1,2},{2,3},{3,0},{4,5},{5,6},{6,7},{7,4},{8,9},{9,10},{10,1... | collective-permute-start | bytes 3342344 | tf_op jit(solution)/shard_map/ppermute | solution.py:491
  1047.8 59.5 %collective-permute-start.70 = (bf16[160,1024]{1,0:T(8,128)(2,1)}, bf16[160,1024]{1,0:T(8,128)(2,1)}, u32[]{:S(2)}, u32[]{:S(2)}) collective-permute-start(bf16[160,1024]{1,0:T(8,128)(2,1)} %get-tuple-element.1215), channel_id=1, source_target_pairs={{0,3},{1,0},{2,1},{3,2},{4,7},{5,4},{6,5},{7,6},{8,11},{9,8},{10,9... | collective-permute-start | bytes 983048 | tf_op jit(solution)/shard_map/ppermute | solution.py:491
  1050.1 57.2 %collective-permute-start.71 = (bf16[160,1024]{1,0:T(8,128)(2,1)}, bf16[160,1024]{1,0:T(8,128)(2,1)}, u32[]{:S(2)}, u32[]{:S(2)}) collective-permute-start(bf16[160,1024]{1,0:T(8,128)(2,1)} %get-tuple-element.1214), channel_id=1, source_target_pairs={{0,2},{1,3},{2,0},{3,1},{4,6},{5,7},{6,4},{7,5},{8,10},{9,11},{10,... | collective-permute-start | bytes 983048 | tf_op jit(solution)/shard_map/ppermute | solution.py:491
  1055.7 48.2 %collective-permute-start.67 = (bf16[512,2048]{1,0:T(8,128)(2,1)}, bf16[512,2048]{1,0:T(8,128)(2,1)}, u32[]{:S(2)}, u32[]{:S(2)}) collective-permute-start(bf16[512,2048]{1,0:T(8,128)(2,1)} %add_convert_fusion), channel_id=1, source_target_pairs={{0,8},{4,12},{8,0},{12,4},{16,24},{20,28},{24,16},{28,20},{1,9},{5... | collective-permute-start | bytes 6291464 | tf_op jit(solution)/shard_map/ppermute | solution.py:483
  1123.3 50.0 %collective-permute-start.75 = (bf16[592,512]{1,0:T(8,128)(2,1)S(1)}, bf16[592,512]{1,0:T(8,128)(2,1)S(1)}, u32[]{:S(2)}, u32[]{:S(2)}) collective-permute-start(bf16[592,512]{1,0:T(8,128)(2,1)S(1)} %pad_maximum_fusion.23), channel_id=1, source_target_pairs={{0,1},{1,2},{2,3},{3,0},{4,5},{5,6},{6,7},{7,4},{8,9},{9,10},{10,1... | collective-permute-start | bytes 1818632 | tf_op jit(solution)/shard_map/ppermute | solution.py:491
  (136 other events, 2104.6 us)

commit v6 on v5

--- a/solution.py
+++ b/solution.py
@@ -221,7 +221,7 @@
     dm_ref,
 ):
     length, width = lam_ref.shape[1:]
-    block_rows = min(256, length)
+    block_rows = min(512, length)
     first = pl.program_id(0) == 0
 
     @pl.when(first)

time: 1210 us -> 1210 us (level)
  transfers between devices with their start and end apart: 83 -> 83, of which waited for: 33 -> 33; matrix products, arithmetic and copies ran while one was open for 24% -> 24% of each run, Pallas kernels for 29% -> 28%
where the time goes in v6:
time: 1210 us; the launch traced here: 1190 us
  Pallas kernels  376 us (31%)
  waiting for transfers between devices  350 us (29%)
  local copies, waits for them, and re-layouts  180 us (15%)
  other arithmetic  142 us (12%)
  starting transfers between devices  105 us (9%)
  matrix products  35.5 us (3%)
    pallas_call x24, Pallas kernels, products(): pl.pallas_call(kernel, grid_spec=pltpu.PrefetchScalarGridSpec(num_scalar_...  285 us
    ppermute x35, waiting for transfers between devices, tp(): return lax.ppermute(value, 'dp', [(i, i ^ j) for i in range(DP)])  176 us
    ppermute x28, waiting for transfers between devices, zshift(): return lax.ppermute(value, 'mp', [(i, (i + k) % M) for i in range(M)])  135 us
    pallas_call x4, Pallas kernels, seq_call(): pl.pallas_call(kernel, grid=(count,), in_specs=block_specs([(a.shape, Tru...  90.9 us
    ppermute x28, starting transfers between devices, zshift(): return lax.ppermute(value, 'mp', [(i, (i + k) % M) for i in range(M)])  58.5 us
    unnamed x206, local copies, waits for them, and re-layouts  44.4 us
    dynamic_update_slice x73, local copies, waits for them, and re-layouts, put(): return lax.dynamic_update_slice(array, piece, starts)  42.7 us
    ppermute x13, waiting for transfers between devices, oshift(): lax.ppermute(value, 'dp', [(i, (i // t + r) % O * t + i % t) for i in ran...  39.4 us
  transfers between devices with their start and end apart: 83, of which 33 were waited for; matrix products, arithmetic and copies ran while one was open for 24% of the time, Pallas kernels for 28%

profile of v6, /device:TPU:8, one launch (start us, length us, event | category | flops | bytes accessed | tf_op | source)
XLA Modules:
  0.0 1193.0 jit_solution(17833566288580098143)
XLA Ops:
  29.8 23.6 %collective-permute-done.1 = bf16[2,1280,256]{2,1,0:T(8,128)(2,1)} collective-permute-done((bf16[2,1280,256]{2,1,0:T(8,128)(2,1)}, bf16[2,1280,256]{2,1,0:T(8,128)(2,1)}, u32[]{:S(2)}, u32[]{:S(2)}) %collective-permute-start.1) | collective-permute-done | bytes 1310752 | tf_op jit(solution)/shard_map/ppermute | solution.py:483
  81.0 17.5 %collective-permute-done.6 = bf16[352,1024]{1,0:T(8,128)(2,1)S(1)} collective-permute-done((bf16[352,1024]{1,0:T(8,128)(2,1)S(1)}, bf16[352,1024]{1,0:T(8,128)(2,1)S(1)}, u32[]{:S(2)}, u32[]{:S(2)}) %collective-permute-start.6) | collective-permute-done | bytes 720928 | tf_op jit(solution)/shard_map/ppermute | solution.py:491
  117.0 14.3 %collective-permute-done.8 = bf16[352,1024]{1,0:T(8,128)(2,1)S(1)} collective-permute-done((bf16[352,1024]{1,0:T(8,128)(2,1)}, bf16[352,1024]{1,0:T(8,128)(2,1)S(1)}, u32[]{:S(2)}, u32[]{:S(2)}) %collective-permute-start.8) | collective-permute-done | bytes 720928 | tf_op jit(solution)/shard_map/ppermute | solution.py:491
  171.5 13.3 %collective-permute-done.14 = bf16[928,1024]{1,0:T(8,128)(2,1)S(1)} collective-permute-done((bf16[928,1024]{1,0:T(8,128)(2,1)S(1)}, bf16[928,1024]{1,0:T(8,128)(2,1)S(1)}, u32[]{:S(2)}, u32[]{:S(2)}) %collective-permute-start.14) | collective-permute-done | bytes 1900576 | tf_op jit(solution)/shard_map/ppermute | solution.py:491
  192.8 11.5 collective-permute-start.16
  230.4 11.6 fusion.147
  276.2 31.4 %recurrence.1 = (f32[4,512,640]{2,1,0:T(8,128)}, f32[4,512,640]{2,1,0:T(8,128)}, f32[4,512,640]{2,1,0:T(8,128)}, f32[4,512,640]{2,1,0:T(8,128)}, f32[4,512,640]{2,1,0:T(8,128)}, /*index=5*/f32[4,8,640]{2,1,0:T(8,128)}) custom-call(f32[4,512,640]{2,1,0:T(8,128)} %bitcast.265, f32[4,8,640]{2,1,0:T(8,128)} %slice.1419.halo_ref, f32[4,520,4]{2,1,0:T(8,128)} %copy.89.mask_ref, ...), custom_call_target="tpu_custom_call" | custom-call | flops 4000000000 | tf_op jit(solution)/shard_map/recurrence/pallas_call | solution.py:325
  371.7 39.4 %collective-permute-done.25 = bf16[512,2048]{1,0:T(8,128)(2,1)} collective-permute-done((bf16[512,2048]{1,0:T(8,128)(2,1)}, bf16[512,2048]{1,0:T(8,128)(2,1)}, u32[]{:S(2)}, u32[]{:S(2)}) %collective-permute-start.25) | collective-permute-done | bytes 2097184 | tf_op jit(solution)/shard_map/ppermute | solution.py:483
  437.3 19.5 %mlp.2 = (f32[1024,1536]{1,0:T(8,128)}, f32[1024,1536]{1,0:T(8,128)}, bf16[1024,1536]{1,0:T(8,128)(2,1)}) custom-call(s32[1]{0:T(128)} %constant.420.clone.1._, bf16[1024,2048]{1,0:T(8,128)(2,1)} %constant_dynamic-update-slice_fusion.5.refs_0_.refs_2_, bf16[1536,2048]{1,0:T(8,128)(2,1)} %get-tuple-element.845.refs_1_.refs_2_, ...), custom_call_target="tpu_custom_call" | custom-call | flops 1894838528 | tf_op jit(solution)/shard_map/mlp/pallas_call | solution.py:394
  478.6 19.4 %mlp.3 = (f32[1024,1536]{1,0:T(8,128)}, f32[1024,1536]{1,0:T(8,128)}, bf16[1024,1536]{1,0:T(8,128)(2,1)}) custom-call(s32[1]{0:T(128)} %constant.420.clone.1._, bf16[1024,2048]{1,0:T(8,128)(2,1)} %constant_dynamic-update-slice_fusion.7.refs_0_.refs_3_, bf16[1536,2048]{1,0:T(8,128)(2,1)} %get-tuple-element.845.refs_1_.refs_2_, ...), custom_call_target="tpu_custom_call" | custom-call | flops 1894838528 | tf_op jit(solution)/shard_map/mlp/pallas_call | solution.py:394
  520.8 11.7 product.10
  532.5 11.7 product.11
  556.7 11.6 gradient.12
  568.3 16.9 %mlp_back.2 = (bf16[1024,1536]{1,0:T(8,128)(2,1)}, bf16[1024,1536]{1,0:T(8,128)(2,1)}) custom-call(s32[1]{0:T(128)} %constant.420.clone.1._, bf16[1024,2048]{1,0:T(8,128)(2,1)} %constant_dynamic-update-slice_fusion.9.refs_0_.refs_3_, bf16[1536,2048]{1,0:T(8,128)(2,1)} %slice_dynamic-update-slice_fusion.2.refs_1_, f32[1024,1536]{1,0:T(8,128)} %get-tuple-element.796.refs_2_, ...), custom_call_target="tpu_custom_call" | custom-call | flops 947419264 | tf_op jit(solution)/shard_map/mlp_back/pallas_call | solution.py:394
  585.2 12.2 %collective-permute-done.40 = bf16[512,2048]{1,0:T(8,128)(2,1)} collective-permute-done((bf16[512,2048]{1,0:T(8,128)(2,1)S(1)}, bf16[512,2048]{1,0:T(8,128)(2,1)}, u32[]{:S(2)}, u32[]{:S(2)}) %collective-permute-start.40) | collective-permute-done | bytes 2097184 | tf_op jit(solution)/shard_map/ppermute | solution.py:483
  603.1 18.7 %product.13 = (bf16[512,2048]{1,0:T(8,128)(2,1)}, bf16[512,2048]{1,0:T(8,128)(2,1)}) custom-call(s32[1]{0:T(128)} %constant.420.clone.1._, bf16[1024,1536]{1,0:T(8,128)(2,1)} %get-tuple-element.892.refs_0_.refs_1_, bf16[1024,1536]{1,0:T(8,128)(2,1)} %get-tuple-element.897.refs_1_, bf16[1536,2048]{1,0:T(8,128)(2,1)} %get-tuple-element.845.refs_1_.refs_2_, ...), custom_call_target="tpu_custom_call" | custom-call | flops 1894838528 | tf_op jit(solution)/shard_map/product/pallas_call | solution.py:394
  640.0 16.6 %mlp_back.3 = (bf16[1024,1536]{1,0:T(8,128)(2,1)}, bf16[1024,1536]{1,0:T(8,128)(2,1)}) custom-call(s32[1]{0:T(128)} %constant.420.clone.1._, bf16[1024,2048]{1,0:T(8,128)(2,1)} %pad_maximum_fusion.1.refs_2_.refs_0_, bf16[1536,2048]{1,0:T(8,128)(2,1)} %slice_dynamic-update-slice_fusion.2.refs_1_, f32[1024,1536]{1,0:T(8,128)} %get-tuple-element.839.refs_2_, ...), custom_call_target="tpu_custom_call" | custom-call | flops 947419264 | tf_op jit(solution)/shard_map/mlp_back/pallas_call | solution.py:394
  656.6 11.6 gradient.13
  668.2 18.7 %product.12 = (bf16[512,2048]{1,0:T(8,128)(2,1)}, bf16[512,2048]{1,0:T(8,128)(2,1)}) custom-call(s32[1]{0:T(128)} %constant.420.clone.1._, bf16[1024,1536]{1,0:T(8,128)(2,1)} %get-tuple-element.891.refs_0_, bf16[1024,1536]{1,0:T(8,128)(2,1)} %get-tuple-element.896.refs_1_.refs_0_, bf16[1536,2048]{1,0:T(8,128)(2,1)} %get-tuple-element.845.refs_1_.refs_2_, ...), custom_call_target="tpu_custom_call" | custom-call | flops 1894838528 | tf_op jit(solution)/shard_map/product/pallas_call | solution.py:394
  704.0 11.6 gradient.17
  722.3 12.0 %gradient.16 = bf16[1536,1024]{1,0:T(8,128)(2,1)} custom-call(s32[1]{0:T(128)} %bitcast.52._, bf16[1024,1536]{1,0:T(8,128)(2,1)} %get-tuple-element.896.refs_1_.refs_0_, bf16[1024,1536]{1,0:T(8,128)(2,1)} %get-tuple-element.897.refs_1_, bf16[1024,2048]{1,0:T(8,128)(2,1)} %constant_dynamic-update-slice_fusion.5.refs_0_.refs_2_, ...), custom_call_target="tpu_custom_call" | custom-call | flops 947419264 | tf_op jit(solution)/shard_map/gradient/pallas_call | solution.py:394
  734.3 11.6 gradient.15
  745.9 11.7 gradient.14
  782.1 12.3 %fusion.148 = f32[2048,640]{1,0:T(8,128)} fusion(bf16[2048,2048]{1,0:T(8,128)(2,1)S(1)} %constant_dynamic-update-slice_fusion.11.refs_1_, bf16[640,2048]{1,0:T(8,128)(2,1)} %constant_dynamic-update-slice_fusion.42.refs_1_), kind=kOutput, calls=%fused_computation.498 | convolution fusion | flops 5368709120 | bytes 16252928 | tf_op jit(solution)/shard_map/dot_general | solution.py:18
  794.4 19.8 %adjoint.1 = (f32[4,512,640]{2,1,0:T(8,128)}, f32[4,512,640]{2,1,0:T(8,128)}, bf16[4,512,640]{2,1,0:T(8,128)(2,1)}, f32[4,8,640]{2,1,0:T(8,128)}) custom-call(f32[4,512,640]{2,1,0:T(8,128)} %bitcast.268, f32[4,512,640]{2,1,0:T(8,128)} %bitcast.260, f32[4,512,640]{2,1,0:T(8,128)} %get-tuple-element.998.state_ref, f32[4,512,640]{2,1,0:T(8,128)} %get-tuple-element.999.ga_ref, ...), custom_call_target="tpu_custom_call" | custom-call | flops 2400000000 | tf_op jit(solution)/shard_map/adjoint/pallas_call | solution.py:325
  828.3 15.9 %collective-permute-done.55 = bf16[1536,1024]{1,0:T(8,128)(2,1)} collective-permute-done((bf16[1536,1024]{1,0:T(8,128)(2,1)}, bf16[1536,1024]{1,0:T(8,128)(2,1)}, u32[]{:S(2)}, u32[]{:S(2)}) %collective-permute-start.55) | collective-permute-done | bytes 3145760 | tf_op jit(solution)/shard_map/ppermute | solution.py:486
  901.9 31.7 %recurrence_back.2 = (bf16[4,512,640]{2,1,0:T(8,128)(2,1)}, f32[4,8,640]{2,1,0:T(8,128)}, f32[4,8,640]{2,1,0:T(8,128)}, f32[640,640]{1,0:T(8,128)}, f32[640,640]{1,0:T(8,128)}, /*index=5*/f32[8,8,640]{2,1,0:T(8,128)}) custom-call(f32[4,512,640]{2,1,0:T(8,128)} %get-tuple-element.996.lam_ref, f32[4,512,640]{2,1,0:T(8,128)} %get-tuple-element.997.q_ref, ...), custom_call_target="tpu_custom_call" | custom-call | flops 4000000000 | tf_op jit(solution)/shard_map/recurrence_back/pallas_call | solution.py:325
  970.1 11.7 product.15
  981.8 11.7 product.14
  994.4 39.7 %collective-permute-done.64 = bf16[320,1024]{1,0:T(8,128)(2,1)} collective-permute-done((bf16[320,1024]{1,0:T(8,128)(2,1)}, bf16[320,1024]{1,0:T(8,128)(2,1)}, u32[]{:S(2)}, u32[]{:S(2)}) %collective-permute-start.64) | collective-permute-done | bytes 655392 | tf_op jit(solution)/shard_map/ppermute | solution.py:491
  1061.1 38.3 %collective-permute-done.67 = bf16[512,2048]{1,0:T(8,128)(2,1)} collective-permute-done((bf16[512,2048]{1,0:T(8,128)(2,1)}, bf16[512,2048]{1,0:T(8,128)(2,1)}, u32[]{:S(2)}, u32[]{:S(2)}) %collective-permute-start.67) | collective-permute-done | bytes 2097184 | tf_op jit(solution)/shard_map/ppermute | solution.py:483
  1122.2 32.8 %collective-permute-done.74 = bf16[2,1632,256]{2,1,0:T(8,128)(2,1)S(1)} collective-permute-done((bf16[2,1632,256]{2,1,0:T(8,128)(2,1)S(1)}, bf16[2,1632,256]{2,1,0:T(8,128)(2,1)S(1)}, u32[]{:S(2)}, u32[]{:S(2)}) %collective-permute-start.74) | collective-permute-done | bytes 1671200 | tf_op jit(solution)/shard_map/ppermute | solution.py:483
  (720 shorter events, 597.5 us)
Async XLA Ops:
  76.6 59.0 %collective-permute-start.9 = (bf16[1280,1024]{1,0:T(8,128)(2,1)S(1)}, bf16[1280,1024]{1,0:T(8,128)(2,1)}, u32[]{:S(2)}, u32[]{:S(2)}) collective-permute-start(bf16[1280,1024]{1,0:T(8,128)(2,1)S(1)} %constant_dynamic-update-slice_fusion.36), channel_id=1, source_target_pairs={{0,16},{4,20},{8,24},{12,28},{16,0},{20,4},{24,8},{28,12},{1,17},{... | collective-permute-start | bytes 7864328 | tf_op jit(solution)/shard_map/ppermute | solution.py:486
  80.4 51.0 %collective-permute-start.5 = (bf16[544,2048]{1,0:T(8,128)(2,1)}, bf16[544,2048]{1,0:T(8,128)(2,1)}, u32[]{:S(2)}, u32[]{:S(2)}) collective-permute-start(bf16[544,2048]{1,0:T(8,128)(2,1)} %pad_maximum_fusion.6), channel_id=1, source_target_pairs={{0,8},{4,12},{8,0},{12,4},{16,24},{20,28},{24,16},{28,20},{1,9},{5... | collective-permute-start | bytes 6684680 | tf_op jit(solution)/shard_map/ppermute | solution.py:483
  139.5 49.5 %collective-permute-start.15 = (bf16[1056,1024]{1,0:T(8,128)(2,1)S(1)}, bf16[1056,1024]{1,0:T(8,128)(2,1)S(1)}, u32[]{:S(2)}, u32[]{:S(2)}) collective-permute-start(bf16[1056,1024]{1,0:T(8,128)(2,1)S(1)} %pad_maximum_fusion.8), channel_id=1, source_target_pairs={{0,16},{4,20},{8,24},{12,28},{16,0},{20,4},{24,8},{28,12},{1,17},{... | collective-permute-start | bytes 6488072 | tf_op jit(solution)/shard_map/ppermute | solution.py:486
  192.8 72.5 %collective-permute-start.16 = (bf16[1312,1024]{1,0:T(8,128)(2,1)}, bf16[1312,1024]{1,0:T(8,128)(2,1)}, u32[]{:S(2)}, u32[]{:S(2)}) collective-permute-start(bf16[1312,1024]{1,0:T(8,128)(2,1)} %pad_maximum_fusion.2), channel_id=1, source_target_pairs={{0,1},{1,2},{2,3},{3,0},{4,5},{5,6},{6,7},{7,4},{8,9},{9,10},{10,1... | collective-permute-start | bytes 8060936 | tf_op jit(solution)/shard_map/ppermute | solution.py:491
  204.3 61.0 %collective-permute-start.17 = (bf16[1312,1024]{1,0:T(8,128)(2,1)}, bf16[1312,1024]{1,0:T(8,128)(2,1)}, u32[]{:S(2)}, u32[]{:S(2)}) collective-permute-start(bf16[1312,1024]{1,0:T(8,128)(2,1)} %pad_maximum_fusion.2), channel_id=1, source_target_pairs={{0,16},{4,20},{8,24},{12,28},{16,0},{20,4},{24,8},{28,12},{1,17},{... | collective-permute-start | bytes 8060936 | tf_op jit(solution)/shard_map/ppermute | solution.py:486
  363.2 47.9 %collective-permute-start.25 = (bf16[512,2048]{1,0:T(8,128)(2,1)}, bf16[512,2048]{1,0:T(8,128)(2,1)}, u32[]{:S(2)}, u32[]{:S(2)}) collective-permute-start(bf16[512,2048]{1,0:T(8,128)(2,1)} %add_convert_fusion.4), channel_id=1, source_target_pairs={{0,8},{4,12},{8,0},{12,4},{16,24},{20,28},{24,16},{28,20},{1,9},{5... | collective-permute-start | bytes 6291464 | tf_op jit(solution)/shard_map/ppermute | solution.py:483
  365.8 53.2 %collective-permute-start.27 = (bf16[1152,1024]{1,0:T(8,128)(2,1)}, bf16[1152,1024]{1,0:T(8,128)(2,1)}, u32[]{:S(2)}, u32[]{:S(2)}) collective-permute-start(bf16[1152,1024]{1,0:T(8,128)(2,1)} %pad_maximum_fusion.4), channel_id=1, source_target_pairs={{0,16},{4,20},{8,24},{12,28},{16,0},{20,4},{24,8},{28,12},{1,17},{... | collective-permute-start | bytes 7077896 | tf_op jit(solution)/shard_map/ppermute | solution.py:486
  368.9 49.1 %collective-permute-start.28 = (bf16[1280,512]{1,0:T(8,128)(2,1)S(1)}, bf16[1280,512]{1,0:T(8,128)(2,1)S(1)}, u32[]{:S(2)}, u32[]{:S(2)}) collective-permute-start(bf16[1280,512]{1,0:T(8,128)(2,1)S(1)} %pad_maximum_fusion.16), channel_id=1, source_target_pairs={{0,1},{1,2},{2,3},{3,0},{4,5},{5,6},{6,7},{7,4},{8,9},{9,10},{10,1... | collective-permute-start | bytes 3932168 | tf_op jit(solution)/shard_map/ppermute | solution.py:491
  369.0 49.1 %collective-permute-start.29 = (bf16[512,512]{1,0:T(8,128)(2,1)S(1)}, bf16[512,512]{1,0:T(8,128)(2,1)S(1)}, u32[]{:S(2)}, u32[]{:S(2)}) collective-permute-start(bf16[512,512]{1,0:T(8,128)(2,1)S(1)} %get-tuple-element.1265), channel_id=1, source_target_pairs={{0,3},{1,0},{2,1},{3,2},{4,7},{5,4},{6,5},{7,6},{8,11},{9,8},{10,9... | collective-permute-start | bytes 1572872 | tf_op jit(solution)/shard_map/ppermute | solution.py:491
  419.3 48.0 %collective-permute-start.32 = (bf16[512,2048]{1,0:T(8,128)(2,1)S(1)}, bf16[512,2048]{1,0:T(8,128)(2,1)}, u32[]{:S(2)}, u32[]{:S(2)}) collective-permute-start(bf16[512,2048]{1,0:T(8,128)(2,1)S(1)} %get-tuple-element.726), channel_id=1, source_target_pairs={{0,8},{4,12},{8,0},{12,4},{16,24},{20,28},{24,16},{28,20},{1,9},{5... | collective-permute-start | bytes 6291464 | tf_op jit(solution)/shard_map/ppermute | solution.py:483
  549.2 48.2 %collective-permute-start.40 = (bf16[512,2048]{1,0:T(8,128)(2,1)S(1)}, bf16[512,2048]{1,0:T(8,128)(2,1)}, u32[]{:S(2)}, u32[]{:S(2)}) collective-permute-start(bf16[512,2048]{1,0:T(8,128)(2,1)S(1)} %add_convert_fusion.3), channel_id=1, source_target_pairs={{0,8},{4,12},{8,0},{12,4},{16,24},{20,28},{24,16},{28,20},{1,9},{5... | collective-permute-start | bytes 6291464 | tf_op jit(solution)/shard_map/ppermute | solution.py:483
  621.7 70.8 %collective-permute-start.44 = (bf16[1536,1024]{1,0:T(8,128)(2,1)}, bf16[1536,1024]{1,0:T(8,128)(2,1)}, u32[]{:S(2)}, u32[]{:S(2)}) collective-permute-start(bf16[1536,1024]{1,0:T(8,128)(2,1)} %gradient.12), channel_id=1, source_target_pairs={{0,16},{4,20},{8,24},{12,28},{16,0},{20,4},{24,8},{28,12},{1,17},{... | collective-permute-start | bytes 9437192 | tf_op jit(solution)/shard_map/ppermute | solution.py:486
  629.8 57.2 %collective-permute-start.43 = (bf16[512,2048]{1,0:T(8,128)(2,1)}, bf16[512,2048]{1,0:T(8,128)(2,1)}, u32[]{:S(2)}, u32[]{:S(2)}) collective-permute-start(bf16[512,2048]{1,0:T(8,128)(2,1)} %add_convert_fusion.1), channel_id=1, source_target_pairs={{0,8},{4,12},{8,0},{12,4},{16,24},{20,28},{24,16},{28,20},{1,9},{5... | collective-permute-start | bytes 6291464 | tf_op jit(solution)/shard_map/ppermute | solution.py:483
  631.8 57.4 %collective-permute-start.45 = (bf16[512,512]{1,0:T(8,128)(2,1)S(1)}, bf16[512,512]{1,0:T(8,128)(2,1)S(1)}, u32[]{:S(2)}, u32[]{:S(2)}) collective-permute-start(bf16[512,512]{1,0:T(8,128)(2,1)S(1)} %get-tuple-element.1263), channel_id=1, source_target_pairs={{0,1},{1,2},{2,3},{3,0},{4,5},{5,6},{6,7},{7,4},{8,9},{9,10},{10,1... | collective-permute-start | bytes 1572872 | tf_op jit(solution)/shard_map/ppermute | solution.py:491
  635.9 53.4 %collective-permute-start.46 = (bf16[512,512]{1,0:T(8,128)(2,1)S(1)}, bf16[512,512]{1,0:T(8,128)(2,1)S(1)}, u32[]{:S(2)}, u32[]{:S(2)}) collective-permute-start(bf16[512,512]{1,0:T(8,128)(2,1)S(1)} %get-tuple-element.1262), channel_id=1, source_target_pairs={{0,2},{1,3},{2,0},{3,1},{4,6},{5,7},{6,4},{7,5},{8,10},{9,11},{10,... | collective-permute-start | bytes 1572872 | tf_op jit(solution)/shard_map/ppermute | solution.py:491
  640.0 49.3 %collective-permute-start.47 = (bf16[512,512]{1,0:T(8,128)(2,1)S(1)}, bf16[512,512]{1,0:T(8,128)(2,1)S(1)}, u32[]{:S(2)}, u32[]{:S(2)}) collective-permute-start(bf16[512,512]{1,0:T(8,128)(2,1)S(1)} %get-tuple-element.1261), channel_id=1, source_target_pairs={{0,3},{1,0},{2,1},{3,2},{4,7},{5,4},{6,5},{7,6},{8,11},{9,8},{10,9... | collective-permute-start | bytes 1572872 | tf_op jit(solution)/shard_map/ppermute | solution.py:491
  692.6 70.8 %collective-permute-start.52 = (bf16[1536,1024]{1,0:T(8,128)(2,1)}, bf16[1536,1024]{1,0:T(8,128)(2,1)}, u32[]{:S(2)}, u32[]{:S(2)}) collective-permute-start(bf16[1536,1024]{1,0:T(8,128)(2,1)} %gradient.13), channel_id=1, source_target_pairs={{0,16},{4,20},{8,24},{12,28},{16,0},{20,4},{24,8},{28,12},{1,17},{... | collective-permute-start | bytes 9437192 | tf_op jit(solution)/shard_map/ppermute | solution.py:486
  703.1 60.3 %collective-permute-start.49 = (bf16[512,2048]{1,0:T(8,128)(2,1)}, bf16[512,2048]{1,0:T(8,128)(2,1)}, u32[]{:S(2)}, u32[]{:S(2)}) collective-permute-start(bf16[512,2048]{1,0:T(8,128)(2,1)} %get-tuple-element.921), channel_id=1, source_target_pairs={{0,8},{4,12},{8,0},{12,4},{16,24},{20,28},{24,16},{28,20},{1,9},{5... | collective-permute-start | bytes 6291464 | tf_op jit(solution)/shard_map/ppermute | solution.py:483
  704.0 59.4 %collective-permute-start.50 = (bf16[512,2048]{1,0:T(8,128)(2,1)}, bf16[512,2048]{1,0:T(8,128)(2,1)}, u32[]{:S(2)}, u32[]{:S(2)}) collective-permute-start(bf16[512,2048]{1,0:T(8,128)(2,1)} %get-tuple-element.921), channel_id=1, source_target_pairs={{0,4},{4,0},{8,12},{12,8},{16,20},{20,16},{24,28},{28,24},{1,5},{5... | collective-permute-start | bytes 6291464 | tf_op jit(solution)/shard_map/ppermute | solution.py:483
  768.2 60.0 %collective-permute-start.54 = (bf16[768,1024]{1,0:T(8,128)(2,1)}, bf16[768,1024]{1,0:T(8,128)(2,1)}, u32[]{:S(2)}, u32[]{:S(2)}) collective-permute-start(bf16[768,1024]{1,0:T(8,128)(2,1)} %pad_maximum_fusion.13), channel_id=1, source_target_pairs={{0,1},{1,2},{2,3},{3,0},{4,5},{5,6},{6,7},{7,4},{8,9},{9,10},{10,1... | collective-permute-start | bytes 4718600 | tf_op jit(solution)/shard_map/ppermute | solution.py:491
  773.6 70.5 %collective-permute-start.55 = (bf16[1536,1024]{1,0:T(8,128)(2,1)}, bf16[1536,1024]{1,0:T(8,128)(2,1)}, u32[]{:S(2)}, u32[]{:S(2)}) collective-permute-start(bf16[1536,1024]{1,0:T(8,128)(2,1)} %gradient.16), channel_id=1, source_target_pairs={{0,16},{4,20},{8,24},{12,28},{16,0},{20,4},{24,8},{28,12},{1,17},{... | collective-permute-start | bytes 9437192 | tf_op jit(solution)/shard_map/ppermute | solution.py:486
  868.6 65.2 %collective-permute-start.61 = (bf16[1280,1024]{1,0:T(8,128)(2,1)}, bf16[1280,1024]{1,0:T(8,128)(2,1)}, u32[]{:S(2)}, u32[]{:S(2)}) collective-permute-start(bf16[1280,1024]{1,0:T(8,128)(2,1)} %pad_maximum_fusion.3), channel_id=1, source_target_pairs={{0,16},{4,20},{8,24},{12,28},{16,0},{20,4},{24,8},{28,12},{1,17},{... | collective-permute-start | bytes 7864328 | tf_op jit(solution)/shard_map/ppermute | solution.py:486
  876.7 57.1 %collective-permute-start.60 = (bf16[1152,1024]{1,0:T(8,128)(2,1)}, bf16[1152,1024]{1,0:T(8,128)(2,1)}, u32[]{:S(2)}, u32[]{:S(2)}) collective-permute-start(bf16[1152,1024]{1,0:T(8,128)(2,1)} %pad_maximum_fusion.5), channel_id=1, source_target_pairs={{0,1},{1,2},{2,3},{3,0},{4,5},{5,6},{6,7},{7,4},{8,9},{9,10},{10,1... | collective-permute-start | bytes 7077896 | tf_op jit(solution)/shard_map/ppermute | solution.py:491
  943.2 93.5 %collective-permute-start.65 = (bf16[1088,1024]{1,0:T(8,128)(2,1)}, bf16[1088,1024]{1,0:T(8,128)(2,1)}, u32[]{:S(2)}, u32[]{:S(2)}) collective-permute-start(bf16[1088,1024]{1,0:T(8,128)(2,1)} %pad_maximum_fusion.7), channel_id=1, source_target_pairs={{0,1},{1,2},{2,3},{3,0},{4,5},{5,6},{6,7},{7,4},{8,9},{9,10},{10,1... | collective-permute-start | bytes 6684680 | tf_op jit(solution)/shard_map/ppermute | solution.py:491
  953.3 83.4 %collective-permute-start.62 = (bf16[640,1024]{1,0:T(8,128)(2,1)}, bf16[640,1024]{1,0:T(8,128)(2,1)}, u32[]{:S(2)}, u32[]{:S(2)}) collective-permute-start(bf16[640,1024]{1,0:T(8,128)(2,1)} %gradient.23), channel_id=1, source_target_pairs={{0,16},{4,20},{8,24},{12,28},{16,0},{20,4},{24,8},{28,12},{1,17},{... | collective-permute-start | bytes 3932168 | tf_op jit(solution)/shard_map/ppermute | solution.py:486
  955.7 78.4 %collective-permute-start.64 = (bf16[320,1024]{1,0:T(8,128)(2,1)}, bf16[320,1024]{1,0:T(8,128)(2,1)}, u32[]{:S(2)}, u32[]{:S(2)}) collective-permute-start(bf16[320,1024]{1,0:T(8,128)(2,1)} %pad_maximum_fusion.21), channel_id=1, source_target_pairs={{0,2},{1,3},{2,0},{3,1},{4,6},{5,7},{6,4},{7,5},{8,10},{9,11},{10,... | collective-permute-start | bytes 1966088 | tf_op jit(solution)/shard_map/ppermute | solution.py:491
  959.1 77.6 %collective-permute-start.63 = (bf16[320,1024]{1,0:T(8,128)(2,1)}, bf16[320,1024]{1,0:T(8,128)(2,1)}, u32[]{:S(2)}, u32[]{:S(2)}) collective-permute-start(bf16[320,1024]{1,0:T(8,128)(2,1)} %pad_maximum_fusion.20), channel_id=1, source_target_pairs={{0,3},{1,0},{2,1},{3,2},{4,7},{5,4},{6,5},{7,6},{8,11},{9,8},{10,9... | collective-permute-start | bytes 1966088 | tf_op jit(solution)/shard_map/ppermute | solution.py:491
  1044.0 58.7 %collective-permute-start.72 = (bf16[544,1024]{1,0:T(8,128)(2,1)S(1)}, bf16[544,1024]{1,0:T(8,128)(2,1)}, u32[]{:S(2)}, u32[]{:S(2)}) collective-permute-start(bf16[544,1024]{1,0:T(8,128)(2,1)S(1)} %pad_maximum_fusion.17), channel_id=1, source_target_pairs={{0,1},{1,2},{2,3},{3,0},{4,5},{5,6},{6,7},{7,4},{8,9},{9,10},{10,1... | collective-permute-start | bytes 3342344 | tf_op jit(solution)/shard_map/ppermute | solution.py:491
  1044.1 58.7 %collective-permute-start.70 = (bf16[160,1024]{1,0:T(8,128)(2,1)}, bf16[160,1024]{1,0:T(8,128)(2,1)}, u32[]{:S(2)}, u32[]{:S(2)}) collective-permute-start(bf16[160,1024]{1,0:T(8,128)(2,1)} %get-tuple-element.1215), channel_id=1, source_target_pairs={{0,3},{1,0},{2,1},{3,2},{4,7},{5,4},{6,5},{7,6},{8,11},{9,8},{10,9... | collective-permute-start | bytes 983048 | tf_op jit(solution)/shard_map/ppermute | solution.py:491
  1046.3 56.5 %collective-permute-start.71 = (bf16[160,1024]{1,0:T(8,128)(2,1)}, bf16[160,1024]{1,0:T(8,128)(2,1)}, u32[]{:S(2)}, u32[]{:S(2)}) collective-permute-start(bf16[160,1024]{1,0:T(8,128)(2,1)} %get-tuple-element.1214), channel_id=1, source_target_pairs={{0,2},{1,3},{2,0},{3,1},{4,6},{5,7},{6,4},{7,5},{8,10},{9,11},{10,... | collective-permute-start | bytes 983048 | tf_op jit(solution)/shard_map/ppermute | solution.py:491
  1051.2 48.2 %collective-permute-start.67 = (bf16[512,2048]{1,0:T(8,128)(2,1)}, bf16[512,2048]{1,0:T(8,128)(2,1)}, u32[]{:S(2)}, u32[]{:S(2)}) collective-permute-start(bf16[512,2048]{1,0:T(8,128)(2,1)} %add_convert_fusion), channel_id=1, source_target_pairs={{0,8},{4,12},{8,0},{12,4},{16,24},{20,28},{24,16},{28,20},{1,9},{5... | collective-permute-start | bytes 6291464 | tf_op jit(solution)/shard_map/ppermute | solution.py:483
  1118.7 50.0 %collective-permute-start.75 = (bf16[592,512]{1,0:T(8,128)(2,1)S(1)}, bf16[592,512]{1,0:T(8,128)(2,1)S(1)}, u32[]{:S(2)}, u32[]{:S(2)}) collective-permute-start(bf16[592,512]{1,0:T(8,128)(2,1)S(1)} %pad_maximum_fusion.23), channel_id=1, source_target_pairs={{0,1},{1,2},{2,3},{3,0},{4,5},{5,6},{6,7},{7,4},{8,9},{9,10},{10,1... | collective-permute-start | bytes 1818632 | tf_op jit(solution)/shard_map/ppermute | solution.py:491
  (136 other events, 2097.2 us)
